TPU v7x, 32 devices: a whole 2x2x4 slice. The times are simulated.
32 devices in a mesh: grid: 8 (over z, y), orb: 4 (over x, core).
Axes of the slice: x: 2, y: 2, z: 4, core: 2. Of those that a mesh axis runs over, the one named last changes fastest.
Arguments:
- orbitals: float32 [16, 64, 32, 128], P('orb', 'grid'), may hold values from -6 to 6
- potential: float32 [64, 32, 128], P('grid'), may hold values from -1 to 1
Outputs:
- filtered: float32 [16, 64, 32, 128], P('orb', 'grid')
- correlation: float32 [16, 16], P('orb')
- hamiltonian: float32 [16, 16], P('orb')
All inputs are finite; a program needn't handle non-finite values.
Results may differ from a plain program's by a relative error of at most 0.00005.
Values sent between devices are 32-bit elements; how exact they have to be, the bound alone decides.
No kernel may reach another device: no remote copies, remote signals or barrier semaphores. Data moves between devices by JAX's collectives and lax.ppermute only.
A program may use at most 64 MiB of HBM per device.

v0:
```python
import jax
import jax.numpy as jnp
from jax import lax
from jax.sharding import PartitionSpec as P

COEFS = (-205.0 / 72.0, 8.0 / 5.0, -1.0 / 5.0, 8.0 / 315.0, -1.0 / 560.0)
LOWER = -1.0
CUT = 4.0
UPPER = 10.0


def padded_2(value, sides, width):
    for axis, dim in sides:
        size, length = (lax.axis_size(axis), value.shape[dim])
        up = [(i, (i + 1) % size) for i in range(size)]
        down = [(j, i) for i, j in up]
        last = lax.slice_in_dim(value, length - width, length, axis=dim)
        first = lax.slice_in_dim(value, 0, width, axis=dim)
        before = lax.ppermute(last, axis, up)
        after = lax.ppermute(first, axis, down)
        value = jnp.concatenate([before, value, after], axis=dim)
    return value


def apply_ham(field, potential):
    width = field.shape[1]
    padded = padded_2(field, (("grid", 1),), 4)
    lap = 3.0 * COEFS[0] * field
    for shift_by in range(1, 5):
        lap = lap + COEFS[shift_by] * (
            padded[:, 4 + shift_by : 4 + shift_by + width]
            + padded[:, 4 - shift_by : 4 - shift_by + width]
        )
    for axis_pos in (2, 3):
        for shift_by in range(1, 5):
            lap = lap + COEFS[shift_by] * (
                jnp.roll(field, shift_by, axis_pos) + jnp.roll(field, -shift_by, axis_pos)
            )
    return -0.5 * lap + potential[None] * field


def cell_product(left, right):
    return lax.dot_general(left, right, (((1,), (1,)), ((), ())), precision=lax.Precision.HIGHEST)


def per_device(orbitals, potential):
    half = (UPPER - CUT) / 2.0
    centre = (UPPER + CUT) / 2.0
    first_sigma = half / (LOWER - centre)
    previous = orbitals
    current = (apply_ham(orbitals, potential) - centre * orbitals) * (first_sigma / half)
    sigma = first_sigma
    for step in range(3):
        sigma_new = 1.0 / (2.0 / first_sigma - sigma)
        following = (
            2.0 * sigma_new / half * (apply_ham(current, potential) - centre * current)
            - sigma * sigma_new * previous
        )
        previous = current
        current = following
        sigma = sigma_new
    applied = apply_ham(current, potential)
    own = current.shape[0]
    cells = current.shape[1] * lax.axis_size("grid") * current.shape[2] * current.shape[3]
    mine_y = current.reshape(own, -1)
    mine_h = applied.reshape(own, -1)
    piece = lax.all_gather(current, "orb", axis=0, tiled=True)
    flat = piece.reshape(piece.shape[0], -1)
    partial_rows = jnp.stack((cell_product(mine_y, flat), cell_product(mine_h, flat)))
    totals = lax.psum(partial_rows, "grid")
    correlation = totals[0] / cells
    hamiltonian = totals[1] / cells
    return (current, correlation, hamiltonian)


def solution(mesh):
    placed = (P("orb", "grid", None, None), P("grid", None, None))
    return jax.shard_map(
        per_device,
        mesh=mesh,
        in_specs=placed,
        out_specs=(P("orb", "grid", None, None), P("orb", None), P("orb", None)),
        check_vma=False,
    )
```

profile of v0, /device:TPU:0, one launch (start us, length us, event | category | flops | bytes accessed | tf_op | source)
XLA Modules:
  0.0 146.2 jit_solution(956359157017652519)
XLA Ops:
  8.4 3.0 %collective-permute-start.1 = (f32[4,4,32,128]{3,2,1,0:T(8,128)S(1)}, f32[4,4,32,128]{3,2,1,0:T(8,128)S(1)}, u32[]{:S(2)}, u32[]{:S(2)}) collective-permute-start(f32[4,4,32,128]{3,2,1,0:T(8,128)S(1)} %get-tuple-element.145), channel_id=1, source_target_pairs={{0,4},{4,8},{8,12},{12,16},{16,20},{20,24},{24,28},{28,0},{1,5},{5... | collective-permute-start | bytes 786440 | tf_op jit(solution)/shard_map/ppermute | solution.py:19
  11.4 3.1 %collective-permute-start = (f32[4,4,32,128]{3,2,1,0:T(8,128)S(1)}, f32[4,4,32,128]{3,2,1,0:T(8,128)S(1)}, u32[]{:S(2)}, u32[]{:S(2)}) collective-permute-start(f32[4,4,32,128]{3,2,1,0:T(8,128)S(1)} %get-tuple-element.144), channel_id=1, source_target_pairs={{4,0},{8,4},{12,8},{16,12},{20,16},{24,20},{28,24},{0,28},{5,1},{9... | collective-permute-start | bytes 786440 | tf_op jit(solution)/shard_map/ppermute | solution.py:20
  18.6 3.9 %collective-permute-done.1 = f32[4,4,32,128]{3,2,1,0:T(8,128)S(1)} collective-permute-done((f32[4,4,32,128]{3,2,1,0:T(8,128)S(1)}, f32[4,4,32,128]{3,2,1,0:T(8,128)S(1)}, u32[]{:S(2)}, u32[]{:S(2)}) %collective-permute-start.1) | collective-permute-done | bytes 262176 | tf_op jit(solution)/shard_map/ppermute | solution.py:19
  24.8 2.6 %broadcast_multiply_fusion = (f32[4,8,32,128]{3,2,1,0:T(8,128)S(1)}, f32[4,8,32,128]{3,2,1,0:T(8,128)S(1)}) fusion(f32[4,8,32,128]{3,2,1,0:T(8,128)S(1)} %copy-done.1, f32[8,32,128]{2,1,0:T(8,128)S(1)} %copy-done.3, f32[4,8,32,4]{3,2,1,0:T(8,128)S(1)} %get-tuple-element.177, f32[4,8,32,124]{3,2,1,0:T(8,128)S(1)} %get-tuple-element.179, ...), kind=kLoop, calls=%fused_computation.285 | loop fusion | flops 7733248 | bytes 14286848 | tf_op jit(solution)/shard_map/mul | solution.py:51
  30.1 4.3 %collective-permute-start.2 = (f32[4,4,32,128]{3,2,1,0:T(8,128)S(1)}, f32[4,4,32,128]{3,2,1,0:T(8,128)S(1)}, u32[]{:S(2)}, u32[]{:S(2)}) collective-permute-start(f32[4,4,32,128]{3,2,1,0:T(8,128)S(1)} %get-tuple-element.110), channel_id=1, source_target_pairs={{4,0},{8,4},{12,8},{16,12},{20,16},{24,20},{28,24},{0,28},{5,1},{9... | collective-permute-start | bytes 786440 | tf_op jit(solution)/shard_map/ppermute | solution.py:20
  34.5 5.9 %collective-permute-done.3 = f32[4,4,32,128]{3,2,1,0:T(8,128)S(1)} collective-permute-done((f32[4,4,32,128]{3,2,1,0:T(8,128)S(1)}, f32[4,4,32,128]{3,2,1,0:T(8,128)S(1)}, u32[]{:S(2)}, u32[]{:S(2)}) %collective-permute-start.3) | collective-permute-done | bytes 262176 | tf_op jit(solution)/shard_map/ppermute | solution.py:19
  40.4 3.8 %collective-permute-done.2 = f32[4,4,32,128]{3,2,1,0:T(8,128)S(1)} collective-permute-done((f32[4,4,32,128]{3,2,1,0:T(8,128)S(1)}, f32[4,4,32,128]{3,2,1,0:T(8,128)S(1)}, u32[]{:S(2)}, u32[]{:S(2)}) %collective-permute-start.2) | collective-permute-done | bytes 262176 | tf_op jit(solution)/shard_map/ppermute | solution.py:20
  44.2 2.6 %multiply_subtract_fusion.2 = f32[4,8,32,128]{3,2,1,0:T(8,128)S(1)} fusion(f32[4,8,32,128]{3,2,1,0:T(8,128)S(1)} %copy-done.1, f32[4,8,32,128]{3,2,1,0:T(8,128)S(1)} %get-tuple-element.7, f32[4,8,32,4]{3,2,1,0:T(8,128)S(1)} %get-tuple-element.141, f32[4,8,32,124]{3,2,1,0:T(8,128)S(1)} %get-tuple-element.143, f32[4,8,32,124]{3,2,1,0:T(8,128)S(1)} %get-tuple-element.142, ...), kind=kLoop, calls=%fused_computation.284 | loop fusion | flops 9043968 | bytes 11141120 | tf_op jit(solution)/shard_map/sub | solution.py:56
  49.1 4.7 %collective-permute-start.4 = (f32[4,4,32,128]{3,2,1,0:T(8,128)S(1)}, f32[4,4,32,128]{3,2,1,0:T(8,128)S(1)}, u32[]{:S(2)}, u32[]{:S(2)}) collective-permute-start(f32[4,4,32,128]{3,2,1,0:T(8,128)S(1)} %get-tuple-element.76), channel_id=1, source_target_pairs={{4,0},{8,4},{12,8},{16,12},{20,16},{24,20},{28,24},{0,28},{5,1},{9... | collective-permute-start | bytes 786440 | tf_op jit(solution)/shard_map/ppermute | solution.py:20
  53.9 6.2 %collective-permute-done.5 = f32[4,4,32,128]{3,2,1,0:T(8,128)S(1)} collective-permute-done((f32[4,4,32,128]{3,2,1,0:T(8,128)S(1)}, f32[4,4,32,128]{3,2,1,0:T(8,128)S(1)}, u32[]{:S(2)}, u32[]{:S(2)}) %collective-permute-start.5) | collective-permute-done | bytes 262176 | tf_op jit(solution)/shard_map/ppermute | solution.py:19
  60.1 3.7 %collective-permute-done.4 = f32[4,4,32,128]{3,2,1,0:T(8,128)S(1)} collective-permute-done((f32[4,4,32,128]{3,2,1,0:T(8,128)S(1)}, f32[4,4,32,128]{3,2,1,0:T(8,128)S(1)}, u32[]{:S(2)}, u32[]{:S(2)}) %collective-permute-start.4) | collective-permute-done | bytes 262176 | tf_op jit(solution)/shard_map/ppermute | solution.py:20
  63.8 2.6 %multiply_subtract_fusion.1 = f32[4,8,32,128]{3,2,1,0:T(8,128)S(1)} fusion(f32[4,8,32,128]{3,2,1,0:T(8,128)S(1)} %get-tuple-element.7, f32[4,8,32,128]{3,2,1,0:T(8,128)S(1)} %multiply_subtract_fusion.2, f32[4,8,32,4]{3,2,1,0:T(8,128)S(1)} %get-tuple-element.107, f32[4,8,32,124]{3,2,1,0:T(8,128)S(1)} %get-tuple-element.109, ...), kind=kLoop, calls=%fused_computation.283 | loop fusion | flops 9043968 | bytes 10616832 | tf_op jit(solution)/shard_map/sub | solution.py:56
  68.7 4.7 %collective-permute-start.6 = (f32[4,4,32,128]{3,2,1,0:T(8,128)S(1)}, f32[4,4,32,128]{3,2,1,0:T(8,128)S(1)}, u32[]{:S(2)}, u32[]{:S(2)}) collective-permute-start(f32[4,4,32,128]{3,2,1,0:T(8,128)S(1)} %get-tuple-element.42), channel_id=1, source_target_pairs={{4,0},{8,4},{12,8},{16,12},{20,16},{24,20},{28,24},{0,28},{5,1},{9... | collective-permute-start | bytes 786440 | tf_op jit(solution)/shard_map/ppermute | solution.py:20
  73.5 6.0 %collective-permute-done.7 = f32[4,4,32,128]{3,2,1,0:T(8,128)S(1)} collective-permute-done((f32[4,4,32,128]{3,2,1,0:T(8,128)S(1)}, f32[4,4,32,128]{3,2,1,0:T(8,128)S(1)}, u32[]{:S(2)}, u32[]{:S(2)}) %collective-permute-start.7) | collective-permute-done | bytes 262176 | tf_op jit(solution)/shard_map/ppermute | solution.py:19
  79.5 3.9 %collective-permute-done.6 = f32[4,4,32,128]{3,2,1,0:T(8,128)S(1)} collective-permute-done((f32[4,4,32,128]{3,2,1,0:T(8,128)S(1)}, f32[4,4,32,128]{3,2,1,0:T(8,128)S(1)}, u32[]{:S(2)}, u32[]{:S(2)}) %collective-permute-start.6) | collective-permute-done | bytes 262176 | tf_op jit(solution)/shard_map/ppermute | solution.py:20
  83.4 3.3 %multiply_subtract_fusion = f32[4,8,32,128]{3,2,1,0:T(8,128)} fusion(f32[4,8,32,128]{3,2,1,0:T(8,128)S(1)} %multiply_subtract_fusion.2, f32[4,8,32,128]{3,2,1,0:T(8,128)S(1)} %multiply_subtract_fusion.1, f32[4,8,32,4]{3,2,1,0:T(8,128)S(1)} %get-tuple-element.73, f32[4,8,32,124]{3,2,1,0:T(8,128)S(1)} %get-tuple-element.75, ...), kind=kLoop, calls=%fused_computation.282 | loop fusion | flops 9043968 | bytes 10616832 | tf_op jit(solution)/shard_map/sub | solution.py:56
  88.3 4.7 %collective-permute-start.8 = (f32[4,4,32,128]{3,2,1,0:T(8,128)S(1)}, f32[4,4,32,128]{3,2,1,0:T(8,128)S(1)}, u32[]{:S(2)}, u32[]{:S(2)}) collective-permute-start(f32[4,4,32,128]{3,2,1,0:T(8,128)S(1)} %get-tuple-element.40), channel_id=1, source_target_pairs={{4,0},{8,4},{12,8},{16,12},{20,16},{24,20},{28,24},{0,28},{5,1},{9... | collective-permute-start | bytes 786440 | tf_op jit(solution)/shard_map/ppermute | solution.py:20
  94.9 4.2 %collective-permute-done.9 = f32[4,4,32,128]{3,2,1,0:T(8,128)S(1)} collective-permute-done((f32[4,4,32,128]{3,2,1,0:T(8,128)S(1)}, f32[4,4,32,128]{3,2,1,0:T(8,128)S(1)}, u32[]{:S(2)}, u32[]{:S(2)}) %collective-permute-start.9) | collective-permute-done | bytes 262176 | tf_op jit(solution)/shard_map/ppermute | solution.py:19
  99.1 2.6 %collective-permute-done.8 = f32[4,4,32,128]{3,2,1,0:T(8,128)S(1)} collective-permute-done((f32[4,4,32,128]{3,2,1,0:T(8,128)S(1)}, f32[4,4,32,128]{3,2,1,0:T(8,128)S(1)}, u32[]{:S(2)}, u32[]{:S(2)}) %collective-permute-start.8) | collective-permute-done | bytes 262176 | tf_op jit(solution)/shard_map/ppermute | solution.py:20
  101.8 2.5 %fusion.24 = f32[4,8,32,128]{3,2,1,0:T(8,128)S(1)} fusion(f32[4,8,32,128]{3,2,1,0:T(8,128)S(1)} %copy-done, f32[4,4,32,128]{3,2,1,0:T(8,128)S(1)} %collective-permute-done.9, f32[4,4,32,128]{3,2,1,0:T(8,128)S(1)} %collective-permute-done.8, f32[4,8,31,128]{3,2,1,0:T(8,128)S(1)} %get-tuple-element.37, f32[4,8,1,128]{3,2,1,0:T(1,128)S(1)} %get-tuple-element.39, ...), kind=kLoop, calls=%fused_computation.68 | loop fusion | flops 8388608 | bytes 10092544 | tf_op jit(solution)/shard_map/add | solution.py:39
  104.2 3.5 %all-gather.2.cloned.1.call-done = f32[16,8,32,128]{3,2,1,0:T(8,128)} async-done(((f32[4,8,32,128]{3,2,1,0:T(8,128)}), f32[16,8,32,128]{3,2,1,0:T(8,128)}) %all-gather.2.cloned.1.call-update) | async-done | bytes 2097168 | tf_op jit(solution)/shard_map/all_gather | solution.py:67
  107.7 5.6 %fusion.4 = f32[1,4,16]{2,1,0:T(4,128)S(1)} fusion(f32[16,8,32,128]{3,2,1,0:T(8,128)} %all-gather.2.cloned.1.call-done, f32[4,8,32,128]{3,2,1,0:T(8,128)S(1)} %copy-done), kind=kOutput, calls=%fused_computation.28 | convolution fusion | flops 25165824 | bytes 2621696 | tf_op jit(solution)/shard_map/dot_general | solution.py:43
  113.3 4.0 %fusion.7 = f32[1,4,16]{2,1,0:T(4,128)S(1)} fusion(f32[16,8,32,128]{3,2,1,0:T(8,128)S(1)} %copy-done.2, f32[4,8,32,128]{3,2,1,0:T(8,128)S(1)} %fusion.24), kind=kOutput, calls=%fused_computation.29 | convolution fusion | flops 25165824 | bytes 2621696 | tf_op jit(solution)/shard_map/dot_general | solution.py:43
  117.4 21.4 %psum.7 = f32[2,4,16]{2,1,0:T(4,128)S(1)} all-reduce(f32[2,4,16]{2,1,0:T(4,128)S(1)} %pad_maximum_fusion.8), channel_id=1, replica_groups=mesh['grid'=8,'orb'=4] {'grid'}, use_global_device_ids=true, to_apply=%region_0.1 | all-reduce | flops 128 | bytes 1024 | tf_op jit(solution)/shard_map/psum | solution.py:70
  (106 shorter events, 18.7 us)
Async XLA Ops:
  7.2 8.7 %copy-start.1 = (f32[4,8,32,128]{3,2,1,0:T(8,128)S(1)}, f32[4,8,32,128]{3,2,1,0:T(8,128)}, u32[]{:S(2)}) copy-start(f32[4,8,32,128]{3,2,1,0:T(8,128)} %param.2) | copy-start | bytes 1572868
  7.2 100.5 %all-gather.2.cloned.1.call-start = ((), (), s32[]{:S(2)}) async-start(), calls=%async_computation | async-start | bytes 2621440 | tf_op jit(solution)/shard_map/all_gather | solution.py:67
  8.4 14.2 %collective-permute-start.1 = (f32[4,4,32,128]{3,2,1,0:T(8,128)S(1)}, f32[4,4,32,128]{3,2,1,0:T(8,128)S(1)}, u32[]{:S(2)}, u32[]{:S(2)}) collective-permute-start(f32[4,4,32,128]{3,2,1,0:T(8,128)S(1)} %get-tuple-element.145), channel_id=1, source_target_pairs={{0,4},{4,8},{8,12},{12,16},{16,20},{20,24},{24,28},{28,0},{1,5},{5... | collective-permute-start | bytes 786440 | tf_op jit(solution)/shard_map/ppermute | solution.py:19
  11.4 13.4 %collective-permute-start = (f32[4,4,32,128]{3,2,1,0:T(8,128)S(1)}, f32[4,4,32,128]{3,2,1,0:T(8,128)S(1)}, u32[]{:S(2)}, u32[]{:S(2)}) collective-permute-start(f32[4,4,32,128]{3,2,1,0:T(8,128)S(1)} %get-tuple-element.144), channel_id=1, source_target_pairs={{4,0},{8,4},{12,8},{16,12},{20,16},{24,20},{28,24},{0,28},{5,1},{9... | collective-permute-start | bytes 786440 | tf_op jit(solution)/shard_map/ppermute | solution.py:20
  17.7 0.9 copy-start.3
  29.6 10.8 %collective-permute-start.3 = (f32[4,4,32,128]{3,2,1,0:T(8,128)S(1)}, f32[4,4,32,128]{3,2,1,0:T(8,128)S(1)}, u32[]{:S(2)}, u32[]{:S(2)}) collective-permute-start(f32[4,4,32,128]{3,2,1,0:T(8,128)S(1)} %get-tuple-element.111), channel_id=1, source_target_pairs={{0,4},{4,8},{8,12},{12,16},{16,20},{20,24},{24,28},{28,0},{1,5},{5... | collective-permute-start | bytes 786440 | tf_op jit(solution)/shard_map/ppermute | solution.py:19
  30.1 14.1 %collective-permute-start.2 = (f32[4,4,32,128]{3,2,1,0:T(8,128)S(1)}, f32[4,4,32,128]{3,2,1,0:T(8,128)S(1)}, u32[]{:S(2)}, u32[]{:S(2)}) collective-permute-start(f32[4,4,32,128]{3,2,1,0:T(8,128)S(1)} %get-tuple-element.110), channel_id=1, source_target_pairs={{4,0},{8,4},{12,8},{16,12},{20,16},{24,20},{28,24},{0,28},{5,1},{9... | collective-permute-start | bytes 786440 | tf_op jit(solution)/shard_map/ppermute | solution.py:20
  49.0 11.1 %collective-permute-start.5 = (f32[4,4,32,128]{3,2,1,0:T(8,128)S(1)}, f32[4,4,32,128]{3,2,1,0:T(8,128)S(1)}, u32[]{:S(2)}, u32[]{:S(2)}) collective-permute-start(f32[4,4,32,128]{3,2,1,0:T(8,128)S(1)} %get-tuple-element.77), channel_id=1, source_target_pairs={{0,4},{4,8},{8,12},{12,16},{16,20},{20,24},{24,28},{28,0},{1,5},{5... | collective-permute-start | bytes 786440 | tf_op jit(solution)/shard_map/ppermute | solution.py:19
  49.1 14.7 %collective-permute-start.4 = (f32[4,4,32,128]{3,2,1,0:T(8,128)S(1)}, f32[4,4,32,128]{3,2,1,0:T(8,128)S(1)}, u32[]{:S(2)}, u32[]{:S(2)}) collective-permute-start(f32[4,4,32,128]{3,2,1,0:T(8,128)S(1)} %get-tuple-element.76), channel_id=1, source_target_pairs={{4,0},{8,4},{12,8},{16,12},{20,16},{24,20},{28,24},{0,28},{5,1},{9... | collective-permute-start | bytes 786440 | tf_op jit(solution)/shard_map/ppermute | solution.py:20
  68.6 10.9 %collective-permute-start.7 = (f32[4,4,32,128]{3,2,1,0:T(8,128)S(1)}, f32[4,4,32,128]{3,2,1,0:T(8,128)S(1)}, u32[]{:S(2)}, u32[]{:S(2)}) collective-permute-start(f32[4,4,32,128]{3,2,1,0:T(8,128)S(1)} %get-tuple-element.43), channel_id=1, source_target_pairs={{0,4},{4,8},{8,12},{12,16},{16,20},{20,24},{24,28},{28,0},{1,5},{5... | collective-permute-start | bytes 786440 | tf_op jit(solution)/shard_map/ppermute | solution.py:19
  68.7 14.7 %collective-permute-start.6 = (f32[4,4,32,128]{3,2,1,0:T(8,128)S(1)}, f32[4,4,32,128]{3,2,1,0:T(8,128)S(1)}, u32[]{:S(2)}, u32[]{:S(2)}) collective-permute-start(f32[4,4,32,128]{3,2,1,0:T(8,128)S(1)} %get-tuple-element.42), channel_id=1, source_target_pairs={{4,0},{8,4},{12,8},{16,12},{20,16},{24,20},{28,24},{0,28},{5,1},{9... | collective-permute-start | bytes 786440 | tf_op jit(solution)/shard_map/ppermute | solution.py:20
  86.7 1.2 copy-start
  88.3 10.9 %collective-permute-start.9 = (f32[4,4,32,128]{3,2,1,0:T(8,128)S(1)}, f32[4,4,32,128]{3,2,1,0:T(8,128)S(1)}, u32[]{:S(2)}, u32[]{:S(2)}) collective-permute-start(f32[4,4,32,128]{3,2,1,0:T(8,128)S(1)} %get-tuple-element.41), channel_id=1, source_target_pairs={{0,4},{4,8},{8,12},{12,16},{16,20},{20,24},{24,28},{28,0},{1,5},{5... | collective-permute-start | bytes 786440 | tf_op jit(solution)/shard_map/ppermute | solution.py:19
  88.3 13.4 %collective-permute-start.8 = (f32[4,4,32,128]{3,2,1,0:T(8,128)S(1)}, f32[4,4,32,128]{3,2,1,0:T(8,128)S(1)}, u32[]{:S(2)}, u32[]{:S(2)}) collective-permute-start(f32[4,4,32,128]{3,2,1,0:T(8,128)S(1)} %get-tuple-element.40), channel_id=1, source_target_pairs={{4,0},{8,4},{12,8},{16,12},{20,16},{24,20},{28,24},{0,28},{5,1},{9... | collective-permute-start | bytes 786440 | tf_op jit(solution)/shard_map/ppermute | solution.py:20
  107.7 5.6 %copy-start.2 = (f32[16,8,32,128]{3,2,1,0:T(8,128)S(1)}, f32[16,8,32,128]{3,2,1,0:T(8,128)}, u32[]{:S(2)}) copy-start(f32[16,8,32,128]{3,2,1,0:T(8,128)} %all-gather.2.cloned.1.call-done) | copy-start | bytes 6291460
Sparse Core Ops, SparseCore 0:
  86.9 20.7 all-gather.1
where the time goes:
time: 146 us
  waiting for transfers between devices  45.8 us (31%)
  starting transfers between devices  25.2 us (17%)
  blocking collectives  21.4 us (15%)
  local copies, waits for them, and re-layouts  15.4 us (11%)
  between operations  14.5 us (10%)
  other arithmetic  14.2 us (10%)
  matrix products  9.63 us (7%)
    ppermute x5, waiting for transfers between devices, padded_2(): before = lax.ppermute(last, axis, up)  26.2 us
    ppermute x5, starting transfers between devices, padded_2(): after = lax.ppermute(first, axis, down)  21.5 us
    psum x1, blocking collectives, per_device(): totals = lax.psum(partial_rows, 'grid')  21.4 us
    ppermute x5, waiting for transfers between devices, padded_2(): after = lax.ppermute(first, axis, down)  16.1 us
    slice x64, local copies, waits for them, and re-layouts, apply_ham(): jnp.roll(field, shift_by, axis_pos) + jnp.roll(field, -shift_by, axis_pos)  9.91 us
    dot_general x2, matrix products, cell_product(): lax.dot_general(left, right, (((1,), (1,)), ((), ())), precision=lax.Prec...  9.63 us
    sub x3, other arithmetic, per_device(): 2.0 * sigma_new / half * (apply_ham(current, potential) - centre * current)  8.51 us
    ppermute x5, starting transfers between devices, padded_2(): before = lax.ppermute(last, axis, up)  3.69 us
  transfers between devices with their start and end apart: 11, of which 11 were waited for; matrix products, arithmetic and copies ran while one was open for 7% of the time, Pallas kernels for 0%

commit v1 on v0

v1 whole, which is shorter than its diff:
```python
import functools

import jax
import jax.numpy as jnp
from jax import lax
from jax.experimental import pallas as pl
from jax.experimental.pallas import tpu as pltpu
from jax.sharding import Mesh, PartitionSpec as P

COEFS = (-205.0 / 72.0, 8.0 / 5.0, -1.0 / 5.0, 8.0 / 315.0, -1.0 / 560.0)
SCALE = 5040.0
WHOLE = (8064.0, -1008.0, 128.0, -9.0)
LOWER = -1.0
CUT = 4.0
UPPER = 10.0
HALF = (UPPER - CUT) / 2.0
CENTRE = (UPPER + CUT) / 2.0
S1 = HALF / (LOWER - CENTRE)
T2 = 2.0 / S1**2 - 1.0
T4 = 2.0 * T2 * T2 - 1.0
PEERS = (1, 6, 7, 4, 2, 5, 3, 0)
CHUNK = 4


def ring_matrix(rows, cols, ring):
    row = lax.broadcasted_iota(jnp.int32, (rows, cols), 0)
    col = lax.broadcasted_iota(jnp.int32, (rows, cols), 1)
    size = min(rows, cols)
    row, col = lax.rem(row, size), lax.rem(col, size)
    gap = jnp.abs(row - col)
    out = jnp.zeros((rows, cols), jnp.float32)
    for k, value in enumerate(WHOLE, 1):
        out = jnp.where((gap == k) | (gap == ring - k), value, out)
    return jnp.where(row // ring == col // ring, out, 0.0).astype(jnp.bfloat16)


def matrices(ymat, zmat, ring):
    ymat[...] = ring_matrix(*ymat.shape, ring)
    zmat[...] = ring_matrix(*zmat.shape, zmat.shape[1])


def sweep(at, count, v_at, gain, centre, emit, mats, yz, one_sided=False):
    ymat, zmat = mats
    ny, nz = ymat.shape[0] // CHUNK, zmat.shape[1]
    share = 0.5 * gain if one_sided else gain

    def along_yz(c):
        f = jnp.concatenate([at(c + j, slice(0, ny)) for j in range(CHUNK)], axis=0)
        high = f.astype(jnp.bfloat16)
        rest = f - high.astype(jnp.float32)
        mid = rest.astype(jnp.bfloat16)
        low = (rest - mid.astype(jnp.float32)).astype(jnp.bfloat16)
        z = jnp.dot(jnp.concatenate([high, mid, low], axis=1), zmat[...], preferred_element_type=jnp.float32)
        y = jnp.dot(ymat[...], jnp.concatenate([high, mid, low], axis=0), preferred_element_type=jnp.float32)
        yz[c // CHUNK] = y + z

    along_yz(0)
    for c in range(0, count, CHUNK):
        if c + CHUNK < count:
            along_yz(c + CHUNK)
        for r in range(0, ny, 8):
            rows = slice(r, r + 8)
            f = {i: at(i, rows) for i in range(c if one_sided else c - 4, c + CHUNK + 4)}
            for j in range(CHUNK):
                i = c + j
                total = (share * v_at(i, rows) + share * (-1.5 * COEFS[0] - centre)) * f[i]
                total = total + (-0.5 * share / SCALE) * yz[c // CHUNK, j * ny + r : j * ny + r + 8, :]
                for k in range(1, 5):
                    if one_sided:
                        total = total + (-0.5 * gain * COEFS[k]) * f[i + k]
                    else:
                        total = total + (-0.5 * gain * COEFS[k]) * (f[i - k] + f[i + k])
                emit(i, rows, total)


def places():
    m, place = lax.axis_index("mem"), lax.axis_index("orb")
    return m, place, m * lax.axis_size("orb") + place


def first_two(ymat, zmat, mine, ra, rb, rc, *refs):
    m = places()[0]
    mats = (ymat, zmat)
    n = rc.shape[1] if len(refs) == 7 else refs[0].shape[0]
    own, blocks = n + n * m, ((ra, 2 * n - n * m), (rb, 3 * n * m), (rc, 3 * n - 3 * n * m))
    if len(refs) == 7:
        v, lo_ref, hi_ref, y0_ref, y0, w, yz = refs
    else:
        potential, lo_ref, hi_ref, y0_ref, v, y0, w, yz = refs
        v[pl.ds(4 + n * m, n)] = potential[...]
        v[pl.ds(4 + n - n * m, n)] = ra[0, n:]
        v[pl.ds((2 * n + 4) * m, 4)] = rb[0, n:]
        v[pl.ds((2 * n + 4) * (1 - m), 4)] = rc[0, n:]
        lo_ref[0, n + 4 :] = v[8 : 4 + n]
    y0[pl.ds(own, n)] = mine[0, :n]
    for ref, at in blocks:
        y0[pl.ds(at, n)] = ref[0, :n]
    y0_ref[0] = y0[n : 3 * n + 4]

    def one(i, rows, total):
        w[i, rows, :] = total

    sweep(lambda i, r: y0[4 + i, r, :], 2 * n + 8, lambda i, r: v[i, r, :], 1.0 / HALF, CENTRE, one, mats, yz)

    def two(i, rows, total):
        y2 = total - (1.0 / T2) * y0[n + i, rows, :]
        if i < n + 4:
            lo_ref[0, i, rows, :] = y2
        if i >= n:
            hi_ref[0, i - n, rows, :] = y2

    sweep(
        lambda i, r: w[4 + i, r, :], 2 * n, lambda i, r: v[4 + i, r, :], 2.0 / (T2 * HALF), CENTRE, two, mats, yz
    )


def last_three(ymat, zmat, rlo, lo, hi, rhi, y0, v, v_above, *refs):
    outs, (both, u, f, yz) = refs[:-4], refs[-4:]
    mats = (ymat, zmat)
    n = hi.shape[1]

    def y2(i, rows):
        for ref, start in ((rlo, -n), (lo, 0), (hi, n)):
            if i < start + n:
                return ref[0, i - start, rows, :]
        return rhi[0, i - 2 * n, rows, :]

    def three(i, rows, total):
        u[i, rows, :] = total

    def v_at(i, rows):
        return v[i + 4, rows, :] if i < 2 * n + 4 else v_above[0, i - n, rows, :]

    sweep(lambda i, r: y2(i - 4, r), 2 * n + 12, lambda i, r: v_at(i - 4, r), 1.0 / HALF, CENTRE, three, mats, yz)

    def four(i, rows, total):
        f[i, rows, :] = total - (2.0 * T2 / T4) * y2(i, rows) - (1.0 / T4) * y0[0, i, rows, :]

    sweep(lambda i, r: u[4 + i, r, :], 2 * n + 4, v_at, 4.0 * T2 / (T4 * HALF), CENTRE, four, mats, yz)

    def five(i, rows, total):
        both[0, i, rows, :] = f[i, rows, :]
        both[1, i, rows, :] = total

    sweep(lambda i, r: f[i, r, :], 2 * n, v_at, 1.0, 0.0, five, mats, yz, one_sided=True)
    m, _, me = places()
    homes = (n * m, n - n * m)

    def cells(which, k, per):
        return both[which, pl.ds(per * jnp.bitwise_xor(me, k), per)]

    if len(outs) == 2:
        blocks, home = outs
        for k in range(blocks.shape[0]):
            for which in range(2):
                blocks[k, which] = cells(which, k, blocks.shape[2])
        for i, start in enumerate(homes):
            home[i] = both[0, pl.ds(start, n)]
    else:
        blocks_a, home_a, keep, send, *blocks = outs
        for k, block in enumerate(blocks):
            block[0] = blocks_a[k]
            for which in range(2):
                block[1, which] = cells(which, k, block.shape[2])
        for i, ref in enumerate((keep, send)):
            ref[0] = home_a[i]
            ref[1] = both[0, pl.ds(homes[i], n)]


def gram(*refs):
    *xs, out_ref, part = refs
    orbs = part.shape[1]
    half, _, per, ny, nz = xs[0].shape
    rows = per * ny // 2
    each = 4 * half
    size = len(xs) * each
    flat = [x.reshape(each * rows, nz) for x in xs]
    fields = jnp.concatenate(
        [
            jnp.concatenate([x[pl.ds(r, each, stride=rows), :] for x in flat], axis=0)
            for r in range(rows)
        ],
        axis=1,
    )

    def product(a, b, contract):
        return lax.dot_general(
            a, b, ((contract[:1], contract[1:]), ((), ())),
            precision=lax.Precision.HIGHEST, preferred_element_type=jnp.float32,
        )

    both = product(fields, fields, (1, 1))
    row = lax.broadcasted_iota(jnp.int32, (size, size), 0)
    col = lax.broadcasted_iota(jnp.int32, (size, size), 1)
    both = jnp.where(row % 2 == col % 2, both, 0.0)
    col = lax.broadcasted_iota(jnp.int32, (2 * orbs, size), 1)
    which_peer = col // each
    peer = jnp.zeros_like(col)
    for i, k in enumerate(PEERS):
        peer = jnp.where(which_peer == i, k, peer)
    peer = jnp.bitwise_xor(peer, places()[2])
    target = orbs * (col // 2 % 2) + 2 * half * (peer % 4) + half * (peer // 4) + col // 4 % half
    order = (lax.broadcasted_iota(jnp.int32, (2 * orbs, size), 0) == target).astype(jnp.float32)
    both = product(order, product(both, order, (1, 1)), (1, 0))
    part[...] = jnp.zeros_like(part)
    part[0, :, :orbs] = both[:orbs, :orbs]
    part[1, :, :orbs] = both[orbs:, :orbs] + both[:orbs, orbs:]
    own = nz // (2 * orbs)
    groups = orbs // own
    packed = part[0, pl.ds(0, groups, stride=own), :]
    for i in range(1, 2 * own):
        packed = packed + pltpu.roll(part[i // own, pl.ds(i % own, groups, stride=own), :], i * orbs, 1)

    def spread(g, _):
        out_ref[pl.ds(g * groups, groups)] = packed.reshape(groups, 1, nz)
        return 0

    lax.fori_loop(0, out_ref.shape[0] // groups, spread, 0)


def finish(cells, x_ref, c_ref, h_ref):
    sums = jnp.sum(x_ref[...], axis=0) * (1.0 / cells)
    own, count = c_ref.shape
    nz = sums.shape[1]
    for r in range(own):
        c_ref[r : r + 1, :] = pltpu.roll(sums, (nz - r * count) % nz, 1)[:, :count]
        h_ref[r : r + 1, :] = pltpu.roll(sums, (nz - (own + r) * count) % nz, 1)[:, :count]


VMEM = pl.BlockSpec(memory_space=pltpu.VMEM)


def call(body, operands, outs, scratch, us, name):
    return pl.pallas_call(
        body,
        out_shape=[s if isinstance(s, jax.ShapeDtypeStruct) else jax.ShapeDtypeStruct(s, jnp.float32) for s in outs],
        in_specs=[VMEM] * len(operands),
        out_specs=[VMEM] * len(outs),
        scratch_shapes=scratch,
        cost_estimate=pl.CostEstimate(flops=int(us * 1e9), bytes_accessed=int(us * 3.5e6), transcendentals=0),
        compiler_params=pltpu.CompilerParams(vmem_limit_bytes=32 << 20),
        name=name,
    )(*operands)


def per_device(cells_x, orbitals, potential):
    pairs, orbs = lax.axis_size("pair"), lax.axis_size("orb")
    size = 2 * pairs
    grid_axes = ("pair", "mem")
    m = lax.axis_index("mem")
    own_orbs, n, ny, nz = orbitals.shape
    half = own_orbs // 2
    count = orbs * own_orbs
    swap = [(g, g ^ 1) for g in range(size)]
    cross = [(g, (g + 1) % size if g % 2 else (g - 1) % size) for g in range(size)]
    along = [(g, (g + 2) % size if g % 2 else (g - 2) % size) for g in range(size)]
    up = [(g, (g + 2) % size) for g in range(size)]
    down = [(g, (g - 2) % size) for g in range(size)]
    f32, bf16 = jnp.float32, jnp.bfloat16
    rows = CHUNK * ny
    mats = call(
        functools.partial(lambda ring, ymat, zmat: matrices(ymat, zmat, ring), ny),
        (),
        [jax.ShapeDtypeStruct((rows, 3 * rows), bf16), jax.ShapeDtypeStruct((3 * nz, nz), bf16)],
        [],
        0.5,
        "matrices",
    )

    v = potential[None]
    v4 = jnp.where(m == 0, v[:, :4], v[:, n - 4 :])
    first = []
    for o in range(half):
        a = b = lax.dynamic_slice_in_dim(orbitals, half * (1 - m) + o, 1, 0)
        c = lax.dynamic_slice_in_dim(orbitals, half * m + o, 1, 0)
        if o == 0:
            a, b, c = jnp.concatenate([a, v], 1), jnp.concatenate([b, v4], 1), jnp.concatenate([c, v4], 1)
        ra = lax.ppermute(a, grid_axes, swap)
        rb = lax.ppermute(b, grid_axes, cross)
        rc = lax.ppermute(c, grid_axes, along)
        first.append((*mats, c, ra, rb, rc))

    def field(layers):
        return pltpu.VMEM((layers, ny, nz), f32)

    def products(layers):
        return pltpu.VMEM((layers // CHUNK, rows, nz), f32)

    second, v_above = [], None
    for o in range(half):
        outs = [(1, n + 4, ny, nz), (1, n, ny, nz), (1, 2 * n + 4, ny, nz)]
        scratch = [field(4 * n), field(2 * n + 8), products(2 * n + 8)]
        if o == 0:
            outs = [(1, 2 * n, ny, nz)] + outs[1:] + [(2 * n + 8, ny, nz)]
            lo, hi, y0, vext = call(first_two, first[o] + (potential,), outs, scratch, 1.0, "filter_1_2")
        else:
            lo, hi, y0 = call(first_two, first[o] + (vext,), outs, scratch, 10.0, "filter_1_2")
        rlo = lax.ppermute(hi, grid_axes, up)
        rhi = lax.ppermute(lo, grid_axes, down)
        v_above = rhi if o == 0 else v_above
        second.append((*mats, rlo, lo, hi, rhi, y0, vext, v_above))

    group = 2 * orbs
    per = 2 * n // group
    scratch = [pltpu.VMEM((2, 2 * n, ny, nz), f32), field(2 * n + 12), field(2 * n + 4), products(2 * n + 12)]
    outs = [(group, 2, per, ny, nz), (2, n, ny, nz)]
    results = call(last_three, second[0], outs, scratch, 1.5, "filter_3_4_hamiltonian")
    outs = [(half, n, ny, nz)] * 2 + [(half, 2, per, ny, nz)] * group
    results = call(last_three, (*second[1], *results), outs, scratch, 1.5, "filter_3_4_hamiltonian")
    keep, send, *blocks = results
    xs = [
        lax.ppermute(blocks[k], ("mem", "orb"), [(t, t ^ k) for t in range(group)]) if k else blocks[0] for k in PEERS
    ]
    send, xs[2] = lax.optimization_barrier((send, xs[2]))
    back = lax.ppermute(send, grid_axes, swap)
    (sums,) = call(
        gram,
        xs,
        [(size * orbs, 1, 2 * own_orbs * count)],
        [pltpu.VMEM((2, count, nz), f32)],
        1.3,
        "gram",
    )
    sums = lax.all_to_all(sums, ("pair", "mem", "orb"), 0, 0, tiled=True)
    filtered = jnp.where(m == 0, jnp.concatenate([keep, back]), jnp.concatenate([back, keep]))
    sums, filtered = lax.optimization_barrier((sums, filtered))
    corr, ham = call(
        functools.partial(finish, float(cells_x * ny * nz)), (sums,), [(own_orbs, count)] * 2, [], 0.3, "finish"
    )
    return filtered, corr, ham


def solution(mesh):
    devices = mesh.devices
    size, orbs = devices.shape
    fine = Mesh(devices.reshape(size // 2, 2, orbs), ("pair", "mem", "orb"))
    grid = ("pair", "mem")

    def whole(orbitals, potential):
        return jax.shard_map(
            functools.partial(per_device, orbitals.shape[1]),
            mesh=fine,
            in_specs=(P("orb", grid, None, None), P(grid, None, None)),
            out_specs=(P("orb", grid, None, None), P("orb", None), P("orb", None)),
            check_vma=False,
        )(orbitals, potential)

    return whole
```

time: 146 us -> 74.7 us (0.51)
  blocking collectives: 21.4 us -> 0 us
  local copies, waits for them, and re-layouts: 15.4 us -> 1.18 us
  waiting for transfers between devices: 45.8 us -> 31.7 us
  between operations: 14.5 us -> 0.75 us
  other arithmetic: 14.2 us -> 0.9 us
  matrix products: 9.63 us -> 0 us
  Pallas kernels: 0 us -> 7.96 us
  starting transfers between devices: 25.2 us -> 32 us
    psum x1 -> x0, blocking collectives: 21.4 us -> none  [per_device(): totals = lax.psum(partial_rows, 'grid')]
    ppermute x10 -> x18, waiting for transfers between devices: 42.3 us -> 25.4 us  [the longest x7 12.6 us: per_device(): lax.ppermute(blocks[k], ('mem', 'orb'), [(t, t ^ k) for t in range(group)])]
    slice x85 -> x0, local copies, waits for them, and re-layouts: 14.4 us -> none  [the longest x64 9.91 us: apply_ham(): jnp.roll(field, shift_by, axis_pos) + jnp.roll(field, -shift_by, axis_pos)]
    dot_general x2 -> x0, matrix products: 9.63 us -> none  [cell_product(): lax.dot_general(left, right, (((1,), (1,)), ((), ())), precision=lax.Prec...]
    sub x3 -> x0, other arithmetic: 8.51 us -> none  [per_device(): 2.0 * sigma_new / half * (apply_ham(current, potential) - centre * current)]
    pallas_call x0 -> x7, Pallas kernels: none -> 7.96 us  [call(): pl.pallas_call(body, out_shape=[s if isinstance(s, jax.ShapeDtypeStruct)...]
    all_to_all x0 -> x1, waiting for transfers between devices: none -> 6.29 us  [per_device(): sums = lax.all_to_all(sums, ('pair', 'mem', 'orb'), 0, 0, tiled=True)]
    all_to_all x0 -> x1, starting transfers between devices: none -> 4.31 us  [per_device(): sums = lax.all_to_all(sums, ('pair', 'mem', 'orb'), 0, 0, tiled=True)]
  transfers between devices with their start and end apart: 11 -> 19, of which waited for: 11 -> 11; matrix products, arithmetic and copies ran while one was open for 7% -> 1% of each run, Pallas kernels for 0% -> 8%
where the time goes in v1:
time: 74.7 us; the launch traced here: 74.5 us
  starting transfers between devices  32 us (43%)
  waiting for transfers between devices  31.7 us (42%)
  Pallas kernels  7.96 us (11%)
  local copies, waits for them, and re-layouts  1.18 us (2%)
  other arithmetic  0.9 us (1%)
  between operations  0.75 us (1%)
    ppermute x7, waiting for transfers between devices, per_device(): lax.ppermute(blocks[k], ('mem', 'orb'), [(t, t ^ k) for t in range(group)])  12.6 us
    pallas_call x7, Pallas kernels, call(): pl.pallas_call(body, out_shape=[s if isinstance(s, jax.ShapeDtypeStruct)...  7.96 us
    ppermute x2, starting transfers between devices, per_device(): rhi = lax.ppermute(lo, grid_axes, down)  6.88 us
    ppermute x7, starting transfers between devices, per_device(): lax.ppermute(blocks[k], ('mem', 'orb'), [(t, t ^ k) for t in range(group)])  6.61 us
    all_to_all x1, waiting for transfers between devices, per_device(): sums = lax.all_to_all(sums, ('pair', 'mem', 'orb'), 0, 0, tiled=True)  6.29 us
    ppermute x2, starting transfers between devices, per_device(): rb = lax.ppermute(b, grid_axes, cross)  5.91 us
    ppermute x2, waiting for transfers between devices, per_device(): rlo = lax.ppermute(hi, grid_axes, up)  5.08 us
    all_to_all x1, starting transfers between devices, per_device(): sums = lax.all_to_all(sums, ('pair', 'mem', 'orb'), 0, 0, tiled=True)  4.31 us
  transfers between devices with their start and end apart: 19, of which 11 were waited for; matrix products, arithmetic and copies ran while one was open for 1% of the time, Pallas kernels for 8%

profile of v1, /device:TPU:0, one launch (start us, length us, event | category | flops | bytes accessed | tf_op | source)
XLA Modules:
  0.0 74.5 jit_solution(13800306593856622222)
XLA Ops:
  0.6 1.2 %constant_dynamic-slice_fusion = (f32[1,8,32,128]{3,2,1,0:T(8,128)S(1)}, f32[1,8,32,128]{3,2,1,0:T(8,128)S(1)}, f32[1,8,32,128]{3,2,1,0:T(8,128)S(1)}, f32[1,8,32,128]{3,2,1,0:T(8,128)S(1)}) fusion(f32[4,8,32,128]{3,2,1,0:T(8,128)} %param.2, s32[]{:T(128)S(6)} %select_n.33, s32[]{:T(128)S(6)} %select_n.29, s32[]{:T(128)S(6)} %select_n.28, s32[]{:T(128)S(6)} %select_n.30), kind=kLoop, calls=%fused_computation.5 | loop fusion | bytes 1048592 | tf_op jit(solution)/shard_map/dynamic_slice | solution.py:274
  1.9 3.0 %collective-permute-start.3 = (f32[1,16,32,128]{3,2,1,0:T(8,128)S(1)}, f32[1,16,32,128]{3,2,1,0:T(8,128)S(1)}, u32[]{:S(2)}, u32[]{:S(2)}) collective-permute-start(f32[1,16,32,128]{3,2,1,0:T(8,128)S(1)} %pad_maximum_fusion), channel_id=1, source_target_pairs={{0,4},{4,0},{8,12},{12,8},{16,20},{20,16},{24,28},{28,24},{1,5},{5... | collective-permute-start | bytes 786440 | tf_op jit(solution)/shard_map/ppermute | solution.py:278
  4.9 3.6 %collective-permute-start.4 = (f32[1,12,32,128]{3,2,1,0:T(8,128)S(1)}, f32[1,12,32,128]{3,2,1,0:T(8,128)S(1)}, u32[]{:S(2)}, u32[]{:S(2)}) collective-permute-start(f32[1,12,32,128]{3,2,1,0:T(8,128)S(1)} %get-tuple-element.61), channel_id=1, source_target_pairs={{0,28},{4,8},{8,4},{12,16},{16,12},{20,24},{24,20},{28,0},{1,29},{... | collective-permute-start | bytes 589832 | tf_op jit(solution)/shard_map/ppermute | solution.py:279
  9.0 2.3 %collective-permute-start.1 = (f32[1,8,32,128]{3,2,1,0:T(8,128)S(1)}, f32[1,8,32,128]{3,2,1,0:T(8,128)S(1)}, u32[]{:S(2)}, u32[]{:S(2)}) collective-permute-start(f32[1,8,32,128]{3,2,1,0:T(8,128)S(1)} %get-tuple-element.58), channel_id=1, source_target_pairs={{0,28},{4,8},{8,4},{12,16},{16,12},{20,24},{24,20},{28,0},{1,29},{... | collective-permute-start | bytes 393224 | tf_op jit(solution)/shard_map/ppermute | solution.py:279
  12.0 3.5 %collective-permute-done.4.rb = f32[1,12,32,128]{3,2,1,0:T(8,128)S(1)} collective-permute-done((f32[1,12,32,128]{3,2,1,0:T(8,128)S(1)}, f32[1,12,32,128]{3,2,1,0:T(8,128)S(1)}, u32[]{:S(2)}, u32[]{:S(2)}) %collective-permute-start.4) | collective-permute-done | bytes 196640 | tf_op jit(solution)/shard_map/ppermute | solution.py:279
  15.6 1.8 %collective-permute-start.2 = (f32[1,8,32,128]{3,2,1,0:T(8,128)S(1)}, f32[1,8,32,128]{3,2,1,0:T(8,128)S(1)}, u32[]{:S(2)}, u32[]{:S(2)}) collective-permute-start(f32[1,8,32,128]{3,2,1,0:T(8,128)S(1)} %get-tuple-element.59.mine), channel_id=1, source_target_pairs={{0,24},{4,12},{8,0},{12,20},{16,8},{20,28},{24,16},{28,4},{1,25},{... | collective-permute-start | bytes 393224 | tf_op jit(solution)/shard_map/ppermute | solution.py:280
  18.5 1.0 %filter_1_2.2 = (f32[1,16,32,128]{3,2,1,0:T(8,128)S(1)}, f32[1,8,32,128]{3,2,1,0:T(8,128)S(1)}, f32[1,20,32,128]{3,2,1,0:T(8,128)S(1)}, f32[24,32,128]{2,1,0:T(8,128)S(1)}) custom-call(bf16[128,384]{1,0:T(8,128)(2,1)S(1)} %get-tuple-element.30.ymat, bf16[384,128]{1,0:T(8,128)(2,1)S(1)} %get-tuple-element.31.zmat, ...), custom_call_target="tpu_custom_call" | custom-call | flops 1000000000 | bytes 3500000 | tf_op jit(solution)/shard_map/filter_1_2/pallas_call | solution.py:234
  19.5 1.6 %collective-permute-start.9 = (f32[1,8,32,128]{3,2,1,0:T(8,128)S(1)}, f32[1,8,32,128]{3,2,1,0:T(8,128)S(1)}, u32[]{:S(2)}, u32[]{:S(2)}) collective-permute-start(f32[1,8,32,128]{3,2,1,0:T(8,128)S(1)} %get-tuple-element.37.hi), channel_id=1, source_target_pairs={{0,8},{4,12},{8,16},{12,20},{16,24},{20,28},{24,0},{28,4},{1,9},{5... | collective-permute-start | bytes 393224 | tf_op jit(solution)/shard_map/ppermute | solution.py:298
  21.0 2.5 %collective-permute-start.8 = (f32[1,16,32,128]{3,2,1,0:T(8,128)S(1)}, f32[1,16,32,128]{3,2,1,0:T(8,128)S(1)}, u32[]{:S(2)}, u32[]{:S(2)}) collective-permute-start(f32[1,16,32,128]{3,2,1,0:T(8,128)S(1)} %get-tuple-element.36.lo), channel_id=1, source_target_pairs={{0,24},{4,28},{8,0},{12,4},{16,8},{20,12},{24,16},{28,20},{1,25},{... | collective-permute-start | bytes 786440 | tf_op jit(solution)/shard_map/ppermute | solution.py:299
  23.8 1.0 %filter_1_2.3 = (f32[1,12,32,128]{3,2,1,0:T(8,128)S(1)}, f32[1,8,32,128]{3,2,1,0:T(8,128)S(1)}, f32[1,20,32,128]{3,2,1,0:T(8,128)S(1)}) custom-call(bf16[128,384]{1,0:T(8,128)(2,1)S(1)} %get-tuple-element.30.ymat, bf16[384,128]{1,0:T(8,128)(2,1)S(1)} %get-tuple-element.31.zmat, f32[1,8,32,128]{3,2,1,0:T(8,128)S(1)} %get-tuple-element.59.mine, ...), custom_call_target="tpu_custom_call" | custom-call | flops 10000000000 | bytes 35000000 | tf_op jit(solution)/shard_map/filter_1_2/pallas_call | solution.py:234
  24.7 4.3 %collective-permute-start.7 = (f32[1,12,32,128]{3,2,1,0:T(8,128)S(1)}, f32[1,12,32,128]{3,2,1,0:T(8,128)S(1)}, u32[]{:S(2)}, u32[]{:S(2)}) collective-permute-start(f32[1,12,32,128]{3,2,1,0:T(8,128)S(1)} %get-tuple-element.34.lo), channel_id=1, source_target_pairs={{0,24},{4,28},{8,0},{12,4},{16,8},{20,12},{24,16},{28,20},{1,25},{... | collective-permute-start | bytes 589832 | tf_op jit(solution)/shard_map/ppermute | solution.py:299
  29.1 3.1 %collective-permute-done.8.rhi.v_above = f32[1,16,32,128]{3,2,1,0:T(8,128)S(1)} collective-permute-done((f32[1,16,32,128]{3,2,1,0:T(8,128)S(1)}, f32[1,16,32,128]{3,2,1,0:T(8,128)S(1)}, u32[]{:S(2)}, u32[]{:S(2)}) %collective-permute-start.8) | collective-permute-done | bytes 262176 | tf_op jit(solution)/shard_map/ppermute | solution.py:299
  32.2 1.4 %filter_3_4_hamiltonian.2 = (f32[8,2,2,32,128]{4,3,2,1,0:T(8,128)S(1)}, f32[2,8,32,128]{3,2,1,0:T(8,128)S(1)}) custom-call(bf16[128,384]{1,0:T(8,128)(2,1)S(1)} %get-tuple-element.30.ymat, bf16[384,128]{1,0:T(8,128)(2,1)S(1)} %get-tuple-element.31.zmat, f32[1,8,32,128]{3,2,1,0:T(8,128)S(1)} %collective-permute-done.9.rlo, ...), custom_call_target="tpu_custom_call" | custom-call | flops 1500000000 | bytes 5250000 | tf_op jit(solution)/shard_map/filter_3_4_hamiltonian/pallas_call | solution.py:234
  33.6 5.1 %collective-permute-done.6.rlo = f32[1,8,32,128]{3,2,1,0:T(8,128)S(1)} collective-permute-done((f32[1,8,32,128]{3,2,1,0:T(8,128)S(1)}, f32[1,8,32,128]{3,2,1,0:T(8,128)S(1)}, u32[]{:S(2)}, u32[]{:S(2)}) %collective-permute-start.6) | collective-permute-done | bytes 131104 | tf_op jit(solution)/shard_map/ppermute | solution.py:298
  38.7 1.4 %filter_3_4_hamiltonian.3 = (f32[2,8,32,128]{3,2,1,0:T(8,128)S(1)}, f32[2,8,32,128]{3,2,1,0:T(8,128)S(1)}, f32[2,2,2,32,128]{4,3,2,1,0:T(8,128)S(1)}, f32[2,2,2,...) custom-call(bf16[128,384]{1,0:T(8,128)(2,1)S(1)} %get-tuple-element., ...), custom_call_target="tpu_custom_call" | custom-call | flops 1500000000 | bytes 5250000 | tf_op jit(solution)/shard_map/filter_3_4_hamiltonian/pallas_call | solution.py:234
  40.1 2.3 %collective-permute-start.10 = (f32[2,2,2,32,128]{4,3,2,1,0:T(8,128)S(1)}, f32[2,2,2,32,128]{4,3,2,1,0:T(8,128)S(1)}, u32[]{:S(2)}, u32[]{:S(2)}) collective-permute-start(f32[2,2,2,32,128]{4,3,2,1,0:T(8,128)S(1)} %get-tuple-element.41), channel_id=1, source_target_pairs={{0,1},{1,0},{2,3},{3,2},{4,5},{5,4},{6,7},{7,6},{8,9},{9,8},{10,11... | collective-permute-start | bytes 393224 | tf_op jit(solution)/shard_map/ppermute | solution.py:312
  43.2 3.5 %collective-permute-done.12.refs_2_ = f32[2,2,2,32,128]{4,3,2,1,0:T(8,128)S(1)} collective-permute-done((f32[2,2,2,32,128]{4,3,2,1,0:T(8,128)S(1)}, f32[2,2,2,32,128]{4,3,2,1,0:T(8,128)S(1)}, u32[]{:S(2)}, u32[]{:S(2)}) %collective-permute-start.12) | collective-permute-done | bytes 131104 | tf_op jit(solution)/shard_map/ppermute | solution.py:312
  47.4 1.3 %collective-permute-start.13 = (f32[2,2,2,32,128]{4,3,2,1,0:T(8,128)S(1)}, f32[2,2,2,32,128]{4,3,2,1,0:T(8,128)S(1)}, u32[]{:S(2)}, u32[]{:S(2)}) collective-permute-start(f32[2,2,2,32,128]{4,3,2,1,0:T(8,128)S(1)} %get-tuple-element.46), channel_id=1, source_target_pairs={{0,4},{1,5},{2,6},{3,7},{4,0},{5,1},{6,2},{7,3},{8,12},{9,13},{10,... | collective-permute-start | bytes 393224 | tf_op jit(solution)/shard_map/ppermute | solution.py:312
  49.5 1.7 %collective-permute-start.16 = (f32[2,2,2,32,128]{4,3,2,1,0:T(8,128)S(1)}, f32[2,2,2,32,128]{4,3,2,1,0:T(8,128)S(1)}, u32[]{:S(2)}, u32[]{:S(2)}) collective-permute-start(f32[2,2,2,32,128]{4,3,2,1,0:T(8,128)S(1)} %get-tuple-element.49), channel_id=1, source_target_pairs={{0,3},{1,2},{2,1},{3,0},{4,7},{5,6},{6,5},{7,4},{8,11},{9,10},{10,... | collective-permute-start | bytes 393224 | tf_op jit(solution)/shard_map/ppermute | solution.py:312
  51.2 7.5 %collective-permute-done.13.refs_3_ = f32[2,2,2,32,128]{4,3,2,1,0:T(8,128)S(1)} collective-permute-done((f32[2,2,2,32,128]{4,3,2,1,0:T(8,128)S(1)}, f32[2,2,2,32,128]{4,3,2,1,0:T(8,128)S(1)}, u32[]{:S(2)}, u32[]{:S(2)}) %collective-permute-start.13) | collective-permute-done | bytes 131104 | tf_op jit(solution)/shard_map/ppermute | solution.py:312
  58.7 1.3 %collective-permute-done.15.refs_5_ = f32[2,2,2,32,128]{4,3,2,1,0:T(8,128)S(1)} collective-permute-done((f32[2,2,2,32,128]{4,3,2,1,0:T(8,128)S(1)}, f32[2,2,2,32,128]{4,3,2,1,0:T(8,128)S(1)}, u32[]{:S(2)}, u32[]{:S(2)}) %collective-permute-start.15) | collective-permute-done | bytes 131104 | tf_op jit(solution)/shard_map/ppermute | solution.py:312
  60.0 2.3 %gram.1 = f32[32,1,128]{2,1,0:T(1,128)} custom-call(f32[2,2,2,32,128]{4,3,2,1,0:T(8,128)S(1)} %collective-permute-done.10.refs_0_, f32[2,2,2,32,128]{4,3,2,1,0:T(8,128)S(1)} %collective-permute-done.11.refs_1_, f32[2,2,2,32,128]{4,3,2,1,0:T(8,128)S(1)} %collective-permute-done.12.refs_2_, f32[2,2,2,32,128]{4,3,2,1,0:T(8,128)S(1)} %collective-permute-done.13.refs_3_, ...), custom_call_target="tpu_custom_call" | custom-call | flops 1300000000 | bytes 4550000 | tf_op jit(solution)/shard_map/gram/pallas_call | solution.py:234
  62.3 4.3 %all-to-all-start = ((f32[32,1,128]{2,1,0:T(1,128)}), f32[32,1,128]{2,1,0:T(1,128)S(1)}, u32[]{:S(2)}, u32[]{:S(2)}) async-start(f32[32,1,128]{2,1,0:T(1,128)} %gram.1), calls=%async_computation | async-start | bytes 32768 | tf_op jit(solution)/shard_map/all_to_all | solution.py:324
  67.5 6.3 %all-to-all-done.x_ref = f32[32,1,128]{2,1,0:T(1,128)S(1)} async-done(((f32[32,1,128]{2,1,0:T(1,128)}), f32[32,1,128]{2,1,0:T(1,128)S(1)}, u32[]{:S(2)}, u32[]{:S(2)}) %all-to-all-start) | async-done | bytes 16416 | tf_op jit(solution)/shard_map/all_to_all | solution.py:324
  (28 shorter events, 6.4 us)
Async XLA Ops:
  0.6 1.2 %copy-start = (f32[8,32,128]{2,1,0:T(8,128)S(1)}, f32[8,32,128]{2,1,0:T(8,128)}, u32[]{:S(2)}) copy-start(f32[8,32,128]{2,1,0:T(8,128)} %refs_0_.1) | copy-start | bytes 393220
  1.9 16.6 %collective-permute-start.3 = (f32[1,16,32,128]{3,2,1,0:T(8,128)S(1)}, f32[1,16,32,128]{3,2,1,0:T(8,128)S(1)}, u32[]{:S(2)}, u32[]{:S(2)}) collective-permute-start(f32[1,16,32,128]{3,2,1,0:T(8,128)S(1)} %pad_maximum_fusion), channel_id=1, source_target_pairs={{0,4},{4,0},{8,12},{12,8},{16,20},{20,16},{24,28},{28,24},{1,5},{5... | collective-permute-start | bytes 786440 | tf_op jit(solution)/shard_map/ppermute | solution.py:278
  4.9 10.6 %collective-permute-start.4 = (f32[1,12,32,128]{3,2,1,0:T(8,128)S(1)}, f32[1,12,32,128]{3,2,1,0:T(8,128)S(1)}, u32[]{:S(2)}, u32[]{:S(2)}) collective-permute-start(f32[1,12,32,128]{3,2,1,0:T(8,128)S(1)} %get-tuple-element.61), channel_id=1, source_target_pairs={{0,28},{4,8},{8,4},{12,16},{16,12},{20,24},{24,20},{28,0},{1,29},{... | collective-permute-start | bytes 589832 | tf_op jit(solution)/shard_map/ppermute | solution.py:279
  8.6 9.6 %collective-permute-start.5 = (f32[1,12,32,128]{3,2,1,0:T(8,128)S(1)}, f32[1,12,32,128]{3,2,1,0:T(8,128)S(1)}, u32[]{:S(2)}, u32[]{:S(2)}) collective-permute-start(f32[1,12,32,128]{3,2,1,0:T(8,128)S(1)} %get-tuple-element.62.mine), channel_id=1, source_target_pairs={{0,24},{4,12},{8,0},{12,20},{16,8},{20,28},{24,16},{28,4},{1,25},{... | collective-permute-start | bytes 589832 | tf_op jit(solution)/shard_map/ppermute | solution.py:280
  9.0 14.6 %collective-permute-start.1 = (f32[1,8,32,128]{3,2,1,0:T(8,128)S(1)}, f32[1,8,32,128]{3,2,1,0:T(8,128)S(1)}, u32[]{:S(2)}, u32[]{:S(2)}) collective-permute-start(f32[1,8,32,128]{3,2,1,0:T(8,128)S(1)} %get-tuple-element.58), channel_id=1, source_target_pairs={{0,28},{4,8},{8,4},{12,16},{16,12},{20,24},{24,20},{28,0},{1,29},{... | collective-permute-start | bytes 393224 | tf_op jit(solution)/shard_map/ppermute | solution.py:279
  11.3 12.3 %collective-permute-start = (f32[1,8,32,128]{3,2,1,0:T(8,128)S(1)}, f32[1,8,32,128]{3,2,1,0:T(8,128)S(1)}, u32[]{:S(2)}, u32[]{:S(2)}) collective-permute-start(f32[1,8,32,128]{3,2,1,0:T(8,128)S(1)} %get-tuple-element.58), channel_id=1, source_target_pairs={{0,4},{4,0},{8,12},{12,8},{16,20},{20,16},{24,28},{28,24},{1,5},{5... | collective-permute-start | bytes 393224 | tf_op jit(solution)/shard_map/ppermute | solution.py:278
  15.6 8.2 %collective-permute-start.2 = (f32[1,8,32,128]{3,2,1,0:T(8,128)S(1)}, f32[1,8,32,128]{3,2,1,0:T(8,128)S(1)}, u32[]{:S(2)}, u32[]{:S(2)}) collective-permute-start(f32[1,8,32,128]{3,2,1,0:T(8,128)S(1)} %get-tuple-element.59.mine), channel_id=1, source_target_pairs={{0,24},{4,12},{8,0},{12,20},{16,8},{20,28},{24,16},{28,4},{1,25},{... | collective-permute-start | bytes 393224 | tf_op jit(solution)/shard_map/ppermute | solution.py:280
  19.5 9.6 %collective-permute-start.9 = (f32[1,8,32,128]{3,2,1,0:T(8,128)S(1)}, f32[1,8,32,128]{3,2,1,0:T(8,128)S(1)}, u32[]{:S(2)}, u32[]{:S(2)}) collective-permute-start(f32[1,8,32,128]{3,2,1,0:T(8,128)S(1)} %get-tuple-element.37.hi), channel_id=1, source_target_pairs={{0,8},{4,12},{8,16},{12,20},{16,24},{20,28},{24,0},{28,4},{1,9},{5... | collective-permute-start | bytes 393224 | tf_op jit(solution)/shard_map/ppermute | solution.py:298
  21.0 11.2 %collective-permute-start.8 = (f32[1,16,32,128]{3,2,1,0:T(8,128)S(1)}, f32[1,16,32,128]{3,2,1,0:T(8,128)S(1)}, u32[]{:S(2)}, u32[]{:S(2)}) collective-permute-start(f32[1,16,32,128]{3,2,1,0:T(8,128)S(1)} %get-tuple-element.36.lo), channel_id=1, source_target_pairs={{0,24},{4,28},{8,0},{12,4},{16,8},{20,12},{24,16},{28,20},{1,25},{... | collective-permute-start | bytes 786440 | tf_op jit(solution)/shard_map/ppermute | solution.py:299
  24.7 13.9 %collective-permute-start.7 = (f32[1,12,32,128]{3,2,1,0:T(8,128)S(1)}, f32[1,12,32,128]{3,2,1,0:T(8,128)S(1)}, u32[]{:S(2)}, u32[]{:S(2)}) collective-permute-start(f32[1,12,32,128]{3,2,1,0:T(8,128)S(1)} %get-tuple-element.34.lo), channel_id=1, source_target_pairs={{0,24},{4,28},{8,0},{12,4},{16,8},{20,12},{24,16},{28,20},{1,25},{... | collective-permute-start | bytes 589832 | tf_op jit(solution)/shard_map/ppermute | solution.py:299
  29.1 9.6 %collective-permute-start.6 = (f32[1,8,32,128]{3,2,1,0:T(8,128)S(1)}, f32[1,8,32,128]{3,2,1,0:T(8,128)S(1)}, u32[]{:S(2)}, u32[]{:S(2)}) collective-permute-start(f32[1,8,32,128]{3,2,1,0:T(8,128)S(1)} %get-tuple-element.33.hi), channel_id=1, source_target_pairs={{0,8},{4,12},{8,16},{12,20},{16,24},{20,28},{24,0},{28,4},{1,9},{5... | collective-permute-start | bytes 393224 | tf_op jit(solution)/shard_map/ppermute | solution.py:298
  40.1 6.7 %collective-permute-start.12 = (f32[2,2,2,32,128]{4,3,2,1,0:T(8,128)S(1)}, f32[2,2,2,32,128]{4,3,2,1,0:T(8,128)S(1)}, u32[]{:S(2)}, u32[]{:S(2)}) collective-permute-start(f32[2,2,2,32,128]{4,3,2,1,0:T(8,128)S(1)} %get-tuple-element.44), channel_id=1, source_target_pairs={{0,7},{1,6},{2,5},{3,4},{4,3},{5,2},{6,1},{7,0},{8,15},{9,14},{10,... | collective-permute-start | bytes 393224 | tf_op jit(solution)/shard_map/ppermute | solution.py:312
  40.1 9.1 %collective-permute-start.10 = (f32[2,2,2,32,128]{4,3,2,1,0:T(8,128)S(1)}, f32[2,2,2,32,128]{4,3,2,1,0:T(8,128)S(1)}, u32[]{:S(2)}, u32[]{:S(2)}) collective-permute-start(f32[2,2,2,32,128]{4,3,2,1,0:T(8,128)S(1)} %get-tuple-element.41), channel_id=1, source_target_pairs={{0,1},{1,0},{2,3},{3,2},{4,5},{5,4},{6,7},{7,6},{8,9},{9,8},{10,11... | collective-permute-start | bytes 393224 | tf_op jit(solution)/shard_map/ppermute | solution.py:312
  42.5 7.1 %collective-permute-start.11 = (f32[2,2,2,32,128]{4,3,2,1,0:T(8,128)S(1)}, f32[2,2,2,32,128]{4,3,2,1,0:T(8,128)S(1)}, u32[]{:S(2)}, u32[]{:S(2)}) collective-permute-start(f32[2,2,2,32,128]{4,3,2,1,0:T(8,128)S(1)} %get-tuple-element.42), channel_id=1, source_target_pairs={{0,6},{1,7},{2,4},{3,5},{4,2},{5,3},{6,0},{7,1},{8,14},{9,15},{10,... | collective-permute-start | bytes 393224 | tf_op jit(solution)/shard_map/ppermute | solution.py:312
  46.7 19.9 %collective-permute-start.17 = (f32[2,8,32,128]{3,2,1,0:T(8,128)S(1)}, f32[2,8,32,128]{3,2,1,0:T(8,128)S(1)}, u32[]{:S(2)}, u32[]{:S(2)}) collective-permute-start(f32[2,8,32,128]{3,2,1,0:T(8,128)S(1)} %get-tuple-element.52), channel_id=1, source_target_pairs={{0,4},{4,0},{8,12},{12,8},{16,20},{20,16},{24,28},{28,24},{1,5},{5... | collective-permute-start | bytes 786440 | tf_op jit(solution)/shard_map/ppermute | solution.py:315
  47.4 11.3 %collective-permute-start.13 = (f32[2,2,2,32,128]{4,3,2,1,0:T(8,128)S(1)}, f32[2,2,2,32,128]{4,3,2,1,0:T(8,128)S(1)}, u32[]{:S(2)}, u32[]{:S(2)}) collective-permute-start(f32[2,2,2,32,128]{4,3,2,1,0:T(8,128)S(1)} %get-tuple-element.46), channel_id=1, source_target_pairs={{0,4},{1,5},{2,6},{3,7},{4,0},{5,1},{6,2},{7,3},{8,12},{9,13},{10,... | collective-permute-start | bytes 393224 | tf_op jit(solution)/shard_map/ppermute | solution.py:312
  48.7 10.0 %collective-permute-start.14 = (f32[2,2,2,32,128]{4,3,2,1,0:T(8,128)S(1)}, f32[2,2,2,32,128]{4,3,2,1,0:T(8,128)S(1)}, u32[]{:S(2)}, u32[]{:S(2)}) collective-permute-start(f32[2,2,2,32,128]{4,3,2,1,0:T(8,128)S(1)} %get-tuple-element.47), channel_id=1, source_target_pairs={{0,2},{1,3},{2,0},{3,1},{4,6},{5,7},{6,4},{7,5},{8,10},{9,11},{10,... | collective-permute-start | bytes 393224 | tf_op jit(solution)/shard_map/ppermute | solution.py:312
  49.3 10.7 %collective-permute-start.15 = (f32[2,2,2,32,128]{4,3,2,1,0:T(8,128)S(1)}, f32[2,2,2,32,128]{4,3,2,1,0:T(8,128)S(1)}, u32[]{:S(2)}, u32[]{:S(2)}) collective-permute-start(f32[2,2,2,32,128]{4,3,2,1,0:T(8,128)S(1)} %get-tuple-element.48), channel_id=1, source_target_pairs={{0,5},{1,4},{2,7},{3,6},{4,1},{5,0},{6,3},{7,2},{8,13},{9,12},{10,... | collective-permute-start | bytes 393224 | tf_op jit(solution)/shard_map/ppermute | solution.py:312
  49.5 10.5 %collective-permute-start.16 = (f32[2,2,2,32,128]{4,3,2,1,0:T(8,128)S(1)}, f32[2,2,2,32,128]{4,3,2,1,0:T(8,128)S(1)}, u32[]{:S(2)}, u32[]{:S(2)}) collective-permute-start(f32[2,2,2,32,128]{4,3,2,1,0:T(8,128)S(1)} %get-tuple-element.49), channel_id=1, source_target_pairs={{0,3},{1,2},{2,1},{3,0},{4,7},{5,6},{6,5},{7,4},{8,11},{9,10},{10,... | collective-permute-start | bytes 393224 | tf_op jit(solution)/shard_map/ppermute | solution.py:312
  62.3 11.5 %all-to-all-start = ((f32[32,1,128]{2,1,0:T(1,128)}), f32[32,1,128]{2,1,0:T(1,128)S(1)}, u32[]{:S(2)}, u32[]{:S(2)}) async-start(f32[32,1,128]{2,1,0:T(1,128)} %gram.1), calls=%async_computation | async-start | bytes 32768 | tf_op jit(solution)/shard_map/all_to_all | solution.py:324

commit v2 on v1

--- a/solution.py
+++ b/solution.py
@@ -311,8 +311,6 @@
     xs = [
         lax.ppermute(blocks[k], ("mem", "orb"), [(t, t ^ k) for t in range(group)]) if k else blocks[0] for k in PEERS
     ]
-    send, xs[2] = lax.optimization_barrier((send, xs[2]))
-    back = lax.ppermute(send, grid_axes, swap)
     (sums,) = call(
         gram,
         xs,
@@ -321,6 +319,8 @@
         1.3,
         "gram",
     )
+    send, sums = lax.optimization_barrier((send, sums))
+    back = lax.ppermute(send, grid_axes, swap)
     sums = lax.all_to_all(sums, ("pair", "mem", "orb"), 0, 0, tiled=True)
     filtered = jnp.where(m == 0, jnp.concatenate([keep, back]), jnp.concatenate([back, keep]))
     sums, filtered = lax.optimization_barrier((sums, filtered))

time: 74.7 us -> 71.8 us (0.961)
  waiting for transfers between devices: 31.7 us -> 28.4 us
    ppermute x7, waiting for transfers between devices: 12.6 us -> 9.3 us  [per_device(): lax.ppermute(blocks[k], ('mem', 'orb'), [(t, t ^ k) for t in range(group)])]
    ppermute x1, waiting for transfers between devices: 0.01 us -> 2.13 us  [per_device(): back = lax.ppermute(send, grid_axes, swap)]
    all_to_all x1, waiting for transfers between devices: 6.29 us -> 4.17 us  [per_device(): sums = lax.all_to_all(sums, ('pair', 'mem', 'orb'), 0, 0, tiled=True)]
  transfers between devices with their start and end apart: 19 -> 19, of which waited for: 11 -> 13; matrix products, arithmetic and copies ran while one was open for 1% -> 1% of each run, Pallas kernels for 8% -> 5%
where the time goes in v2:
time: 71.8 us; the launch traced here: 71.7 us
  starting transfers between devices  32.5 us (45%)
  waiting for transfers between devices  28.4 us (40%)
  Pallas kernels  7.96 us (11%)
  local copies, waits for them, and re-layouts  1.18 us (2%)
  other arithmetic  0.9 us (1%)
  between operations  0.74 us (1%)
    ppermute x7, waiting for transfers between devices, per_device(): lax.ppermute(blocks[k], ('mem', 'orb'), [(t, t ^ k) for t in range(group)])  9.3 us
    pallas_call x7, Pallas kernels, call(): pl.pallas_call(body, out_shape=[s if isinstance(s, jax.ShapeDtypeStruct)...  7.96 us
    ppermute x2, starting transfers between devices, per_device(): rhi = lax.ppermute(lo, grid_axes, down)  6.88 us
    ppermute x7, starting transfers between devices, per_device(): lax.ppermute(blocks[k], ('mem', 'orb'), [(t, t ^ k) for t in range(group)])  5.95 us
    ppermute x2, starting transfers between devices, per_device(): rb = lax.ppermute(b, grid_axes, cross)  5.91 us
    ppermute x2, waiting for transfers between devices, per_device(): rlo = lax.ppermute(hi, grid_axes, up)  5.08 us
    all_to_all x1, starting transfers between devices, per_device(): sums = lax.all_to_all(sums, ('pair', 'mem', 'orb'), 0, 0, tiled=True)  4.88 us
    all_to_all x1, waiting for transfers between devices, per_device(): sums = lax.all_to_all(sums, ('pair', 'mem', 'orb'), 0, 0, tiled=True)  4.17 us
  transfers between devices with their start and end apart: 19, of which 13 were waited for; matrix products, arithmetic and copies ran while one was open for 1% of the time, Pallas kernels for 5%

profile of v2, /device:TPU:0, one launch (start us, length us, event | category | flops | bytes accessed | tf_op | source)
XLA Modules:
  0.0 71.7 jit_solution(649283421069297357)
XLA Ops:
  1.9 3.0 %collective-permute-start.3 = (f32[1,16,32,128]{3,2,1,0:T(8,128)S(1)}, f32[1,16,32,128]{3,2,1,0:T(8,128)S(1)}, u32[]{:S(2)}, u32[]{:S(2)}) collective-permute-start(f32[1,16,32,128]{3,2,1,0:T(8,128)S(1)} %pad_maximum_fusion), channel_id=1, source_target_pairs={{0,4},{4,0},{8,12},{12,8},{16,20},{20,16},{24,28},{28,24},{1,5},{5... | collective-permute-start | bytes 786440 | tf_op jit(solution)/shard_map/ppermute | solution.py:278
  4.9 3.6 %collective-permute-start.4 = (f32[1,12,32,128]{3,2,1,0:T(8,128)S(1)}, f32[1,12,32,128]{3,2,1,0:T(8,128)S(1)}, u32[]{:S(2)}, u32[]{:S(2)}) collective-permute-start(f32[1,12,32,128]{3,2,1,0:T(8,128)S(1)} %get-tuple-element.61), channel_id=1, source_target_pairs={{0,28},{4,8},{8,4},{12,16},{16,12},{20,24},{24,20},{28,0},{1,29},{... | collective-permute-start | bytes 589832 | tf_op jit(solution)/shard_map/ppermute | solution.py:279
  9.0 2.3 %collective-permute-start.1 = (f32[1,8,32,128]{3,2,1,0:T(8,128)S(1)}, f32[1,8,32,128]{3,2,1,0:T(8,128)S(1)}, u32[]{:S(2)}, u32[]{:S(2)}) collective-permute-start(f32[1,8,32,128]{3,2,1,0:T(8,128)S(1)} %get-tuple-element.58), channel_id=1, source_target_pairs={{0,28},{4,8},{8,4},{12,16},{16,12},{20,24},{24,20},{28,0},{1,29},{... | collective-permute-start | bytes 393224 | tf_op jit(solution)/shard_map/ppermute | solution.py:279
  12.0 3.5 %collective-permute-done.4.rb = f32[1,12,32,128]{3,2,1,0:T(8,128)S(1)} collective-permute-done((f32[1,12,32,128]{3,2,1,0:T(8,128)S(1)}, f32[1,12,32,128]{3,2,1,0:T(8,128)S(1)}, u32[]{:S(2)}, u32[]{:S(2)}) %collective-permute-start.4) | collective-permute-done | bytes 196640 | tf_op jit(solution)/shard_map/ppermute | solution.py:279
  15.6 1.8 %collective-permute-start.2 = (f32[1,8,32,128]{3,2,1,0:T(8,128)S(1)}, f32[1,8,32,128]{3,2,1,0:T(8,128)S(1)}, u32[]{:S(2)}, u32[]{:S(2)}) collective-permute-start(f32[1,8,32,128]{3,2,1,0:T(8,128)S(1)} %get-tuple-element.59.mine), channel_id=1, source_target_pairs={{0,24},{4,12},{8,0},{12,20},{16,8},{20,28},{24,16},{28,4},{1,25},{... | collective-permute-start | bytes 393224 | tf_op jit(solution)/shard_map/ppermute | solution.py:280
  19.5 1.6 %collective-permute-start.9 = (f32[1,8,32,128]{3,2,1,0:T(8,128)S(1)}, f32[1,8,32,128]{3,2,1,0:T(8,128)S(1)}, u32[]{:S(2)}, u32[]{:S(2)}) collective-permute-start(f32[1,8,32,128]{3,2,1,0:T(8,128)S(1)} %get-tuple-element.37.hi), channel_id=1, source_target_pairs={{0,8},{4,12},{8,16},{12,20},{16,24},{20,28},{24,0},{28,4},{1,9},{5... | collective-permute-start | bytes 393224 | tf_op jit(solution)/shard_map/ppermute | solution.py:298
  21.0 2.5 %collective-permute-start.8 = (f32[1,16,32,128]{3,2,1,0:T(8,128)S(1)}, f32[1,16,32,128]{3,2,1,0:T(8,128)S(1)}, u32[]{:S(2)}, u32[]{:S(2)}) collective-permute-start(f32[1,16,32,128]{3,2,1,0:T(8,128)S(1)} %get-tuple-element.36.lo), channel_id=1, source_target_pairs={{0,24},{4,28},{8,0},{12,4},{16,8},{20,12},{24,16},{28,20},{1,25},{... | collective-permute-start | bytes 786440 | tf_op jit(solution)/shard_map/ppermute | solution.py:299
  24.7 4.3 %collective-permute-start.7 = (f32[1,12,32,128]{3,2,1,0:T(8,128)S(1)}, f32[1,12,32,128]{3,2,1,0:T(8,128)S(1)}, u32[]{:S(2)}, u32[]{:S(2)}) collective-permute-start(f32[1,12,32,128]{3,2,1,0:T(8,128)S(1)} %get-tuple-element.34.lo), channel_id=1, source_target_pairs={{0,24},{4,28},{8,0},{12,4},{16,8},{20,12},{24,16},{28,20},{1,25},{... | collective-permute-start | bytes 589832 | tf_op jit(solution)/shard_map/ppermute | solution.py:299
  29.1 3.1 %collective-permute-done.8.rhi.v_above = f32[1,16,32,128]{3,2,1,0:T(8,128)S(1)} collective-permute-done((f32[1,16,32,128]{3,2,1,0:T(8,128)S(1)}, f32[1,16,32,128]{3,2,1,0:T(8,128)S(1)}, u32[]{:S(2)}, u32[]{:S(2)}) %collective-permute-start.8) | collective-permute-done | bytes 262176 | tf_op jit(solution)/shard_map/ppermute | solution.py:299
  32.2 1.4 %filter_3_4_hamiltonian.2 = (f32[8,2,2,32,128]{4,3,2,1,0:T(8,128)S(1)}, f32[2,8,32,128]{3,2,1,0:T(8,128)S(1)}) custom-call(bf16[128,384]{1,0:T(8,128)(2,1)S(1)} %get-tuple-element.30.ymat, bf16[384,128]{1,0:T(8,128)(2,1)S(1)} %get-tuple-element.31.zmat, f32[1,8,32,128]{3,2,1,0:T(8,128)S(1)} %collective-permute-done.9.rlo, ...), custom_call_target="tpu_custom_call" | custom-call | flops 1500000000 | bytes 5250000 | tf_op jit(solution)/shard_map/filter_3_4_hamiltonian/pallas_call | solution.py:234
  33.6 5.1 %collective-permute-done.6.rlo = f32[1,8,32,128]{3,2,1,0:T(8,128)S(1)} collective-permute-done((f32[1,8,32,128]{3,2,1,0:T(8,128)S(1)}, f32[1,8,32,128]{3,2,1,0:T(8,128)S(1)}, u32[]{:S(2)}, u32[]{:S(2)}) %collective-permute-start.6) | collective-permute-done | bytes 131104 | tf_op jit(solution)/shard_map/ppermute | solution.py:298
  38.7 1.4 %filter_3_4_hamiltonian.3 = (f32[2,8,32,128]{3,2,1,0:T(8,128)S(1)}, f32[2,8,32,128]{3,2,1,0:T(8,128)S(1)}, f32[2,2,2,32,128]{4,3,2,1,0:T(8,128)S(1)}, f32[2,2,2,...) custom-call(bf16[128,384]{1,0:T(8,128)(2,1)S(1)} %get-tuple-element., ...), custom_call_target="tpu_custom_call" | custom-call | flops 1500000000 | bytes 5250000 | tf_op jit(solution)/shard_map/filter_3_4_hamiltonian/pallas_call | solution.py:234
  40.1 2.3 %collective-permute-start.11 = (f32[2,2,2,32,128]{4,3,2,1,0:T(8,128)S(1)}, f32[2,2,2,32,128]{4,3,2,1,0:T(8,128)S(1)}, u32[]{:S(2)}, u32[]{:S(2)}) collective-permute-start(f32[2,2,2,32,128]{4,3,2,1,0:T(8,128)S(1)} %get-tuple-element.43), channel_id=1, source_target_pairs={{0,6},{1,7},{2,4},{3,5},{4,2},{5,3},{6,0},{7,1},{8,14},{9,15},{10,... | collective-permute-start | bytes 393224 | tf_op jit(solution)/shard_map/ppermute | solution.py:312
  42.9 1.3 %collective-permute-start.13 = (f32[2,2,2,32,128]{4,3,2,1,0:T(8,128)S(1)}, f32[2,2,2,32,128]{4,3,2,1,0:T(8,128)S(1)}, u32[]{:S(2)}, u32[]{:S(2)}) collective-permute-start(f32[2,2,2,32,128]{4,3,2,1,0:T(8,128)S(1)} %get-tuple-element.45), channel_id=1, source_target_pairs={{0,4},{1,5},{2,6},{3,7},{4,0},{5,1},{6,2},{7,3},{8,12},{9,13},{10,... | collective-permute-start | bytes 393224 | tf_op jit(solution)/shard_map/ppermute | solution.py:312
  44.2 1.5 %collective-permute-start.14 = (f32[2,2,2,32,128]{4,3,2,1,0:T(8,128)S(1)}, f32[2,2,2,32,128]{4,3,2,1,0:T(8,128)S(1)}, u32[]{:S(2)}, u32[]{:S(2)}) collective-permute-start(f32[2,2,2,32,128]{4,3,2,1,0:T(8,128)S(1)} %get-tuple-element.46), channel_id=1, source_target_pairs={{0,2},{1,3},{2,0},{3,1},{4,6},{5,7},{6,4},{7,5},{8,10},{9,11},{10,... | collective-permute-start | bytes 393224 | tf_op jit(solution)/shard_map/ppermute | solution.py:312
  45.8 1.7 %collective-permute-done.11.refs_1_ = f32[2,2,2,32,128]{4,3,2,1,0:T(8,128)S(1)} collective-permute-done((f32[2,2,2,32,128]{4,3,2,1,0:T(8,128)S(1)}, f32[2,2,2,32,128]{4,3,2,1,0:T(8,128)S(1)}, u32[]{:S(2)}, u32[]{:S(2)}) %collective-permute-start.11) | collective-permute-done | bytes 131104 | tf_op jit(solution)/shard_map/ppermute | solution.py:312
  47.7 1.7 %collective-permute-done.12.refs_2_ = f32[2,2,2,32,128]{4,3,2,1,0:T(8,128)S(1)} collective-permute-done((f32[2,2,2,32,128]{4,3,2,1,0:T(8,128)S(1)}, f32[2,2,2,32,128]{4,3,2,1,0:T(8,128)S(1)}, u32[]{:S(2)}, u32[]{:S(2)}) %collective-permute-start.12) | collective-permute-done | bytes 131104 | tf_op jit(solution)/shard_map/ppermute | solution.py:312
  49.4 3.2 %collective-permute-done.13.refs_3_ = f32[2,2,2,32,128]{4,3,2,1,0:T(8,128)S(1)} collective-permute-done((f32[2,2,2,32,128]{4,3,2,1,0:T(8,128)S(1)}, f32[2,2,2,32,128]{4,3,2,1,0:T(8,128)S(1)}, u32[]{:S(2)}, u32[]{:S(2)}) %collective-permute-start.13) | collective-permute-done | bytes 131104 | tf_op jit(solution)/shard_map/ppermute | solution.py:312
  52.9 2.4 %collective-permute-done.15.refs_5_ = f32[2,2,2,32,128]{4,3,2,1,0:T(8,128)S(1)} collective-permute-done((f32[2,2,2,32,128]{4,3,2,1,0:T(8,128)S(1)}, f32[2,2,2,32,128]{4,3,2,1,0:T(8,128)S(1)}, u32[]{:S(2)}, u32[]{:S(2)}) %collective-permute-start.15) | collective-permute-done | bytes 131104 | tf_op jit(solution)/shard_map/ppermute | solution.py:312
  55.3 2.3 %gram.1 = f32[32,1,128]{2,1,0:T(1,128)} custom-call(f32[2,2,2,32,128]{4,3,2,1,0:T(8,128)S(1)} %collective-permute-done.10.refs_0_, f32[2,2,2,32,128]{4,3,2,1,0:T(8,128)S(1)} %collective-permute-done.11.refs_1_, f32[2,2,2,32,128]{4,3,2,1,0:T(8,128)S(1)} %collective-permute-done.12.refs_2_, f32[2,2,2,32,128]{4,3,2,1,0:T(8,128)S(1)} %collective-permute-done.13.refs_3_, ...), custom_call_target="tpu_custom_call" | custom-call | flops 1300000000 | bytes 4550000 | tf_op jit(solution)/shard_map/gram/pallas_call | solution.py:234
  57.6 1.3 %collective-permute-start.17 = (f32[2,8,32,128]{3,2,1,0:T(8,128)S(1)}, f32[2,8,32,128]{3,2,1,0:T(8,128)S(1)}, u32[]{:S(2)}, u32[]{:S(2)}) collective-permute-start(f32[2,8,32,128]{3,2,1,0:T(8,128)S(1)} %get-tuple-element.52), channel_id=1, source_target_pairs={{0,4},{4,0},{8,12},{12,8},{16,20},{20,16},{24,28},{28,24},{1,5},{5... | collective-permute-start | bytes 786440 | tf_op jit(solution)/shard_map/ppermute | solution.py:323
  58.9 4.9 %all-to-all-start = ((f32[32,1,128]{2,1,0:T(1,128)}), f32[32,1,128]{2,1,0:T(1,128)S(1)}, u32[]{:S(2)}, u32[]{:S(2)}) async-start(f32[32,1,128]{2,1,0:T(1,128)} %gram.1), calls=%async_computation | async-start | bytes 32768 | tf_op jit(solution)/shard_map/all_to_all | solution.py:324
  63.8 2.1 %collective-permute-done.17 = f32[2,8,32,128]{3,2,1,0:T(8,128)S(1)} collective-permute-done((f32[2,8,32,128]{3,2,1,0:T(8,128)S(1)}, f32[2,8,32,128]{3,2,1,0:T(8,128)S(1)}, u32[]{:S(2)}, u32[]{:S(2)}) %collective-permute-start.17) | collective-permute-done | bytes 262176 | tf_op jit(solution)/shard_map/ppermute | solution.py:323
  66.8 4.2 %all-to-all-done.x_ref = f32[32,1,128]{2,1,0:T(1,128)S(1)} async-done(((f32[32,1,128]{2,1,0:T(1,128)}), f32[32,1,128]{2,1,0:T(1,128)S(1)}, u32[]{:S(2)}, u32[]{:S(2)}) %all-to-all-start) | async-done | bytes 16416 | tf_op jit(solution)/shard_map/all_to_all | solution.py:324
  (28 shorter events, 8.4 us)
Async XLA Ops:
  0.6 1.2 %copy-start = (f32[8,32,128]{2,1,0:T(8,128)S(1)}, f32[8,32,128]{2,1,0:T(8,128)}, u32[]{:S(2)}) copy-start(f32[8,32,128]{2,1,0:T(8,128)} %refs_0_.1) | copy-start | bytes 393220
  1.9 16.6 %collective-permute-start.3 = (f32[1,16,32,128]{3,2,1,0:T(8,128)S(1)}, f32[1,16,32,128]{3,2,1,0:T(8,128)S(1)}, u32[]{:S(2)}, u32[]{:S(2)}) collective-permute-start(f32[1,16,32,128]{3,2,1,0:T(8,128)S(1)} %pad_maximum_fusion), channel_id=1, source_target_pairs={{0,4},{4,0},{8,12},{12,8},{16,20},{20,16},{24,28},{28,24},{1,5},{5... | collective-permute-start | bytes 786440 | tf_op jit(solution)/shard_map/ppermute | solution.py:278
  4.9 10.6 %collective-permute-start.4 = (f32[1,12,32,128]{3,2,1,0:T(8,128)S(1)}, f32[1,12,32,128]{3,2,1,0:T(8,128)S(1)}, u32[]{:S(2)}, u32[]{:S(2)}) collective-permute-start(f32[1,12,32,128]{3,2,1,0:T(8,128)S(1)} %get-tuple-element.61), channel_id=1, source_target_pairs={{0,28},{4,8},{8,4},{12,16},{16,12},{20,24},{24,20},{28,0},{1,29},{... | collective-permute-start | bytes 589832 | tf_op jit(solution)/shard_map/ppermute | solution.py:279
  8.6 9.6 %collective-permute-start.5 = (f32[1,12,32,128]{3,2,1,0:T(8,128)S(1)}, f32[1,12,32,128]{3,2,1,0:T(8,128)S(1)}, u32[]{:S(2)}, u32[]{:S(2)}) collective-permute-start(f32[1,12,32,128]{3,2,1,0:T(8,128)S(1)} %get-tuple-element.62.mine), channel_id=1, source_target_pairs={{0,24},{4,12},{8,0},{12,20},{16,8},{20,28},{24,16},{28,4},{1,25},{... | collective-permute-start | bytes 589832 | tf_op jit(solution)/shard_map/ppermute | solution.py:280
  9.0 14.6 %collective-permute-start.1 = (f32[1,8,32,128]{3,2,1,0:T(8,128)S(1)}, f32[1,8,32,128]{3,2,1,0:T(8,128)S(1)}, u32[]{:S(2)}, u32[]{:S(2)}) collective-permute-start(f32[1,8,32,128]{3,2,1,0:T(8,128)S(1)} %get-tuple-element.58), channel_id=1, source_target_pairs={{0,28},{4,8},{8,4},{12,16},{16,12},{20,24},{24,20},{28,0},{1,29},{... | collective-permute-start | bytes 393224 | tf_op jit(solution)/shard_map/ppermute | solution.py:279
  11.3 12.3 %collective-permute-start = (f32[1,8,32,128]{3,2,1,0:T(8,128)S(1)}, f32[1,8,32,128]{3,2,1,0:T(8,128)S(1)}, u32[]{:S(2)}, u32[]{:S(2)}) collective-permute-start(f32[1,8,32,128]{3,2,1,0:T(8,128)S(1)} %get-tuple-element.58), channel_id=1, source_target_pairs={{0,4},{4,0},{8,12},{12,8},{16,20},{20,16},{24,28},{28,24},{1,5},{5... | collective-permute-start | bytes 393224 | tf_op jit(solution)/shard_map/ppermute | solution.py:278
  15.6 8.2 %collective-permute-start.2 = (f32[1,8,32,128]{3,2,1,0:T(8,128)S(1)}, f32[1,8,32,128]{3,2,1,0:T(8,128)S(1)}, u32[]{:S(2)}, u32[]{:S(2)}) collective-permute-start(f32[1,8,32,128]{3,2,1,0:T(8,128)S(1)} %get-tuple-element.59.mine), channel_id=1, source_target_pairs={{0,24},{4,12},{8,0},{12,20},{16,8},{20,28},{24,16},{28,4},{1,25},{... | collective-permute-start | bytes 393224 | tf_op jit(solution)/shard_map/ppermute | solution.py:280
  19.5 9.6 %collective-permute-start.9 = (f32[1,8,32,128]{3,2,1,0:T(8,128)S(1)}, f32[1,8,32,128]{3,2,1,0:T(8,128)S(1)}, u32[]{:S(2)}, u32[]{:S(2)}) collective-permute-start(f32[1,8,32,128]{3,2,1,0:T(8,128)S(1)} %get-tuple-element.37.hi), channel_id=1, source_target_pairs={{0,8},{4,12},{8,16},{12,20},{16,24},{20,28},{24,0},{28,4},{1,9},{5... | collective-permute-start | bytes 393224 | tf_op jit(solution)/shard_map/ppermute | solution.py:298
  21.0 11.2 %collective-permute-start.8 = (f32[1,16,32,128]{3,2,1,0:T(8,128)S(1)}, f32[1,16,32,128]{3,2,1,0:T(8,128)S(1)}, u32[]{:S(2)}, u32[]{:S(2)}) collective-permute-start(f32[1,16,32,128]{3,2,1,0:T(8,128)S(1)} %get-tuple-element.36.lo), channel_id=1, source_target_pairs={{0,24},{4,28},{8,0},{12,4},{16,8},{20,12},{24,16},{28,20},{1,25},{... | collective-permute-start | bytes 786440 | tf_op jit(solution)/shard_map/ppermute | solution.py:299
  24.7 13.9 %collective-permute-start.7 = (f32[1,12,32,128]{3,2,1,0:T(8,128)S(1)}, f32[1,12,32,128]{3,2,1,0:T(8,128)S(1)}, u32[]{:S(2)}, u32[]{:S(2)}) collective-permute-start(f32[1,12,32,128]{3,2,1,0:T(8,128)S(1)} %get-tuple-element.34.lo), channel_id=1, source_target_pairs={{0,24},{4,28},{8,0},{12,4},{16,8},{20,12},{24,16},{28,20},{1,25},{... | collective-permute-start | bytes 589832 | tf_op jit(solution)/shard_map/ppermute | solution.py:299
  29.1 9.6 %collective-permute-start.6 = (f32[1,8,32,128]{3,2,1,0:T(8,128)S(1)}, f32[1,8,32,128]{3,2,1,0:T(8,128)S(1)}, u32[]{:S(2)}, u32[]{:S(2)}) collective-permute-start(f32[1,8,32,128]{3,2,1,0:T(8,128)S(1)} %get-tuple-element.33.hi), channel_id=1, source_target_pairs={{0,8},{4,12},{8,16},{12,20},{16,24},{20,28},{24,0},{28,4},{1,9},{5... | collective-permute-start | bytes 393224 | tf_op jit(solution)/shard_map/ppermute | solution.py:298
  40.1 5.6 %collective-permute-start.10 = (f32[2,2,2,32,128]{4,3,2,1,0:T(8,128)S(1)}, f32[2,2,2,32,128]{4,3,2,1,0:T(8,128)S(1)}, u32[]{:S(2)}, u32[]{:S(2)}) collective-permute-start(f32[2,2,2,32,128]{4,3,2,1,0:T(8,128)S(1)} %get-tuple-element.42), channel_id=1, source_target_pairs={{0,1},{1,0},{2,3},{3,2},{4,5},{5,4},{6,7},{7,6},{8,9},{9,8},{10,11... | collective-permute-start | bytes 393224 | tf_op jit(solution)/shard_map/ppermute | solution.py:312
  40.1 7.4 %collective-permute-start.11 = (f32[2,2,2,32,128]{4,3,2,1,0:T(8,128)S(1)}, f32[2,2,2,32,128]{4,3,2,1,0:T(8,128)S(1)}, u32[]{:S(2)}, u32[]{:S(2)}) collective-permute-start(f32[2,2,2,32,128]{4,3,2,1,0:T(8,128)S(1)} %get-tuple-element.43), channel_id=1, source_target_pairs={{0,6},{1,7},{2,4},{3,5},{4,2},{5,3},{6,0},{7,1},{8,14},{9,15},{10,... | collective-permute-start | bytes 393224 | tf_op jit(solution)/shard_map/ppermute | solution.py:312
  42.4 7.0 %collective-permute-start.12 = (f32[2,2,2,32,128]{4,3,2,1,0:T(8,128)S(1)}, f32[2,2,2,32,128]{4,3,2,1,0:T(8,128)S(1)}, u32[]{:S(2)}, u32[]{:S(2)}) collective-permute-start(f32[2,2,2,32,128]{4,3,2,1,0:T(8,128)S(1)} %get-tuple-element.44), channel_id=1, source_target_pairs={{0,7},{1,6},{2,5},{3,4},{4,3},{5,2},{6,1},{7,0},{8,15},{9,14},{10,... | collective-permute-start | bytes 393224 | tf_op jit(solution)/shard_map/ppermute | solution.py:312
  42.9 9.7 %collective-permute-start.13 = (f32[2,2,2,32,128]{4,3,2,1,0:T(8,128)S(1)}, f32[2,2,2,32,128]{4,3,2,1,0:T(8,128)S(1)}, u32[]{:S(2)}, u32[]{:S(2)}) collective-permute-start(f32[2,2,2,32,128]{4,3,2,1,0:T(8,128)S(1)} %get-tuple-element.45), channel_id=1, source_target_pairs={{0,4},{1,5},{2,6},{3,7},{4,0},{5,1},{6,2},{7,3},{8,12},{9,13},{10,... | collective-permute-start | bytes 393224 | tf_op jit(solution)/shard_map/ppermute | solution.py:312
  44.2 8.7 %collective-permute-start.14 = (f32[2,2,2,32,128]{4,3,2,1,0:T(8,128)S(1)}, f32[2,2,2,32,128]{4,3,2,1,0:T(8,128)S(1)}, u32[]{:S(2)}, u32[]{:S(2)}) collective-permute-start(f32[2,2,2,32,128]{4,3,2,1,0:T(8,128)S(1)} %get-tuple-element.46), channel_id=1, source_target_pairs={{0,2},{1,3},{2,0},{3,1},{4,6},{5,7},{6,4},{7,5},{8,10},{9,11},{10,... | collective-permute-start | bytes 393224 | tf_op jit(solution)/shard_map/ppermute | solution.py:312
  45.7 9.6 %collective-permute-start.15 = (f32[2,2,2,32,128]{4,3,2,1,0:T(8,128)S(1)}, f32[2,2,2,32,128]{4,3,2,1,0:T(8,128)S(1)}, u32[]{:S(2)}, u32[]{:S(2)}) collective-permute-start(f32[2,2,2,32,128]{4,3,2,1,0:T(8,128)S(1)} %get-tuple-element.47), channel_id=1, source_target_pairs={{0,5},{1,4},{2,7},{3,6},{4,1},{5,0},{6,3},{7,2},{8,13},{9,12},{10,... | collective-permute-start | bytes 393224 | tf_op jit(solution)/shard_map/ppermute | solution.py:312
  47.5 7.8 %collective-permute-start.16 = (f32[2,2,2,32,128]{4,3,2,1,0:T(8,128)S(1)}, f32[2,2,2,32,128]{4,3,2,1,0:T(8,128)S(1)}, u32[]{:S(2)}, u32[]{:S(2)}) collective-permute-start(f32[2,2,2,32,128]{4,3,2,1,0:T(8,128)S(1)} %get-tuple-element.48), channel_id=1, source_target_pairs={{0,3},{1,2},{2,1},{3,0},{4,7},{5,6},{6,5},{7,4},{8,11},{9,10},{10,... | collective-permute-start | bytes 393224 | tf_op jit(solution)/shard_map/ppermute | solution.py:312
  57.6 8.3 %collective-permute-start.17 = (f32[2,8,32,128]{3,2,1,0:T(8,128)S(1)}, f32[2,8,32,128]{3,2,1,0:T(8,128)S(1)}, u32[]{:S(2)}, u32[]{:S(2)}) collective-permute-start(f32[2,8,32,128]{3,2,1,0:T(8,128)S(1)} %get-tuple-element.52), channel_id=1, source_target_pairs={{0,4},{4,0},{8,12},{12,8},{16,20},{20,16},{24,28},{28,24},{1,5},{5... | collective-permute-start | bytes 786440 | tf_op jit(solution)/shard_map/ppermute | solution.py:323
  58.9 12.0 %all-to-all-start = ((f32[32,1,128]{2,1,0:T(1,128)}), f32[32,1,128]{2,1,0:T(1,128)S(1)}, u32[]{:S(2)}, u32[]{:S(2)}) async-start(f32[32,1,128]{2,1,0:T(1,128)} %gram.1), calls=%async_computation | async-start | bytes 32768 | tf_op jit(solution)/shard_map/all_to_all | solution.py:324

commit v3 on v2

--- a/solution.py
+++ b/solution.py
@@ -149,28 +149,40 @@
     def cells(which, k, per):
         return both[which, pl.ds(per * jnp.bitwise_xor(me, k), per)]
 
-    if len(outs) == 2:
-        blocks, home = outs
+    if len(outs) == 3:
+        blocks, keep, to_y = outs
+        per = blocks.shape[2]
         for k in range(blocks.shape[0]):
             for which in range(2):
-                blocks[k, which] = cells(which, k, blocks.shape[2])
-        for i, start in enumerate(homes):
-            home[i] = both[0, pl.ds(start, n)]
+                blocks[k, which] = cells(which, k, per)
+        keep[...] = both[0, pl.ds(homes[0], n)]
+        to_y[:n] = both[0, pl.ds(homes[1], n)]
+        to_y[n:] = cells(1, 4, per)
     else:
-        blocks_a, home_a, keep, send, *blocks = outs
+        blocks_a, keep_a, keep, *blocks = outs
+        per = blocks_a.shape[2]
+        keep[0] = keep_a[...]
+        keep[1] = both[0, pl.ds(homes[0], n)]
         for k, block in enumerate(blocks):
-            block[0] = blocks_a[k]
-            for which in range(2):
-                block[1, which] = cells(which, k, block.shape[2])
-        for i, ref in enumerate((keep, send)):
-            ref[0] = home_a[i]
-            ref[1] = both[0, pl.ds(homes[i], n)]
+            if k == 4:
+                block[:n] = both[0, pl.ds(homes[1], n)]
+                block[n:] = cells(1, k, per)
+            else:
+                block[0] = blocks_a[k]
+                for which in range(2):
+                    block[1, which] = cells(which, k, per)
 
 
 def gram(*refs):
-    *xs, out_ref, part = refs
+    *xs, out_ref, part, from_y = refs
     orbs = part.shape[1]
-    half, _, per, ny, nz = xs[0].shape
+    half, _, per, ny, nz = from_y.shape
+    at_y = PEERS.index(4)
+    n = xs[at_y].shape[0] - per
+    for o, x in enumerate(xs[at_y : at_y + 2]):
+        from_y[o, 0] = x[pl.ds(per * places()[1], per)]
+        from_y[o, 1] = x[n:]
+    xs[at_y : at_y + 2] = [from_y]
     rows = per * ny // 2
     each = 4 * half
     size = len(xs) * each
@@ -303,24 +315,36 @@
     group = 2 * orbs
     per = 2 * n // group
     scratch = [pltpu.VMEM((2, 2 * n, ny, nz), f32), field(2 * n + 12), field(2 * n + 4), products(2 * n + 12)]
-    outs = [(group, 2, per, ny, nz), (2, n, ny, nz)]
-    results = call(last_three, second[0], outs, scratch, 1.5, "filter_3_4_hamiltonian")
-    outs = [(half, n, ny, nz)] * 2 + [(half, 2, per, ny, nz)] * group
-    results = call(last_three, (*second[1], *results), outs, scratch, 1.5, "filter_3_4_hamiltonian")
-    keep, send, *blocks = results
-    xs = [
-        lax.ppermute(blocks[k], ("mem", "orb"), [(t, t ^ k) for t in range(group)]) if k else blocks[0] for k in PEERS
-    ]
+
+    def peer(x, k):
+        return lax.ppermute(x, ("mem", "orb"), [(t, t ^ k) for t in range(group)]) if k else x
+
+    outs = [(group, 2, per, ny, nz), (n, ny, nz), (n + per, ny, nz)]
+    blocks_a, keep, to_y = call(last_three, second[0], outs, scratch, 1.5, "filter_3_4_hamiltonian")
+    y_a = peer(to_y, 4)
+    shapes = [(half, 2, per, ny, nz)] * group
+    shapes[4] = (n + per, ny, nz)
+    keep, *blocks = call(
+        last_three,
+        (*second[1], blocks_a, keep),
+        [(half, n, ny, nz)] + shapes,
+        scratch,
+        1.5,
+        "filter_3_4_hamiltonian",
+    )
+    blocks[4], y_a = lax.optimization_barrier((blocks[4], y_a))
+    xs = [peer(blocks[k], k) for k in PEERS]
+    y_b = xs[PEERS.index(4)]
+    xs.insert(PEERS.index(4), y_a)
+    back = jnp.stack([y_a[:n], y_b[:n]])
     (sums,) = call(
         gram,
         xs,
         [(size * orbs, 1, 2 * own_orbs * count)],
-        [pltpu.VMEM((2, count, nz), f32)],
+        [pltpu.VMEM((2, count, nz), f32), pltpu.VMEM((half, 2, per, ny, nz), f32)],
         1.3,
         "gram",
     )
-    send, sums = lax.optimization_barrier((send, sums))
-    back = lax.ppermute(send, grid_axes, swap)
     sums = lax.all_to_all(sums, ("pair", "mem", "orb"), 0, 0, tiled=True)
     filtered = jnp.where(m == 0, jnp.concatenate([keep, back]), jnp.concatenate([back, keep]))
     sums, filtered = lax.optimization_barrier((sums, filtered))

time: 71.8 us -> 71.8 us (level)
  starting transfers between devices: 32.5 us -> 35.2 us
  waiting for transfers between devices: 28.4 us -> 25.7 us
    ppermute x8, waiting for transfers between devices: 11.4 us -> 8.79 us  [peer(): lax.ppermute(x, ('mem', 'orb'), [(t, t ^ k) for t in range(group)])]
    ppermute x2, waiting for transfers between devices: 5.08 us -> 2.87 us  [per_device(): rlo = lax.ppermute(hi, grid_axes, up)]
    ppermute x8, starting transfers between devices: 7.25 us -> 9.41 us  [peer(): lax.ppermute(x, ('mem', 'orb'), [(t, t ^ k) for t in range(group)])]
    all_to_all x1, waiting for transfers between devices: 4.17 us -> 6.28 us  [per_device(): sums = lax.all_to_all(sums, ('pair', 'mem', 'orb'), 0, 0, tiled=True)]
  transfers between devices with their start and end apart: 19 -> 19, of which waited for: 13 -> 12; matrix products, arithmetic and copies ran while one was open for 1% -> 1% of each run, Pallas kernels for 5% -> 7%
where the time goes in v3:
time: 71.8 us; the launch traced here: 71.6 us
  starting transfers between devices  35.2 us (49%)
  waiting for transfers between devices  25.7 us (36%)
  Pallas kernels  7.96 us (11%)
  local copies, waits for them, and re-layouts  1.2 us (2%)
  other arithmetic  0.9 us (1%)
  between operations  0.75 us (1%)
    ppermute x8, starting transfers between devices, peer(): lax.ppermute(x, ('mem', 'orb'), [(t, t ^ k) for t in range(group)])  9.41 us
    ppermute x8, waiting for transfers between devices, peer(): lax.ppermute(x, ('mem', 'orb'), [(t, t ^ k) for t in range(group)])  8.79 us
    pallas_call x7, Pallas kernels, call(): pl.pallas_call(body, out_shape=[s if isinstance(s, jax.ShapeDtypeStruct)...  7.96 us
    ppermute x2, starting transfers between devices, per_device(): rhi = lax.ppermute(lo, grid_axes, down)  6.88 us
    all_to_all x1, waiting for transfers between devices, per_device(): sums = lax.all_to_all(sums, ('pair', 'mem', 'orb'), 0, 0, tiled=True)  6.28 us
    ppermute x2, starting transfers between devices, per_device(): rb = lax.ppermute(b, grid_axes, cross)  5.91 us
    all_to_all x1, starting transfers between devices, per_device(): sums = lax.all_to_all(sums, ('pair', 'mem', 'orb'), 0, 0, tiled=True)  5.41 us
    ppermute x2, starting transfers between devices, per_device(): ra = lax.ppermute(a, grid_axes, swap)  3.77 us
  transfers between devices with their start and end apart: 19, of which 12 were waited for; matrix products, arithmetic and copies ran while one was open for 1% of the time, Pallas kernels for 7%

profile of v3, /device:TPU:0, one launch (start us, length us, event | category | flops | bytes accessed | tf_op | source)
XLA Modules:
  0.0 71.6 jit_solution(2454902745303195023)
XLA Ops:
  0.6 1.2 %constant_dynamic-slice_fusion = (f32[1,8,32,128]{3,2,1,0:T(8,128)S(1)}, f32[1,8,32,128]{3,2,1,0:T(8,128)S(1)}, f32[1,8,32,128]{3,2,1,0:T(8,128)S(1)}, f32[1,8,32,128]{3,2,1,0:T(8,128)S(1)}) fusion(f32[4,8,32,128]{3,2,1,0:T(8,128)} %param.2, s32[]{:T(128)S(6)} %select_n.33, s32[]{:T(128)S(6)} %select_n.29, s32[]{:T(128)S(6)} %select_n.28, s32[]{:T(128)S(6)} %select_n.30), kind=kLoop, calls=%fused_computation.7 | loop fusion | bytes 1048592 | tf_op jit(solution)/shard_map/dynamic_slice | solution.py:286
  1.9 3.0 %collective-permute-start.3 = (f32[1,16,32,128]{3,2,1,0:T(8,128)S(1)}, f32[1,16,32,128]{3,2,1,0:T(8,128)S(1)}, u32[]{:S(2)}, u32[]{:S(2)}) collective-permute-start(f32[1,16,32,128]{3,2,1,0:T(8,128)S(1)} %pad_maximum_fusion), channel_id=1, source_target_pairs={{0,4},{4,0},{8,12},{12,8},{16,20},{20,16},{24,28},{28,24},{1,5},{5... | collective-permute-start | bytes 786440 | tf_op jit(solution)/shard_map/ppermute | solution.py:290
  4.9 3.6 %collective-permute-start.4 = (f32[1,12,32,128]{3,2,1,0:T(8,128)S(1)}, f32[1,12,32,128]{3,2,1,0:T(8,128)S(1)}, u32[]{:S(2)}, u32[]{:S(2)}) collective-permute-start(f32[1,12,32,128]{3,2,1,0:T(8,128)S(1)} %get-tuple-element.61), channel_id=1, source_target_pairs={{0,28},{4,8},{8,4},{12,16},{16,12},{20,24},{24,20},{28,0},{1,29},{... | collective-permute-start | bytes 589832 | tf_op jit(solution)/shard_map/ppermute | solution.py:291
  9.0 2.3 %collective-permute-start.1 = (f32[1,8,32,128]{3,2,1,0:T(8,128)S(1)}, f32[1,8,32,128]{3,2,1,0:T(8,128)S(1)}, u32[]{:S(2)}, u32[]{:S(2)}) collective-permute-start(f32[1,8,32,128]{3,2,1,0:T(8,128)S(1)} %get-tuple-element.58), channel_id=1, source_target_pairs={{0,28},{4,8},{8,4},{12,16},{16,12},{20,24},{24,20},{28,0},{1,29},{... | collective-permute-start | bytes 393224 | tf_op jit(solution)/shard_map/ppermute | solution.py:291
  12.0 3.5 %collective-permute-done.4.rb = f32[1,12,32,128]{3,2,1,0:T(8,128)S(1)} collective-permute-done((f32[1,12,32,128]{3,2,1,0:T(8,128)S(1)}, f32[1,12,32,128]{3,2,1,0:T(8,128)S(1)}, u32[]{:S(2)}, u32[]{:S(2)}) %collective-permute-start.4) | collective-permute-done | bytes 196640 | tf_op jit(solution)/shard_map/ppermute | solution.py:291
  15.6 1.8 %collective-permute-start.2 = (f32[1,8,32,128]{3,2,1,0:T(8,128)S(1)}, f32[1,8,32,128]{3,2,1,0:T(8,128)S(1)}, u32[]{:S(2)}, u32[]{:S(2)}) collective-permute-start(f32[1,8,32,128]{3,2,1,0:T(8,128)S(1)} %get-tuple-element.59.mine), channel_id=1, source_target_pairs={{0,24},{4,12},{8,0},{12,20},{16,8},{20,28},{24,16},{28,4},{1,25},{... | collective-permute-start | bytes 393224 | tf_op jit(solution)/shard_map/ppermute | solution.py:292
  19.5 1.6 %collective-permute-start.9 = (f32[1,8,32,128]{3,2,1,0:T(8,128)S(1)}, f32[1,8,32,128]{3,2,1,0:T(8,128)S(1)}, u32[]{:S(2)}, u32[]{:S(2)}) collective-permute-start(f32[1,8,32,128]{3,2,1,0:T(8,128)S(1)} %get-tuple-element.37.hi), channel_id=1, source_target_pairs={{0,8},{4,12},{8,16},{12,20},{16,24},{20,28},{24,0},{28,4},{1,9},{5... | collective-permute-start | bytes 393224 | tf_op jit(solution)/shard_map/ppermute | solution.py:310
  21.0 2.5 %collective-permute-start.8 = (f32[1,16,32,128]{3,2,1,0:T(8,128)S(1)}, f32[1,16,32,128]{3,2,1,0:T(8,128)S(1)}, u32[]{:S(2)}, u32[]{:S(2)}) collective-permute-start(f32[1,16,32,128]{3,2,1,0:T(8,128)S(1)} %get-tuple-element.36.lo), channel_id=1, source_target_pairs={{0,24},{4,28},{8,0},{12,4},{16,8},{20,12},{24,16},{28,20},{1,25},{... | collective-permute-start | bytes 786440 | tf_op jit(solution)/shard_map/ppermute | solution.py:311
  24.7 4.3 %collective-permute-start.7 = (f32[1,12,32,128]{3,2,1,0:T(8,128)S(1)}, f32[1,12,32,128]{3,2,1,0:T(8,128)S(1)}, u32[]{:S(2)}, u32[]{:S(2)}) collective-permute-start(f32[1,12,32,128]{3,2,1,0:T(8,128)S(1)} %get-tuple-element.34.lo), channel_id=1, source_target_pairs={{0,24},{4,28},{8,0},{12,4},{16,8},{20,12},{24,16},{28,20},{1,25},{... | collective-permute-start | bytes 589832 | tf_op jit(solution)/shard_map/ppermute | solution.py:311
  29.1 3.1 %collective-permute-done.8.rhi.v_above = f32[1,16,32,128]{3,2,1,0:T(8,128)S(1)} collective-permute-done((f32[1,16,32,128]{3,2,1,0:T(8,128)S(1)}, f32[1,16,32,128]{3,2,1,0:T(8,128)S(1)}, u32[]{:S(2)}, u32[]{:S(2)}) %collective-permute-start.8) | collective-permute-done | bytes 262176 | tf_op jit(solution)/shard_map/ppermute | solution.py:311
  32.2 1.4 %filter_3_4_hamiltonian.2 = (f32[8,2,2,32,128]{4,3,2,1,0:T(8,128)S(1)}, f32[8,32,128]{2,1,0:T(8,128)S(1)}, f32[10,32,128]{2,1,0:T(8,128)S(1)}) custom-call(bf16[128,384]{1,0:T(8,128)(2,1)S(1)} %get-tuple-element.30.ymat, bf16[384,128]{1,0:T(8,128)(2,1)S(1)} %get-tuple-element.31.zmat, f32[1,8,32,128]{3,2,1,0:T(8,128)S(1)} %collective-permute-done.9.rlo, ...), custom_call_target="tpu_custom_call" | custom-call | flops 1500000000 | bytes 5250000 | tf_op jit(solution)/shard_map/filter_3_4_hamiltonian/pallas_call | solution.py:246
  33.6 2.2 %collective-permute-start.13 = (f32[10,32,128]{2,1,0:T(8,128)S(1)}, f32[10,32,128]{2,1,0:T(8,128)S(1)}, u32[]{:S(2)}, u32[]{:S(2)}) collective-permute-start(f32[10,32,128]{2,1,0:T(8,128)S(1)} %get-tuple-element.45), channel_id=1, source_target_pairs={{0,4},{1,5},{2,6},{3,7},{4,0},{5,1},{6,2},{7,3},{8,12},{9,13},{10,... | collective-permute-start | bytes 491528 | tf_op jit(solution)/shard_map/ppermute | solution.py:320
  35.8 2.9 %collective-permute-done.6.rlo = f32[1,8,32,128]{3,2,1,0:T(8,128)S(1)} collective-permute-done((f32[1,8,32,128]{3,2,1,0:T(8,128)S(1)}, f32[1,8,32,128]{3,2,1,0:T(8,128)S(1)}, u32[]{:S(2)}, u32[]{:S(2)}) %collective-permute-start.6) | collective-permute-done | bytes 131104 | tf_op jit(solution)/shard_map/ppermute | solution.py:310
  38.7 1.4 %filter_3_4_hamiltonian.3 = (f32[2,8,32,128]{3,2,1,0:T(8,128)S(1)}, f32[2,2,2,32,128]{4,3,2,1,0:T(8,128)S(1)}, f32[2,2,2,32,128]{4,3,2,1,0:T(8,128)S(1)}, f32[2,...) custom-call(bf16[128,384]{1,0:T(8,128)(2,1)S(1)} %get-tuple-element., ...), custom_call_target="tpu_custom_call" | custom-call | flops 1500000000 | bytes 5250000 | tf_op jit(solution)/shard_map/filter_3_4_hamiltonian/pallas_call | solution.py:246
  40.1 2.3 %collective-permute-start.11 = (f32[2,2,2,32,128]{4,3,2,1,0:T(8,128)S(1)}, f32[2,2,2,32,128]{4,3,2,1,0:T(8,128)S(1)}, u32[]{:S(2)}, u32[]{:S(2)}) collective-permute-start(f32[2,2,2,32,128]{4,3,2,1,0:T(8,128)S(1)} %get-tuple-element.42), channel_id=1, source_target_pairs={{0,6},{1,7},{2,4},{3,5},{4,2},{5,3},{6,0},{7,1},{8,14},{9,15},{10,... | collective-permute-start | bytes 393224 | tf_op jit(solution)/shard_map/ppermute | solution.py:320
  42.9 1.5 %collective-permute-start.15 = (f32[2,2,2,32,128]{4,3,2,1,0:T(8,128)S(1)}, f32[2,2,2,32,128]{4,3,2,1,0:T(8,128)S(1)}, u32[]{:S(2)}, u32[]{:S(2)}) collective-permute-start(f32[2,2,2,32,128]{4,3,2,1,0:T(8,128)S(1)} %get-tuple-element.48), channel_id=1, source_target_pairs={{0,2},{1,3},{2,0},{3,1},{4,6},{5,7},{6,4},{7,5},{8,10},{9,11},{10,... | collective-permute-start | bytes 393224 | tf_op jit(solution)/shard_map/ppermute | solution.py:320
  46.0 1.4 %collective-permute-done.11.refs_1_ = f32[2,2,2,32,128]{4,3,2,1,0:T(8,128)S(1)} collective-permute-done((f32[2,2,2,32,128]{4,3,2,1,0:T(8,128)S(1)}, f32[2,2,2,32,128]{4,3,2,1,0:T(8,128)S(1)}, u32[]{:S(2)}, u32[]{:S(2)}) %collective-permute-start.11) | collective-permute-done | bytes 131104 | tf_op jit(solution)/shard_map/ppermute | solution.py:320
  47.4 1.3 %collective-permute-start.14 = (f32[10,32,128]{2,1,0:T(8,128)S(1)}, f32[10,32,128]{2,1,0:T(8,128)S(1)}, u32[]{:S(2)}, u32[]{:S(2)}) collective-permute-start(f32[10,32,128]{2,1,0:T(8,128)S(1)} %get-tuple-element.47), channel_id=1, source_target_pairs={{0,4},{1,5},{2,6},{3,7},{4,0},{5,1},{6,2},{7,3},{8,12},{9,13},{10,... | collective-permute-start | bytes 491528 | tf_op jit(solution)/shard_map/ppermute | solution.py:320
  49.4 3.5 %collective-permute-done.15.refs_5_ = f32[2,2,2,32,128]{4,3,2,1,0:T(8,128)S(1)} collective-permute-done((f32[2,2,2,32,128]{4,3,2,1,0:T(8,128)S(1)}, f32[2,2,2,32,128]{4,3,2,1,0:T(8,128)S(1)}, u32[]{:S(2)}, u32[]{:S(2)}) %collective-permute-start.15) | collective-permute-done | bytes 131104 | tf_op jit(solution)/shard_map/ppermute | solution.py:320
  52.9 1.9 %collective-permute-done.17.refs_7_ = f32[2,2,2,32,128]{4,3,2,1,0:T(8,128)S(1)} collective-permute-done((f32[2,2,2,32,128]{4,3,2,1,0:T(8,128)S(1)}, f32[2,2,2,32,128]{4,3,2,1,0:T(8,128)S(1)}, u32[]{:S(2)}, u32[]{:S(2)}) %collective-permute-start.17) | collective-permute-done | bytes 131104 | tf_op jit(solution)/shard_map/ppermute | solution.py:320
  54.8 1.3 %collective-permute-done.14.refs_4_ = f32[10,32,128]{2,1,0:T(8,128)S(1)} collective-permute-done((f32[10,32,128]{2,1,0:T(8,128)S(1)}, f32[10,32,128]{2,1,0:T(8,128)S(1)}, u32[]{:S(2)}, u32[]{:S(2)}) %collective-permute-start.14) | collective-permute-done | bytes 163872 | tf_op jit(solution)/shard_map/ppermute | solution.py:320
  56.1 2.3 %gram.1 = f32[32,1,128]{2,1,0:T(1,128)} custom-call(f32[2,2,2,32,128]{4,3,2,1,0:T(8,128)S(1)} %collective-permute-done.10.refs_0_, f32[2,2,2,32,128]{4,3,2,1,0:T(8,128)S(1)} %collective-permute-done.11.refs_1_, f32[2,2,2,32,128]{4,3,2,1,0:T(8,128)S(1)} %collective-permute-done.12.refs_2_, f32[10,32,128]{2,1,0:T(8,128)S(1)} %collective-permute-done.13.refs_3_, ...), custom_call_target="tpu_custom_call" | custom-call | flops 1300000000 | bytes 4550000 | tf_op jit(solution)/shard_map/gram/pallas_call | solution.py:246
  58.4 5.4 %all-to-all-start = ((f32[32,1,128]{2,1,0:T(1,128)}), f32[32,1,128]{2,1,0:T(1,128)S(1)}, u32[]{:S(2)}, u32[]{:S(2)}) async-start(f32[32,1,128]{2,1,0:T(1,128)} %gram.1), calls=%async_computation | async-start | bytes 32768 | tf_op jit(solution)/shard_map/all_to_all | solution.py:348
  64.7 6.3 %all-to-all-done.x_ref = f32[32,1,128]{2,1,0:T(1,128)S(1)} async-done(((f32[32,1,128]{2,1,0:T(1,128)}), f32[32,1,128]{2,1,0:T(1,128)S(1)}, u32[]{:S(2)}, u32[]{:S(2)}) %all-to-all-start) | async-done | bytes 16416 | tf_op jit(solution)/shard_map/all_to_all | solution.py:348
  (30 shorter events, 8.9 us)
Async XLA Ops:
  0.6 1.2 %copy-start = (f32[8,32,128]{2,1,0:T(8,128)S(1)}, f32[8,32,128]{2,1,0:T(8,128)}, u32[]{:S(2)}) copy-start(f32[8,32,128]{2,1,0:T(8,128)} %refs_0_.1) | copy-start | bytes 393220
  1.9 16.6 %collective-permute-start.3 = (f32[1,16,32,128]{3,2,1,0:T(8,128)S(1)}, f32[1,16,32,128]{3,2,1,0:T(8,128)S(1)}, u32[]{:S(2)}, u32[]{:S(2)}) collective-permute-start(f32[1,16,32,128]{3,2,1,0:T(8,128)S(1)} %pad_maximum_fusion), channel_id=1, source_target_pairs={{0,4},{4,0},{8,12},{12,8},{16,20},{20,16},{24,28},{28,24},{1,5},{5... | collective-permute-start | bytes 786440 | tf_op jit(solution)/shard_map/ppermute | solution.py:290
  4.9 10.6 %collective-permute-start.4 = (f32[1,12,32,128]{3,2,1,0:T(8,128)S(1)}, f32[1,12,32,128]{3,2,1,0:T(8,128)S(1)}, u32[]{:S(2)}, u32[]{:S(2)}) collective-permute-start(f32[1,12,32,128]{3,2,1,0:T(8,128)S(1)} %get-tuple-element.61), channel_id=1, source_target_pairs={{0,28},{4,8},{8,4},{12,16},{16,12},{20,24},{24,20},{28,0},{1,29},{... | collective-permute-start | bytes 589832 | tf_op jit(solution)/shard_map/ppermute | solution.py:291
  8.6 9.6 %collective-permute-start.5 = (f32[1,12,32,128]{3,2,1,0:T(8,128)S(1)}, f32[1,12,32,128]{3,2,1,0:T(8,128)S(1)}, u32[]{:S(2)}, u32[]{:S(2)}) collective-permute-start(f32[1,12,32,128]{3,2,1,0:T(8,128)S(1)} %get-tuple-element.62.mine), channel_id=1, source_target_pairs={{0,24},{4,12},{8,0},{12,20},{16,8},{20,28},{24,16},{28,4},{1,25},{... | collective-permute-start | bytes 589832 | tf_op jit(solution)/shard_map/ppermute | solution.py:292
  9.0 14.6 %collective-permute-start.1 = (f32[1,8,32,128]{3,2,1,0:T(8,128)S(1)}, f32[1,8,32,128]{3,2,1,0:T(8,128)S(1)}, u32[]{:S(2)}, u32[]{:S(2)}) collective-permute-start(f32[1,8,32,128]{3,2,1,0:T(8,128)S(1)} %get-tuple-element.58), channel_id=1, source_target_pairs={{0,28},{4,8},{8,4},{12,16},{16,12},{20,24},{24,20},{28,0},{1,29},{... | collective-permute-start | bytes 393224 | tf_op jit(solution)/shard_map/ppermute | solution.py:291
  11.3 12.3 %collective-permute-start = (f32[1,8,32,128]{3,2,1,0:T(8,128)S(1)}, f32[1,8,32,128]{3,2,1,0:T(8,128)S(1)}, u32[]{:S(2)}, u32[]{:S(2)}) collective-permute-start(f32[1,8,32,128]{3,2,1,0:T(8,128)S(1)} %get-tuple-element.58), channel_id=1, source_target_pairs={{0,4},{4,0},{8,12},{12,8},{16,20},{20,16},{24,28},{28,24},{1,5},{5... | collective-permute-start | bytes 393224 | tf_op jit(solution)/shard_map/ppermute | solution.py:290
  15.6 8.2 %collective-permute-start.2 = (f32[1,8,32,128]{3,2,1,0:T(8,128)S(1)}, f32[1,8,32,128]{3,2,1,0:T(8,128)S(1)}, u32[]{:S(2)}, u32[]{:S(2)}) collective-permute-start(f32[1,8,32,128]{3,2,1,0:T(8,128)S(1)} %get-tuple-element.59.mine), channel_id=1, source_target_pairs={{0,24},{4,12},{8,0},{12,20},{16,8},{20,28},{24,16},{28,4},{1,25},{... | collective-permute-start | bytes 393224 | tf_op jit(solution)/shard_map/ppermute | solution.py:292
  19.5 9.6 %collective-permute-start.9 = (f32[1,8,32,128]{3,2,1,0:T(8,128)S(1)}, f32[1,8,32,128]{3,2,1,0:T(8,128)S(1)}, u32[]{:S(2)}, u32[]{:S(2)}) collective-permute-start(f32[1,8,32,128]{3,2,1,0:T(8,128)S(1)} %get-tuple-element.37.hi), channel_id=1, source_target_pairs={{0,8},{4,12},{8,16},{12,20},{16,24},{20,28},{24,0},{28,4},{1,9},{5... | collective-permute-start | bytes 393224 | tf_op jit(solution)/shard_map/ppermute | solution.py:310
  21.0 11.2 %collective-permute-start.8 = (f32[1,16,32,128]{3,2,1,0:T(8,128)S(1)}, f32[1,16,32,128]{3,2,1,0:T(8,128)S(1)}, u32[]{:S(2)}, u32[]{:S(2)}) collective-permute-start(f32[1,16,32,128]{3,2,1,0:T(8,128)S(1)} %get-tuple-element.36.lo), channel_id=1, source_target_pairs={{0,24},{4,28},{8,0},{12,4},{16,8},{20,12},{24,16},{28,20},{1,25},{... | collective-permute-start | bytes 786440 | tf_op jit(solution)/shard_map/ppermute | solution.py:311
  24.7 13.9 %collective-permute-start.7 = (f32[1,12,32,128]{3,2,1,0:T(8,128)S(1)}, f32[1,12,32,128]{3,2,1,0:T(8,128)S(1)}, u32[]{:S(2)}, u32[]{:S(2)}) collective-permute-start(f32[1,12,32,128]{3,2,1,0:T(8,128)S(1)} %get-tuple-element.34.lo), channel_id=1, source_target_pairs={{0,24},{4,28},{8,0},{12,4},{16,8},{20,12},{24,16},{28,20},{1,25},{... | collective-permute-start | bytes 589832 | tf_op jit(solution)/shard_map/ppermute | solution.py:311
  29.1 9.6 %collective-permute-start.6 = (f32[1,8,32,128]{3,2,1,0:T(8,128)S(1)}, f32[1,8,32,128]{3,2,1,0:T(8,128)S(1)}, u32[]{:S(2)}, u32[]{:S(2)}) collective-permute-start(f32[1,8,32,128]{3,2,1,0:T(8,128)S(1)} %get-tuple-element.33.hi), channel_id=1, source_target_pairs={{0,8},{4,12},{8,16},{12,20},{16,24},{20,28},{24,0},{28,4},{1,9},{5... | collective-permute-start | bytes 393224 | tf_op jit(solution)/shard_map/ppermute | solution.py:310
  33.6 10.8 %collective-permute-start.13 = (f32[10,32,128]{2,1,0:T(8,128)S(1)}, f32[10,32,128]{2,1,0:T(8,128)S(1)}, u32[]{:S(2)}, u32[]{:S(2)}) collective-permute-start(f32[10,32,128]{2,1,0:T(8,128)S(1)} %get-tuple-element.45), channel_id=1, source_target_pairs={{0,4},{1,5},{2,6},{3,7},{4,0},{5,1},{6,2},{7,3},{8,12},{9,13},{10,... | collective-permute-start | bytes 491528 | tf_op jit(solution)/shard_map/ppermute | solution.py:320
  40.0 5.3 %collective-permute-start.10 = (f32[2,2,2,32,128]{4,3,2,1,0:T(8,128)S(1)}, f32[2,2,2,32,128]{4,3,2,1,0:T(8,128)S(1)}, u32[]{:S(2)}, u32[]{:S(2)}) collective-permute-start(f32[2,2,2,32,128]{4,3,2,1,0:T(8,128)S(1)} %get-tuple-element.41), channel_id=1, source_target_pairs={{0,1},{1,0},{2,3},{3,2},{4,5},{5,4},{6,7},{7,6},{8,9},{9,8},{10,11... | collective-permute-start | bytes 393224 | tf_op jit(solution)/shard_map/ppermute | solution.py:320
  40.1 7.3 %collective-permute-start.11 = (f32[2,2,2,32,128]{4,3,2,1,0:T(8,128)S(1)}, f32[2,2,2,32,128]{4,3,2,1,0:T(8,128)S(1)}, u32[]{:S(2)}, u32[]{:S(2)}) collective-permute-start(f32[2,2,2,32,128]{4,3,2,1,0:T(8,128)S(1)} %get-tuple-element.42), channel_id=1, source_target_pairs={{0,6},{1,7},{2,4},{3,5},{4,2},{5,3},{6,0},{7,1},{8,14},{9,15},{10,... | collective-permute-start | bytes 393224 | tf_op jit(solution)/shard_map/ppermute | solution.py:320
  42.4 7.0 %collective-permute-start.12 = (f32[2,2,2,32,128]{4,3,2,1,0:T(8,128)S(1)}, f32[2,2,2,32,128]{4,3,2,1,0:T(8,128)S(1)}, u32[]{:S(2)}, u32[]{:S(2)}) collective-permute-start(f32[2,2,2,32,128]{4,3,2,1,0:T(8,128)S(1)} %get-tuple-element.43), channel_id=1, source_target_pairs={{0,7},{1,6},{2,5},{3,4},{4,3},{5,2},{6,1},{7,0},{8,15},{9,14},{10,... | collective-permute-start | bytes 393224 | tf_op jit(solution)/shard_map/ppermute | solution.py:320
  42.9 10.0 %collective-permute-start.15 = (f32[2,2,2,32,128]{4,3,2,1,0:T(8,128)S(1)}, f32[2,2,2,32,128]{4,3,2,1,0:T(8,128)S(1)}, u32[]{:S(2)}, u32[]{:S(2)}) collective-permute-start(f32[2,2,2,32,128]{4,3,2,1,0:T(8,128)S(1)} %get-tuple-element.48), channel_id=1, source_target_pairs={{0,2},{1,3},{2,0},{3,1},{4,6},{5,7},{6,4},{7,5},{8,10},{9,11},{10,... | collective-permute-start | bytes 393224 | tf_op jit(solution)/shard_map/ppermute | solution.py:320
  44.4 8.5 %collective-permute-start.16 = (f32[2,2,2,32,128]{4,3,2,1,0:T(8,128)S(1)}, f32[2,2,2,32,128]{4,3,2,1,0:T(8,128)S(1)}, u32[]{:S(2)}, u32[]{:S(2)}) collective-permute-start(f32[2,2,2,32,128]{4,3,2,1,0:T(8,128)S(1)} %get-tuple-element.49), channel_id=1, source_target_pairs={{0,5},{1,4},{2,7},{3,6},{4,1},{5,0},{6,3},{7,2},{8,13},{9,12},{10,... | collective-permute-start | bytes 393224 | tf_op jit(solution)/shard_map/ppermute | solution.py:320
  45.4 9.4 %collective-permute-start.17 = (f32[2,2,2,32,128]{4,3,2,1,0:T(8,128)S(1)}, f32[2,2,2,32,128]{4,3,2,1,0:T(8,128)S(1)}, u32[]{:S(2)}, u32[]{:S(2)}) collective-permute-start(f32[2,2,2,32,128]{4,3,2,1,0:T(8,128)S(1)} %get-tuple-element.50), channel_id=1, source_target_pairs={{0,3},{1,2},{2,1},{3,0},{4,7},{5,6},{6,5},{7,4},{8,11},{9,10},{10,... | collective-permute-start | bytes 393224 | tf_op jit(solution)/shard_map/ppermute | solution.py:320
  47.4 8.7 %collective-permute-start.14 = (f32[10,32,128]{2,1,0:T(8,128)S(1)}, f32[10,32,128]{2,1,0:T(8,128)S(1)}, u32[]{:S(2)}, u32[]{:S(2)}) collective-permute-start(f32[10,32,128]{2,1,0:T(8,128)S(1)} %get-tuple-element.47), channel_id=1, source_target_pairs={{0,4},{1,5},{2,6},{3,7},{4,0},{5,1},{6,2},{7,3},{8,12},{9,13},{10,... | collective-permute-start | bytes 491528 | tf_op jit(solution)/shard_map/ppermute | solution.py:320
  58.4 12.6 %all-to-all-start = ((f32[32,1,128]{2,1,0:T(1,128)}), f32[32,1,128]{2,1,0:T(1,128)S(1)}, u32[]{:S(2)}, u32[]{:S(2)}) async-start(f32[32,1,128]{2,1,0:T(1,128)} %gram.1), calls=%async_computation | async-start | bytes 32768 | tf_op jit(solution)/shard_map/all_to_all | solution.py:348

commit v4 on v2

--- a/solution.py
+++ b/solution.py
@@ -18,7 +18,7 @@
 S1 = HALF / (LOWER - CENTRE)
 T2 = 2.0 / S1**2 - 1.0
 T4 = 2.0 * T2 * T2 - 1.0
-PEERS = (1, 6, 7, 4, 2, 5, 3, 0)
+PEERS = (6, 7, 4, 5, 2, 3, 1, 0)
 CHUNK = 4
 
 
@@ -149,35 +149,44 @@
     def cells(which, k, per):
         return both[which, pl.ds(per * jnp.bitwise_xor(me, k), per)]
 
+    keep, *outs = outs
+    keep[...] = both[0, pl.ds(homes[0], n)]
     if len(outs) == 2:
-        blocks, home = outs
-        for k in range(blocks.shape[0]):
-            for which in range(2):
-                blocks[k, which] = cells(which, k, blocks.shape[2])
-        for i, start in enumerate(homes):
-            home[i] = both[0, pl.ds(start, n)]
+        blocks, send = outs
+        per = blocks.shape[2]
+        for t in range(blocks.shape[0]):
+            blocks[t] = both[:, per * t : per * (t + 1)]
+        send[...] = both[0, pl.ds(homes[1], n)]
     else:
-        blocks_a, home_a, keep, send, *blocks = outs
-        for k, block in enumerate(blocks):
-            block[0] = blocks_a[k]
-            for which in range(2):
-                block[1, which] = cells(which, k, block.shape[2])
-        for i, ref in enumerate((keep, send)):
-            ref[0] = home_a[i]
-            ref[1] = both[0, pl.ds(homes[i], n)]
-
-
-def gram(*refs):
-    *xs, out_ref, part = refs
+        per = outs[0].shape[1]
+        for k, block in enumerate(outs):
+            if k == 4:
+                block[:n] = both[0, pl.ds(homes[1], n)]
+                block[n:] = cells(1, k, per)
+            else:
+                for which in range(2):
+                    block[which] = cells(which, k, per)
+
+
+def gram(first, *refs):
+    *xs, out_ref, part, second = refs
     orbs = part.shape[1]
-    half, _, per, ny, nz = xs[0].shape
-    rows = per * ny // 2
-    each = 4 * half
-    size = len(xs) * each
-    flat = [x.reshape(each * rows, nz) for x in xs]
+    peers, _, per, ny, nz = first.shape
+    _, place, me = places()
+    for k, x in zip(PEERS, xs):
+        peer = jnp.bitwise_xor(me, k)
+        if k == 4:
+            second[peer, 0] = x[pl.ds(per * place, per)]
+            second[peer, 1] = x[x.shape[0] - per :]
+        else:
+            second[peer] = x[...]
+    rows = per * ny
+    flat = [x.reshape(peers * 2 * rows, nz) for x in (first, second)]
     fields = jnp.concatenate(
         [
-            jnp.concatenate([x[pl.ds(r, each, stride=rows), :] for x in flat], axis=0)
+            jnp.concatenate(
+                [x[pl.ds(which * rows + r, peers, stride=2 * rows), :] for which in range(2) for x in flat], axis=0
+            )
             for r in range(rows)
         ],
         axis=1,
@@ -190,32 +199,27 @@
         )
 
     both = product(fields, fields, (1, 1))
-    row = lax.broadcasted_iota(jnp.int32, (size, size), 0)
-    col = lax.broadcasted_iota(jnp.int32, (size, size), 1)
-    both = jnp.where(row % 2 == col % 2, both, 0.0)
-    col = lax.broadcasted_iota(jnp.int32, (2 * orbs, size), 1)
-    which_peer = col // each
-    peer = jnp.zeros_like(col)
-    for i, k in enumerate(PEERS):
-        peer = jnp.where(which_peer == i, k, peer)
-    peer = jnp.bitwise_xor(peer, places()[2])
-    target = orbs * (col // 2 % 2) + 2 * half * (peer % 4) + half * (peer // 4) + col // 4 % half
-    order = (lax.broadcasted_iota(jnp.int32, (2 * orbs, size), 0) == target).astype(jnp.float32)
-    both = product(order, product(both, order, (1, 1)), (1, 0))
+    both = jnp.concatenate([both[:orbs, :orbs], both[orbs:, :orbs] + both[:orbs, orbs:]], axis=0)
+    row = lax.broadcasted_iota(jnp.int32, (orbs, orbs), 0)
+    quarter = peers // 2
+    target = 4 * (row % quarter) + 2 * (row // quarter % 2) + row // peers
+    order = (lax.broadcasted_iota(jnp.int32, (orbs, orbs), 1) == target).astype(jnp.float32)
+    both = product(both, order, (1, 0))
     part[...] = jnp.zeros_like(part)
-    part[0, :, :orbs] = both[:orbs, :orbs]
-    part[1, :, :orbs] = both[orbs:, :orbs] + both[:orbs, orbs:]
+    for which in range(2):
+        part[which, :, :orbs] = both[which * orbs : (which + 1) * orbs]
     own = nz // (2 * orbs)
-    groups = orbs // own
-    packed = part[0, pl.ds(0, groups, stride=own), :]
-    for i in range(1, 2 * own):
-        packed = packed + pltpu.roll(part[i // own, pl.ds(i % own, groups, stride=own), :], i * orbs, 1)
+    packed = jnp.zeros((quarter, nz), jnp.float32)
+    for i in range(2 * own):
+        start = i % 2 * peers + i % own // 2 * quarter
+        rolled = part[i // own, start : start + quarter, :]
+        packed = packed + (pltpu.roll(rolled, i * orbs, 1) if i else rolled)
 
     def spread(g, _):
-        out_ref[pl.ds(g * groups, groups)] = packed.reshape(groups, 1, nz)
+        out_ref[pl.ds(g * quarter, quarter)] = packed.reshape(quarter, 1, nz)
         return 0
 
-    lax.fori_loop(0, out_ref.shape[0] // groups, spread, 0)
+    lax.fori_loop(0, out_ref.shape[0] // quarter, spread, 0)
 
 
 def finish(cells, x_ref, c_ref, h_ref):
@@ -303,25 +307,33 @@
     group = 2 * orbs
     per = 2 * n // group
     scratch = [pltpu.VMEM((2, 2 * n, ny, nz), f32), field(2 * n + 12), field(2 * n + 4), products(2 * n + 12)]
-    outs = [(group, 2, per, ny, nz), (2, n, ny, nz)]
-    results = call(last_three, second[0], outs, scratch, 1.5, "filter_3_4_hamiltonian")
-    outs = [(half, n, ny, nz)] * 2 + [(half, 2, per, ny, nz)] * group
-    results = call(last_three, (*second[1], *results), outs, scratch, 1.5, "filter_3_4_hamiltonian")
-    keep, send, *blocks = results
-    xs = [
-        lax.ppermute(blocks[k], ("mem", "orb"), [(t, t ^ k) for t in range(group)]) if k else blocks[0] for k in PEERS
-    ]
+
+    def peer(x, k):
+        return lax.ppermute(x, ("mem", "orb"), [(t, t ^ k) for t in range(group)]) if k else x
+
+    block = (2, per, ny, nz)
+    outs = [(n, ny, nz), (group, *block), (n, ny, nz)]
+    keep_a, blocks, send = call(last_three, second[0], outs, scratch, 1.5, "filter_3_4_hamiltonian")
+    first = lax.all_to_all(blocks, ("mem", "orb"), 0, 0, tiled=True)
+    back_a = peer(send, 4)
+    hi, _ = lax.optimization_barrier((second[1][4], keep_a))
+    outs = [(n, ny, nz)] + [block] * 4 + [(n + per, ny, nz)] + [block] * 3
+    keep_b, *blocks = call(
+        last_three, (*second[1][:4], hi, *second[1][5:]), outs, scratch, 1.5, "filter_3_4_hamiltonian"
+    )
+    blocks[1], first = lax.optimization_barrier((blocks[1], first))
+    xs = [peer(blocks[k], k) for k in PEERS]
+    back_b = xs[PEERS.index(4)][:n]
     (sums,) = call(
         gram,
-        xs,
+        (first, *xs),
         [(size * orbs, 1, 2 * own_orbs * count)],
-        [pltpu.VMEM((2, count, nz), f32)],
+        [pltpu.VMEM((2, count, nz), f32), pltpu.VMEM((group, *block), f32)],
         1.3,
         "gram",
     )
-    send, sums = lax.optimization_barrier((send, sums))
-    back = lax.ppermute(send, grid_axes, swap)
     sums = lax.all_to_all(sums, ("pair", "mem", "orb"), 0, 0, tiled=True)
+    keep, back = jnp.stack([keep_a, keep_b]), jnp.stack([back_a, back_b])
     filtered = jnp.where(m == 0, jnp.concatenate([keep, back]), jnp.concatenate([back, keep]))
     sums, filtered = lax.optimization_barrier((sums, filtered))
     corr, ham = call(

time: 71.8 us -> 75.3 us (1.049)
  starting transfers between devices: 32.5 us -> 35.8 us
    ppermute x8, waiting for transfers between devices: 11.4 us -> 4.61 us  [peer(): lax.ppermute(x, ('mem', 'orb'), [(t, t ^ k) for t in range(group)])]
    ppermute x2, waiting for transfers between devices: 5.08 us -> 11.6 us  [per_device(): rlo = lax.ppermute(hi, grid_axes, up)]
    all_to_all x0 -> x1, starting transfers between devices: none -> 4.98 us  [per_device(): first = lax.all_to_all(blocks, ('mem', 'orb'), 0, 0, tiled=True)]
    ppermute x2, waiting for transfers between devices: 3.12 us -> 0.01 us  [per_device(): rhi = lax.ppermute(lo, grid_axes, down)]
    all_to_all x1, starting transfers between devices: 4.88 us -> 2.52 us  [per_device(): sums = lax.all_to_all(sums, ('pair', 'mem', 'orb'), 0, 0, tiled=True)]
    all_to_all x1, waiting for transfers between devices: 4.17 us -> 6.28 us  [per_device(): sums = lax.all_to_all(sums, ('pair', 'mem', 'orb'), 0, 0, tiled=True)]
    ppermute x2, starting transfers between devices: 6.88 us -> 8.45 us  [per_device(): rhi = lax.ppermute(lo, grid_axes, down)]
    ppermute x2, starting transfers between devices: 1.56 us -> 0.42 us  [per_device(): rlo = lax.ppermute(hi, grid_axes, up)]
  transfers between devices with their start and end apart: 19 -> 20, of which waited for: 13 -> 10; matrix products, arithmetic and copies ran while one was open for 1% -> 1% of each run, Pallas kernels for 5% -> 10%
where the time goes in v4:
time: 75.3 us; the launch traced here: 75 us
  starting transfers between devices  35.8 us (48%)
  waiting for transfers between devices  28 us (37%)
  Pallas kernels  8.41 us (11%)
  local copies, waits for them, and re-layouts  1.18 us (2%)
  other arithmetic  0.91 us (1%)
    ppermute x2, waiting for transfers between devices, per_device(): rlo = lax.ppermute(hi, grid_axes, up)  11.6 us
    ppermute x2, starting transfers between devices, per_device(): rhi = lax.ppermute(lo, grid_axes, down)  8.45 us
    pallas_call x7, Pallas kernels, call(): pl.pallas_call(body, out_shape=[s if isinstance(s, jax.ShapeDtypeStruct)...  8.41 us
    ppermute x8, starting transfers between devices, peer(): lax.ppermute(x, ('mem', 'orb'), [(t, t ^ k) for t in range(group)])  8.28 us
    all_to_all x1, waiting for transfers between devices, per_device(): sums = lax.all_to_all(sums, ('pair', 'mem', 'orb'), 0, 0, tiled=True)  6.28 us
    ppermute x2, starting transfers between devices, per_device(): rb = lax.ppermute(b, grid_axes, cross)  5.3 us
    all_to_all x1, starting transfers between devices, per_device(): first = lax.all_to_all(blocks, ('mem', 'orb'), 0, 0, tiled=True)  4.98 us
    ppermute x8, waiting for transfers between devices, peer(): lax.ppermute(x, ('mem', 'orb'), [(t, t ^ k) for t in range(group)])  4.61 us
  transfers between devices with their start and end apart: 20, of which 10 were waited for; matrix products, arithmetic and copies ran while one was open for 1% of the time, Pallas kernels for 10%

profile of v4, /device:TPU:0, one launch (start us, length us, event | category | flops | bytes accessed | tf_op | source)
XLA Modules:
  0.0 75.0 jit_solution(8294078426710472919)
XLA Ops:
  0.6 1.2 %constant_dynamic-slice_fusion = (f32[1,8,32,128]{3,2,1,0:T(8,128)S(1)}, f32[1,8,32,128]{3,2,1,0:T(8,128)S(1)}, f32[1,8,32,128]{3,2,1,0:T(8,128)S(1)}, f32[1,8,32,128]{3,2,1,0:T(8,128)S(1)}) fusion(f32[4,8,32,128]{3,2,1,0:T(8,128)} %param.2, s32[]{:T(128)S(6)} %select_n.33, s32[]{:T(128)S(6)} %select_n.29, s32[]{:T(128)S(6)} %select_n.28, s32[]{:T(128)S(6)} %select_n.30), kind=kLoop, calls=%fused_computation.6 | loop fusion | bytes 1048592 | tf_op jit(solution)/shard_map/dynamic_slice | solution.py:278
  1.9 3.0 %collective-permute-start.3 = (f32[1,16,32,128]{3,2,1,0:T(8,128)S(1)}, f32[1,16,32,128]{3,2,1,0:T(8,128)S(1)}, u32[]{:S(2)}, u32[]{:S(2)}) collective-permute-start(f32[1,16,32,128]{3,2,1,0:T(8,128)S(1)} %pad_maximum_fusion), channel_id=1, source_target_pairs={{0,4},{4,0},{8,12},{12,8},{16,20},{20,16},{24,28},{28,24},{1,5},{5... | collective-permute-start | bytes 786440 | tf_op jit(solution)/shard_map/ppermute | solution.py:282
  4.9 3.6 %collective-permute-start.4 = (f32[1,12,32,128]{3,2,1,0:T(8,128)S(1)}, f32[1,12,32,128]{3,2,1,0:T(8,128)S(1)}, u32[]{:S(2)}, u32[]{:S(2)}) collective-permute-start(f32[1,12,32,128]{3,2,1,0:T(8,128)S(1)} %get-tuple-element.63), channel_id=1, source_target_pairs={{0,28},{4,8},{8,4},{12,16},{16,12},{20,24},{24,20},{28,0},{1,29},{... | collective-permute-start | bytes 589832 | tf_op jit(solution)/shard_map/ppermute | solution.py:283
  9.6 1.7 %collective-permute-start.1 = (f32[1,8,32,128]{3,2,1,0:T(8,128)S(1)}, f32[1,8,32,128]{3,2,1,0:T(8,128)S(1)}, u32[]{:S(2)}, u32[]{:S(2)}) collective-permute-start(f32[1,8,32,128]{3,2,1,0:T(8,128)S(1)} %get-tuple-element.60), channel_id=1, source_target_pairs={{0,28},{4,8},{8,4},{12,16},{16,12},{20,24},{24,20},{28,0},{1,29},{... | collective-permute-start | bytes 393224 | tf_op jit(solution)/shard_map/ppermute | solution.py:283
  11.3 4.3 %collective-permute-done.4.rb = f32[1,12,32,128]{3,2,1,0:T(8,128)S(1)} collective-permute-done((f32[1,12,32,128]{3,2,1,0:T(8,128)S(1)}, f32[1,12,32,128]{3,2,1,0:T(8,128)S(1)}, u32[]{:S(2)}, u32[]{:S(2)}) %collective-permute-start.4) | collective-permute-done | bytes 196640 | tf_op jit(solution)/shard_map/ppermute | solution.py:283
  15.6 1.8 %collective-permute-start.2 = (f32[1,8,32,128]{3,2,1,0:T(8,128)S(1)}, f32[1,8,32,128]{3,2,1,0:T(8,128)S(1)}, u32[]{:S(2)}, u32[]{:S(2)}) collective-permute-start(f32[1,8,32,128]{3,2,1,0:T(8,128)S(1)} %get-tuple-element.61.mine), channel_id=1, source_target_pairs={{0,24},{4,12},{8,0},{12,20},{16,8},{20,28},{24,16},{28,4},{1,25},{... | collective-permute-start | bytes 393224 | tf_op jit(solution)/shard_map/ppermute | solution.py:284
  18.5 1.0 %filter_1_2.2 = (f32[1,16,32,128]{3,2,1,0:T(8,128)S(1)}, f32[1,8,32,128]{3,2,1,0:T(8,128)S(1)}, f32[1,20,32,128]{3,2,1,0:T(8,128)S(1)}, f32[24,32,128]{2,1,0:T(8,128)S(1)}) custom-call(bf16[128,384]{1,0:T(8,128)(2,1)S(1)} %get-tuple-element.31.ymat, bf16[384,128]{1,0:T(8,128)(2,1)S(1)} %get-tuple-element.32.zmat, ...), custom_call_target="tpu_custom_call" | custom-call | flops 1000000000 | bytes 3500000 | tf_op jit(solution)/shard_map/filter_1_2/pallas_call | solution.py:238
  19.5 4.0 %collective-permute-start.8 = (f32[1,16,32,128]{3,2,1,0:T(8,128)S(1)}, f32[1,16,32,128]{3,2,1,0:T(8,128)S(1)}, u32[]{:S(2)}, u32[]{:S(2)}) collective-permute-start(f32[1,16,32,128]{3,2,1,0:T(8,128)S(1)} %get-tuple-element.37.lo), channel_id=1, source_target_pairs={{0,24},{4,28},{8,0},{12,4},{16,8},{20,12},{24,16},{28,20},{1,25},{... | collective-permute-start | bytes 786440 | tf_op jit(solution)/shard_map/ppermute | solution.py:303
  23.8 1.0 %filter_1_2.3 = (f32[1,12,32,128]{3,2,1,0:T(8,128)S(1)}, f32[1,8,32,128]{3,2,1,0:T(8,128)S(1)}, f32[1,20,32,128]{3,2,1,0:T(8,128)S(1)}) custom-call(bf16[128,384]{1,0:T(8,128)(2,1)S(1)} %get-tuple-element.31.ymat, bf16[384,128]{1,0:T(8,128)(2,1)S(1)} %get-tuple-element.32.zmat, f32[1,8,32,128]{3,2,1,0:T(8,128)S(1)} %get-tuple-element.61.mine, ...), custom_call_target="tpu_custom_call" | custom-call | flops 10000000000 | bytes 35000000 | tf_op jit(solution)/shard_map/filter_1_2/pallas_call | solution.py:238
  24.8 4.4 %collective-permute-start.9 = (f32[1,12,32,128]{3,2,1,0:T(8,128)S(1)}, f32[1,12,32,128]{3,2,1,0:T(8,128)S(1)}, u32[]{:S(2)}, u32[]{:S(2)}) collective-permute-start(f32[1,12,32,128]{3,2,1,0:T(8,128)S(1)} %get-tuple-element.35.lo), channel_id=1, source_target_pairs={{0,24},{4,28},{8,0},{12,4},{16,8},{20,12},{24,16},{28,20},{1,25},{... | collective-permute-start | bytes 589832 | tf_op jit(solution)/shard_map/ppermute | solution.py:303
  29.2 4.3 %collective-permute-done.7.rlo = f32[1,8,32,128]{3,2,1,0:T(8,128)S(1)} collective-permute-done((f32[1,8,32,128]{3,2,1,0:T(8,128)S(1)}, f32[1,8,32,128]{3,2,1,0:T(8,128)S(1)}, u32[]{:S(2)}, u32[]{:S(2)}) %collective-permute-start.7) | collective-permute-done | bytes 131104 | tf_op jit(solution)/shard_map/ppermute | solution.py:302
  33.5 2.1 %filter_3_4_hamiltonian.2 = (f32[8,32,128]{2,1,0:T(8,128)S(1)}, f32[8,2,2,32,128]{4,3,2,1,0:T(8,128)}, f32[8,32,128]{2,1,0:T(8,128)S(1)}) custom-call(bf16[128,384]{1,0:T(8,128)(2,1)S(1)} %get-tuple-element.31.ymat, bf16[384,128]{1,0:T(8,128)(2,1)S(1)} %get-tuple-element.32.zmat, f32[1,8,32,128]{3,2,1,0:T(8,128)S(1)} %collective-permute-done.7.rlo, ...), custom_call_target="tpu_custom_call" | custom-call | flops 1500000000 | bytes 5250000 | tf_op jit(solution)/shard_map/filter_3_4_hamiltonian/pallas_call | solution.py:238
  35.7 5.0 %all-to-all-start = ((f32[8,2,2,32,128]{4,3,2,1,0:T(8,128)}), f32[8,2,2,32,128]{4,3,2,1,0:T(8,128)S(1)}, u32[]{:S(2)}, u32[]{:S(2)}) async-start(f32[8,2,2,32,128]{4,3,2,1,0:T(8,128)} %get-tuple-element.43), calls=%async_computation | async-start | bytes 1048576 | tf_op jit(solution)/shard_map/all_to_all | solution.py:317
  41.0 7.3 %collective-permute-done.6.rlo = f32[1,8,32,128]{3,2,1,0:T(8,128)S(1)} collective-permute-done((f32[1,8,32,128]{3,2,1,0:T(8,128)S(1)}, f32[1,8,32,128]{3,2,1,0:T(8,128)S(1)}, u32[]{:S(2)}, u32[]{:S(2)}) %collective-permute-start.6) | collective-permute-done | bytes 131104 | tf_op jit(solution)/shard_map/ppermute | solution.py:302
  48.3 1.4 %filter_3_4_hamiltonian.3 = (f32[8,32,128]{2,1,0:T(8,128)S(1)}, f32[2,2,32,128]{3,2,1,0:T(8,128)S(1)}, f32[2,2,32,128]{3,2,1,0:T(8,128)S(1)}, f32[2,2,32,128]{3,...) custom-call(bf16[128,384]{1,0:T(8,128)(2,1)S(1)} %get-tuple-element., ...), custom_call_target="tpu_custom_call" | custom-call | flops 1500000000 | bytes 5250000 | tf_op jit(solution)/shard_map/filter_3_4_hamiltonian/pallas_call | solution.py:238
  49.7 1.7 %collective-permute-start.12 = (f32[10,32,128]{2,1,0:T(8,128)S(1)}, f32[10,32,128]{2,1,0:T(8,128)S(1)}, u32[]{:S(2)}, u32[]{:S(2)}) collective-permute-start(f32[10,32,128]{2,1,0:T(8,128)S(1)} %get-tuple-element.47), channel_id=1, source_target_pairs={{0,4},{1,5},{2,6},{3,7},{4,0},{5,1},{6,2},{7,3},{8,12},{9,13},{10,... | collective-permute-start | bytes 491528 | tf_op jit(solution)/shard_map/ppermute | solution.py:312
  51.5 1.4 %collective-permute-start.10 = (f32[2,2,32,128]{3,2,1,0:T(8,128)S(1)}, f32[2,2,32,128]{3,2,1,0:T(8,128)S(1)}, u32[]{:S(2)}, u32[]{:S(2)}) collective-permute-start(f32[2,2,32,128]{3,2,1,0:T(8,128)S(1)} %get-tuple-element.45), channel_id=1, source_target_pairs={{0,6},{1,7},{2,4},{3,5},{4,2},{5,3},{6,0},{7,1},{8,14},{9,15},{10,... | collective-permute-start | bytes 196616 | tf_op jit(solution)/shard_map/ppermute | solution.py:312
  52.9 1.5 %collective-permute-start.17 = (f32[8,32,128]{2,1,0:T(8,128)S(1)}, f32[8,32,128]{2,1,0:T(8,128)S(1)}, u32[]{:S(2)}, u32[]{:S(2)}) collective-permute-start(f32[8,32,128]{2,1,0:T(8,128)S(1)} %get-tuple-element.54), channel_id=1, source_target_pairs={{0,4},{1,5},{2,6},{3,7},{4,0},{5,1},{6,2},{7,3},{8,12},{9,13},{10,... | collective-permute-start | bytes 393224 | tf_op jit(solution)/shard_map/ppermute | solution.py:312
  54.4 1.5 %collective-permute-start.13 = (f32[2,2,32,128]{3,2,1,0:T(8,128)S(1)}, f32[2,2,32,128]{3,2,1,0:T(8,128)S(1)}, u32[]{:S(2)}, u32[]{:S(2)}) collective-permute-start(f32[2,2,32,128]{3,2,1,0:T(8,128)S(1)} %get-tuple-element.48), channel_id=1, source_target_pairs={{0,5},{1,4},{2,7},{3,6},{4,1},{5,0},{6,3},{7,2},{8,13},{9,12},{10,... | collective-permute-start | bytes 196616 | tf_op jit(solution)/shard_map/ppermute | solution.py:312
  56.7 1.9 %collective-permute-start.14 = (f32[2,2,32,128]{3,2,1,0:T(8,128)S(1)}, f32[2,2,32,128]{3,2,1,0:T(8,128)S(1)}, u32[]{:S(2)}, u32[]{:S(2)}) collective-permute-start(f32[2,2,32,128]{3,2,1,0:T(8,128)S(1)} %get-tuple-element.49), channel_id=1, source_target_pairs={{0,2},{1,3},{2,0},{3,1},{4,6},{5,7},{6,4},{7,5},{8,10},{9,11},{10,... | collective-permute-start | bytes 196616 | tf_op jit(solution)/shard_map/ppermute | solution.py:312
  58.9 3.5 %collective-permute-done.13.refs_3_ = f32[2,2,32,128]{3,2,1,0:T(8,128)S(1)} collective-permute-done((f32[2,2,32,128]{3,2,1,0:T(8,128)S(1)}, f32[2,2,32,128]{3,2,1,0:T(8,128)S(1)}, u32[]{:S(2)}, u32[]{:S(2)}) %collective-permute-start.13) | collective-permute-done | bytes 65568 | tf_op jit(solution)/shard_map/ppermute | solution.py:312
  62.6 2.0 %gram.1 = f32[32,1,128]{2,1,0:T(1,128)} custom-call(f32[8,2,2,32,128]{4,3,2,1,0:T(8,128)S(1)} %all-to-all-done.first, f32[2,2,32,128]{3,2,1,0:T(8,128)S(1)} %collective-permute-done.10.refs_0_, f32[2,2,32,128]{3,2,1,0:T(8,128)S(1)} %collective-permute-done.11.refs_1_, f32[10,32,128]{2,1,0:T(8,128)S(1)} %collective-permute-done.12.refs_2_, ...), custom_call_target="tpu_custom_call" | custom-call | flops 1300000000 | bytes 4550000 | tf_op jit(solution)/shard_map/gram/pallas_call | solution.py:238
  64.7 2.5 %all-to-all-start.1 = ((f32[32,1,128]{2,1,0:T(1,128)}), f32[32,1,128]{2,1,0:T(1,128)S(1)}, u32[]{:S(2)}, u32[]{:S(2)}) async-start(f32[32,1,128]{2,1,0:T(1,128)} %gram.1), calls=%async_computation.1 | async-start | bytes 32768 | tf_op jit(solution)/shard_map/all_to_all | solution.py:335
  68.1 6.3 %all-to-all-done.1.x_ref = f32[32,1,128]{2,1,0:T(1,128)S(1)} async-done(((f32[32,1,128]{2,1,0:T(1,128)}), f32[32,1,128]{2,1,0:T(1,128)S(1)}, u32[]{:S(2)}, u32[]{:S(2)}) %all-to-all-start.1) | async-done | bytes 16416 | tf_op jit(solution)/shard_map/all_to_all | solution.py:335
  (31 shorter events, 5.9 us)
Async XLA Ops:
  0.6 1.2 %copy-start = (f32[8,32,128]{2,1,0:T(8,128)S(1)}, f32[8,32,128]{2,1,0:T(8,128)}, u32[]{:S(2)}) copy-start(f32[8,32,128]{2,1,0:T(8,128)} %refs_0_.1) | copy-start | bytes 393220
  1.9 16.6 %collective-permute-start.3 = (f32[1,16,32,128]{3,2,1,0:T(8,128)S(1)}, f32[1,16,32,128]{3,2,1,0:T(8,128)S(1)}, u32[]{:S(2)}, u32[]{:S(2)}) collective-permute-start(f32[1,16,32,128]{3,2,1,0:T(8,128)S(1)} %pad_maximum_fusion), channel_id=1, source_target_pairs={{0,4},{4,0},{8,12},{12,8},{16,20},{20,16},{24,28},{28,24},{1,5},{5... | collective-permute-start | bytes 786440 | tf_op jit(solution)/shard_map/ppermute | solution.py:282
  4.9 10.6 %collective-permute-start.4 = (f32[1,12,32,128]{3,2,1,0:T(8,128)S(1)}, f32[1,12,32,128]{3,2,1,0:T(8,128)S(1)}, u32[]{:S(2)}, u32[]{:S(2)}) collective-permute-start(f32[1,12,32,128]{3,2,1,0:T(8,128)S(1)} %get-tuple-element.63), channel_id=1, source_target_pairs={{0,28},{4,8},{8,4},{12,16},{16,12},{20,24},{24,20},{28,0},{1,29},{... | collective-permute-start | bytes 589832 | tf_op jit(solution)/shard_map/ppermute | solution.py:283
  8.6 9.6 %collective-permute-start.5 = (f32[1,12,32,128]{3,2,1,0:T(8,128)S(1)}, f32[1,12,32,128]{3,2,1,0:T(8,128)S(1)}, u32[]{:S(2)}, u32[]{:S(2)}) collective-permute-start(f32[1,12,32,128]{3,2,1,0:T(8,128)S(1)} %get-tuple-element.64.mine), channel_id=1, source_target_pairs={{0,24},{4,12},{8,0},{12,20},{16,8},{20,28},{24,16},{28,4},{1,25},{... | collective-permute-start | bytes 589832 | tf_op jit(solution)/shard_map/ppermute | solution.py:284
  9.0 14.5 %collective-permute-start = (f32[1,8,32,128]{3,2,1,0:T(8,128)S(1)}, f32[1,8,32,128]{3,2,1,0:T(8,128)S(1)}, u32[]{:S(2)}, u32[]{:S(2)}) collective-permute-start(f32[1,8,32,128]{3,2,1,0:T(8,128)S(1)} %get-tuple-element.60), channel_id=1, source_target_pairs={{0,4},{4,0},{8,12},{12,8},{16,20},{20,16},{24,28},{28,24},{1,5},{5... | collective-permute-start | bytes 393224 | tf_op jit(solution)/shard_map/ppermute | solution.py:282
  9.6 13.9 %collective-permute-start.1 = (f32[1,8,32,128]{3,2,1,0:T(8,128)S(1)}, f32[1,8,32,128]{3,2,1,0:T(8,128)S(1)}, u32[]{:S(2)}, u32[]{:S(2)}) collective-permute-start(f32[1,8,32,128]{3,2,1,0:T(8,128)S(1)} %get-tuple-element.60), channel_id=1, source_target_pairs={{0,28},{4,8},{8,4},{12,16},{16,12},{20,24},{24,20},{28,0},{1,29},{... | collective-permute-start | bytes 393224 | tf_op jit(solution)/shard_map/ppermute | solution.py:283
  15.6 8.2 %collective-permute-start.2 = (f32[1,8,32,128]{3,2,1,0:T(8,128)S(1)}, f32[1,8,32,128]{3,2,1,0:T(8,128)S(1)}, u32[]{:S(2)}, u32[]{:S(2)}) collective-permute-start(f32[1,8,32,128]{3,2,1,0:T(8,128)S(1)} %get-tuple-element.61.mine), channel_id=1, source_target_pairs={{0,24},{4,12},{8,0},{12,20},{16,8},{20,28},{24,16},{28,4},{1,25},{... | collective-permute-start | bytes 393224 | tf_op jit(solution)/shard_map/ppermute | solution.py:284
  19.5 14.1 %collective-permute-start.8 = (f32[1,16,32,128]{3,2,1,0:T(8,128)S(1)}, f32[1,16,32,128]{3,2,1,0:T(8,128)S(1)}, u32[]{:S(2)}, u32[]{:S(2)}) collective-permute-start(f32[1,16,32,128]{3,2,1,0:T(8,128)S(1)} %get-tuple-element.37.lo), channel_id=1, source_target_pairs={{0,24},{4,28},{8,0},{12,4},{16,8},{20,12},{24,16},{28,20},{1,25},{... | collective-permute-start | bytes 786440 | tf_op jit(solution)/shard_map/ppermute | solution.py:303
  23.5 10.0 %collective-permute-start.7 = (f32[1,8,32,128]{3,2,1,0:T(8,128)S(1)}, f32[1,8,32,128]{3,2,1,0:T(8,128)S(1)}, u32[]{:S(2)}, u32[]{:S(2)}) collective-permute-start(f32[1,8,32,128]{3,2,1,0:T(8,128)S(1)} %get-tuple-element.36.hi), channel_id=1, source_target_pairs={{0,8},{4,12},{8,16},{12,20},{16,24},{20,28},{24,0},{28,4},{1,9},{5... | collective-permute-start | bytes 393224 | tf_op jit(solution)/shard_map/ppermute | solution.py:302
  24.8 23.6 %collective-permute-start.9 = (f32[1,12,32,128]{3,2,1,0:T(8,128)S(1)}, f32[1,12,32,128]{3,2,1,0:T(8,128)S(1)}, u32[]{:S(2)}, u32[]{:S(2)}) collective-permute-start(f32[1,12,32,128]{3,2,1,0:T(8,128)S(1)} %get-tuple-element.35.lo), channel_id=1, source_target_pairs={{0,24},{4,28},{8,0},{12,4},{16,8},{20,12},{24,16},{28,20},{1,25},{... | collective-permute-start | bytes 589832 | tf_op jit(solution)/shard_map/ppermute | solution.py:303
  35.7 20.2 %all-to-all-start = ((f32[8,2,2,32,128]{4,3,2,1,0:T(8,128)}), f32[8,2,2,32,128]{4,3,2,1,0:T(8,128)S(1)}, u32[]{:S(2)}, u32[]{:S(2)}) async-start(f32[8,2,2,32,128]{4,3,2,1,0:T(8,128)} %get-tuple-element.43), calls=%async_computation | async-start | bytes 1048576 | tf_op jit(solution)/shard_map/all_to_all | solution.py:317
  40.6 7.7 %collective-permute-start.6 = (f32[1,8,32,128]{3,2,1,0:T(8,128)S(1)}, f32[1,8,32,128]{3,2,1,0:T(8,128)S(1)}, u32[]{:S(2)}, u32[]{:S(2)}) collective-permute-start(f32[1,8,32,128]{3,2,1,0:T(8,128)S(1)} %get-tuple-element.40.hi), channel_id=1, source_target_pairs={{0,8},{4,12},{8,16},{12,20},{16,24},{20,28},{24,0},{28,4},{1,9},{5... | collective-permute-start | bytes 393224 | tf_op jit(solution)/shard_map/ppermute | solution.py:302
  49.7 9.1 %collective-permute-start.12 = (f32[10,32,128]{2,1,0:T(8,128)S(1)}, f32[10,32,128]{2,1,0:T(8,128)S(1)}, u32[]{:S(2)}, u32[]{:S(2)}) collective-permute-start(f32[10,32,128]{2,1,0:T(8,128)S(1)} %get-tuple-element.47), channel_id=1, source_target_pairs={{0,4},{1,5},{2,6},{3,7},{4,0},{5,1},{6,2},{7,3},{8,12},{9,13},{10,... | collective-permute-start | bytes 491528 | tf_op jit(solution)/shard_map/ppermute | solution.py:312
  51.5 5.3 %collective-permute-start.10 = (f32[2,2,32,128]{3,2,1,0:T(8,128)S(1)}, f32[2,2,32,128]{3,2,1,0:T(8,128)S(1)}, u32[]{:S(2)}, u32[]{:S(2)}) collective-permute-start(f32[2,2,32,128]{3,2,1,0:T(8,128)S(1)} %get-tuple-element.45), channel_id=1, source_target_pairs={{0,6},{1,7},{2,4},{3,5},{4,2},{5,3},{6,0},{7,1},{8,14},{9,15},{10,... | collective-permute-start | bytes 196616 | tf_op jit(solution)/shard_map/ppermute | solution.py:312
  52.9 5.8 %collective-permute-start.11 = (f32[2,2,32,128]{3,2,1,0:T(8,128)S(1)}, f32[2,2,32,128]{3,2,1,0:T(8,128)S(1)}, u32[]{:S(2)}, u32[]{:S(2)}) collective-permute-start(f32[2,2,32,128]{3,2,1,0:T(8,128)S(1)} %get-tuple-element.46), channel_id=1, source_target_pairs={{0,7},{1,6},{2,5},{3,4},{4,3},{5,2},{6,1},{7,0},{8,15},{9,14},{10,... | collective-permute-start | bytes 196616 | tf_op jit(solution)/shard_map/ppermute | solution.py:312
  52.9 14.3 %collective-permute-start.17 = (f32[8,32,128]{2,1,0:T(8,128)S(1)}, f32[8,32,128]{2,1,0:T(8,128)S(1)}, u32[]{:S(2)}, u32[]{:S(2)}) collective-permute-start(f32[8,32,128]{2,1,0:T(8,128)S(1)} %get-tuple-element.54), channel_id=1, source_target_pairs={{0,4},{1,5},{2,6},{3,7},{4,0},{5,1},{6,2},{7,3},{8,12},{9,13},{10,... | collective-permute-start | bytes 393224 | tf_op jit(solution)/shard_map/ppermute | solution.py:312
  54.4 8.0 %collective-permute-start.13 = (f32[2,2,32,128]{3,2,1,0:T(8,128)S(1)}, f32[2,2,32,128]{3,2,1,0:T(8,128)S(1)}, u32[]{:S(2)}, u32[]{:S(2)}) collective-permute-start(f32[2,2,32,128]{3,2,1,0:T(8,128)S(1)} %get-tuple-element.48), channel_id=1, source_target_pairs={{0,5},{1,4},{2,7},{3,6},{4,1},{5,0},{6,3},{7,2},{8,13},{9,12},{10,... | collective-permute-start | bytes 196616 | tf_op jit(solution)/shard_map/ppermute | solution.py:312
  56.7 5.7 %collective-permute-start.14 = (f32[2,2,32,128]{3,2,1,0:T(8,128)S(1)}, f32[2,2,32,128]{3,2,1,0:T(8,128)S(1)}, u32[]{:S(2)}, u32[]{:S(2)}) collective-permute-start(f32[2,2,32,128]{3,2,1,0:T(8,128)S(1)} %get-tuple-element.49), channel_id=1, source_target_pairs={{0,2},{1,3},{2,0},{3,1},{4,6},{5,7},{6,4},{7,5},{8,10},{9,11},{10,... | collective-permute-start | bytes 196616 | tf_op jit(solution)/shard_map/ppermute | solution.py:312
  58.7 3.9 %collective-permute-start.15 = (f32[2,2,32,128]{3,2,1,0:T(8,128)S(1)}, f32[2,2,32,128]{3,2,1,0:T(8,128)S(1)}, u32[]{:S(2)}, u32[]{:S(2)}) collective-permute-start(f32[2,2,32,128]{3,2,1,0:T(8,128)S(1)} %get-tuple-element.50), channel_id=1, source_target_pairs={{0,3},{1,2},{2,1},{3,0},{4,7},{5,6},{6,5},{7,4},{8,11},{9,10},{10,... | collective-permute-start | bytes 196616 | tf_op jit(solution)/shard_map/ppermute | solution.py:312
  58.8 3.8 %collective-permute-start.16 = (f32[2,2,32,128]{3,2,1,0:T(8,128)S(1)}, f32[2,2,32,128]{3,2,1,0:T(8,128)S(1)}, u32[]{:S(2)}, u32[]{:S(2)}) collective-permute-start(f32[2,2,32,128]{3,2,1,0:T(8,128)S(1)} %get-tuple-element.51), channel_id=1, source_target_pairs={{0,1},{1,0},{2,3},{3,2},{4,5},{5,4},{6,7},{7,6},{8,9},{9,8},{10,11... | collective-permute-start | bytes 196616 | tf_op jit(solution)/shard_map/ppermute | solution.py:312
  64.7 9.7 %all-to-all-start.1 = ((f32[32,1,128]{2,1,0:T(1,128)}), f32[32,1,128]{2,1,0:T(1,128)S(1)}, u32[]{:S(2)}, u32[]{:S(2)}) async-start(f32[32,1,128]{2,1,0:T(1,128)} %gram.1), calls=%async_computation.1 | async-start | bytes 32768 | tf_op jit(solution)/shard_map/all_to_all | solution.py:335

commit v5 on v4

--- a/solution.py
+++ b/solution.py
@@ -18,7 +18,7 @@
 S1 = HALF / (LOWER - CENTRE)
 T2 = 2.0 / S1**2 - 1.0
 T4 = 2.0 * T2 * T2 - 1.0
-PEERS = (6, 7, 4, 5, 2, 3, 1, 0)
+PEERS = (6, 4, 2, 7, 5, 3, 1, 0)
 CHUNK = 4
 
 
@@ -149,62 +149,65 @@
     def cells(which, k, per):
         return both[which, pl.ds(per * jnp.bitwise_xor(me, k), per)]
 
-    keep, *outs = outs
-    keep[...] = both[0, pl.ds(homes[0], n)]
     if len(outs) == 2:
-        blocks, send = outs
-        per = blocks.shape[2]
-        for t in range(blocks.shape[0]):
-            blocks[t] = both[:, per * t : per * (t + 1)]
-        send[...] = both[0, pl.ds(homes[1], n)]
+        home, blocks = outs
+        for i, start in enumerate(homes):
+            home[i] = both[0, pl.ds(start, n)]
+        for i, k in enumerate(PEERS):
+            for which in range(2):
+                blocks[i, which] = cells(which, k, blocks.shape[2])
     else:
-        per = outs[0].shape[1]
-        for k, block in enumerate(outs):
-            if k == 4:
-                block[:n] = both[0, pl.ds(homes[1], n)]
-                block[n:] = cells(1, k, per)
-            else:
-                for which in range(2):
-                    block[which] = cells(which, k, per)
-
-
-def gram(first, *refs):
-    *xs, out_ref, part, second = refs
+        home_a, blocks_a, keep, send, *blocks = outs
+        for i, ref in enumerate((keep, send)):
+            ref[0] = home_a[i]
+            ref[1] = both[0, pl.ds(homes[i], n)]
+        for i, (k, block) in enumerate(zip(PEERS, blocks)):
+            block[0] = blocks_a[i]
+            for which in range(2):
+                block[1, which] = cells(which, k, block.shape[2])
+
+
+def gram(*refs):
+    *xs, out_ref, part, blocks = refs
     orbs = part.shape[1]
-    peers, _, per, ny, nz = first.shape
-    _, place, me = places()
+    half, peers, _, per, ny, nz = blocks.shape
+    me = places()[2]
     for k, x in zip(PEERS, xs):
-        peer = jnp.bitwise_xor(me, k)
-        if k == 4:
-            second[peer, 0] = x[pl.ds(per * place, per)]
-            second[peer, 1] = x[x.shape[0] - per :]
-        else:
-            second[peer] = x[...]
+        for o in range(half):
+            blocks[o, jnp.bitwise_xor(me, k)] = x[o]
     rows = per * ny
-    flat = [x.reshape(peers * 2 * rows, nz) for x in (first, second)]
+    flat = blocks.reshape(half * peers * 2 * rows, nz)
     fields = jnp.concatenate(
         [
             jnp.concatenate(
-                [x[pl.ds(which * rows + r, peers, stride=2 * rows), :] for which in range(2) for x in flat], axis=0
+                [
+                    flat[pl.ds((o * peers * 2 + which) * rows + r, peers, stride=2 * rows), :]
+                    for which in range(2)
+                    for o in range(half)
+                ],
+                axis=0,
             )
             for r in range(rows)
         ],
         axis=1,
     )
-
-    def product(a, b, contract):
-        return lax.dot_general(
-            a, b, ((contract[:1], contract[1:]), ((), ())),
-            precision=lax.Precision.HIGHEST, preferred_element_type=jnp.float32,
-        )
-
-    both = product(fields, fields, (1, 1))
+    high = fields.astype(jnp.bfloat16)
+    rest = fields - high.astype(jnp.float32)
+    mid = rest.astype(jnp.bfloat16)
+    low = (rest - mid.astype(jnp.float32)).astype(jnp.bfloat16)
+    terms = jnp.concatenate([high, mid, low], axis=0)
+    products = lax.dot_general(terms, terms, (((1,), (1,)), ((), ())), preferred_element_type=jnp.float32)
+    size = 2 * orbs
+    both = jnp.zeros((size, size), jnp.float32)
+    for i in (2, 1, 0):
+        for j in (2, 1, 0):
+            both = both + products[i * size : (i + 1) * size, j * size : (j + 1) * size]
     both = jnp.concatenate([both[:orbs, :orbs], both[orbs:, :orbs] + both[:orbs, orbs:]], axis=0)
     row = lax.broadcasted_iota(jnp.int32, (orbs, orbs), 0)
     quarter = peers // 2
     target = 4 * (row % quarter) + 2 * (row // quarter % 2) + row // peers
     order = (lax.broadcasted_iota(jnp.int32, (orbs, orbs), 1) == target).astype(jnp.float32)
-    both = product(both, order, (1, 0))
+    both = jnp.dot(both, order, precision=lax.Precision.HIGHEST, preferred_element_type=jnp.float32)
     part[...] = jnp.zeros_like(part)
     for which in range(2):
         part[which, :, :orbs] = both[which * orbs : (which + 1) * orbs]
@@ -215,11 +218,8 @@
         rolled = part[i // own, start : start + quarter, :]
         packed = packed + (pltpu.roll(rolled, i * orbs, 1) if i else rolled)
 
-    def spread(g, _):
-        out_ref[pl.ds(g * quarter, quarter)] = packed.reshape(quarter, 1, nz)
-        return 0
-
-    lax.fori_loop(0, out_ref.shape[0] // quarter, spread, 0)
+    for g in range(out_ref.shape[0] // quarter):
+        out_ref[g * quarter : (g + 1) * quarter] = packed.reshape(quarter, 1, nz)
 
 
 def finish(cells, x_ref, c_ref, h_ref):
@@ -312,28 +312,21 @@
         return lax.ppermute(x, ("mem", "orb"), [(t, t ^ k) for t in range(group)]) if k else x
 
     block = (2, per, ny, nz)
-    outs = [(n, ny, nz), (group, *block), (n, ny, nz)]
-    keep_a, blocks, send = call(last_three, second[0], outs, scratch, 1.5, "filter_3_4_hamiltonian")
-    first = lax.all_to_all(blocks, ("mem", "orb"), 0, 0, tiled=True)
-    back_a = peer(send, 4)
-    hi, _ = lax.optimization_barrier((second[1][4], keep_a))
-    outs = [(n, ny, nz)] + [block] * 4 + [(n + per, ny, nz)] + [block] * 3
-    keep_b, *blocks = call(
-        last_three, (*second[1][:4], hi, *second[1][5:]), outs, scratch, 1.5, "filter_3_4_hamiltonian"
-    )
-    blocks[1], first = lax.optimization_barrier((blocks[1], first))
-    xs = [peer(blocks[k], k) for k in PEERS]
-    back_b = xs[PEERS.index(4)][:n]
+    results = call(last_three, second[0], [(2, n, ny, nz), (group, *block)], scratch, 1.5, "filter_3_4_hamiltonian")
+    outs = [(half, n, ny, nz)] * 2 + [(half, *block)] * group
+    keep, send, *blocks = call(last_three, (*second[1], *results), outs, scratch, 1.5, "filter_3_4_hamiltonian")
+    xs = [peer(x, k) for k, x in zip(PEERS, blocks)]
     (sums,) = call(
         gram,
-        (first, *xs),
+        xs,
         [(size * orbs, 1, 2 * own_orbs * count)],
-        [pltpu.VMEM((2, count, nz), f32), pltpu.VMEM((group, *block), f32)],
+        [pltpu.VMEM((2, count, nz), f32), pltpu.VMEM((half, group, *block), f32)],
         1.3,
         "gram",
     )
+    send, sums = lax.optimization_barrier((send, sums))
+    back = lax.ppermute(send, grid_axes, swap)
     sums = lax.all_to_all(sums, ("pair", "mem", "orb"), 0, 0, tiled=True)
-    keep, back = jnp.stack([keep_a, keep_b]), jnp.stack([back_a, back_b])
     filtered = jnp.where(m == 0, jnp.concatenate([keep, back]), jnp.concatenate([back, keep]))
     sums, filtered = lax.optimization_barrier((sums, filtered))
     corr, ham = call(

time: 75.3 us -> 68.9 us (0.915)
  starting transfers between devices: 35.8 us -> 32.7 us
  waiting for transfers between devices: 28 us -> 25.5 us
  Pallas kernels: 8.41 us -> 7.6 us
    ppermute x2, waiting for transfers between devices: 11.6 us -> 5.08 us  [per_device(): rlo = lax.ppermute(hi, grid_axes, up)]
    all_to_all x1 -> x0, starting transfers between devices: 4.98 us -> none  [per_device(): first = lax.all_to_all(blocks, ('mem', 'orb'), 0, 0, tiled=True)]
    ppermute x2, waiting for transfers between devices: 0.01 us -> 3.12 us  [per_device(): rhi = lax.ppermute(lo, grid_axes, down)]
    ppermute x0 -> x1, waiting for transfers between devices: none -> 2.8 us  [per_device(): back = lax.ppermute(send, grid_axes, swap)]
    all_to_all x1, waiting for transfers between devices: 6.28 us -> 3.51 us  [per_device(): sums = lax.all_to_all(sums, ('pair', 'mem', 'orb'), 0, 0, tiled=True)]
    all_to_all x1, starting transfers between devices: 2.52 us -> 4.95 us  [per_device(): sums = lax.all_to_all(sums, ('pair', 'mem', 'orb'), 0, 0, tiled=True)]
    ppermute x8 -> x7, starting transfers between devices: 8.28 us -> 6.44 us  [peer(): lax.ppermute(x, ('mem', 'orb'), [(t, t ^ k) for t in range(group)])]
    ppermute x8 -> x7, waiting for transfers between devices: 4.61 us -> 6.42 us  [peer(): lax.ppermute(x, ('mem', 'orb'), [(t, t ^ k) for t in range(group)])]
  transfers between devices with their start and end apart: 20 -> 19, of which waited for: 10 -> 13; matrix products, arithmetic and copies ran while one was open for 1% -> 1% of each run, Pallas kernels for 10% -> 5%
where the time goes in v5:
time: 68.9 us; the launch traced here: 68.7 us
  starting transfers between devices  32.7 us (47%)
  waiting for transfers between devices  25.5 us (37%)
  Pallas kernels  7.6 us (11%)
  local copies, waits for them, and re-layouts  1.18 us (2%)
  other arithmetic  0.9 us (1%)
  between operations  0.73 us (1%)
    pallas_call x7, Pallas kernels, call(): pl.pallas_call(body, out_shape=[s if isinstance(s, jax.ShapeDtypeStruct)...  7.6 us
    ppermute x2, starting transfers between devices, per_device(): rhi = lax.ppermute(lo, grid_axes, down)  6.88 us
    ppermute x7, starting transfers between devices, peer(): lax.ppermute(x, ('mem', 'orb'), [(t, t ^ k) for t in range(group)])  6.44 us
    ppermute x7, waiting for transfers between devices, peer(): lax.ppermute(x, ('mem', 'orb'), [(t, t ^ k) for t in range(group)])  6.42 us
    ppermute x2, starting transfers between devices, per_device(): rb = lax.ppermute(b, grid_axes, cross)  5.91 us
    ppermute x2, waiting for transfers between devices, per_device(): rlo = lax.ppermute(hi, grid_axes, up)  5.08 us
    all_to_all x1, starting transfers between devices, per_device(): sums = lax.all_to_all(sums, ('pair', 'mem', 'orb'), 0, 0, tiled=True)  4.95 us
    ppermute x2, starting transfers between devices, per_device(): ra = lax.ppermute(a, grid_axes, swap)  3.77 us
  transfers between devices with their start and end apart: 19, of which 13 were waited for; matrix products, arithmetic and copies ran while one was open for 1% of the time, Pallas kernels for 5%

profile of v5, /device:TPU:0, one launch (start us, length us, event | category | flops | bytes accessed | tf_op | source)
XLA Modules:
  0.0 68.7 jit_solution(9513584932216862581)
XLA Ops:
  0.6 1.2 %constant_dynamic-slice_fusion = (f32[1,8,32,128]{3,2,1,0:T(8,128)S(1)}, f32[1,8,32,128]{3,2,1,0:T(8,128)S(1)}, f32[1,8,32,128]{3,2,1,0:T(8,128)S(1)}, f32[1,8,32,128]{3,2,1,0:T(8,128)S(1)}) fusion(f32[4,8,32,128]{3,2,1,0:T(8,128)} %param.2, s32[]{:T(128)S(6)} %select_n.33, s32[]{:T(128)S(6)} %select_n.29, s32[]{:T(128)S(6)} %select_n.28, s32[]{:T(128)S(6)} %select_n.30), kind=kLoop, calls=%fused_computation.5 | loop fusion | bytes 1048592 | tf_op jit(solution)/shard_map/dynamic_slice | solution.py:278
  1.9 3.0 %collective-permute-start.3 = (f32[1,16,32,128]{3,2,1,0:T(8,128)S(1)}, f32[1,16,32,128]{3,2,1,0:T(8,128)S(1)}, u32[]{:S(2)}, u32[]{:S(2)}) collective-permute-start(f32[1,16,32,128]{3,2,1,0:T(8,128)S(1)} %pad_maximum_fusion), channel_id=1, source_target_pairs={{0,4},{4,0},{8,12},{12,8},{16,20},{20,16},{24,28},{28,24},{1,5},{5... | collective-permute-start | bytes 786440 | tf_op jit(solution)/shard_map/ppermute | solution.py:282
  4.9 3.6 %collective-permute-start.4 = (f32[1,12,32,128]{3,2,1,0:T(8,128)S(1)}, f32[1,12,32,128]{3,2,1,0:T(8,128)S(1)}, u32[]{:S(2)}, u32[]{:S(2)}) collective-permute-start(f32[1,12,32,128]{3,2,1,0:T(8,128)S(1)} %get-tuple-element.61), channel_id=1, source_target_pairs={{0,28},{4,8},{8,4},{12,16},{16,12},{20,24},{24,20},{28,0},{1,29},{... | collective-permute-start | bytes 589832 | tf_op jit(solution)/shard_map/ppermute | solution.py:283
  9.0 2.3 %collective-permute-start.1 = (f32[1,8,32,128]{3,2,1,0:T(8,128)S(1)}, f32[1,8,32,128]{3,2,1,0:T(8,128)S(1)}, u32[]{:S(2)}, u32[]{:S(2)}) collective-permute-start(f32[1,8,32,128]{3,2,1,0:T(8,128)S(1)} %get-tuple-element.58), channel_id=1, source_target_pairs={{0,28},{4,8},{8,4},{12,16},{16,12},{20,24},{24,20},{28,0},{1,29},{... | collective-permute-start | bytes 393224 | tf_op jit(solution)/shard_map/ppermute | solution.py:283
  12.0 3.5 %collective-permute-done.4.rb = f32[1,12,32,128]{3,2,1,0:T(8,128)S(1)} collective-permute-done((f32[1,12,32,128]{3,2,1,0:T(8,128)S(1)}, f32[1,12,32,128]{3,2,1,0:T(8,128)S(1)}, u32[]{:S(2)}, u32[]{:S(2)}) %collective-permute-start.4) | collective-permute-done | bytes 196640 | tf_op jit(solution)/shard_map/ppermute | solution.py:283
  15.6 1.8 %collective-permute-start.2 = (f32[1,8,32,128]{3,2,1,0:T(8,128)S(1)}, f32[1,8,32,128]{3,2,1,0:T(8,128)S(1)}, u32[]{:S(2)}, u32[]{:S(2)}) collective-permute-start(f32[1,8,32,128]{3,2,1,0:T(8,128)S(1)} %get-tuple-element.59.mine), channel_id=1, source_target_pairs={{0,24},{4,12},{8,0},{12,20},{16,8},{20,28},{24,16},{28,4},{1,25},{... | collective-permute-start | bytes 393224 | tf_op jit(solution)/shard_map/ppermute | solution.py:284
  19.5 1.6 %collective-permute-start.9 = (f32[1,8,32,128]{3,2,1,0:T(8,128)S(1)}, f32[1,8,32,128]{3,2,1,0:T(8,128)S(1)}, u32[]{:S(2)}, u32[]{:S(2)}) collective-permute-start(f32[1,8,32,128]{3,2,1,0:T(8,128)S(1)} %get-tuple-element.37.hi), channel_id=1, source_target_pairs={{0,8},{4,12},{8,16},{12,20},{16,24},{20,28},{24,0},{28,4},{1,9},{5... | collective-permute-start | bytes 393224 | tf_op jit(solution)/shard_map/ppermute | solution.py:302
  21.0 2.5 %collective-permute-start.8 = (f32[1,16,32,128]{3,2,1,0:T(8,128)S(1)}, f32[1,16,32,128]{3,2,1,0:T(8,128)S(1)}, u32[]{:S(2)}, u32[]{:S(2)}) collective-permute-start(f32[1,16,32,128]{3,2,1,0:T(8,128)S(1)} %get-tuple-element.36.lo), channel_id=1, source_target_pairs={{0,24},{4,28},{8,0},{12,4},{16,8},{20,12},{24,16},{28,20},{1,25},{... | collective-permute-start | bytes 786440 | tf_op jit(solution)/shard_map/ppermute | solution.py:303
  24.7 4.3 %collective-permute-start.7 = (f32[1,12,32,128]{3,2,1,0:T(8,128)S(1)}, f32[1,12,32,128]{3,2,1,0:T(8,128)S(1)}, u32[]{:S(2)}, u32[]{:S(2)}) collective-permute-start(f32[1,12,32,128]{3,2,1,0:T(8,128)S(1)} %get-tuple-element.34.lo), channel_id=1, source_target_pairs={{0,24},{4,28},{8,0},{12,4},{16,8},{20,12},{24,16},{28,20},{1,25},{... | collective-permute-start | bytes 589832 | tf_op jit(solution)/shard_map/ppermute | solution.py:303
  29.1 3.1 %collective-permute-done.8.rhi.v_above = f32[1,16,32,128]{3,2,1,0:T(8,128)S(1)} collective-permute-done((f32[1,16,32,128]{3,2,1,0:T(8,128)S(1)}, f32[1,16,32,128]{3,2,1,0:T(8,128)S(1)}, u32[]{:S(2)}, u32[]{:S(2)}) %collective-permute-start.8) | collective-permute-done | bytes 262176 | tf_op jit(solution)/shard_map/ppermute | solution.py:303
  32.2 1.4 %filter_3_4_hamiltonian.2 = (f32[2,8,32,128]{3,2,1,0:T(8,128)S(1)}, f32[8,2,2,32,128]{4,3,2,1,0:T(8,128)S(1)}) custom-call(bf16[128,384]{1,0:T(8,128)(2,1)S(1)} %get-tuple-element.30.ymat, bf16[384,128]{1,0:T(8,128)(2,1)S(1)} %get-tuple-element.31.zmat, f32[1,8,32,128]{3,2,1,0:T(8,128)S(1)} %collective-permute-done.9.rlo, ...), custom_call_target="tpu_custom_call" | custom-call | flops 1500000000 | bytes 5250000 | tf_op jit(solution)/shard_map/filter_3_4_hamiltonian/pallas_call | solution.py:238
  33.6 5.1 %collective-permute-done.6.rlo = f32[1,8,32,128]{3,2,1,0:T(8,128)S(1)} collective-permute-done((f32[1,8,32,128]{3,2,1,0:T(8,128)S(1)}, f32[1,8,32,128]{3,2,1,0:T(8,128)S(1)}, u32[]{:S(2)}, u32[]{:S(2)}) %collective-permute-start.6) | collective-permute-done | bytes 131104 | tf_op jit(solution)/shard_map/ppermute | solution.py:302
  38.7 1.4 %filter_3_4_hamiltonian.3 = (f32[2,8,32,128]{3,2,1,0:T(8,128)S(1)}, f32[2,8,32,128]{3,2,1,0:T(8,128)S(1)}, f32[2,2,2,32,128]{4,3,2,1,0:T(8,128)S(1)}, f32[2,2,2,...) custom-call(bf16[128,384]{1,0:T(8,128)(2,1)S(1)} %get-tuple-element., ...), custom_call_target="tpu_custom_call" | custom-call | flops 1500000000 | bytes 5250000 | tf_op jit(solution)/shard_map/filter_3_4_hamiltonian/pallas_call | solution.py:238
  40.1 2.3 %collective-permute-start.10 = (f32[2,2,2,32,128]{4,3,2,1,0:T(8,128)S(1)}, f32[2,2,2,32,128]{4,3,2,1,0:T(8,128)S(1)}, u32[]{:S(2)}, u32[]{:S(2)}) collective-permute-start(f32[2,2,2,32,128]{4,3,2,1,0:T(8,128)S(1)} %get-tuple-element.42), channel_id=1, source_target_pairs={{0,6},{1,7},{2,4},{3,5},{4,2},{5,3},{6,0},{7,1},{8,14},{9,15},{10,... | collective-permute-start | bytes 393224 | tf_op jit(solution)/shard_map/ppermute | solution.py:312
  43.6 2.7 %collective-permute-start.14 = (f32[2,2,2,32,128]{4,3,2,1,0:T(8,128)S(1)}, f32[2,2,2,32,128]{4,3,2,1,0:T(8,128)S(1)}, u32[]{:S(2)}, u32[]{:S(2)}) collective-permute-start(f32[2,2,2,32,128]{4,3,2,1,0:T(8,128)S(1)} %get-tuple-element.46), channel_id=1, source_target_pairs={{0,5},{1,4},{2,7},{3,6},{4,1},{5,0},{6,3},{7,2},{8,13},{9,12},{10,... | collective-permute-start | bytes 393224 | tf_op jit(solution)/shard_map/ppermute | solution.py:312
  46.3 1.2 %collective-permute-done.11.refs_1_ = f32[2,2,2,32,128]{4,3,2,1,0:T(8,128)S(1)} collective-permute-done((f32[2,2,2,32,128]{4,3,2,1,0:T(8,128)S(1)}, f32[2,2,2,32,128]{4,3,2,1,0:T(8,128)S(1)}, u32[]{:S(2)}, u32[]{:S(2)}) %collective-permute-start.11) | collective-permute-done | bytes 131104 | tf_op jit(solution)/shard_map/ppermute | solution.py:312
  47.7 1.1 %collective-permute-done.12.refs_2_ = f32[2,2,2,32,128]{4,3,2,1,0:T(8,128)S(1)} collective-permute-done((f32[2,2,2,32,128]{4,3,2,1,0:T(8,128)S(1)}, f32[2,2,2,32,128]{4,3,2,1,0:T(8,128)S(1)}, u32[]{:S(2)}, u32[]{:S(2)}) %collective-permute-start.12) | collective-permute-done | bytes 131104 | tf_op jit(solution)/shard_map/ppermute | solution.py:312
  48.8 1.6 %collective-permute-done.13.refs_3_ = f32[2,2,2,32,128]{4,3,2,1,0:T(8,128)S(1)} collective-permute-done((f32[2,2,2,32,128]{4,3,2,1,0:T(8,128)S(1)}, f32[2,2,2,32,128]{4,3,2,1,0:T(8,128)S(1)}, u32[]{:S(2)}, u32[]{:S(2)}) %collective-permute-start.13) | collective-permute-done | bytes 131104 | tf_op jit(solution)/shard_map/ppermute | solution.py:312
  50.4 1.5 %collective-permute-done.14.refs_4_ = f32[2,2,2,32,128]{4,3,2,1,0:T(8,128)S(1)} collective-permute-done((f32[2,2,2,32,128]{4,3,2,1,0:T(8,128)S(1)}, f32[2,2,2,32,128]{4,3,2,1,0:T(8,128)S(1)}, u32[]{:S(2)}, u32[]{:S(2)}) %collective-permute-start.14) | collective-permute-done | bytes 131104 | tf_op jit(solution)/shard_map/ppermute | solution.py:312
  52.9 2.0 %gram.1 = f32[32,1,128]{2,1,0:T(1,128)} custom-call(f32[2,2,2,32,128]{4,3,2,1,0:T(8,128)S(1)} %collective-permute-done.10.refs_0_, f32[2,2,2,32,128]{4,3,2,1,0:T(8,128)S(1)} %collective-permute-done.11.refs_1_, f32[2,2,2,32,128]{4,3,2,1,0:T(8,128)S(1)} %collective-permute-done.12.refs_2_, f32[2,2,2,32,128]{4,3,2,1,0:T(8,128)S(1)} %collective-permute-done.13.refs_3_, ...), custom_call_target="tpu_custom_call" | custom-call | flops 1300000000 | bytes 4550000 | tf_op jit(solution)/shard_map/gram/pallas_call | solution.py:238
  54.9 1.0 %collective-permute-start.17 = (f32[2,8,32,128]{3,2,1,0:T(8,128)S(1)}, f32[2,8,32,128]{3,2,1,0:T(8,128)S(1)}, u32[]{:S(2)}, u32[]{:S(2)}) collective-permute-start(f32[2,8,32,128]{3,2,1,0:T(8,128)S(1)} %get-tuple-element.52), channel_id=1, source_target_pairs={{0,4},{4,0},{8,12},{12,8},{16,20},{20,16},{24,28},{28,24},{1,5},{5... | collective-permute-start | bytes 786440 | tf_op jit(solution)/shard_map/ppermute | solution.py:328
  55.9 4.9 %all-to-all-start = ((f32[32,1,128]{2,1,0:T(1,128)}), f32[32,1,128]{2,1,0:T(1,128)S(1)}, u32[]{:S(2)}, u32[]{:S(2)}) async-start(f32[32,1,128]{2,1,0:T(1,128)} %gram.1), calls=%async_computation | async-start | bytes 32768 | tf_op jit(solution)/shard_map/all_to_all | solution.py:329
  60.9 2.8 %collective-permute-done.17 = f32[2,8,32,128]{3,2,1,0:T(8,128)S(1)} collective-permute-done((f32[2,8,32,128]{3,2,1,0:T(8,128)S(1)}, f32[2,8,32,128]{3,2,1,0:T(8,128)S(1)}, u32[]{:S(2)}, u32[]{:S(2)}) %collective-permute-start.17) | collective-permute-done | bytes 262176 | tf_op jit(solution)/shard_map/ppermute | solution.py:328
  64.5 3.5 %all-to-all-done.x_ref = f32[32,1,128]{2,1,0:T(1,128)S(1)} async-done(((f32[32,1,128]{2,1,0:T(1,128)}), f32[32,1,128]{2,1,0:T(1,128)S(1)}, u32[]{:S(2)}, u32[]{:S(2)}) %all-to-all-start) | async-done | bytes 16416 | tf_op jit(solution)/shard_map/all_to_all | solution.py:329
  (28 shorter events, 8.5 us)
Async XLA Ops:
  0.6 1.2 %copy-start = (f32[8,32,128]{2,1,0:T(8,128)S(1)}, f32[8,32,128]{2,1,0:T(8,128)}, u32[]{:S(2)}) copy-start(f32[8,32,128]{2,1,0:T(8,128)} %refs_0_.1) | copy-start | bytes 393220
  1.9 16.6 %collective-permute-start.3 = (f32[1,16,32,128]{3,2,1,0:T(8,128)S(1)}, f32[1,16,32,128]{3,2,1,0:T(8,128)S(1)}, u32[]{:S(2)}, u32[]{:S(2)}) collective-permute-start(f32[1,16,32,128]{3,2,1,0:T(8,128)S(1)} %pad_maximum_fusion), channel_id=1, source_target_pairs={{0,4},{4,0},{8,12},{12,8},{16,20},{20,16},{24,28},{28,24},{1,5},{5... | collective-permute-start | bytes 786440 | tf_op jit(solution)/shard_map/ppermute | solution.py:282
  4.9 10.6 %collective-permute-start.4 = (f32[1,12,32,128]{3,2,1,0:T(8,128)S(1)}, f32[1,12,32,128]{3,2,1,0:T(8,128)S(1)}, u32[]{:S(2)}, u32[]{:S(2)}) collective-permute-start(f32[1,12,32,128]{3,2,1,0:T(8,128)S(1)} %get-tuple-element.61), channel_id=1, source_target_pairs={{0,28},{4,8},{8,4},{12,16},{16,12},{20,24},{24,20},{28,0},{1,29},{... | collective-permute-start | bytes 589832 | tf_op jit(solution)/shard_map/ppermute | solution.py:283
  8.6 9.6 %collective-permute-start.5 = (f32[1,12,32,128]{3,2,1,0:T(8,128)S(1)}, f32[1,12,32,128]{3,2,1,0:T(8,128)S(1)}, u32[]{:S(2)}, u32[]{:S(2)}) collective-permute-start(f32[1,12,32,128]{3,2,1,0:T(8,128)S(1)} %get-tuple-element.62.mine), channel_id=1, source_target_pairs={{0,24},{4,12},{8,0},{12,20},{16,8},{20,28},{24,16},{28,4},{1,25},{... | collective-permute-start | bytes 589832 | tf_op jit(solution)/shard_map/ppermute | solution.py:284
  9.0 14.6 %collective-permute-start.1 = (f32[1,8,32,128]{3,2,1,0:T(8,128)S(1)}, f32[1,8,32,128]{3,2,1,0:T(8,128)S(1)}, u32[]{:S(2)}, u32[]{:S(2)}) collective-permute-start(f32[1,8,32,128]{3,2,1,0:T(8,128)S(1)} %get-tuple-element.58), channel_id=1, source_target_pairs={{0,28},{4,8},{8,4},{12,16},{16,12},{20,24},{24,20},{28,0},{1,29},{... | collective-permute-start | bytes 393224 | tf_op jit(solution)/shard_map/ppermute | solution.py:283
  11.3 12.3 %collective-permute-start = (f32[1,8,32,128]{3,2,1,0:T(8,128)S(1)}, f32[1,8,32,128]{3,2,1,0:T(8,128)S(1)}, u32[]{:S(2)}, u32[]{:S(2)}) collective-permute-start(f32[1,8,32,128]{3,2,1,0:T(8,128)S(1)} %get-tuple-element.58), channel_id=1, source_target_pairs={{0,4},{4,0},{8,12},{12,8},{16,20},{20,16},{24,28},{28,24},{1,5},{5... | collective-permute-start | bytes 393224 | tf_op jit(solution)/shard_map/ppermute | solution.py:282
  15.6 8.2 %collective-permute-start.2 = (f32[1,8,32,128]{3,2,1,0:T(8,128)S(1)}, f32[1,8,32,128]{3,2,1,0:T(8,128)S(1)}, u32[]{:S(2)}, u32[]{:S(2)}) collective-permute-start(f32[1,8,32,128]{3,2,1,0:T(8,128)S(1)} %get-tuple-element.59.mine), channel_id=1, source_target_pairs={{0,24},{4,12},{8,0},{12,20},{16,8},{20,28},{24,16},{28,4},{1,25},{... | collective-permute-start | bytes 393224 | tf_op jit(solution)/shard_map/ppermute | solution.py:284
  19.5 9.6 %collective-permute-start.9 = (f32[1,8,32,128]{3,2,1,0:T(8,128)S(1)}, f32[1,8,32,128]{3,2,1,0:T(8,128)S(1)}, u32[]{:S(2)}, u32[]{:S(2)}) collective-permute-start(f32[1,8,32,128]{3,2,1,0:T(8,128)S(1)} %get-tuple-element.37.hi), channel_id=1, source_target_pairs={{0,8},{4,12},{8,16},{12,20},{16,24},{20,28},{24,0},{28,4},{1,9},{5... | collective-permute-start | bytes 393224 | tf_op jit(solution)/shard_map/ppermute | solution.py:302
  21.0 11.2 %collective-permute-start.8 = (f32[1,16,32,128]{3,2,1,0:T(8,128)S(1)}, f32[1,16,32,128]{3,2,1,0:T(8,128)S(1)}, u32[]{:S(2)}, u32[]{:S(2)}) collective-permute-start(f32[1,16,32,128]{3,2,1,0:T(8,128)S(1)} %get-tuple-element.36.lo), channel_id=1, source_target_pairs={{0,24},{4,28},{8,0},{12,4},{16,8},{20,12},{24,16},{28,20},{1,25},{... | collective-permute-start | bytes 786440 | tf_op jit(solution)/shard_map/ppermute | solution.py:303
  24.7 13.9 %collective-permute-start.7 = (f32[1,12,32,128]{3,2,1,0:T(8,128)S(1)}, f32[1,12,32,128]{3,2,1,0:T(8,128)S(1)}, u32[]{:S(2)}, u32[]{:S(2)}) collective-permute-start(f32[1,12,32,128]{3,2,1,0:T(8,128)S(1)} %get-tuple-element.34.lo), channel_id=1, source_target_pairs={{0,24},{4,28},{8,0},{12,4},{16,8},{20,12},{24,16},{28,20},{1,25},{... | collective-permute-start | bytes 589832 | tf_op jit(solution)/shard_map/ppermute | solution.py:303
  29.1 9.6 %collective-permute-start.6 = (f32[1,8,32,128]{3,2,1,0:T(8,128)S(1)}, f32[1,8,32,128]{3,2,1,0:T(8,128)S(1)}, u32[]{:S(2)}, u32[]{:S(2)}) collective-permute-start(f32[1,8,32,128]{3,2,1,0:T(8,128)S(1)} %get-tuple-element.33.hi), channel_id=1, source_target_pairs={{0,8},{4,12},{8,16},{12,20},{16,24},{20,28},{24,0},{28,4},{1,9},{5... | collective-permute-start | bytes 393224 | tf_op jit(solution)/shard_map/ppermute | solution.py:302
  40.1 6.2 %collective-permute-start.10 = (f32[2,2,2,32,128]{4,3,2,1,0:T(8,128)S(1)}, f32[2,2,2,32,128]{4,3,2,1,0:T(8,128)S(1)}, u32[]{:S(2)}, u32[]{:S(2)}) collective-permute-start(f32[2,2,2,32,128]{4,3,2,1,0:T(8,128)S(1)} %get-tuple-element.42), channel_id=1, source_target_pairs={{0,6},{1,7},{2,4},{3,5},{4,2},{5,3},{6,0},{7,1},{8,14},{9,15},{10,... | collective-permute-start | bytes 393224 | tf_op jit(solution)/shard_map/ppermute | solution.py:312
  42.4 5.1 %collective-permute-start.11 = (f32[2,2,2,32,128]{4,3,2,1,0:T(8,128)S(1)}, f32[2,2,2,32,128]{4,3,2,1,0:T(8,128)S(1)}, u32[]{:S(2)}, u32[]{:S(2)}) collective-permute-start(f32[2,2,2,32,128]{4,3,2,1,0:T(8,128)S(1)} %get-tuple-element.43), channel_id=1, source_target_pairs={{0,4},{1,5},{2,6},{3,7},{4,0},{5,1},{6,2},{7,3},{8,12},{9,13},{10,... | collective-permute-start | bytes 393224 | tf_op jit(solution)/shard_map/ppermute | solution.py:312
  43.1 5.7 %collective-permute-start.12 = (f32[2,2,2,32,128]{4,3,2,1,0:T(8,128)S(1)}, f32[2,2,2,32,128]{4,3,2,1,0:T(8,128)S(1)}, u32[]{:S(2)}, u32[]{:S(2)}) collective-permute-start(f32[2,2,2,32,128]{4,3,2,1,0:T(8,128)S(1)} %get-tuple-element.44), channel_id=1, source_target_pairs={{0,2},{1,3},{2,0},{3,1},{4,6},{5,7},{6,4},{7,5},{8,10},{9,11},{10,... | collective-permute-start | bytes 393224 | tf_op jit(solution)/shard_map/ppermute | solution.py:312
  43.6 6.8 %collective-permute-start.13 = (f32[2,2,2,32,128]{4,3,2,1,0:T(8,128)S(1)}, f32[2,2,2,32,128]{4,3,2,1,0:T(8,128)S(1)}, u32[]{:S(2)}, u32[]{:S(2)}) collective-permute-start(f32[2,2,2,32,128]{4,3,2,1,0:T(8,128)S(1)} %get-tuple-element.45), channel_id=1, source_target_pairs={{0,7},{1,6},{2,5},{3,4},{4,3},{5,2},{6,1},{7,0},{8,15},{9,14},{10,... | collective-permute-start | bytes 393224 | tf_op jit(solution)/shard_map/ppermute | solution.py:312
  43.6 8.3 %collective-permute-start.14 = (f32[2,2,2,32,128]{4,3,2,1,0:T(8,128)S(1)}, f32[2,2,2,32,128]{4,3,2,1,0:T(8,128)S(1)}, u32[]{:S(2)}, u32[]{:S(2)}) collective-permute-start(f32[2,2,2,32,128]{4,3,2,1,0:T(8,128)S(1)} %get-tuple-element.46), channel_id=1, source_target_pairs={{0,5},{1,4},{2,7},{3,6},{4,1},{5,0},{6,3},{7,2},{8,13},{9,12},{10,... | collective-permute-start | bytes 393224 | tf_op jit(solution)/shard_map/ppermute | solution.py:312
  46.3 6.6 %collective-permute-start.15 = (f32[2,2,2,32,128]{4,3,2,1,0:T(8,128)S(1)}, f32[2,2,2,32,128]{4,3,2,1,0:T(8,128)S(1)}, u32[]{:S(2)}, u32[]{:S(2)}) collective-permute-start(f32[2,2,2,32,128]{4,3,2,1,0:T(8,128)S(1)} %get-tuple-element.47), channel_id=1, source_target_pairs={{0,3},{1,2},{2,1},{3,0},{4,7},{5,6},{6,5},{7,4},{8,11},{9,10},{10,... | collective-permute-start | bytes 393224 | tf_op jit(solution)/shard_map/ppermute | solution.py:312
  47.5 5.4 %collective-permute-start.16 = (f32[2,2,2,32,128]{4,3,2,1,0:T(8,128)S(1)}, f32[2,2,2,32,128]{4,3,2,1,0:T(8,128)S(1)}, u32[]{:S(2)}, u32[]{:S(2)}) collective-permute-start(f32[2,2,2,32,128]{4,3,2,1,0:T(8,128)S(1)} %get-tuple-element.48), channel_id=1, source_target_pairs={{0,1},{1,0},{2,3},{3,2},{4,5},{5,4},{6,7},{7,6},{8,9},{9,8},{10,11... | collective-permute-start | bytes 393224 | tf_op jit(solution)/shard_map/ppermute | solution.py:312
  54.9 8.8 %collective-permute-start.17 = (f32[2,8,32,128]{3,2,1,0:T(8,128)S(1)}, f32[2,8,32,128]{3,2,1,0:T(8,128)S(1)}, u32[]{:S(2)}, u32[]{:S(2)}) collective-permute-start(f32[2,8,32,128]{3,2,1,0:T(8,128)S(1)} %get-tuple-element.52), channel_id=1, source_target_pairs={{0,4},{4,0},{8,12},{12,8},{16,20},{20,16},{24,28},{28,24},{1,5},{5... | collective-permute-start | bytes 786440 | tf_op jit(solution)/shard_map/ppermute | solution.py:328
  55.9 12.1 %all-to-all-start = ((f32[32,1,128]{2,1,0:T(1,128)}), f32[32,1,128]{2,1,0:T(1,128)S(1)}, u32[]{:S(2)}, u32[]{:S(2)}) async-start(f32[32,1,128]{2,1,0:T(1,128)} %gram.1), calls=%async_computation | async-start | bytes 32768 | tf_op jit(solution)/shard_map/all_to_all | solution.py:329

commit v6 on v5

--- a/solution.py
+++ b/solution.py
@@ -18,7 +18,8 @@
 S1 = HALF / (LOWER - CENTRE)
 T2 = 2.0 / S1**2 - 1.0
 T4 = 2.0 * T2 * T2 - 1.0
-PEERS = (6, 4, 2, 7, 5, 3, 1, 0)
+EARLY = (6, 4, 2)
+LATE = (7, 5, 3, 1, 0)
 CHUNK = 4
 
 
@@ -149,22 +150,26 @@
     def cells(which, k, per):
         return both[which, pl.ds(per * jnp.bitwise_xor(me, k), per)]
 
-    if len(outs) == 2:
-        home, blocks = outs
+    early = len(EARLY)
+    if len(outs) == 2 + early:
+        home, late, *blocks = outs
         for i, start in enumerate(homes):
             home[i] = both[0, pl.ds(start, n)]
-        for i, k in enumerate(PEERS):
+        for i, k in enumerate(LATE):
             for which in range(2):
-                blocks[i, which] = cells(which, k, blocks.shape[2])
+                late[i, which] = cells(which, k, late.shape[2])
     else:
-        home_a, blocks_a, keep, send, *blocks = outs
+        home_a, late_a, keep, send, *blocks = outs
         for i, ref in enumerate((keep, send)):
             ref[0] = home_a[i]
             ref[1] = both[0, pl.ds(homes[i], n)]
-        for i, (k, block) in enumerate(zip(PEERS, blocks)):
-            block[0] = blocks_a[i]
+        for i, (k, block) in enumerate(zip(LATE, blocks[early:])):
+            block[0] = late_a[i]
             for which in range(2):
                 block[1, which] = cells(which, k, block.shape[2])
+    for k, block in zip(EARLY, blocks):
+        for which in range(2):
+            block[which] = cells(which, k, block.shape[1])
 
 
 def gram(*refs):
@@ -172,8 +177,11 @@
     orbs = part.shape[1]
     half, peers, _, per, ny, nz = blocks.shape
     me = places()[2]
-    for k, x in zip(PEERS, xs):
-        for o in range(half):
+    early = len(EARLY)
+    for o in range(half):
+        for k, x in zip(EARLY, xs[early * o :]):
+            blocks[o, jnp.bitwise_xor(me, k)] = x[...]
+        for k, x in zip(LATE, xs[early * half :]):
             blocks[o, jnp.bitwise_xor(me, k)] = x[o]
     rows = per * ny
     flat = blocks.reshape(half * peers * 2 * rows, nz)
@@ -312,10 +320,18 @@
         return lax.ppermute(x, ("mem", "orb"), [(t, t ^ k) for t in range(group)]) if k else x
 
     block = (2, per, ny, nz)
-    results = call(last_three, second[0], [(2, n, ny, nz), (group, *block)], scratch, 1.5, "filter_3_4_hamiltonian")
-    outs = [(half, n, ny, nz)] * 2 + [(half, *block)] * group
-    keep, send, *blocks = call(last_three, (*second[1], *results), outs, scratch, 1.5, "filter_3_4_hamiltonian")
-    xs = [peer(x, k) for k, x in zip(PEERS, blocks)]
+    early = len(EARLY)
+    outs = [(2, n, ny, nz), (len(LATE), *block)] + [block] * early
+    home, late, *early_a = call(last_three, second[0], outs, scratch, 1.5, "filter_3_4_hamiltonian")
+    early_a = [peer(x, k) for k, x in zip(EARLY, early_a)]
+    outs = [(half, n, ny, nz)] * 2 + [block] * early + [(half, *block)] * len(LATE)
+    keep, send, *blocks = call(
+        last_three, (*second[1], home, late), outs, scratch, 1.5, "filter_3_4_hamiltonian"
+    )
+    tied = lax.optimization_barrier((*blocks[early:-1], *early_a))
+    late = [peer(x, k) for k, x in zip(LATE[:-1], tied)] + blocks[-1:]
+    early_b = [peer(x, k) for k, x in zip(EARLY, blocks)]
+    xs = [*tied[-early:], *early_b, *late]
     (sums,) = call(
         gram,
         xs,

time: 68.9 us -> 71.7 us (1.041)
  starting transfers between devices: 32.7 us -> 38 us
  waiting for transfers between devices: 25.5 us -> 23.1 us
    ppermute x2, waiting for transfers between devices: 5.08 us -> 1.28 us  [per_device(): rlo = lax.ppermute(hi, grid_axes, up)]
    ppermute x7 -> x10, starting transfers between devices: 6.44 us -> 10.2 us  [peer(): lax.ppermute(x, ('mem', 'orb'), [(t, t ^ k) for t in range(group)])]
    ppermute x1, waiting for transfers between devices: 2.8 us -> 0.01 us  [per_device(): back = lax.ppermute(send, grid_axes, swap)]
    all_to_all x1, waiting for transfers between devices: 3.51 us -> 6.29 us  [per_device(): sums = lax.all_to_all(sums, ('pair', 'mem', 'orb'), 0, 0, tiled=True)]
    all_to_all x1, starting transfers between devices: 4.95 us -> 6.8 us  [per_device(): sums = lax.all_to_all(sums, ('pair', 'mem', 'orb'), 0, 0, tiled=True)]
    ppermute x7 -> x10, waiting for transfers between devices: 6.42 us -> 7.78 us  [peer(): lax.ppermute(x, ('mem', 'orb'), [(t, t ^ k) for t in range(group)])]
  transfers between devices with their start and end apart: 19 -> 22, of which waited for: 13 -> 9; matrix products, arithmetic and copies ran while one was open for 1% -> 1% of each run, Pallas kernels for 5% -> 7%
where the time goes in v6:
time: 71.7 us; the launch traced here: 71.6 us
  starting transfers between devices  38 us (53%)
  waiting for transfers between devices  23.1 us (32%)
  Pallas kernels  7.6 us (11%)
  local copies, waits for them, and re-layouts  1.18 us (2%)
  other arithmetic  0.9 us (1%)
  between operations  0.76 us (1%)
    ppermute x10, starting transfers between devices, peer(): lax.ppermute(x, ('mem', 'orb'), [(t, t ^ k) for t in range(group)])  10.2 us
    ppermute x10, waiting for transfers between devices, peer(): lax.ppermute(x, ('mem', 'orb'), [(t, t ^ k) for t in range(group)])  7.78 us
    pallas_call x7, Pallas kernels, call(): pl.pallas_call(body, out_shape=[s if isinstance(s, jax.ShapeDtypeStruct)...  7.6 us
    ppermute x2, starting transfers between devices, per_device(): rhi = lax.ppermute(lo, grid_axes, down)  6.88 us
    all_to_all x1, starting transfers between devices, per_device(): sums = lax.all_to_all(sums, ('pair', 'mem', 'orb'), 0, 0, tiled=True)  6.8 us
    all_to_all x1, waiting for transfers between devices, per_device(): sums = lax.all_to_all(sums, ('pair', 'mem', 'orb'), 0, 0, tiled=True)  6.29 us
    ppermute x2, starting transfers between devices, per_device(): rb = lax.ppermute(b, grid_axes, cross)  5.91 us
    ppermute x2, starting transfers between devices, per_device(): ra = lax.ppermute(a, grid_axes, swap)  3.77 us
  transfers between devices with their start and end apart: 22, of which 9 were waited for; matrix products, arithmetic and copies ran while one was open for 1% of the time, Pallas kernels for 7%

profile of v6, /device:TPU:0, one launch (start us, length us, event | category | flops | bytes accessed | tf_op | source)
XLA Modules:
  0.0 71.6 jit_solution(3704192626842563994)
XLA Ops:
  0.6 1.2 %constant_dynamic-slice_fusion = (f32[1,8,32,128]{3,2,1,0:T(8,128)S(1)}, f32[1,8,32,128]{3,2,1,0:T(8,128)S(1)}, f32[1,8,32,128]{3,2,1,0:T(8,128)S(1)}, f32[1,8,32,128]{3,2,1,0:T(8,128)S(1)}) fusion(f32[4,8,32,128]{3,2,1,0:T(8,128)} %param.2, s32[]{:T(128)S(6)} %select_n.33, s32[]{:T(128)S(6)} %select_n.29, s32[]{:T(128)S(6)} %select_n.28, s32[]{:T(128)S(6)} %select_n.30), kind=kLoop, calls=%fused_computation.5 | loop fusion | bytes 1048592 | tf_op jit(solution)/shard_map/dynamic_slice | solution.py:286
  1.9 3.0 %collective-permute-start.3 = (f32[1,16,32,128]{3,2,1,0:T(8,128)S(1)}, f32[1,16,32,128]{3,2,1,0:T(8,128)S(1)}, u32[]{:S(2)}, u32[]{:S(2)}) collective-permute-start(f32[1,16,32,128]{3,2,1,0:T(8,128)S(1)} %pad_maximum_fusion), channel_id=1, source_target_pairs={{0,4},{4,0},{8,12},{12,8},{16,20},{20,16},{24,28},{28,24},{1,5},{5... | collective-permute-start | bytes 786440 | tf_op jit(solution)/shard_map/ppermute | solution.py:290
  4.9 3.6 %collective-permute-start.4 = (f32[1,12,32,128]{3,2,1,0:T(8,128)S(1)}, f32[1,12,32,128]{3,2,1,0:T(8,128)S(1)}, u32[]{:S(2)}, u32[]{:S(2)}) collective-permute-start(f32[1,12,32,128]{3,2,1,0:T(8,128)S(1)} %get-tuple-element.81), channel_id=1, source_target_pairs={{0,28},{4,8},{8,4},{12,16},{16,12},{20,24},{24,20},{28,0},{1,29},{... | collective-permute-start | bytes 589832 | tf_op jit(solution)/shard_map/ppermute | solution.py:291
  9.0 2.3 %collective-permute-start.1 = (f32[1,8,32,128]{3,2,1,0:T(8,128)S(1)}, f32[1,8,32,128]{3,2,1,0:T(8,128)S(1)}, u32[]{:S(2)}, u32[]{:S(2)}) collective-permute-start(f32[1,8,32,128]{3,2,1,0:T(8,128)S(1)} %get-tuple-element.78), channel_id=1, source_target_pairs={{0,28},{4,8},{8,4},{12,16},{16,12},{20,24},{24,20},{28,0},{1,29},{... | collective-permute-start | bytes 393224 | tf_op jit(solution)/shard_map/ppermute | solution.py:291
  12.0 3.5 %collective-permute-done.4.rb = f32[1,12,32,128]{3,2,1,0:T(8,128)S(1)} collective-permute-done((f32[1,12,32,128]{3,2,1,0:T(8,128)S(1)}, f32[1,12,32,128]{3,2,1,0:T(8,128)S(1)}, u32[]{:S(2)}, u32[]{:S(2)}) %collective-permute-start.4) | collective-permute-done | bytes 196640 | tf_op jit(solution)/shard_map/ppermute | solution.py:291
  15.6 1.8 %collective-permute-start.2 = (f32[1,8,32,128]{3,2,1,0:T(8,128)S(1)}, f32[1,8,32,128]{3,2,1,0:T(8,128)S(1)}, u32[]{:S(2)}, u32[]{:S(2)}) collective-permute-start(f32[1,8,32,128]{3,2,1,0:T(8,128)S(1)} %get-tuple-element.79.mine), channel_id=1, source_target_pairs={{0,24},{4,12},{8,0},{12,20},{16,8},{20,28},{24,16},{28,4},{1,25},{... | collective-permute-start | bytes 393224 | tf_op jit(solution)/shard_map/ppermute | solution.py:292
  18.5 1.0 %filter_1_2.2 = (f32[1,16,32,128]{3,2,1,0:T(8,128)S(1)}, f32[1,8,32,128]{3,2,1,0:T(8,128)S(1)}, f32[1,20,32,128]{3,2,1,0:T(8,128)S(1)}, f32[24,32,128]{2,1,0:T(8,128)S(1)}) custom-call(bf16[128,384]{1,0:T(8,128)(2,1)S(1)} %get-tuple-element.40.ymat, bf16[384,128]{1,0:T(8,128)(2,1)S(1)} %get-tuple-element.41.zmat, ...), custom_call_target="tpu_custom_call" | custom-call | flops 1000000000 | bytes 3500000 | tf_op jit(solution)/shard_map/filter_1_2/pallas_call | solution.py:246
  19.5 1.6 %collective-permute-start.9 = (f32[1,8,32,128]{3,2,1,0:T(8,128)S(1)}, f32[1,8,32,128]{3,2,1,0:T(8,128)S(1)}, u32[]{:S(2)}, u32[]{:S(2)}) collective-permute-start(f32[1,8,32,128]{3,2,1,0:T(8,128)S(1)} %get-tuple-element.47.hi), channel_id=1, source_target_pairs={{0,8},{4,12},{8,16},{12,20},{16,24},{20,28},{24,0},{28,4},{1,9},{5... | collective-permute-start | bytes 393224 | tf_op jit(solution)/shard_map/ppermute | solution.py:310
  21.0 2.5 %collective-permute-start.8 = (f32[1,16,32,128]{3,2,1,0:T(8,128)S(1)}, f32[1,16,32,128]{3,2,1,0:T(8,128)S(1)}, u32[]{:S(2)}, u32[]{:S(2)}) collective-permute-start(f32[1,16,32,128]{3,2,1,0:T(8,128)S(1)} %get-tuple-element.46.lo), channel_id=1, source_target_pairs={{0,24},{4,28},{8,0},{12,4},{16,8},{20,12},{24,16},{28,20},{1,25},{... | collective-permute-start | bytes 786440 | tf_op jit(solution)/shard_map/ppermute | solution.py:311
  23.8 1.0 %filter_1_2.3 = (f32[1,12,32,128]{3,2,1,0:T(8,128)S(1)}, f32[1,8,32,128]{3,2,1,0:T(8,128)S(1)}, f32[1,20,32,128]{3,2,1,0:T(8,128)S(1)}) custom-call(bf16[128,384]{1,0:T(8,128)(2,1)S(1)} %get-tuple-element.40.ymat, bf16[384,128]{1,0:T(8,128)(2,1)S(1)} %get-tuple-element.41.zmat, f32[1,8,32,128]{3,2,1,0:T(8,128)S(1)} %get-tuple-element.79.mine, ...), custom_call_target="tpu_custom_call" | custom-call | flops 10000000000 | bytes 35000000 | tf_op jit(solution)/shard_map/filter_1_2/pallas_call | solution.py:246
  24.7 4.3 %collective-permute-start.7 = (f32[1,12,32,128]{3,2,1,0:T(8,128)S(1)}, f32[1,12,32,128]{3,2,1,0:T(8,128)S(1)}, u32[]{:S(2)}, u32[]{:S(2)}) collective-permute-start(f32[1,12,32,128]{3,2,1,0:T(8,128)S(1)} %get-tuple-element.44.lo), channel_id=1, source_target_pairs={{0,24},{4,28},{8,0},{12,4},{16,8},{20,12},{24,16},{28,20},{1,25},{... | collective-permute-start | bytes 589832 | tf_op jit(solution)/shard_map/ppermute | solution.py:311
  29.1 3.1 %collective-permute-done.8.rhi.v_above = f32[1,16,32,128]{3,2,1,0:T(8,128)S(1)} collective-permute-done((f32[1,16,32,128]{3,2,1,0:T(8,128)S(1)}, f32[1,16,32,128]{3,2,1,0:T(8,128)S(1)}, u32[]{:S(2)}, u32[]{:S(2)}) %collective-permute-start.8) | collective-permute-done | bytes 262176 | tf_op jit(solution)/shard_map/ppermute | solution.py:311
  32.2 1.4 %filter_3_4_hamiltonian.2 = (f32[2,8,32,128]{3,2,1,0:T(8,128)S(1)}, f32[5,2,2,32,128]{4,3,2,1,0:T(8,128)S(1)}, f32[2,2,32,128]{3,2,1,0:T(8,128)S(1)}, f32[2,2,32,128]{3,2,1,0:T(8,128)S(1)}, f32[2,2,32,128]{3,2,1,0:T(8,128)S(1)}) custom-call(bf16[128,384]{1,0:T(8,128)(2,1)S(1)} %get-tuple-element.40.ymat, bf16[384,128]{1,0:T(8,128)(2,1)S(1)} %get-tuple-element.41.zmat, ...), custom_call_target="tpu_custom_call" | custom-call | flops 1500000000 | bytes 5250000 | tf_op jit(solution)/shard_map/filter_3_4_hamiltonian/pallas_call | solution.py:246
  33.6 3.2 %collective-permute-start.10 = (f32[2,2,32,128]{3,2,1,0:T(8,128)S(1)}, f32[2,2,32,128]{3,2,1,0:T(8,128)S(1)}, u32[]{:S(2)}, u32[]{:S(2)}) collective-permute-start(f32[2,2,32,128]{3,2,1,0:T(8,128)S(1)} %get-tuple-element.56), channel_id=1, source_target_pairs={{0,6},{1,7},{2,4},{3,5},{4,2},{5,3},{6,0},{7,1},{8,14},{9,15},{10,... | collective-permute-start | bytes 196616 | tf_op jit(solution)/shard_map/ppermute | solution.py:320
  37.4 1.3 %collective-permute-done.6.rlo = f32[1,8,32,128]{3,2,1,0:T(8,128)S(1)} collective-permute-done((f32[1,8,32,128]{3,2,1,0:T(8,128)S(1)}, f32[1,8,32,128]{3,2,1,0:T(8,128)S(1)}, u32[]{:S(2)}, u32[]{:S(2)}) %collective-permute-start.6) | collective-permute-done | bytes 131104 | tf_op jit(solution)/shard_map/ppermute | solution.py:310
  38.7 1.4 %filter_3_4_hamiltonian.3 = (f32[2,8,32,128]{3,2,1,0:T(8,128)S(1)}, f32[2,8,32,128]{3,2,1,0:T(8,128)S(1)}, f32[2,2,32,128]{3,2,1,0:T(8,128)S(1)}, f32[2,2,32,128...) custom-call(bf16[128,384]{1,0:T(8,128)(2,1)S(1)} %get-tuple-element., ...), custom_call_target="tpu_custom_call" | custom-call | flops 1500000000 | bytes 5250000 | tf_op jit(solution)/shard_map/filter_3_4_hamiltonian/pallas_call | solution.py:246
  40.0 2.3 %collective-permute-start.13 = (f32[2,2,32,128]{3,2,1,0:T(8,128)S(1)}, f32[2,2,32,128]{3,2,1,0:T(8,128)S(1)}, u32[]{:S(2)}, u32[]{:S(2)}) collective-permute-start(f32[2,2,32,128]{3,2,1,0:T(8,128)S(1)} %get-tuple-element.62), channel_id=1, source_target_pairs={{0,6},{1,7},{2,4},{3,5},{4,2},{5,3},{6,0},{7,1},{8,14},{9,15},{10,... | collective-permute-start | bytes 196616 | tf_op jit(solution)/shard_map/ppermute | solution.py:320
  43.2 1.7 %collective-permute-start.17 = (f32[2,2,2,32,128]{4,3,2,1,0:T(8,128)S(1)}, f32[2,2,2,32,128]{4,3,2,1,0:T(8,128)S(1)}, u32[]{:S(2)}, u32[]{:S(2)}) collective-permute-start(f32[2,2,2,32,128]{4,3,2,1,0:T(8,128)S(1)} %get-tuple-element.66), channel_id=1, source_target_pairs={{0,5},{1,4},{2,7},{3,6},{4,1},{5,0},{6,3},{7,2},{8,13},{9,12},{10,... | collective-permute-start | bytes 393224 | tf_op jit(solution)/shard_map/ppermute | solution.py:320
  46.5 3.5 %collective-permute-done.14.refs_4_ = f32[2,2,32,128]{3,2,1,0:T(8,128)S(1)} collective-permute-done((f32[2,2,32,128]{3,2,1,0:T(8,128)S(1)}, f32[2,2,32,128]{3,2,1,0:T(8,128)S(1)}, u32[]{:S(2)}, u32[]{:S(2)}) %collective-permute-start.14) | collective-permute-done | bytes 65568 | tf_op jit(solution)/shard_map/ppermute | solution.py:320
  50.0 4.3 %collective-permute-done.15.refs_5_ = f32[2,2,32,128]{3,2,1,0:T(8,128)S(1)} collective-permute-done((f32[2,2,32,128]{3,2,1,0:T(8,128)S(1)}, f32[2,2,32,128]{3,2,1,0:T(8,128)S(1)}, u32[]{:S(2)}, u32[]{:S(2)}) %collective-permute-start.15) | collective-permute-done | bytes 65568 | tf_op jit(solution)/shard_map/ppermute | solution.py:320
  54.3 2.0 %gram.1 = f32[32,1,128]{2,1,0:T(1,128)} custom-call(f32[2,2,32,128]{3,2,1,0:T(8,128)S(1)} %collective-permute-done.10.refs_0_, f32[2,2,32,128]{3,2,1,0:T(8,128)S(1)} %collective-permute-done.11.refs_1_, f32[2,2,32,128]{3,2,1,0:T(8,128)S(1)} %collective-permute-done.12.refs_2_, f32[2,2,32,128]{3,2,1,0:T(8,128)S(1)} %collective-permute-done.13.refs_3_, ...), custom_call_target="tpu_custom_call" | custom-call | flops 1300000000 | bytes 4550000 | tf_op jit(solution)/shard_map/gram/pallas_call | solution.py:246
  56.9 6.8 %all-to-all-start = ((f32[32,1,128]{2,1,0:T(1,128)}), f32[32,1,128]{2,1,0:T(1,128)S(1)}, u32[]{:S(2)}, u32[]{:S(2)}) async-start(f32[32,1,128]{2,1,0:T(1,128)} %gram.1), calls=%async_computation | async-start | bytes 32768 | tf_op jit(solution)/shard_map/all_to_all | solution.py:345
  63.7 0.8 %maximum_select_fusion = f32[4,8,32,128]{3,2,1,0:T(8,128)} fusion(f32[2,8,32,128]{3,2,1,0:T(8,128)S(1)} %collective-permute-done.20, f32[2,8,32,128]{3,2,1,0:T(8,128)S(1)} %get-tuple-element.71, pred[]{:T(512)S(6)} %eq.4), kind=kLoop, calls=%fused_computation | loop fusion | flops 393216 | bytes 1048577 | tf_op jit(solution)/shard_map/jit(_where)/select_n | solution.py:346
  64.6 6.3 %all-to-all-done.x_ref = f32[32,1,128]{2,1,0:T(1,128)S(1)} async-done(((f32[32,1,128]{2,1,0:T(1,128)}), f32[32,1,128]{2,1,0:T(1,128)S(1)}, u32[]{:S(2)}, u32[]{:S(2)}) %all-to-all-start) | async-done | bytes 16416 | tf_op jit(solution)/shard_map/all_to_all | solution.py:345
  (34 shorter events, 7.0 us)
Async XLA Ops:
  0.6 1.2 %copy-start = (f32[8,32,128]{2,1,0:T(8,128)S(1)}, f32[8,32,128]{2,1,0:T(8,128)}, u32[]{:S(2)}) copy-start(f32[8,32,128]{2,1,0:T(8,128)} %refs_0_.1) | copy-start | bytes 393220
  1.9 16.6 %collective-permute-start.3 = (f32[1,16,32,128]{3,2,1,0:T(8,128)S(1)}, f32[1,16,32,128]{3,2,1,0:T(8,128)S(1)}, u32[]{:S(2)}, u32[]{:S(2)}) collective-permute-start(f32[1,16,32,128]{3,2,1,0:T(8,128)S(1)} %pad_maximum_fusion), channel_id=1, source_target_pairs={{0,4},{4,0},{8,12},{12,8},{16,20},{20,16},{24,28},{28,24},{1,5},{5... | collective-permute-start | bytes 786440 | tf_op jit(solution)/shard_map/ppermute | solution.py:290
  4.9 10.6 %collective-permute-start.4 = (f32[1,12,32,128]{3,2,1,0:T(8,128)S(1)}, f32[1,12,32,128]{3,2,1,0:T(8,128)S(1)}, u32[]{:S(2)}, u32[]{:S(2)}) collective-permute-start(f32[1,12,32,128]{3,2,1,0:T(8,128)S(1)} %get-tuple-element.81), channel_id=1, source_target_pairs={{0,28},{4,8},{8,4},{12,16},{16,12},{20,24},{24,20},{28,0},{1,29},{... | collective-permute-start | bytes 589832 | tf_op jit(solution)/shard_map/ppermute | solution.py:291
  8.6 9.6 %collective-permute-start.5 = (f32[1,12,32,128]{3,2,1,0:T(8,128)S(1)}, f32[1,12,32,128]{3,2,1,0:T(8,128)S(1)}, u32[]{:S(2)}, u32[]{:S(2)}) collective-permute-start(f32[1,12,32,128]{3,2,1,0:T(8,128)S(1)} %get-tuple-element.82.mine), channel_id=1, source_target_pairs={{0,24},{4,12},{8,0},{12,20},{16,8},{20,28},{24,16},{28,4},{1,25},{... | collective-permute-start | bytes 589832 | tf_op jit(solution)/shard_map/ppermute | solution.py:292
  9.0 14.6 %collective-permute-start.1 = (f32[1,8,32,128]{3,2,1,0:T(8,128)S(1)}, f32[1,8,32,128]{3,2,1,0:T(8,128)S(1)}, u32[]{:S(2)}, u32[]{:S(2)}) collective-permute-start(f32[1,8,32,128]{3,2,1,0:T(8,128)S(1)} %get-tuple-element.78), channel_id=1, source_target_pairs={{0,28},{4,8},{8,4},{12,16},{16,12},{20,24},{24,20},{28,0},{1,29},{... | collective-permute-start | bytes 393224 | tf_op jit(solution)/shard_map/ppermute | solution.py:291
  11.3 12.3 %collective-permute-start = (f32[1,8,32,128]{3,2,1,0:T(8,128)S(1)}, f32[1,8,32,128]{3,2,1,0:T(8,128)S(1)}, u32[]{:S(2)}, u32[]{:S(2)}) collective-permute-start(f32[1,8,32,128]{3,2,1,0:T(8,128)S(1)} %get-tuple-element.78), channel_id=1, source_target_pairs={{0,4},{4,0},{8,12},{12,8},{16,20},{20,16},{24,28},{28,24},{1,5},{5... | collective-permute-start | bytes 393224 | tf_op jit(solution)/shard_map/ppermute | solution.py:290
  15.6 8.2 %collective-permute-start.2 = (f32[1,8,32,128]{3,2,1,0:T(8,128)S(1)}, f32[1,8,32,128]{3,2,1,0:T(8,128)S(1)}, u32[]{:S(2)}, u32[]{:S(2)}) collective-permute-start(f32[1,8,32,128]{3,2,1,0:T(8,128)S(1)} %get-tuple-element.79.mine), channel_id=1, source_target_pairs={{0,24},{4,12},{8,0},{12,20},{16,8},{20,28},{24,16},{28,4},{1,25},{... | collective-permute-start | bytes 393224 | tf_op jit(solution)/shard_map/ppermute | solution.py:292
  19.5 9.6 %collective-permute-start.9 = (f32[1,8,32,128]{3,2,1,0:T(8,128)S(1)}, f32[1,8,32,128]{3,2,1,0:T(8,128)S(1)}, u32[]{:S(2)}, u32[]{:S(2)}) collective-permute-start(f32[1,8,32,128]{3,2,1,0:T(8,128)S(1)} %get-tuple-element.47.hi), channel_id=1, source_target_pairs={{0,8},{4,12},{8,16},{12,20},{16,24},{20,28},{24,0},{28,4},{1,9},{5... | collective-permute-start | bytes 393224 | tf_op jit(solution)/shard_map/ppermute | solution.py:310
  21.0 11.2 %collective-permute-start.8 = (f32[1,16,32,128]{3,2,1,0:T(8,128)S(1)}, f32[1,16,32,128]{3,2,1,0:T(8,128)S(1)}, u32[]{:S(2)}, u32[]{:S(2)}) collective-permute-start(f32[1,16,32,128]{3,2,1,0:T(8,128)S(1)} %get-tuple-element.46.lo), channel_id=1, source_target_pairs={{0,24},{4,28},{8,0},{12,4},{16,8},{20,12},{24,16},{28,20},{1,25},{... | collective-permute-start | bytes 786440 | tf_op jit(solution)/shard_map/ppermute | solution.py:311
  24.7 13.9 %collective-permute-start.7 = (f32[1,12,32,128]{3,2,1,0:T(8,128)S(1)}, f32[1,12,32,128]{3,2,1,0:T(8,128)S(1)}, u32[]{:S(2)}, u32[]{:S(2)}) collective-permute-start(f32[1,12,32,128]{3,2,1,0:T(8,128)S(1)} %get-tuple-element.44.lo), channel_id=1, source_target_pairs={{0,24},{4,28},{8,0},{12,4},{16,8},{20,12},{24,16},{28,20},{1,25},{... | collective-permute-start | bytes 589832 | tf_op jit(solution)/shard_map/ppermute | solution.py:311
  29.1 9.6 %collective-permute-start.6 = (f32[1,8,32,128]{3,2,1,0:T(8,128)S(1)}, f32[1,8,32,128]{3,2,1,0:T(8,128)S(1)}, u32[]{:S(2)}, u32[]{:S(2)}) collective-permute-start(f32[1,8,32,128]{3,2,1,0:T(8,128)S(1)} %get-tuple-element.43.hi), channel_id=1, source_target_pairs={{0,8},{4,12},{8,16},{12,20},{16,24},{20,28},{24,0},{28,4},{1,9},{5... | collective-permute-start | bytes 393224 | tf_op jit(solution)/shard_map/ppermute | solution.py:310
  33.6 9.5 %collective-permute-start.10 = (f32[2,2,32,128]{3,2,1,0:T(8,128)S(1)}, f32[2,2,32,128]{3,2,1,0:T(8,128)S(1)}, u32[]{:S(2)}, u32[]{:S(2)}) collective-permute-start(f32[2,2,32,128]{3,2,1,0:T(8,128)S(1)} %get-tuple-element.56), channel_id=1, source_target_pairs={{0,6},{1,7},{2,4},{3,5},{4,2},{5,3},{6,0},{7,1},{8,14},{9,15},{10,... | collective-permute-start | bytes 196616 | tf_op jit(solution)/shard_map/ppermute | solution.py:320
  36.7 6.3 %collective-permute-start.11 = (f32[2,2,32,128]{3,2,1,0:T(8,128)S(1)}, f32[2,2,32,128]{3,2,1,0:T(8,128)S(1)}, u32[]{:S(2)}, u32[]{:S(2)}) collective-permute-start(f32[2,2,32,128]{3,2,1,0:T(8,128)S(1)} %get-tuple-element.57), channel_id=1, source_target_pairs={{0,4},{1,5},{2,6},{3,7},{4,0},{5,1},{6,2},{7,3},{8,12},{9,13},{10,... | collective-permute-start | bytes 196616 | tf_op jit(solution)/shard_map/ppermute | solution.py:320
  36.7 6.3 %collective-permute-start.12 = (f32[2,2,32,128]{3,2,1,0:T(8,128)S(1)}, f32[2,2,32,128]{3,2,1,0:T(8,128)S(1)}, u32[]{:S(2)}, u32[]{:S(2)}) collective-permute-start(f32[2,2,32,128]{3,2,1,0:T(8,128)S(1)} %get-tuple-element.58), channel_id=1, source_target_pairs={{0,2},{1,3},{2,0},{3,1},{4,6},{5,7},{6,4},{7,5},{8,10},{9,11},{10,... | collective-permute-start | bytes 196616 | tf_op jit(solution)/shard_map/ppermute | solution.py:320
  40.0 5.6 %collective-permute-start.13 = (f32[2,2,32,128]{3,2,1,0:T(8,128)S(1)}, f32[2,2,32,128]{3,2,1,0:T(8,128)S(1)}, u32[]{:S(2)}, u32[]{:S(2)}) collective-permute-start(f32[2,2,32,128]{3,2,1,0:T(8,128)S(1)} %get-tuple-element.62), channel_id=1, source_target_pairs={{0,6},{1,7},{2,4},{3,5},{4,2},{5,3},{6,0},{7,1},{8,14},{9,15},{10,... | collective-permute-start | bytes 196616 | tf_op jit(solution)/shard_map/ppermute | solution.py:320
  42.3 7.6 %collective-permute-start.14 = (f32[2,2,32,128]{3,2,1,0:T(8,128)S(1)}, f32[2,2,32,128]{3,2,1,0:T(8,128)S(1)}, u32[]{:S(2)}, u32[]{:S(2)}) collective-permute-start(f32[2,2,32,128]{3,2,1,0:T(8,128)S(1)} %get-tuple-element.63), channel_id=1, source_target_pairs={{0,4},{1,5},{2,6},{3,7},{4,0},{5,1},{6,2},{7,3},{8,12},{9,13},{10,... | collective-permute-start | bytes 196616 | tf_op jit(solution)/shard_map/ppermute | solution.py:320
  43.1 11.2 %collective-permute-start.16 = (f32[2,2,2,32,128]{4,3,2,1,0:T(8,128)S(1)}, f32[2,2,2,32,128]{4,3,2,1,0:T(8,128)S(1)}, u32[]{:S(2)}, u32[]{:S(2)}) collective-permute-start(f32[2,2,2,32,128]{4,3,2,1,0:T(8,128)S(1)} %get-tuple-element.65), channel_id=1, source_target_pairs={{0,7},{1,6},{2,5},{3,4},{4,3},{5,2},{6,1},{7,0},{8,15},{9,14},{10,... | collective-permute-start | bytes 393224 | tf_op jit(solution)/shard_map/ppermute | solution.py:320
  43.2 11.1 %collective-permute-start.17 = (f32[2,2,2,32,128]{4,3,2,1,0:T(8,128)S(1)}, f32[2,2,2,32,128]{4,3,2,1,0:T(8,128)S(1)}, u32[]{:S(2)}, u32[]{:S(2)}) collective-permute-start(f32[2,2,2,32,128]{4,3,2,1,0:T(8,128)S(1)} %get-tuple-element.66), channel_id=1, source_target_pairs={{0,5},{1,4},{2,7},{3,6},{4,1},{5,0},{6,3},{7,2},{8,13},{9,12},{10,... | collective-permute-start | bytes 393224 | tf_op jit(solution)/shard_map/ppermute | solution.py:320
  44.9 9.4 %collective-permute-start.18 = (f32[2,2,2,32,128]{4,3,2,1,0:T(8,128)S(1)}, f32[2,2,2,32,128]{4,3,2,1,0:T(8,128)S(1)}, u32[]{:S(2)}, u32[]{:S(2)}) collective-permute-start(f32[2,2,2,32,128]{4,3,2,1,0:T(8,128)S(1)} %get-tuple-element.67), channel_id=1, source_target_pairs={{0,3},{1,2},{2,1},{3,0},{4,7},{5,6},{6,5},{7,4},{8,11},{9,10},{10,... | collective-permute-start | bytes 393224 | tf_op jit(solution)/shard_map/ppermute | solution.py:320
  45.6 8.6 %collective-permute-start.19 = (f32[2,2,2,32,128]{4,3,2,1,0:T(8,128)S(1)}, f32[2,2,2,32,128]{4,3,2,1,0:T(8,128)S(1)}, u32[]{:S(2)}, u32[]{:S(2)}) collective-permute-start(f32[2,2,2,32,128]{4,3,2,1,0:T(8,128)S(1)} %get-tuple-element.68), channel_id=1, source_target_pairs={{0,1},{1,0},{2,3},{3,2},{4,5},{5,4},{6,7},{7,6},{8,9},{9,8},{10,11... | collective-permute-start | bytes 393224 | tf_op jit(solution)/shard_map/ppermute | solution.py:320
  50.0 4.3 %collective-permute-start.15 = (f32[2,2,32,128]{3,2,1,0:T(8,128)S(1)}, f32[2,2,32,128]{3,2,1,0:T(8,128)S(1)}, u32[]{:S(2)}, u32[]{:S(2)}) collective-permute-start(f32[2,2,32,128]{3,2,1,0:T(8,128)S(1)} %get-tuple-element.64), channel_id=1, source_target_pairs={{0,2},{1,3},{2,0},{3,1},{4,6},{5,7},{6,4},{7,5},{8,10},{9,11},{10,... | collective-permute-start | bytes 196616 | tf_op jit(solution)/shard_map/ppermute | solution.py:320
  56.2 7.5 %collective-permute-start.20 = (f32[2,8,32,128]{3,2,1,0:T(8,128)S(1)}, f32[2,8,32,128]{3,2,1,0:T(8,128)S(1)}, u32[]{:S(2)}, u32[]{:S(2)}) collective-permute-start(f32[2,8,32,128]{3,2,1,0:T(8,128)S(1)} %get-tuple-element.72), channel_id=1, source_target_pairs={{0,4},{4,0},{8,12},{12,8},{16,20},{20,16},{24,28},{28,24},{1,5},{5... | collective-permute-start | bytes 786440 | tf_op jit(solution)/shard_map/ppermute | solution.py:344
  56.9 14.0 %all-to-all-start = ((f32[32,1,128]{2,1,0:T(1,128)}), f32[32,1,128]{2,1,0:T(1,128)S(1)}, u32[]{:S(2)}, u32[]{:S(2)}) async-start(f32[32,1,128]{2,1,0:T(1,128)} %gram.1), calls=%async_computation | async-start | bytes 32768 | tf_op jit(solution)/shard_map/all_to_all | solution.py:345

commit v7 on v6

--- a/solution.py
+++ b/solution.py
@@ -18,8 +18,8 @@
 S1 = HALF / (LOWER - CENTRE)
 T2 = 2.0 / S1**2 - 1.0
 T4 = 2.0 * T2 * T2 - 1.0
-EARLY = (6, 4, 2)
-LATE = (7, 5, 3, 1, 0)
+EARLY = (6, 4)
+LATE = (2, 7, 5, 3, 1, 0)
 CHUNK = 4
 
 

time: 71.7 us -> 70.7 us (0.986)
  waiting for transfers between devices: 23.1 us -> 22.3 us
    ppermute x10 -> x9, waiting for transfers between devices: 7.78 us -> 6.31 us  [peer(): lax.ppermute(x, ('mem', 'orb'), [(t, t ^ k) for t in range(group)])]
    ppermute x1, waiting for transfers between devices: 0.01 us -> 0.98 us  [per_device(): back = lax.ppermute(send, grid_axes, swap)]
    all_to_all x1, waiting for transfers between devices: 6.29 us -> 5.33 us  [per_device(): sums = lax.all_to_all(sums, ('pair', 'mem', 'orb'), 0, 0, tiled=True)]
    ppermute x10 -> x9, starting transfers between devices: 10.2 us -> 9.72 us  [peer(): lax.ppermute(x, ('mem', 'orb'), [(t, t ^ k) for t in range(group)])]
  transfers between devices with their start and end apart: 22 -> 21, of which waited for: 9 -> 13; matrix products, arithmetic and copies ran while one was open for 1% -> 1% of each run, Pallas kernels for 7% -> 7%
where the time goes in v7:
time: 70.7 us; the launch traced here: 70.5 us
  starting transfers between devices  37.8 us (53%)
  waiting for transfers between devices  22.3 us (32%)
  Pallas kernels  7.59 us (11%)
  local copies, waits for them, and re-layouts  1.18 us (2%)
  other arithmetic  0.9 us (1%)
  between operations  0.74 us (1%)
    ppermute x9, starting transfers between devices, peer(): lax.ppermute(x, ('mem', 'orb'), [(t, t ^ k) for t in range(group)])  9.72 us
    pallas_call x7, Pallas kernels, call(): pl.pallas_call(body, out_shape=[s if isinstance(s, jax.ShapeDtypeStruct)...  7.59 us
    ppermute x2, starting transfers between devices, per_device(): rhi = lax.ppermute(lo, grid_axes, down)  6.88 us
    all_to_all x1, starting transfers between devices, per_device(): sums = lax.all_to_all(sums, ('pair', 'mem', 'orb'), 0, 0, tiled=True)  6.76 us
    ppermute x9, waiting for transfers between devices, peer(): lax.ppermute(x, ('mem', 'orb'), [(t, t ^ k) for t in range(group)])  6.31 us
    ppermute x2, starting transfers between devices, per_device(): rb = lax.ppermute(b, grid_axes, cross)  5.91 us
    all_to_all x1, waiting for transfers between devices, per_device(): sums = lax.all_to_all(sums, ('pair', 'mem', 'orb'), 0, 0, tiled=True)  5.33 us
    ppermute x2, starting transfers between devices, per_device(): ra = lax.ppermute(a, grid_axes, swap)  3.77 us
  transfers between devices with their start and end apart: 21, of which 13 were waited for; matrix products, arithmetic and copies ran while one was open for 1% of the time, Pallas kernels for 7%

profile of v7, /device:TPU:0, one launch (start us, length us, event | category | flops | bytes accessed | tf_op | source)
XLA Modules:
  0.0 70.5 jit_solution(8172045353289683567)
XLA Ops:
  0.6 1.2 %constant_dynamic-slice_fusion = (f32[1,8,32,128]{3,2,1,0:T(8,128)S(1)}, f32[1,8,32,128]{3,2,1,0:T(8,128)S(1)}, f32[1,8,32,128]{3,2,1,0:T(8,128)S(1)}, f32[1,8,32,128]{3,2,1,0:T(8,128)S(1)}) fusion(f32[4,8,32,128]{3,2,1,0:T(8,128)} %param.2, s32[]{:T(128)S(6)} %select_n.33, s32[]{:T(128)S(6)} %select_n.29, s32[]{:T(128)S(6)} %select_n.28, s32[]{:T(128)S(6)} %select_n.30), kind=kLoop, calls=%fused_computation.5 | loop fusion | bytes 1048592 | tf_op jit(solution)/shard_map/dynamic_slice | solution.py:286
  1.9 3.0 %collective-permute-start.3 = (f32[1,16,32,128]{3,2,1,0:T(8,128)S(1)}, f32[1,16,32,128]{3,2,1,0:T(8,128)S(1)}, u32[]{:S(2)}, u32[]{:S(2)}) collective-permute-start(f32[1,16,32,128]{3,2,1,0:T(8,128)S(1)} %pad_maximum_fusion), channel_id=1, source_target_pairs={{0,4},{4,0},{8,12},{12,8},{16,20},{20,16},{24,28},{28,24},{1,5},{5... | collective-permute-start | bytes 786440 | tf_op jit(solution)/shard_map/ppermute | solution.py:290
  4.9 3.6 %collective-permute-start.4 = (f32[1,12,32,128]{3,2,1,0:T(8,128)S(1)}, f32[1,12,32,128]{3,2,1,0:T(8,128)S(1)}, u32[]{:S(2)}, u32[]{:S(2)}) collective-permute-start(f32[1,12,32,128]{3,2,1,0:T(8,128)S(1)} %get-tuple-element.79), channel_id=1, source_target_pairs={{0,28},{4,8},{8,4},{12,16},{16,12},{20,24},{24,20},{28,0},{1,29},{... | collective-permute-start | bytes 589832 | tf_op jit(solution)/shard_map/ppermute | solution.py:291
  9.0 2.3 %collective-permute-start.1 = (f32[1,8,32,128]{3,2,1,0:T(8,128)S(1)}, f32[1,8,32,128]{3,2,1,0:T(8,128)S(1)}, u32[]{:S(2)}, u32[]{:S(2)}) collective-permute-start(f32[1,8,32,128]{3,2,1,0:T(8,128)S(1)} %get-tuple-element.76), channel_id=1, source_target_pairs={{0,28},{4,8},{8,4},{12,16},{16,12},{20,24},{24,20},{28,0},{1,29},{... | collective-permute-start | bytes 393224 | tf_op jit(solution)/shard_map/ppermute | solution.py:291
  12.0 3.5 %collective-permute-done.4.rb = f32[1,12,32,128]{3,2,1,0:T(8,128)S(1)} collective-permute-done((f32[1,12,32,128]{3,2,1,0:T(8,128)S(1)}, f32[1,12,32,128]{3,2,1,0:T(8,128)S(1)}, u32[]{:S(2)}, u32[]{:S(2)}) %collective-permute-start.4) | collective-permute-done | bytes 196640 | tf_op jit(solution)/shard_map/ppermute | solution.py:291
  15.6 1.8 %collective-permute-start.2 = (f32[1,8,32,128]{3,2,1,0:T(8,128)S(1)}, f32[1,8,32,128]{3,2,1,0:T(8,128)S(1)}, u32[]{:S(2)}, u32[]{:S(2)}) collective-permute-start(f32[1,8,32,128]{3,2,1,0:T(8,128)S(1)} %get-tuple-element.77.mine), channel_id=1, source_target_pairs={{0,24},{4,12},{8,0},{12,20},{16,8},{20,28},{24,16},{28,4},{1,25},{... | collective-permute-start | bytes 393224 | tf_op jit(solution)/shard_map/ppermute | solution.py:292
  19.5 1.6 %collective-permute-start.9 = (f32[1,8,32,128]{3,2,1,0:T(8,128)S(1)}, f32[1,8,32,128]{3,2,1,0:T(8,128)S(1)}, u32[]{:S(2)}, u32[]{:S(2)}) collective-permute-start(f32[1,8,32,128]{3,2,1,0:T(8,128)S(1)} %get-tuple-element.46.hi), channel_id=1, source_target_pairs={{0,8},{4,12},{8,16},{12,20},{16,24},{20,28},{24,0},{28,4},{1,9},{5... | collective-permute-start | bytes 393224 | tf_op jit(solution)/shard_map/ppermute | solution.py:310
  21.0 2.5 %collective-permute-start.8 = (f32[1,16,32,128]{3,2,1,0:T(8,128)S(1)}, f32[1,16,32,128]{3,2,1,0:T(8,128)S(1)}, u32[]{:S(2)}, u32[]{:S(2)}) collective-permute-start(f32[1,16,32,128]{3,2,1,0:T(8,128)S(1)} %get-tuple-element.45.lo), channel_id=1, source_target_pairs={{0,24},{4,28},{8,0},{12,4},{16,8},{20,12},{24,16},{28,20},{1,25},{... | collective-permute-start | bytes 786440 | tf_op jit(solution)/shard_map/ppermute | solution.py:311
  24.7 4.3 %collective-permute-start.7 = (f32[1,12,32,128]{3,2,1,0:T(8,128)S(1)}, f32[1,12,32,128]{3,2,1,0:T(8,128)S(1)}, u32[]{:S(2)}, u32[]{:S(2)}) collective-permute-start(f32[1,12,32,128]{3,2,1,0:T(8,128)S(1)} %get-tuple-element.43.lo), channel_id=1, source_target_pairs={{0,24},{4,28},{8,0},{12,4},{16,8},{20,12},{24,16},{28,20},{1,25},{... | collective-permute-start | bytes 589832 | tf_op jit(solution)/shard_map/ppermute | solution.py:311
  29.1 3.1 %collective-permute-done.8.rhi.v_above = f32[1,16,32,128]{3,2,1,0:T(8,128)S(1)} collective-permute-done((f32[1,16,32,128]{3,2,1,0:T(8,128)S(1)}, f32[1,16,32,128]{3,2,1,0:T(8,128)S(1)}, u32[]{:S(2)}, u32[]{:S(2)}) %collective-permute-start.8) | collective-permute-done | bytes 262176 | tf_op jit(solution)/shard_map/ppermute | solution.py:311
  32.2 1.4 %filter_3_4_hamiltonian.2 = (f32[2,8,32,128]{3,2,1,0:T(8,128)S(1)}, f32[6,2,2,32,128]{4,3,2,1,0:T(8,128)S(1)}, f32[2,2,32,128]{3,2,1,0:T(8,128)S(1)}, f32[2,2,32,128]{3,2,1,0:T(8,128)S(1)}) custom-call(bf16[128,384]{1,0:T(8,128)(2,1)S(1)} %get-tuple-element.39.ymat, bf16[384,128]{1,0:T(8,128)(2,1)S(1)} %get-tuple-element.40.zmat, ...), custom_call_target="tpu_custom_call" | custom-call | flops 1500000000 | bytes 5250000 | tf_op jit(solution)/shard_map/filter_3_4_hamiltonian/pallas_call | solution.py:246
  33.6 3.2 %collective-permute-start.10 = (f32[2,2,32,128]{3,2,1,0:T(8,128)S(1)}, f32[2,2,32,128]{3,2,1,0:T(8,128)S(1)}, u32[]{:S(2)}, u32[]{:S(2)}) collective-permute-start(f32[2,2,32,128]{3,2,1,0:T(8,128)S(1)} %get-tuple-element.56), channel_id=1, source_target_pairs={{0,6},{1,7},{2,4},{3,5},{4,2},{5,3},{6,0},{7,1},{8,14},{9,15},{10,... | collective-permute-start | bytes 196616 | tf_op jit(solution)/shard_map/ppermute | solution.py:320
  36.7 1.9 %collective-permute-done.6.rlo = f32[1,8,32,128]{3,2,1,0:T(8,128)S(1)} collective-permute-done((f32[1,8,32,128]{3,2,1,0:T(8,128)S(1)}, f32[1,8,32,128]{3,2,1,0:T(8,128)S(1)}, u32[]{:S(2)}, u32[]{:S(2)}) %collective-permute-start.6) | collective-permute-done | bytes 131104 | tf_op jit(solution)/shard_map/ppermute | solution.py:310
  38.7 1.4 %filter_3_4_hamiltonian.3 = (f32[2,8,32,128]{3,2,1,0:T(8,128)S(1)}, f32[2,8,32,128]{3,2,1,0:T(8,128)S(1)}, f32[2,2,32,128]{3,2,1,0:T(8,128)S(1)}, f32[2,2,32,128...) custom-call(bf16[128,384]{1,0:T(8,128)(2,1)S(1)} %get-tuple-element., ...), custom_call_target="tpu_custom_call" | custom-call | flops 1500000000 | bytes 5250000 | tf_op jit(solution)/shard_map/filter_3_4_hamiltonian/pallas_call | solution.py:246
  40.0 2.3 %collective-permute-start.12 = (f32[2,2,32,128]{3,2,1,0:T(8,128)S(1)}, f32[2,2,32,128]{3,2,1,0:T(8,128)S(1)}, u32[]{:S(2)}, u32[]{:S(2)}) collective-permute-start(f32[2,2,32,128]{3,2,1,0:T(8,128)S(1)} %get-tuple-element.60), channel_id=1, source_target_pairs={{0,6},{1,7},{2,4},{3,5},{4,2},{5,3},{6,0},{7,1},{8,14},{9,15},{10,... | collective-permute-start | bytes 196616 | tf_op jit(solution)/shard_map/ppermute | solution.py:320
  43.6 2.7 %collective-permute-start.16 = (f32[2,2,2,32,128]{4,3,2,1,0:T(8,128)S(1)}, f32[2,2,2,32,128]{4,3,2,1,0:T(8,128)S(1)}, u32[]{:S(2)}, u32[]{:S(2)}) collective-permute-start(f32[2,2,2,32,128]{4,3,2,1,0:T(8,128)S(1)} %get-tuple-element.64), channel_id=1, source_target_pairs={{0,5},{1,4},{2,7},{3,6},{4,1},{5,0},{6,3},{7,2},{8,13},{9,12},{10,... | collective-permute-start | bytes 393224 | tf_op jit(solution)/shard_map/ppermute | solution.py:320
  46.9 1.8 %collective-permute-done.14.refs_4_ = f32[2,2,2,32,128]{4,3,2,1,0:T(8,128)S(1)} collective-permute-done((f32[2,2,2,32,128]{4,3,2,1,0:T(8,128)S(1)}, f32[2,2,2,32,128]{4,3,2,1,0:T(8,128)S(1)}, u32[]{:S(2)}, u32[]{:S(2)}) %collective-permute-start.14) | collective-permute-done | bytes 131104 | tf_op jit(solution)/shard_map/ppermute | solution.py:320
  48.8 1.6 %collective-permute-done.15.refs_5_ = f32[2,2,2,32,128]{4,3,2,1,0:T(8,128)S(1)} collective-permute-done((f32[2,2,2,32,128]{4,3,2,1,0:T(8,128)S(1)}, f32[2,2,2,32,128]{4,3,2,1,0:T(8,128)S(1)}, u32[]{:S(2)}, u32[]{:S(2)}) %collective-permute-start.15) | collective-permute-done | bytes 131104 | tf_op jit(solution)/shard_map/ppermute | solution.py:320
  50.4 1.5 %collective-permute-done.16.refs_6_ = f32[2,2,2,32,128]{4,3,2,1,0:T(8,128)S(1)} collective-permute-done((f32[2,2,2,32,128]{4,3,2,1,0:T(8,128)S(1)}, f32[2,2,2,32,128]{4,3,2,1,0:T(8,128)S(1)}, u32[]{:S(2)}, u32[]{:S(2)}) %collective-permute-start.16) | collective-permute-done | bytes 131104 | tf_op jit(solution)/shard_map/ppermute | solution.py:320
  52.9 2.0 %gram.1 = f32[32,1,128]{2,1,0:T(1,128)} custom-call(f32[2,2,32,128]{3,2,1,0:T(8,128)S(1)} %collective-permute-done.10.refs_0_, f32[2,2,32,128]{3,2,1,0:T(8,128)S(1)} %collective-permute-done.11.refs_1_, f32[2,2,32,128]{3,2,1,0:T(8,128)S(1)} %collective-permute-done.12.refs_2_, f32[2,2,32,128]{3,2,1,0:T(8,128)S(1)} %collective-permute-done.13.refs_3_, ...), custom_call_target="tpu_custom_call" | custom-call | flops 1300000000 | bytes 4550000 | tf_op jit(solution)/shard_map/gram/pallas_call | solution.py:246
  54.9 1.0 %collective-permute-start.19 = (f32[2,8,32,128]{3,2,1,0:T(8,128)S(1)}, f32[2,8,32,128]{3,2,1,0:T(8,128)S(1)}, u32[]{:S(2)}, u32[]{:S(2)}) collective-permute-start(f32[2,8,32,128]{3,2,1,0:T(8,128)S(1)} %get-tuple-element.70), channel_id=1, source_target_pairs={{0,4},{4,0},{8,12},{12,8},{16,20},{20,16},{24,28},{28,24},{1,5},{5... | collective-permute-start | bytes 786440 | tf_op jit(solution)/shard_map/ppermute | solution.py:344
  55.9 6.8 %all-to-all-start = ((f32[32,1,128]{2,1,0:T(1,128)}), f32[32,1,128]{2,1,0:T(1,128)S(1)}, u32[]{:S(2)}, u32[]{:S(2)}) async-start(f32[32,1,128]{2,1,0:T(1,128)} %gram.1), calls=%async_computation | async-start | bytes 32768 | tf_op jit(solution)/shard_map/all_to_all | solution.py:345
  62.7 1.0 %collective-permute-done.19 = f32[2,8,32,128]{3,2,1,0:T(8,128)S(1)} collective-permute-done((f32[2,8,32,128]{3,2,1,0:T(8,128)S(1)}, f32[2,8,32,128]{3,2,1,0:T(8,128)S(1)}, u32[]{:S(2)}, u32[]{:S(2)}) %collective-permute-start.19) | collective-permute-done | bytes 262176 | tf_op jit(solution)/shard_map/ppermute | solution.py:344
  64.5 5.3 %all-to-all-done.x_ref = f32[32,1,128]{2,1,0:T(1,128)S(1)} async-done(((f32[32,1,128]{2,1,0:T(1,128)}), f32[32,1,128]{2,1,0:T(1,128)S(1)}, u32[]{:S(2)}, u32[]{:S(2)}) %all-to-all-start) | async-done | bytes 16416 | tf_op jit(solution)/shard_map/all_to_all | solution.py:345
  (32 shorter events, 9.0 us)
Async XLA Ops:
  0.6 1.2 %copy-start = (f32[8,32,128]{2,1,0:T(8,128)S(1)}, f32[8,32,128]{2,1,0:T(8,128)}, u32[]{:S(2)}) copy-start(f32[8,32,128]{2,1,0:T(8,128)} %refs_0_.1) | copy-start | bytes 393220
  1.9 16.6 %collective-permute-start.3 = (f32[1,16,32,128]{3,2,1,0:T(8,128)S(1)}, f32[1,16,32,128]{3,2,1,0:T(8,128)S(1)}, u32[]{:S(2)}, u32[]{:S(2)}) collective-permute-start(f32[1,16,32,128]{3,2,1,0:T(8,128)S(1)} %pad_maximum_fusion), channel_id=1, source_target_pairs={{0,4},{4,0},{8,12},{12,8},{16,20},{20,16},{24,28},{28,24},{1,5},{5... | collective-permute-start | bytes 786440 | tf_op jit(solution)/shard_map/ppermute | solution.py:290
  4.9 10.6 %collective-permute-start.4 = (f32[1,12,32,128]{3,2,1,0:T(8,128)S(1)}, f32[1,12,32,128]{3,2,1,0:T(8,128)S(1)}, u32[]{:S(2)}, u32[]{:S(2)}) collective-permute-start(f32[1,12,32,128]{3,2,1,0:T(8,128)S(1)} %get-tuple-element.79), channel_id=1, source_target_pairs={{0,28},{4,8},{8,4},{12,16},{16,12},{20,24},{24,20},{28,0},{1,29},{... | collective-permute-start | bytes 589832 | tf_op jit(solution)/shard_map/ppermute | solution.py:291
  8.6 9.6 %collective-permute-start.5 = (f32[1,12,32,128]{3,2,1,0:T(8,128)S(1)}, f32[1,12,32,128]{3,2,1,0:T(8,128)S(1)}, u32[]{:S(2)}, u32[]{:S(2)}) collective-permute-start(f32[1,12,32,128]{3,2,1,0:T(8,128)S(1)} %get-tuple-element.80.mine), channel_id=1, source_target_pairs={{0,24},{4,12},{8,0},{12,20},{16,8},{20,28},{24,16},{28,4},{1,25},{... | collective-permute-start | bytes 589832 | tf_op jit(solution)/shard_map/ppermute | solution.py:292
  9.0 14.6 %collective-permute-start.1 = (f32[1,8,32,128]{3,2,1,0:T(8,128)S(1)}, f32[1,8,32,128]{3,2,1,0:T(8,128)S(1)}, u32[]{:S(2)}, u32[]{:S(2)}) collective-permute-start(f32[1,8,32,128]{3,2,1,0:T(8,128)S(1)} %get-tuple-element.76), channel_id=1, source_target_pairs={{0,28},{4,8},{8,4},{12,16},{16,12},{20,24},{24,20},{28,0},{1,29},{... | collective-permute-start | bytes 393224 | tf_op jit(solution)/shard_map/ppermute | solution.py:291
  11.3 12.3 %collective-permute-start = (f32[1,8,32,128]{3,2,1,0:T(8,128)S(1)}, f32[1,8,32,128]{3,2,1,0:T(8,128)S(1)}, u32[]{:S(2)}, u32[]{:S(2)}) collective-permute-start(f32[1,8,32,128]{3,2,1,0:T(8,128)S(1)} %get-tuple-element.76), channel_id=1, source_target_pairs={{0,4},{4,0},{8,12},{12,8},{16,20},{20,16},{24,28},{28,24},{1,5},{5... | collective-permute-start | bytes 393224 | tf_op jit(solution)/shard_map/ppermute | solution.py:290
  15.6 8.2 %collective-permute-start.2 = (f32[1,8,32,128]{3,2,1,0:T(8,128)S(1)}, f32[1,8,32,128]{3,2,1,0:T(8,128)S(1)}, u32[]{:S(2)}, u32[]{:S(2)}) collective-permute-start(f32[1,8,32,128]{3,2,1,0:T(8,128)S(1)} %get-tuple-element.77.mine), channel_id=1, source_target_pairs={{0,24},{4,12},{8,0},{12,20},{16,8},{20,28},{24,16},{28,4},{1,25},{... | collective-permute-start | bytes 393224 | tf_op jit(solution)/shard_map/ppermute | solution.py:292
  19.5 9.6 %collective-permute-start.9 = (f32[1,8,32,128]{3,2,1,0:T(8,128)S(1)}, f32[1,8,32,128]{3,2,1,0:T(8,128)S(1)}, u32[]{:S(2)}, u32[]{:S(2)}) collective-permute-start(f32[1,8,32,128]{3,2,1,0:T(8,128)S(1)} %get-tuple-element.46.hi), channel_id=1, source_target_pairs={{0,8},{4,12},{8,16},{12,20},{16,24},{20,28},{24,0},{28,4},{1,9},{5... | collective-permute-start | bytes 393224 | tf_op jit(solution)/shard_map/ppermute | solution.py:310
  21.0 11.2 %collective-permute-start.8 = (f32[1,16,32,128]{3,2,1,0:T(8,128)S(1)}, f32[1,16,32,128]{3,2,1,0:T(8,128)S(1)}, u32[]{:S(2)}, u32[]{:S(2)}) collective-permute-start(f32[1,16,32,128]{3,2,1,0:T(8,128)S(1)} %get-tuple-element.45.lo), channel_id=1, source_target_pairs={{0,24},{4,28},{8,0},{12,4},{16,8},{20,12},{24,16},{28,20},{1,25},{... | collective-permute-start | bytes 786440 | tf_op jit(solution)/shard_map/ppermute | solution.py:311
  24.7 13.9 %collective-permute-start.7 = (f32[1,12,32,128]{3,2,1,0:T(8,128)S(1)}, f32[1,12,32,128]{3,2,1,0:T(8,128)S(1)}, u32[]{:S(2)}, u32[]{:S(2)}) collective-permute-start(f32[1,12,32,128]{3,2,1,0:T(8,128)S(1)} %get-tuple-element.43.lo), channel_id=1, source_target_pairs={{0,24},{4,28},{8,0},{12,4},{16,8},{20,12},{24,16},{28,20},{1,25},{... | collective-permute-start | bytes 589832 | tf_op jit(solution)/shard_map/ppermute | solution.py:311
  29.1 9.6 %collective-permute-start.6 = (f32[1,8,32,128]{3,2,1,0:T(8,128)S(1)}, f32[1,8,32,128]{3,2,1,0:T(8,128)S(1)}, u32[]{:S(2)}, u32[]{:S(2)}) collective-permute-start(f32[1,8,32,128]{3,2,1,0:T(8,128)S(1)} %get-tuple-element.42.hi), channel_id=1, source_target_pairs={{0,8},{4,12},{8,16},{12,20},{16,24},{20,28},{24,0},{28,4},{1,9},{5... | collective-permute-start | bytes 393224 | tf_op jit(solution)/shard_map/ppermute | solution.py:310
  33.6 9.5 %collective-permute-start.10 = (f32[2,2,32,128]{3,2,1,0:T(8,128)S(1)}, f32[2,2,32,128]{3,2,1,0:T(8,128)S(1)}, u32[]{:S(2)}, u32[]{:S(2)}) collective-permute-start(f32[2,2,32,128]{3,2,1,0:T(8,128)S(1)} %get-tuple-element.56), channel_id=1, source_target_pairs={{0,6},{1,7},{2,4},{3,5},{4,2},{5,3},{6,0},{7,1},{8,14},{9,15},{10,... | collective-permute-start | bytes 196616 | tf_op jit(solution)/shard_map/ppermute | solution.py:320
  36.7 6.3 %collective-permute-start.11 = (f32[2,2,32,128]{3,2,1,0:T(8,128)S(1)}, f32[2,2,32,128]{3,2,1,0:T(8,128)S(1)}, u32[]{:S(2)}, u32[]{:S(2)}) collective-permute-start(f32[2,2,32,128]{3,2,1,0:T(8,128)S(1)} %get-tuple-element.57), channel_id=1, source_target_pairs={{0,4},{1,5},{2,6},{3,7},{4,0},{5,1},{6,2},{7,3},{8,12},{9,13},{10,... | collective-permute-start | bytes 196616 | tf_op jit(solution)/shard_map/ppermute | solution.py:320
  40.0 6.2 %collective-permute-start.12 = (f32[2,2,32,128]{3,2,1,0:T(8,128)S(1)}, f32[2,2,32,128]{3,2,1,0:T(8,128)S(1)}, u32[]{:S(2)}, u32[]{:S(2)}) collective-permute-start(f32[2,2,32,128]{3,2,1,0:T(8,128)S(1)} %get-tuple-element.60), channel_id=1, source_target_pairs={{0,6},{1,7},{2,4},{3,5},{4,2},{5,3},{6,0},{7,1},{8,14},{9,15},{10,... | collective-permute-start | bytes 196616 | tf_op jit(solution)/shard_map/ppermute | solution.py:320
  42.4 4.3 %collective-permute-start.13 = (f32[2,2,32,128]{3,2,1,0:T(8,128)S(1)}, f32[2,2,32,128]{3,2,1,0:T(8,128)S(1)}, u32[]{:S(2)}, u32[]{:S(2)}) collective-permute-start(f32[2,2,32,128]{3,2,1,0:T(8,128)S(1)} %get-tuple-element.61), channel_id=1, source_target_pairs={{0,4},{1,5},{2,6},{3,7},{4,0},{5,1},{6,2},{7,3},{8,12},{9,13},{10,... | collective-permute-start | bytes 196616 | tf_op jit(solution)/shard_map/ppermute | solution.py:320
  43.1 5.7 %collective-permute-start.14 = (f32[2,2,2,32,128]{4,3,2,1,0:T(8,128)S(1)}, f32[2,2,2,32,128]{4,3,2,1,0:T(8,128)S(1)}, u32[]{:S(2)}, u32[]{:S(2)}) collective-permute-start(f32[2,2,2,32,128]{4,3,2,1,0:T(8,128)S(1)} %get-tuple-element.62), channel_id=1, source_target_pairs={{0,2},{1,3},{2,0},{3,1},{4,6},{5,7},{6,4},{7,5},{8,10},{9,11},{10,... | collective-permute-start | bytes 393224 | tf_op jit(solution)/shard_map/ppermute | solution.py:320
  43.6 6.8 %collective-permute-start.15 = (f32[2,2,2,32,128]{4,3,2,1,0:T(8,128)S(1)}, f32[2,2,2,32,128]{4,3,2,1,0:T(8,128)S(1)}, u32[]{:S(2)}, u32[]{:S(2)}) collective-permute-start(f32[2,2,2,32,128]{4,3,2,1,0:T(8,128)S(1)} %get-tuple-element.63), channel_id=1, source_target_pairs={{0,7},{1,6},{2,5},{3,4},{4,3},{5,2},{6,1},{7,0},{8,15},{9,14},{10,... | collective-permute-start | bytes 393224 | tf_op jit(solution)/shard_map/ppermute | solution.py:320
  43.6 8.3 %collective-permute-start.16 = (f32[2,2,2,32,128]{4,3,2,1,0:T(8,128)S(1)}, f32[2,2,2,32,128]{4,3,2,1,0:T(8,128)S(1)}, u32[]{:S(2)}, u32[]{:S(2)}) collective-permute-start(f32[2,2,2,32,128]{4,3,2,1,0:T(8,128)S(1)} %get-tuple-element.64), channel_id=1, source_target_pairs={{0,5},{1,4},{2,7},{3,6},{4,1},{5,0},{6,3},{7,2},{8,13},{9,12},{10,... | collective-permute-start | bytes 393224 | tf_op jit(solution)/shard_map/ppermute | solution.py:320
  46.3 6.6 %collective-permute-start.17 = (f32[2,2,2,32,128]{4,3,2,1,0:T(8,128)S(1)}, f32[2,2,2,32,128]{4,3,2,1,0:T(8,128)S(1)}, u32[]{:S(2)}, u32[]{:S(2)}) collective-permute-start(f32[2,2,2,32,128]{4,3,2,1,0:T(8,128)S(1)} %get-tuple-element.65), channel_id=1, source_target_pairs={{0,3},{1,2},{2,1},{3,0},{4,7},{5,6},{6,5},{7,4},{8,11},{9,10},{10,... | collective-permute-start | bytes 393224 | tf_op jit(solution)/shard_map/ppermute | solution.py:320
  46.6 6.3 %collective-permute-start.18 = (f32[2,2,2,32,128]{4,3,2,1,0:T(8,128)S(1)}, f32[2,2,2,32,128]{4,3,2,1,0:T(8,128)S(1)}, u32[]{:S(2)}, u32[]{:S(2)}) collective-permute-start(f32[2,2,2,32,128]{4,3,2,1,0:T(8,128)S(1)} %get-tuple-element.66), channel_id=1, source_target_pairs={{0,1},{1,0},{2,3},{3,2},{4,5},{5,4},{6,7},{7,6},{8,9},{9,8},{10,11... | collective-permute-start | bytes 393224 | tf_op jit(solution)/shard_map/ppermute | solution.py:320
  54.9 8.8 %collective-permute-start.19 = (f32[2,8,32,128]{3,2,1,0:T(8,128)S(1)}, f32[2,8,32,128]{3,2,1,0:T(8,128)S(1)}, u32[]{:S(2)}, u32[]{:S(2)}) collective-permute-start(f32[2,8,32,128]{3,2,1,0:T(8,128)S(1)} %get-tuple-element.70), channel_id=1, source_target_pairs={{0,4},{4,0},{8,12},{12,8},{16,20},{20,16},{24,28},{28,24},{1,5},{5... | collective-permute-start | bytes 786440 | tf_op jit(solution)/shard_map/ppermute | solution.py:344
  55.9 13.9 %all-to-all-start = ((f32[32,1,128]{2,1,0:T(1,128)}), f32[32,1,128]{2,1,0:T(1,128)S(1)}, u32[]{:S(2)}, u32[]{:S(2)}) async-start(f32[32,1,128]{2,1,0:T(1,128)} %gram.1), calls=%async_computation | async-start | bytes 32768 | tf_op jit(solution)/shard_map/all_to_all | solution.py:345

commit v8 on v5

--- a/solution.py
+++ b/solution.py
@@ -324,7 +324,6 @@
         1.3,
         "gram",
     )
-    send, sums = lax.optimization_barrier((send, sums))
     back = lax.ppermute(send, grid_axes, swap)
     sums = lax.all_to_all(sums, ("pair", "mem", "orb"), 0, 0, tiled=True)
     filtered = jnp.where(m == 0, jnp.concatenate([keep, back]), jnp.concatenate([back, keep]))

time: 68.9 us -> 72.9 us (1.058)
  waiting for transfers between devices: 25.5 us -> 28.9 us
    ppermute x7, waiting for transfers between devices: 6.42 us -> 9.76 us  [peer(): lax.ppermute(x, ('mem', 'orb'), [(t, t ^ k) for t in range(group)])]
    ppermute x1, waiting for transfers between devices: 2.8 us -> 0.01 us  [per_device(): back = lax.ppermute(send, grid_axes, swap)]
    all_to_all x1, waiting for transfers between devices: 3.51 us -> 6.29 us  [per_device(): sums = lax.all_to_all(sums, ('pair', 'mem', 'orb'), 0, 0, tiled=True)]
  transfers between devices with their start and end apart: 19 -> 19, of which waited for: 13 -> 11; matrix products, arithmetic and copies ran while one was open for 1% -> 1% of each run, Pallas kernels for 5% -> 8%
where the time goes in v8:
time: 72.9 us; the launch traced here: 72.7 us
  starting transfers between devices  33.4 us (46%)
  waiting for transfers between devices  28.9 us (40%)
  Pallas kernels  7.6 us (10%)
  local copies, waits for them, and re-layouts  1.18 us (2%)
  other arithmetic  0.9 us (1%)
  between operations  0.74 us (1%)
    ppermute x7, waiting for transfers between devices, peer(): lax.ppermute(x, ('mem', 'orb'), [(t, t ^ k) for t in range(group)])  9.76 us
    pallas_call x7, Pallas kernels, call(): pl.pallas_call(body, out_shape=[s if isinstance(s, jax.ShapeDtypeStruct)...  7.6 us
    ppermute x2, starting transfers between devices, per_device(): rhi = lax.ppermute(lo, grid_axes, down)  6.88 us
    ppermute x7, starting transfers between devices, peer(): lax.ppermute(x, ('mem', 'orb'), [(t, t ^ k) for t in range(group)])  6.48 us
    all_to_all x1, waiting for transfers between devices, per_device(): sums = lax.all_to_all(sums, ('pair', 'mem', 'orb'), 0, 0, tiled=True)  6.29 us
    ppermute x2, starting transfers between devices, per_device(): rb = lax.ppermute(b, grid_axes, cross)  5.91 us
    all_to_all x1, starting transfers between devices, per_device(): sums = lax.all_to_all(sums, ('pair', 'mem', 'orb'), 0, 0, tiled=True)  5.31 us
    ppermute x2, waiting for transfers between devices, per_device(): rlo = lax.ppermute(hi, grid_axes, up)  5.08 us
  transfers between devices with their start and end apart: 19, of which 11 were waited for; matrix products, arithmetic and copies ran while one was open for 1% of the time, Pallas kernels for 8%

profile of v8, /device:TPU:0, one launch (start us, length us, event | category | flops | bytes accessed | tf_op | source)
XLA Modules:
  0.0 72.7 jit_solution(13179735394535991279)
XLA Ops:
  0.6 1.2 %constant_dynamic-slice_fusion = (f32[1,8,32,128]{3,2,1,0:T(8,128)S(1)}, f32[1,8,32,128]{3,2,1,0:T(8,128)S(1)}, f32[1,8,32,128]{3,2,1,0:T(8,128)S(1)}, f32[1,8,32,128]{3,2,1,0:T(8,128)S(1)}) fusion(f32[4,8,32,128]{3,2,1,0:T(8,128)} %param.2, s32[]{:T(128)S(6)} %select_n.33, s32[]{:T(128)S(6)} %select_n.29, s32[]{:T(128)S(6)} %select_n.28, s32[]{:T(128)S(6)} %select_n.30), kind=kLoop, calls=%fused_computation.5 | loop fusion | bytes 1048592 | tf_op jit(solution)/shard_map/dynamic_slice | solution.py:278
  1.9 3.0 %collective-permute-start.3 = (f32[1,16,32,128]{3,2,1,0:T(8,128)S(1)}, f32[1,16,32,128]{3,2,1,0:T(8,128)S(1)}, u32[]{:S(2)}, u32[]{:S(2)}) collective-permute-start(f32[1,16,32,128]{3,2,1,0:T(8,128)S(1)} %pad_maximum_fusion), channel_id=1, source_target_pairs={{0,4},{4,0},{8,12},{12,8},{16,20},{20,16},{24,28},{28,24},{1,5},{5... | collective-permute-start | bytes 786440 | tf_op jit(solution)/shard_map/ppermute | solution.py:282
  4.9 3.6 %collective-permute-start.4 = (f32[1,12,32,128]{3,2,1,0:T(8,128)S(1)}, f32[1,12,32,128]{3,2,1,0:T(8,128)S(1)}, u32[]{:S(2)}, u32[]{:S(2)}) collective-permute-start(f32[1,12,32,128]{3,2,1,0:T(8,128)S(1)} %get-tuple-element.57), channel_id=1, source_target_pairs={{0,28},{4,8},{8,4},{12,16},{16,12},{20,24},{24,20},{28,0},{1,29},{... | collective-permute-start | bytes 589832 | tf_op jit(solution)/shard_map/ppermute | solution.py:283
  9.0 2.3 %collective-permute-start.1 = (f32[1,8,32,128]{3,2,1,0:T(8,128)S(1)}, f32[1,8,32,128]{3,2,1,0:T(8,128)S(1)}, u32[]{:S(2)}, u32[]{:S(2)}) collective-permute-start(f32[1,8,32,128]{3,2,1,0:T(8,128)S(1)} %get-tuple-element.54), channel_id=1, source_target_pairs={{0,28},{4,8},{8,4},{12,16},{16,12},{20,24},{24,20},{28,0},{1,29},{... | collective-permute-start | bytes 393224 | tf_op jit(solution)/shard_map/ppermute | solution.py:283
  12.0 3.5 %collective-permute-done.4.rb = f32[1,12,32,128]{3,2,1,0:T(8,128)S(1)} collective-permute-done((f32[1,12,32,128]{3,2,1,0:T(8,128)S(1)}, f32[1,12,32,128]{3,2,1,0:T(8,128)S(1)}, u32[]{:S(2)}, u32[]{:S(2)}) %collective-permute-start.4) | collective-permute-done | bytes 196640 | tf_op jit(solution)/shard_map/ppermute | solution.py:283
  15.6 1.8 %collective-permute-start.2 = (f32[1,8,32,128]{3,2,1,0:T(8,128)S(1)}, f32[1,8,32,128]{3,2,1,0:T(8,128)S(1)}, u32[]{:S(2)}, u32[]{:S(2)}) collective-permute-start(f32[1,8,32,128]{3,2,1,0:T(8,128)S(1)} %get-tuple-element.55.mine), channel_id=1, source_target_pairs={{0,24},{4,12},{8,0},{12,20},{16,8},{20,28},{24,16},{28,4},{1,25},{... | collective-permute-start | bytes 393224 | tf_op jit(solution)/shard_map/ppermute | solution.py:284
  18.5 1.0 %filter_1_2.2 = (f32[1,16,32,128]{3,2,1,0:T(8,128)S(1)}, f32[1,8,32,128]{3,2,1,0:T(8,128)S(1)}, f32[1,20,32,128]{3,2,1,0:T(8,128)S(1)}, f32[24,32,128]{2,1,0:T(8,128)S(1)}) custom-call(bf16[128,384]{1,0:T(8,128)(2,1)S(1)} %get-tuple-element.28.ymat, bf16[384,128]{1,0:T(8,128)(2,1)S(1)} %get-tuple-element.29.zmat, ...), custom_call_target="tpu_custom_call" | custom-call | flops 1000000000 | bytes 3500000 | tf_op jit(solution)/shard_map/filter_1_2/pallas_call | solution.py:238
  19.5 1.6 %collective-permute-start.9 = (f32[1,8,32,128]{3,2,1,0:T(8,128)S(1)}, f32[1,8,32,128]{3,2,1,0:T(8,128)S(1)}, u32[]{:S(2)}, u32[]{:S(2)}) collective-permute-start(f32[1,8,32,128]{3,2,1,0:T(8,128)S(1)} %get-tuple-element.35.hi), channel_id=1, source_target_pairs={{0,8},{4,12},{8,16},{12,20},{16,24},{20,28},{24,0},{28,4},{1,9},{5... | collective-permute-start | bytes 393224 | tf_op jit(solution)/shard_map/ppermute | solution.py:302
  21.0 2.5 %collective-permute-start.8 = (f32[1,16,32,128]{3,2,1,0:T(8,128)S(1)}, f32[1,16,32,128]{3,2,1,0:T(8,128)S(1)}, u32[]{:S(2)}, u32[]{:S(2)}) collective-permute-start(f32[1,16,32,128]{3,2,1,0:T(8,128)S(1)} %get-tuple-element.34.lo), channel_id=1, source_target_pairs={{0,24},{4,28},{8,0},{12,4},{16,8},{20,12},{24,16},{28,20},{1,25},{... | collective-permute-start | bytes 786440 | tf_op jit(solution)/shard_map/ppermute | solution.py:303
  24.7 4.3 %collective-permute-start.7 = (f32[1,12,32,128]{3,2,1,0:T(8,128)S(1)}, f32[1,12,32,128]{3,2,1,0:T(8,128)S(1)}, u32[]{:S(2)}, u32[]{:S(2)}) collective-permute-start(f32[1,12,32,128]{3,2,1,0:T(8,128)S(1)} %get-tuple-element.32.lo), channel_id=1, source_target_pairs={{0,24},{4,28},{8,0},{12,4},{16,8},{20,12},{24,16},{28,20},{1,25},{... | collective-permute-start | bytes 589832 | tf_op jit(solution)/shard_map/ppermute | solution.py:303
  29.1 3.1 %collective-permute-done.8.rhi.v_above = f32[1,16,32,128]{3,2,1,0:T(8,128)S(1)} collective-permute-done((f32[1,16,32,128]{3,2,1,0:T(8,128)S(1)}, f32[1,16,32,128]{3,2,1,0:T(8,128)S(1)}, u32[]{:S(2)}, u32[]{:S(2)}) %collective-permute-start.8) | collective-permute-done | bytes 262176 | tf_op jit(solution)/shard_map/ppermute | solution.py:303
  32.2 1.4 %filter_3_4_hamiltonian.2 = (f32[2,8,32,128]{3,2,1,0:T(8,128)S(1)}, f32[8,2,2,32,128]{4,3,2,1,0:T(8,128)S(1)}) custom-call(bf16[128,384]{1,0:T(8,128)(2,1)S(1)} %get-tuple-element.28.ymat, bf16[384,128]{1,0:T(8,128)(2,1)S(1)} %get-tuple-element.29.zmat, f32[1,8,32,128]{3,2,1,0:T(8,128)S(1)} %collective-permute-done.9.rlo, ...), custom_call_target="tpu_custom_call" | custom-call | flops 1500000000 | bytes 5250000 | tf_op jit(solution)/shard_map/filter_3_4_hamiltonian/pallas_call | solution.py:238
  33.6 5.1 %collective-permute-done.6.rlo = f32[1,8,32,128]{3,2,1,0:T(8,128)S(1)} collective-permute-done((f32[1,8,32,128]{3,2,1,0:T(8,128)S(1)}, f32[1,8,32,128]{3,2,1,0:T(8,128)S(1)}, u32[]{:S(2)}, u32[]{:S(2)}) %collective-permute-start.6) | collective-permute-done | bytes 131104 | tf_op jit(solution)/shard_map/ppermute | solution.py:302
  38.7 1.4 %filter_3_4_hamiltonian.3 = (f32[2,8,32,128]{3,2,1,0:T(8,128)S(1)}, f32[2,8,32,128]{3,2,1,0:T(8,128)S(1)}, f32[2,2,2,32,128]{4,3,2,1,0:T(8,128)S(1)}, f32[2,2,2,...) custom-call(bf16[128,384]{1,0:T(8,128)(2,1)S(1)} %get-tuple-element., ...), custom_call_target="tpu_custom_call" | custom-call | flops 1500000000 | bytes 5250000 | tf_op jit(solution)/shard_map/filter_3_4_hamiltonian/pallas_call | solution.py:238
  40.1 2.3 %collective-permute-start.10 = (f32[2,2,2,32,128]{4,3,2,1,0:T(8,128)S(1)}, f32[2,2,2,32,128]{4,3,2,1,0:T(8,128)S(1)}, u32[]{:S(2)}, u32[]{:S(2)}) collective-permute-start(f32[2,2,2,32,128]{4,3,2,1,0:T(8,128)S(1)} %get-tuple-element.39), channel_id=1, source_target_pairs={{0,6},{1,7},{2,4},{3,5},{4,2},{5,3},{6,0},{7,1},{8,14},{9,15},{10,... | collective-permute-start | bytes 393224 | tf_op jit(solution)/shard_map/ppermute | solution.py:312
  43.6 1.3 %collective-permute-start.17 = (f32[2,8,32,128]{3,2,1,0:T(8,128)S(1)}, f32[2,8,32,128]{3,2,1,0:T(8,128)S(1)}, u32[]{:S(2)}, u32[]{:S(2)}) collective-permute-start(f32[2,8,32,128]{3,2,1,0:T(8,128)S(1)} %get-tuple-element.48), channel_id=1, source_target_pairs={{0,4},{4,0},{8,12},{12,8},{16,20},{20,16},{24,28},{28,24},{1,5},{5... | collective-permute-start | bytes 786440 | tf_op jit(solution)/shard_map/ppermute | solution.py:327
  44.9 1.3 %collective-permute-done.10.refs_0_ = f32[2,2,2,32,128]{4,3,2,1,0:T(8,128)S(1)} collective-permute-done((f32[2,2,2,32,128]{4,3,2,1,0:T(8,128)S(1)}, f32[2,2,2,32,128]{4,3,2,1,0:T(8,128)S(1)}, u32[]{:S(2)}, u32[]{:S(2)}) %collective-permute-start.10) | collective-permute-done | bytes 131104 | tf_op jit(solution)/shard_map/ppermute | solution.py:312
  46.2 1.4 %collective-permute-start.14 = (f32[2,2,2,32,128]{4,3,2,1,0:T(8,128)S(1)}, f32[2,2,2,32,128]{4,3,2,1,0:T(8,128)S(1)}, u32[]{:S(2)}, u32[]{:S(2)}) collective-permute-start(f32[2,2,2,32,128]{4,3,2,1,0:T(8,128)S(1)} %get-tuple-element.43), channel_id=1, source_target_pairs={{0,5},{1,4},{2,7},{3,6},{4,1},{5,0},{6,3},{7,2},{8,13},{9,12},{10,... | collective-permute-start | bytes 393224 | tf_op jit(solution)/shard_map/ppermute | solution.py:312
  47.6 4.3 %collective-permute-done.11.refs_1_ = f32[2,2,2,32,128]{4,3,2,1,0:T(8,128)S(1)} collective-permute-done((f32[2,2,2,32,128]{4,3,2,1,0:T(8,128)S(1)}, f32[2,2,2,32,128]{4,3,2,1,0:T(8,128)S(1)}, u32[]{:S(2)}, u32[]{:S(2)}) %collective-permute-start.11) | collective-permute-done | bytes 131104 | tf_op jit(solution)/shard_map/ppermute | solution.py:312
  51.9 1.5 %collective-permute-start.16 = (f32[2,2,2,32,128]{4,3,2,1,0:T(8,128)S(1)}, f32[2,2,2,32,128]{4,3,2,1,0:T(8,128)S(1)}, u32[]{:S(2)}, u32[]{:S(2)}) collective-permute-start(f32[2,2,2,32,128]{4,3,2,1,0:T(8,128)S(1)} %get-tuple-element.45), channel_id=1, source_target_pairs={{0,1},{1,0},{2,3},{3,2},{4,5},{5,4},{6,7},{7,6},{8,9},{9,8},{10,11... | collective-permute-start | bytes 393224 | tf_op jit(solution)/shard_map/ppermute | solution.py:312
  53.4 3.3 %collective-permute-done.14.refs_4_ = f32[2,2,2,32,128]{4,3,2,1,0:T(8,128)S(1)} collective-permute-done((f32[2,2,2,32,128]{4,3,2,1,0:T(8,128)S(1)}, f32[2,2,2,32,128]{4,3,2,1,0:T(8,128)S(1)}, u32[]{:S(2)}, u32[]{:S(2)}) %collective-permute-start.14) | collective-permute-done | bytes 131104 | tf_op jit(solution)/shard_map/ppermute | solution.py:312
  57.6 2.0 %gram.1 = f32[32,1,128]{2,1,0:T(1,128)} custom-call(f32[2,2,2,32,128]{4,3,2,1,0:T(8,128)S(1)} %collective-permute-done.10.refs_0_, f32[2,2,2,32,128]{4,3,2,1,0:T(8,128)S(1)} %collective-permute-done.11.refs_1_, f32[2,2,2,32,128]{4,3,2,1,0:T(8,128)S(1)} %collective-permute-done.12.refs_2_, f32[2,2,2,32,128]{4,3,2,1,0:T(8,128)S(1)} %collective-permute-done.13.refs_3_, ...), custom_call_target="tpu_custom_call" | custom-call | flops 1300000000 | bytes 4550000 | tf_op jit(solution)/shard_map/gram/pallas_call | solution.py:238
  59.6 5.3 %all-to-all-start = ((f32[32,1,128]{2,1,0:T(1,128)}), f32[32,1,128]{2,1,0:T(1,128)S(1)}, u32[]{:S(2)}, u32[]{:S(2)}) async-start(f32[32,1,128]{2,1,0:T(1,128)} %gram.1), calls=%async_computation | async-start | bytes 32768 | tf_op jit(solution)/shard_map/all_to_all | solution.py:328
  65.8 6.3 %all-to-all-done.x_ref = f32[32,1,128]{2,1,0:T(1,128)S(1)} async-done(((f32[32,1,128]{2,1,0:T(1,128)}), f32[32,1,128]{2,1,0:T(1,128)S(1)}, u32[]{:S(2)}, u32[]{:S(2)}) %all-to-all-start) | async-done | bytes 16416 | tf_op jit(solution)/shard_map/all_to_all | solution.py:328
  (28 shorter events, 7.2 us)
Async XLA Ops:
  0.6 1.2 %copy-start = (f32[8,32,128]{2,1,0:T(8,128)S(1)}, f32[8,32,128]{2,1,0:T(8,128)}, u32[]{:S(2)}) copy-start(f32[8,32,128]{2,1,0:T(8,128)} %refs_0_.1) | copy-start | bytes 393220
  1.9 16.6 %collective-permute-start.3 = (f32[1,16,32,128]{3,2,1,0:T(8,128)S(1)}, f32[1,16,32,128]{3,2,1,0:T(8,128)S(1)}, u32[]{:S(2)}, u32[]{:S(2)}) collective-permute-start(f32[1,16,32,128]{3,2,1,0:T(8,128)S(1)} %pad_maximum_fusion), channel_id=1, source_target_pairs={{0,4},{4,0},{8,12},{12,8},{16,20},{20,16},{24,28},{28,24},{1,5},{5... | collective-permute-start | bytes 786440 | tf_op jit(solution)/shard_map/ppermute | solution.py:282
  4.9 10.6 %collective-permute-start.4 = (f32[1,12,32,128]{3,2,1,0:T(8,128)S(1)}, f32[1,12,32,128]{3,2,1,0:T(8,128)S(1)}, u32[]{:S(2)}, u32[]{:S(2)}) collective-permute-start(f32[1,12,32,128]{3,2,1,0:T(8,128)S(1)} %get-tuple-element.57), channel_id=1, source_target_pairs={{0,28},{4,8},{8,4},{12,16},{16,12},{20,24},{24,20},{28,0},{1,29},{... | collective-permute-start | bytes 589832 | tf_op jit(solution)/shard_map/ppermute | solution.py:283
  8.6 9.6 %collective-permute-start.5 = (f32[1,12,32,128]{3,2,1,0:T(8,128)S(1)}, f32[1,12,32,128]{3,2,1,0:T(8,128)S(1)}, u32[]{:S(2)}, u32[]{:S(2)}) collective-permute-start(f32[1,12,32,128]{3,2,1,0:T(8,128)S(1)} %get-tuple-element.58.mine), channel_id=1, source_target_pairs={{0,24},{4,12},{8,0},{12,20},{16,8},{20,28},{24,16},{28,4},{1,25},{... | collective-permute-start | bytes 589832 | tf_op jit(solution)/shard_map/ppermute | solution.py:284
  9.0 14.6 %collective-permute-start.1 = (f32[1,8,32,128]{3,2,1,0:T(8,128)S(1)}, f32[1,8,32,128]{3,2,1,0:T(8,128)S(1)}, u32[]{:S(2)}, u32[]{:S(2)}) collective-permute-start(f32[1,8,32,128]{3,2,1,0:T(8,128)S(1)} %get-tuple-element.54), channel_id=1, source_target_pairs={{0,28},{4,8},{8,4},{12,16},{16,12},{20,24},{24,20},{28,0},{1,29},{... | collective-permute-start | bytes 393224 | tf_op jit(solution)/shard_map/ppermute | solution.py:283
  11.3 12.3 %collective-permute-start = (f32[1,8,32,128]{3,2,1,0:T(8,128)S(1)}, f32[1,8,32,128]{3,2,1,0:T(8,128)S(1)}, u32[]{:S(2)}, u32[]{:S(2)}) collective-permute-start(f32[1,8,32,128]{3,2,1,0:T(8,128)S(1)} %get-tuple-element.54), channel_id=1, source_target_pairs={{0,4},{4,0},{8,12},{12,8},{16,20},{20,16},{24,28},{28,24},{1,5},{5... | collective-permute-start | bytes 393224 | tf_op jit(solution)/shard_map/ppermute | solution.py:282
  15.6 8.2 %collective-permute-start.2 = (f32[1,8,32,128]{3,2,1,0:T(8,128)S(1)}, f32[1,8,32,128]{3,2,1,0:T(8,128)S(1)}, u32[]{:S(2)}, u32[]{:S(2)}) collective-permute-start(f32[1,8,32,128]{3,2,1,0:T(8,128)S(1)} %get-tuple-element.55.mine), channel_id=1, source_target_pairs={{0,24},{4,12},{8,0},{12,20},{16,8},{20,28},{24,16},{28,4},{1,25},{... | collective-permute-start | bytes 393224 | tf_op jit(solution)/shard_map/ppermute | solution.py:284
  19.5 9.6 %collective-permute-start.9 = (f32[1,8,32,128]{3,2,1,0:T(8,128)S(1)}, f32[1,8,32,128]{3,2,1,0:T(8,128)S(1)}, u32[]{:S(2)}, u32[]{:S(2)}) collective-permute-start(f32[1,8,32,128]{3,2,1,0:T(8,128)S(1)} %get-tuple-element.35.hi), channel_id=1, source_target_pairs={{0,8},{4,12},{8,16},{12,20},{16,24},{20,28},{24,0},{28,4},{1,9},{5... | collective-permute-start | bytes 393224 | tf_op jit(solution)/shard_map/ppermute | solution.py:302
  21.0 11.2 %collective-permute-start.8 = (f32[1,16,32,128]{3,2,1,0:T(8,128)S(1)}, f32[1,16,32,128]{3,2,1,0:T(8,128)S(1)}, u32[]{:S(2)}, u32[]{:S(2)}) collective-permute-start(f32[1,16,32,128]{3,2,1,0:T(8,128)S(1)} %get-tuple-element.34.lo), channel_id=1, source_target_pairs={{0,24},{4,28},{8,0},{12,4},{16,8},{20,12},{24,16},{28,20},{1,25},{... | collective-permute-start | bytes 786440 | tf_op jit(solution)/shard_map/ppermute | solution.py:303
  24.7 13.9 %collective-permute-start.7 = (f32[1,12,32,128]{3,2,1,0:T(8,128)S(1)}, f32[1,12,32,128]{3,2,1,0:T(8,128)S(1)}, u32[]{:S(2)}, u32[]{:S(2)}) collective-permute-start(f32[1,12,32,128]{3,2,1,0:T(8,128)S(1)} %get-tuple-element.32.lo), channel_id=1, source_target_pairs={{0,24},{4,28},{8,0},{12,4},{16,8},{20,12},{24,16},{28,20},{1,25},{... | collective-permute-start | bytes 589832 | tf_op jit(solution)/shard_map/ppermute | solution.py:303
  29.1 9.6 %collective-permute-start.6 = (f32[1,8,32,128]{3,2,1,0:T(8,128)S(1)}, f32[1,8,32,128]{3,2,1,0:T(8,128)S(1)}, u32[]{:S(2)}, u32[]{:S(2)}) collective-permute-start(f32[1,8,32,128]{3,2,1,0:T(8,128)S(1)} %get-tuple-element.31.hi), channel_id=1, source_target_pairs={{0,8},{4,12},{8,16},{12,20},{16,24},{20,28},{24,0},{28,4},{1,9},{5... | collective-permute-start | bytes 393224 | tf_op jit(solution)/shard_map/ppermute | solution.py:302
  40.1 6.1 %collective-permute-start.10 = (f32[2,2,2,32,128]{4,3,2,1,0:T(8,128)S(1)}, f32[2,2,2,32,128]{4,3,2,1,0:T(8,128)S(1)}, u32[]{:S(2)}, u32[]{:S(2)}) collective-permute-start(f32[2,2,2,32,128]{4,3,2,1,0:T(8,128)S(1)} %get-tuple-element.39), channel_id=1, source_target_pairs={{0,6},{1,7},{2,4},{3,5},{4,2},{5,3},{6,0},{7,1},{8,14},{9,15},{10,... | collective-permute-start | bytes 393224 | tf_op jit(solution)/shard_map/ppermute | solution.py:312
  42.4 9.5 %collective-permute-start.11 = (f32[2,2,2,32,128]{4,3,2,1,0:T(8,128)S(1)}, f32[2,2,2,32,128]{4,3,2,1,0:T(8,128)S(1)}, u32[]{:S(2)}, u32[]{:S(2)}) collective-permute-start(f32[2,2,2,32,128]{4,3,2,1,0:T(8,128)S(1)} %get-tuple-element.40), channel_id=1, source_target_pairs={{0,4},{1,5},{2,6},{3,7},{4,0},{5,1},{6,2},{7,3},{8,12},{9,13},{10,... | collective-permute-start | bytes 393224 | tf_op jit(solution)/shard_map/ppermute | solution.py:312
  43.1 8.8 %collective-permute-start.12 = (f32[2,2,2,32,128]{4,3,2,1,0:T(8,128)S(1)}, f32[2,2,2,32,128]{4,3,2,1,0:T(8,128)S(1)}, u32[]{:S(2)}, u32[]{:S(2)}) collective-permute-start(f32[2,2,2,32,128]{4,3,2,1,0:T(8,128)S(1)} %get-tuple-element.41), channel_id=1, source_target_pairs={{0,2},{1,3},{2,0},{3,1},{4,6},{5,7},{6,4},{7,5},{8,10},{9,11},{10,... | collective-permute-start | bytes 393224 | tf_op jit(solution)/shard_map/ppermute | solution.py:312
  43.6 21.3 %collective-permute-start.17 = (f32[2,8,32,128]{3,2,1,0:T(8,128)S(1)}, f32[2,8,32,128]{3,2,1,0:T(8,128)S(1)}, u32[]{:S(2)}, u32[]{:S(2)}) collective-permute-start(f32[2,8,32,128]{3,2,1,0:T(8,128)S(1)} %get-tuple-element.48), channel_id=1, source_target_pairs={{0,4},{4,0},{8,12},{12,8},{16,20},{20,16},{24,28},{28,24},{1,5},{5... | collective-permute-start | bytes 786440 | tf_op jit(solution)/shard_map/ppermute | solution.py:327
  44.9 8.5 %collective-permute-start.13 = (f32[2,2,2,32,128]{4,3,2,1,0:T(8,128)S(1)}, f32[2,2,2,32,128]{4,3,2,1,0:T(8,128)S(1)}, u32[]{:S(2)}, u32[]{:S(2)}) collective-permute-start(f32[2,2,2,32,128]{4,3,2,1,0:T(8,128)S(1)} %get-tuple-element.42), channel_id=1, source_target_pairs={{0,7},{1,6},{2,5},{3,4},{4,3},{5,2},{6,1},{7,0},{8,15},{9,14},{10,... | collective-permute-start | bytes 393224 | tf_op jit(solution)/shard_map/ppermute | solution.py:312
  46.2 10.5 %collective-permute-start.14 = (f32[2,2,2,32,128]{4,3,2,1,0:T(8,128)S(1)}, f32[2,2,2,32,128]{4,3,2,1,0:T(8,128)S(1)}, u32[]{:S(2)}, u32[]{:S(2)}) collective-permute-start(f32[2,2,2,32,128]{4,3,2,1,0:T(8,128)S(1)} %get-tuple-element.43), channel_id=1, source_target_pairs={{0,5},{1,4},{2,7},{3,6},{4,1},{5,0},{6,3},{7,2},{8,13},{9,12},{10,... | collective-permute-start | bytes 393224 | tf_op jit(solution)/shard_map/ppermute | solution.py:312
  51.9 5.7 %collective-permute-start.15 = (f32[2,2,2,32,128]{4,3,2,1,0:T(8,128)S(1)}, f32[2,2,2,32,128]{4,3,2,1,0:T(8,128)S(1)}, u32[]{:S(2)}, u32[]{:S(2)}) collective-permute-start(f32[2,2,2,32,128]{4,3,2,1,0:T(8,128)S(1)} %get-tuple-element.44), channel_id=1, source_target_pairs={{0,3},{1,2},{2,1},{3,0},{4,7},{5,6},{6,5},{7,4},{8,11},{9,10},{10,... | collective-permute-start | bytes 393224 | tf_op jit(solution)/shard_map/ppermute | solution.py:312
  51.9 5.7 %collective-permute-start.16 = (f32[2,2,2,32,128]{4,3,2,1,0:T(8,128)S(1)}, f32[2,2,2,32,128]{4,3,2,1,0:T(8,128)S(1)}, u32[]{:S(2)}, u32[]{:S(2)}) collective-permute-start(f32[2,2,2,32,128]{4,3,2,1,0:T(8,128)S(1)} %get-tuple-element.45), channel_id=1, source_target_pairs={{0,1},{1,0},{2,3},{3,2},{4,5},{5,4},{6,7},{7,6},{8,9},{9,8},{10,11... | collective-permute-start | bytes 393224 | tf_op jit(solution)/shard_map/ppermute | solution.py:312
  59.6 12.5 %all-to-all-start = ((f32[32,1,128]{2,1,0:T(1,128)}), f32[32,1,128]{2,1,0:T(1,128)S(1)}, u32[]{:S(2)}, u32[]{:S(2)}) async-start(f32[32,1,128]{2,1,0:T(1,128)} %gram.1), calls=%async_computation | async-start | bytes 32768 | tf_op jit(solution)/shard_map/all_to_all | solution.py:328

commit v9 on v5

--- a/solution.py
+++ b/solution.py
@@ -170,18 +170,18 @@
 def gram(*refs):
     *xs, out_ref, part, blocks = refs
     orbs = part.shape[1]
-    half, peers, _, per, ny, nz = blocks.shape
+    half, peers, reach, nz = blocks.shape
+    rows = xs[0].shape[2] * xs[0].shape[3]
     me = places()[2]
     for k, x in zip(PEERS, xs):
         for o in range(half):
-            blocks[o, jnp.bitwise_xor(me, k)] = x[o]
-    rows = per * ny
-    flat = blocks.reshape(half * peers * 2 * rows, nz)
+            blocks[o, jnp.bitwise_xor(me, k), : 2 * rows] = x[o].reshape(2 * rows, nz)
+    flat = blocks.reshape(half * peers * reach, nz)
     fields = jnp.concatenate(
         [
             jnp.concatenate(
                 [
-                    flat[pl.ds((o * peers * 2 + which) * rows + r, peers, stride=2 * rows), :]
+                    flat[pl.ds(o * peers * reach + which * rows + r, peers, stride=reach), :]
                     for which in range(2)
                     for o in range(half)
                 ],
@@ -320,7 +320,7 @@
         gram,
         xs,
         [(size * orbs, 1, 2 * own_orbs * count)],
-        [pltpu.VMEM((2, count, nz), f32), pltpu.VMEM((half, group, *block), f32)],
+        [pltpu.VMEM((2, count, nz), f32), pltpu.VMEM((half, group, 2 * per * ny + 8, nz), f32)],
         1.3,
         "gram",
     )

time: 68.9 us -> 68.6 us (level)
  no operation moved by 1% of the time
where the time goes in v9:
time: 68.6 us; the launch traced here: 68.5 us
  starting transfers between devices  32.7 us (48%)
  waiting for transfers between devices  25.5 us (37%)
  Pallas kernels  7.35 us (11%)
  local copies, waits for them, and re-layouts  1.18 us (2%)
  other arithmetic  0.9 us (1%)
  between operations  0.73 us (1%)
    pallas_call x7, Pallas kernels, call(): pl.pallas_call(body, out_shape=[s if isinstance(s, jax.ShapeDtypeStruct)...  7.35 us
    ppermute x2, starting transfers between devices, per_device(): rhi = lax.ppermute(lo, grid_axes, down)  6.88 us
    ppermute x7, starting transfers between devices, peer(): lax.ppermute(x, ('mem', 'orb'), [(t, t ^ k) for t in range(group)])  6.44 us
    ppermute x7, waiting for transfers between devices, peer(): lax.ppermute(x, ('mem', 'orb'), [(t, t ^ k) for t in range(group)])  6.42 us
    ppermute x2, starting transfers between devices, per_device(): rb = lax.ppermute(b, grid_axes, cross)  5.91 us
    ppermute x2, waiting for transfers between devices, per_device(): rlo = lax.ppermute(hi, grid_axes, up)  5.08 us
    all_to_all x1, starting transfers between devices, per_device(): sums = lax.all_to_all(sums, ('pair', 'mem', 'orb'), 0, 0, tiled=True)  4.95 us
    ppermute x2, starting transfers between devices, per_device(): ra = lax.ppermute(a, grid_axes, swap)  3.77 us
  transfers between devices with their start and end apart: 19, of which 13 were waited for; matrix products, arithmetic and copies ran while one was open for 1% of the time, Pallas kernels for 5%

profile of v9, /device:TPU:0, one launch (start us, length us, event | category | flops | bytes accessed | tf_op | source)
XLA Modules:
  0.0 68.5 jit_solution(12382714938876079427)
XLA Ops:
  0.6 1.2 %constant_dynamic-slice_fusion = (f32[1,8,32,128]{3,2,1,0:T(8,128)S(1)}, f32[1,8,32,128]{3,2,1,0:T(8,128)S(1)}, f32[1,8,32,128]{3,2,1,0:T(8,128)S(1)}, f32[1,8,32,128]{3,2,1,0:T(8,128)S(1)}) fusion(f32[4,8,32,128]{3,2,1,0:T(8,128)} %param.2, s32[]{:T(128)S(6)} %select_n.33, s32[]{:T(128)S(6)} %select_n.29, s32[]{:T(128)S(6)} %select_n.28, s32[]{:T(128)S(6)} %select_n.30), kind=kLoop, calls=%fused_computation.5 | loop fusion | bytes 1048592 | tf_op jit(solution)/shard_map/dynamic_slice | solution.py:278
  1.9 3.0 %collective-permute-start.3 = (f32[1,16,32,128]{3,2,1,0:T(8,128)S(1)}, f32[1,16,32,128]{3,2,1,0:T(8,128)S(1)}, u32[]{:S(2)}, u32[]{:S(2)}) collective-permute-start(f32[1,16,32,128]{3,2,1,0:T(8,128)S(1)} %pad_maximum_fusion), channel_id=1, source_target_pairs={{0,4},{4,0},{8,12},{12,8},{16,20},{20,16},{24,28},{28,24},{1,5},{5... | collective-permute-start | bytes 786440 | tf_op jit(solution)/shard_map/ppermute | solution.py:282
  4.9 3.6 %collective-permute-start.4 = (f32[1,12,32,128]{3,2,1,0:T(8,128)S(1)}, f32[1,12,32,128]{3,2,1,0:T(8,128)S(1)}, u32[]{:S(2)}, u32[]{:S(2)}) collective-permute-start(f32[1,12,32,128]{3,2,1,0:T(8,128)S(1)} %get-tuple-element.61), channel_id=1, source_target_pairs={{0,28},{4,8},{8,4},{12,16},{16,12},{20,24},{24,20},{28,0},{1,29},{... | collective-permute-start | bytes 589832 | tf_op jit(solution)/shard_map/ppermute | solution.py:283
  9.0 2.3 %collective-permute-start.1 = (f32[1,8,32,128]{3,2,1,0:T(8,128)S(1)}, f32[1,8,32,128]{3,2,1,0:T(8,128)S(1)}, u32[]{:S(2)}, u32[]{:S(2)}) collective-permute-start(f32[1,8,32,128]{3,2,1,0:T(8,128)S(1)} %get-tuple-element.58), channel_id=1, source_target_pairs={{0,28},{4,8},{8,4},{12,16},{16,12},{20,24},{24,20},{28,0},{1,29},{... | collective-permute-start | bytes 393224 | tf_op jit(solution)/shard_map/ppermute | solution.py:283
  12.0 3.5 %collective-permute-done.4.rb = f32[1,12,32,128]{3,2,1,0:T(8,128)S(1)} collective-permute-done((f32[1,12,32,128]{3,2,1,0:T(8,128)S(1)}, f32[1,12,32,128]{3,2,1,0:T(8,128)S(1)}, u32[]{:S(2)}, u32[]{:S(2)}) %collective-permute-start.4) | collective-permute-done | bytes 196640 | tf_op jit(solution)/shard_map/ppermute | solution.py:283
  15.6 1.8 %collective-permute-start.2 = (f32[1,8,32,128]{3,2,1,0:T(8,128)S(1)}, f32[1,8,32,128]{3,2,1,0:T(8,128)S(1)}, u32[]{:S(2)}, u32[]{:S(2)}) collective-permute-start(f32[1,8,32,128]{3,2,1,0:T(8,128)S(1)} %get-tuple-element.59.mine), channel_id=1, source_target_pairs={{0,24},{4,12},{8,0},{12,20},{16,8},{20,28},{24,16},{28,4},{1,25},{... | collective-permute-start | bytes 393224 | tf_op jit(solution)/shard_map/ppermute | solution.py:284
  19.5 1.6 %collective-permute-start.9 = (f32[1,8,32,128]{3,2,1,0:T(8,128)S(1)}, f32[1,8,32,128]{3,2,1,0:T(8,128)S(1)}, u32[]{:S(2)}, u32[]{:S(2)}) collective-permute-start(f32[1,8,32,128]{3,2,1,0:T(8,128)S(1)} %get-tuple-element.37.hi), channel_id=1, source_target_pairs={{0,8},{4,12},{8,16},{12,20},{16,24},{20,28},{24,0},{28,4},{1,9},{5... | collective-permute-start | bytes 393224 | tf_op jit(solution)/shard_map/ppermute | solution.py:302
  21.0 2.5 %collective-permute-start.8 = (f32[1,16,32,128]{3,2,1,0:T(8,128)S(1)}, f32[1,16,32,128]{3,2,1,0:T(8,128)S(1)}, u32[]{:S(2)}, u32[]{:S(2)}) collective-permute-start(f32[1,16,32,128]{3,2,1,0:T(8,128)S(1)} %get-tuple-element.36.lo), channel_id=1, source_target_pairs={{0,24},{4,28},{8,0},{12,4},{16,8},{20,12},{24,16},{28,20},{1,25},{... | collective-permute-start | bytes 786440 | tf_op jit(solution)/shard_map/ppermute | solution.py:303
  24.7 4.3 %collective-permute-start.7 = (f32[1,12,32,128]{3,2,1,0:T(8,128)S(1)}, f32[1,12,32,128]{3,2,1,0:T(8,128)S(1)}, u32[]{:S(2)}, u32[]{:S(2)}) collective-permute-start(f32[1,12,32,128]{3,2,1,0:T(8,128)S(1)} %get-tuple-element.34.lo), channel_id=1, source_target_pairs={{0,24},{4,28},{8,0},{12,4},{16,8},{20,12},{24,16},{28,20},{1,25},{... | collective-permute-start | bytes 589832 | tf_op jit(solution)/shard_map/ppermute | solution.py:303
  29.1 3.1 %collective-permute-done.8.rhi.v_above = f32[1,16,32,128]{3,2,1,0:T(8,128)S(1)} collective-permute-done((f32[1,16,32,128]{3,2,1,0:T(8,128)S(1)}, f32[1,16,32,128]{3,2,1,0:T(8,128)S(1)}, u32[]{:S(2)}, u32[]{:S(2)}) %collective-permute-start.8) | collective-permute-done | bytes 262176 | tf_op jit(solution)/shard_map/ppermute | solution.py:303
  32.2 1.4 %filter_3_4_hamiltonian.2 = (f32[2,8,32,128]{3,2,1,0:T(8,128)S(1)}, f32[8,2,2,32,128]{4,3,2,1,0:T(8,128)S(1)}) custom-call(bf16[128,384]{1,0:T(8,128)(2,1)S(1)} %get-tuple-element.30.ymat, bf16[384,128]{1,0:T(8,128)(2,1)S(1)} %get-tuple-element.31.zmat, f32[1,8,32,128]{3,2,1,0:T(8,128)S(1)} %collective-permute-done.9.rlo, ...), custom_call_target="tpu_custom_call" | custom-call | flops 1500000000 | bytes 5250000 | tf_op jit(solution)/shard_map/filter_3_4_hamiltonian/pallas_call | solution.py:238
  33.6 5.1 %collective-permute-done.6.rlo = f32[1,8,32,128]{3,2,1,0:T(8,128)S(1)} collective-permute-done((f32[1,8,32,128]{3,2,1,0:T(8,128)S(1)}, f32[1,8,32,128]{3,2,1,0:T(8,128)S(1)}, u32[]{:S(2)}, u32[]{:S(2)}) %collective-permute-start.6) | collective-permute-done | bytes 131104 | tf_op jit(solution)/shard_map/ppermute | solution.py:302
  38.7 1.4 %filter_3_4_hamiltonian.3 = (f32[2,8,32,128]{3,2,1,0:T(8,128)S(1)}, f32[2,8,32,128]{3,2,1,0:T(8,128)S(1)}, f32[2,2,2,32,128]{4,3,2,1,0:T(8,128)S(1)}, f32[2,2,2,...) custom-call(bf16[128,384]{1,0:T(8,128)(2,1)S(1)} %get-tuple-element., ...), custom_call_target="tpu_custom_call" | custom-call | flops 1500000000 | bytes 5250000 | tf_op jit(solution)/shard_map/filter_3_4_hamiltonian/pallas_call | solution.py:238
  40.1 2.3 %collective-permute-start.10 = (f32[2,2,2,32,128]{4,3,2,1,0:T(8,128)S(1)}, f32[2,2,2,32,128]{4,3,2,1,0:T(8,128)S(1)}, u32[]{:S(2)}, u32[]{:S(2)}) collective-permute-start(f32[2,2,2,32,128]{4,3,2,1,0:T(8,128)S(1)} %get-tuple-element.42), channel_id=1, source_target_pairs={{0,6},{1,7},{2,4},{3,5},{4,2},{5,3},{6,0},{7,1},{8,14},{9,15},{10,... | collective-permute-start | bytes 393224 | tf_op jit(solution)/shard_map/ppermute | solution.py:312
  43.6 2.7 %collective-permute-start.14 = (f32[2,2,2,32,128]{4,3,2,1,0:T(8,128)S(1)}, f32[2,2,2,32,128]{4,3,2,1,0:T(8,128)S(1)}, u32[]{:S(2)}, u32[]{:S(2)}) collective-permute-start(f32[2,2,2,32,128]{4,3,2,1,0:T(8,128)S(1)} %get-tuple-element.46), channel_id=1, source_target_pairs={{0,5},{1,4},{2,7},{3,6},{4,1},{5,0},{6,3},{7,2},{8,13},{9,12},{10,... | collective-permute-start | bytes 393224 | tf_op jit(solution)/shard_map/ppermute | solution.py:312
  46.3 1.2 %collective-permute-done.11.refs_1_ = f32[2,2,2,32,128]{4,3,2,1,0:T(8,128)S(1)} collective-permute-done((f32[2,2,2,32,128]{4,3,2,1,0:T(8,128)S(1)}, f32[2,2,2,32,128]{4,3,2,1,0:T(8,128)S(1)}, u32[]{:S(2)}, u32[]{:S(2)}) %collective-permute-start.11) | collective-permute-done | bytes 131104 | tf_op jit(solution)/shard_map/ppermute | solution.py:312
  47.7 1.1 %collective-permute-done.12.refs_2_ = f32[2,2,2,32,128]{4,3,2,1,0:T(8,128)S(1)} collective-permute-done((f32[2,2,2,32,128]{4,3,2,1,0:T(8,128)S(1)}, f32[2,2,2,32,128]{4,3,2,1,0:T(8,128)S(1)}, u32[]{:S(2)}, u32[]{:S(2)}) %collective-permute-start.12) | collective-permute-done | bytes 131104 | tf_op jit(solution)/shard_map/ppermute | solution.py:312
  48.8 1.6 %collective-permute-done.13.refs_3_ = f32[2,2,2,32,128]{4,3,2,1,0:T(8,128)S(1)} collective-permute-done((f32[2,2,2,32,128]{4,3,2,1,0:T(8,128)S(1)}, f32[2,2,2,32,128]{4,3,2,1,0:T(8,128)S(1)}, u32[]{:S(2)}, u32[]{:S(2)}) %collective-permute-start.13) | collective-permute-done | bytes 131104 | tf_op jit(solution)/shard_map/ppermute | solution.py:312
  50.4 1.5 %collective-permute-done.14.refs_4_ = f32[2,2,2,32,128]{4,3,2,1,0:T(8,128)S(1)} collective-permute-done((f32[2,2,2,32,128]{4,3,2,1,0:T(8,128)S(1)}, f32[2,2,2,32,128]{4,3,2,1,0:T(8,128)S(1)}, u32[]{:S(2)}, u32[]{:S(2)}) %collective-permute-start.14) | collective-permute-done | bytes 131104 | tf_op jit(solution)/shard_map/ppermute | solution.py:312
  52.9 1.7 %gram.1 = f32[32,1,128]{2,1,0:T(1,128)} custom-call(f32[2,2,2,32,128]{4,3,2,1,0:T(8,128)S(1)} %collective-permute-done.10.refs_0_, f32[2,2,2,32,128]{4,3,2,1,0:T(8,128)S(1)} %collective-permute-done.11.refs_1_, f32[2,2,2,32,128]{4,3,2,1,0:T(8,128)S(1)} %collective-permute-done.12.refs_2_, f32[2,2,2,32,128]{4,3,2,1,0:T(8,128)S(1)} %collective-permute-done.13.refs_3_, ...), custom_call_target="tpu_custom_call" | custom-call | flops 1300000000 | bytes 4550000 | tf_op jit(solution)/shard_map/gram/pallas_call | solution.py:238
  54.6 1.0 %collective-permute-start.17 = (f32[2,8,32,128]{3,2,1,0:T(8,128)S(1)}, f32[2,8,32,128]{3,2,1,0:T(8,128)S(1)}, u32[]{:S(2)}, u32[]{:S(2)}) collective-permute-start(f32[2,8,32,128]{3,2,1,0:T(8,128)S(1)} %get-tuple-element.52), channel_id=1, source_target_pairs={{0,4},{4,0},{8,12},{12,8},{16,20},{20,16},{24,28},{28,24},{1,5},{5... | collective-permute-start | bytes 786440 | tf_op jit(solution)/shard_map/ppermute | solution.py:328
  55.7 4.9 %all-to-all-start = ((f32[32,1,128]{2,1,0:T(1,128)}), f32[32,1,128]{2,1,0:T(1,128)S(1)}, u32[]{:S(2)}, u32[]{:S(2)}) async-start(f32[32,1,128]{2,1,0:T(1,128)} %gram.1), calls=%async_computation | async-start | bytes 32768 | tf_op jit(solution)/shard_map/all_to_all | solution.py:329
  60.6 2.8 %collective-permute-done.17 = f32[2,8,32,128]{3,2,1,0:T(8,128)S(1)} collective-permute-done((f32[2,8,32,128]{3,2,1,0:T(8,128)S(1)}, f32[2,8,32,128]{3,2,1,0:T(8,128)S(1)}, u32[]{:S(2)}, u32[]{:S(2)}) %collective-permute-start.17) | collective-permute-done | bytes 262176 | tf_op jit(solution)/shard_map/ppermute | solution.py:328
  64.2 3.5 %all-to-all-done.x_ref = f32[32,1,128]{2,1,0:T(1,128)S(1)} async-done(((f32[32,1,128]{2,1,0:T(1,128)}), f32[32,1,128]{2,1,0:T(1,128)S(1)}, u32[]{:S(2)}, u32[]{:S(2)}) %all-to-all-start) | async-done | bytes 16416 | tf_op jit(solution)/shard_map/all_to_all | solution.py:329
  (28 shorter events, 8.5 us)
Async XLA Ops:
  0.6 1.2 %copy-start = (f32[8,32,128]{2,1,0:T(8,128)S(1)}, f32[8,32,128]{2,1,0:T(8,128)}, u32[]{:S(2)}) copy-start(f32[8,32,128]{2,1,0:T(8,128)} %refs_0_.1) | copy-start | bytes 393220
  1.9 16.6 %collective-permute-start.3 = (f32[1,16,32,128]{3,2,1,0:T(8,128)S(1)}, f32[1,16,32,128]{3,2,1,0:T(8,128)S(1)}, u32[]{:S(2)}, u32[]{:S(2)}) collective-permute-start(f32[1,16,32,128]{3,2,1,0:T(8,128)S(1)} %pad_maximum_fusion), channel_id=1, source_target_pairs={{0,4},{4,0},{8,12},{12,8},{16,20},{20,16},{24,28},{28,24},{1,5},{5... | collective-permute-start | bytes 786440 | tf_op jit(solution)/shard_map/ppermute | solution.py:282
  4.9 10.6 %collective-permute-start.4 = (f32[1,12,32,128]{3,2,1,0:T(8,128)S(1)}, f32[1,12,32,128]{3,2,1,0:T(8,128)S(1)}, u32[]{:S(2)}, u32[]{:S(2)}) collective-permute-start(f32[1,12,32,128]{3,2,1,0:T(8,128)S(1)} %get-tuple-element.61), channel_id=1, source_target_pairs={{0,28},{4,8},{8,4},{12,16},{16,12},{20,24},{24,20},{28,0},{1,29},{... | collective-permute-start | bytes 589832 | tf_op jit(solution)/shard_map/ppermute | solution.py:283
  8.6 9.6 %collective-permute-start.5 = (f32[1,12,32,128]{3,2,1,0:T(8,128)S(1)}, f32[1,12,32,128]{3,2,1,0:T(8,128)S(1)}, u32[]{:S(2)}, u32[]{:S(2)}) collective-permute-start(f32[1,12,32,128]{3,2,1,0:T(8,128)S(1)} %get-tuple-element.62.mine), channel_id=1, source_target_pairs={{0,24},{4,12},{8,0},{12,20},{16,8},{20,28},{24,16},{28,4},{1,25},{... | collective-permute-start | bytes 589832 | tf_op jit(solution)/shard_map/ppermute | solution.py:284
  9.0 14.6 %collective-permute-start.1 = (f32[1,8,32,128]{3,2,1,0:T(8,128)S(1)}, f32[1,8,32,128]{3,2,1,0:T(8,128)S(1)}, u32[]{:S(2)}, u32[]{:S(2)}) collective-permute-start(f32[1,8,32,128]{3,2,1,0:T(8,128)S(1)} %get-tuple-element.58), channel_id=1, source_target_pairs={{0,28},{4,8},{8,4},{12,16},{16,12},{20,24},{24,20},{28,0},{1,29},{... | collective-permute-start | bytes 393224 | tf_op jit(solution)/shard_map/ppermute | solution.py:283
  11.3 12.3 %collective-permute-start = (f32[1,8,32,128]{3,2,1,0:T(8,128)S(1)}, f32[1,8,32,128]{3,2,1,0:T(8,128)S(1)}, u32[]{:S(2)}, u32[]{:S(2)}) collective-permute-start(f32[1,8,32,128]{3,2,1,0:T(8,128)S(1)} %get-tuple-element.58), channel_id=1, source_target_pairs={{0,4},{4,0},{8,12},{12,8},{16,20},{20,16},{24,28},{28,24},{1,5},{5... | collective-permute-start | bytes 393224 | tf_op jit(solution)/shard_map/ppermute | solution.py:282
  15.6 8.2 %collective-permute-start.2 = (f32[1,8,32,128]{3,2,1,0:T(8,128)S(1)}, f32[1,8,32,128]{3,2,1,0:T(8,128)S(1)}, u32[]{:S(2)}, u32[]{:S(2)}) collective-permute-start(f32[1,8,32,128]{3,2,1,0:T(8,128)S(1)} %get-tuple-element.59.mine), channel_id=1, source_target_pairs={{0,24},{4,12},{8,0},{12,20},{16,8},{20,28},{24,16},{28,4},{1,25},{... | collective-permute-start | bytes 393224 | tf_op jit(solution)/shard_map/ppermute | solution.py:284
  19.5 9.6 %collective-permute-start.9 = (f32[1,8,32,128]{3,2,1,0:T(8,128)S(1)}, f32[1,8,32,128]{3,2,1,0:T(8,128)S(1)}, u32[]{:S(2)}, u32[]{:S(2)}) collective-permute-start(f32[1,8,32,128]{3,2,1,0:T(8,128)S(1)} %get-tuple-element.37.hi), channel_id=1, source_target_pairs={{0,8},{4,12},{8,16},{12,20},{16,24},{20,28},{24,0},{28,4},{1,9},{5... | collective-permute-start | bytes 393224 | tf_op jit(solution)/shard_map/ppermute | solution.py:302
  21.0 11.2 %collective-permute-start.8 = (f32[1,16,32,128]{3,2,1,0:T(8,128)S(1)}, f32[1,16,32,128]{3,2,1,0:T(8,128)S(1)}, u32[]{:S(2)}, u32[]{:S(2)}) collective-permute-start(f32[1,16,32,128]{3,2,1,0:T(8,128)S(1)} %get-tuple-element.36.lo), channel_id=1, source_target_pairs={{0,24},{4,28},{8,0},{12,4},{16,8},{20,12},{24,16},{28,20},{1,25},{... | collective-permute-start | bytes 786440 | tf_op jit(solution)/shard_map/ppermute | solution.py:303
  24.7 13.9 %collective-permute-start.7 = (f32[1,12,32,128]{3,2,1,0:T(8,128)S(1)}, f32[1,12,32,128]{3,2,1,0:T(8,128)S(1)}, u32[]{:S(2)}, u32[]{:S(2)}) collective-permute-start(f32[1,12,32,128]{3,2,1,0:T(8,128)S(1)} %get-tuple-element.34.lo), channel_id=1, source_target_pairs={{0,24},{4,28},{8,0},{12,4},{16,8},{20,12},{24,16},{28,20},{1,25},{... | collective-permute-start | bytes 589832 | tf_op jit(solution)/shard_map/ppermute | solution.py:303
  29.1 9.6 %collective-permute-start.6 = (f32[1,8,32,128]{3,2,1,0:T(8,128)S(1)}, f32[1,8,32,128]{3,2,1,0:T(8,128)S(1)}, u32[]{:S(2)}, u32[]{:S(2)}) collective-permute-start(f32[1,8,32,128]{3,2,1,0:T(8,128)S(1)} %get-tuple-element.33.hi), channel_id=1, source_target_pairs={{0,8},{4,12},{8,16},{12,20},{16,24},{20,28},{24,0},{28,4},{1,9},{5... | collective-permute-start | bytes 393224 | tf_op jit(solution)/shard_map/ppermute | solution.py:302
  40.1 6.2 %collective-permute-start.10 = (f32[2,2,2,32,128]{4,3,2,1,0:T(8,128)S(1)}, f32[2,2,2,32,128]{4,3,2,1,0:T(8,128)S(1)}, u32[]{:S(2)}, u32[]{:S(2)}) collective-permute-start(f32[2,2,2,32,128]{4,3,2,1,0:T(8,128)S(1)} %get-tuple-element.42), channel_id=1, source_target_pairs={{0,6},{1,7},{2,4},{3,5},{4,2},{5,3},{6,0},{7,1},{8,14},{9,15},{10,... | collective-permute-start | bytes 393224 | tf_op jit(solution)/shard_map/ppermute | solution.py:312
  42.4 5.1 %collective-permute-start.11 = (f32[2,2,2,32,128]{4,3,2,1,0:T(8,128)S(1)}, f32[2,2,2,32,128]{4,3,2,1,0:T(8,128)S(1)}, u32[]{:S(2)}, u32[]{:S(2)}) collective-permute-start(f32[2,2,2,32,128]{4,3,2,1,0:T(8,128)S(1)} %get-tuple-element.43), channel_id=1, source_target_pairs={{0,4},{1,5},{2,6},{3,7},{4,0},{5,1},{6,2},{7,3},{8,12},{9,13},{10,... | collective-permute-start | bytes 393224 | tf_op jit(solution)/shard_map/ppermute | solution.py:312
  43.1 5.7 %collective-permute-start.12 = (f32[2,2,2,32,128]{4,3,2,1,0:T(8,128)S(1)}, f32[2,2,2,32,128]{4,3,2,1,0:T(8,128)S(1)}, u32[]{:S(2)}, u32[]{:S(2)}) collective-permute-start(f32[2,2,2,32,128]{4,3,2,1,0:T(8,128)S(1)} %get-tuple-element.44), channel_id=1, source_target_pairs={{0,2},{1,3},{2,0},{3,1},{4,6},{5,7},{6,4},{7,5},{8,10},{9,11},{10,... | collective-permute-start | bytes 393224 | tf_op jit(solution)/shard_map/ppermute | solution.py:312
  43.6 6.8 %collective-permute-start.13 = (f32[2,2,2,32,128]{4,3,2,1,0:T(8,128)S(1)}, f32[2,2,2,32,128]{4,3,2,1,0:T(8,128)S(1)}, u32[]{:S(2)}, u32[]{:S(2)}) collective-permute-start(f32[2,2,2,32,128]{4,3,2,1,0:T(8,128)S(1)} %get-tuple-element.45), channel_id=1, source_target_pairs={{0,7},{1,6},{2,5},{3,4},{4,3},{5,2},{6,1},{7,0},{8,15},{9,14},{10,... | collective-permute-start | bytes 393224 | tf_op jit(solution)/shard_map/ppermute | solution.py:312
  43.6 8.3 %collective-permute-start.14 = (f32[2,2,2,32,128]{4,3,2,1,0:T(8,128)S(1)}, f32[2,2,2,32,128]{4,3,2,1,0:T(8,128)S(1)}, u32[]{:S(2)}, u32[]{:S(2)}) collective-permute-start(f32[2,2,2,32,128]{4,3,2,1,0:T(8,128)S(1)} %get-tuple-element.46), channel_id=1, source_target_pairs={{0,5},{1,4},{2,7},{3,6},{4,1},{5,0},{6,3},{7,2},{8,13},{9,12},{10,... | collective-permute-start | bytes 393224 | tf_op jit(solution)/shard_map/ppermute | solution.py:312
  46.3 6.6 %collective-permute-start.15 = (f32[2,2,2,32,128]{4,3,2,1,0:T(8,128)S(1)}, f32[2,2,2,32,128]{4,3,2,1,0:T(8,128)S(1)}, u32[]{:S(2)}, u32[]{:S(2)}) collective-permute-start(f32[2,2,2,32,128]{4,3,2,1,0:T(8,128)S(1)} %get-tuple-element.47), channel_id=1, source_target_pairs={{0,3},{1,2},{2,1},{3,0},{4,7},{5,6},{6,5},{7,4},{8,11},{9,10},{10,... | collective-permute-start | bytes 393224 | tf_op jit(solution)/shard_map/ppermute | solution.py:312
  47.5 5.4 %collective-permute-start.16 = (f32[2,2,2,32,128]{4,3,2,1,0:T(8,128)S(1)}, f32[2,2,2,32,128]{4,3,2,1,0:T(8,128)S(1)}, u32[]{:S(2)}, u32[]{:S(2)}) collective-permute-start(f32[2,2,2,32,128]{4,3,2,1,0:T(8,128)S(1)} %get-tuple-element.48), channel_id=1, source_target_pairs={{0,1},{1,0},{2,3},{3,2},{4,5},{5,4},{6,7},{7,6},{8,9},{9,8},{10,11... | collective-permute-start | bytes 393224 | tf_op jit(solution)/shard_map/ppermute | solution.py:312
  54.6 8.8 %collective-permute-start.17 = (f32[2,8,32,128]{3,2,1,0:T(8,128)S(1)}, f32[2,8,32,128]{3,2,1,0:T(8,128)S(1)}, u32[]{:S(2)}, u32[]{:S(2)}) collective-permute-start(f32[2,8,32,128]{3,2,1,0:T(8,128)S(1)} %get-tuple-element.52), channel_id=1, source_target_pairs={{0,4},{4,0},{8,12},{12,8},{16,20},{20,16},{24,28},{28,24},{1,5},{5... | collective-permute-start | bytes 786440 | tf_op jit(solution)/shard_map/ppermute | solution.py:328
  55.7 12.1 %all-to-all-start = ((f32[32,1,128]{2,1,0:T(1,128)}), f32[32,1,128]{2,1,0:T(1,128)S(1)}, u32[]{:S(2)}, u32[]{:S(2)}) async-start(f32[32,1,128]{2,1,0:T(1,128)} %gram.1), calls=%async_computation | async-start | bytes 32768 | tf_op jit(solution)/shard_map/all_to_all | solution.py:329

commit v10 on v9

--- a/solution.py
+++ b/solution.py
@@ -18,7 +18,7 @@
 S1 = HALF / (LOWER - CENTRE)
 T2 = 2.0 / S1**2 - 1.0
 T4 = 2.0 * T2 * T2 - 1.0
-PEERS = (6, 4, 2, 7, 5, 3, 1, 0)
+PEERS = (4, 2, 6, 7, 5, 3, 1, 0)
 CHUNK = 4
 
 
@@ -283,6 +283,7 @@
         rb = lax.ppermute(b, grid_axes, cross)
         rc = lax.ppermute(c, grid_axes, along)
         first.append((*mats, c, ra, rb, rc))
+        orbitals, _ = lax.optimization_barrier((orbitals, a))
 
     def field(layers):
         return pltpu.VMEM((layers, ny, nz), f32)

time: 68.6 us -> 69.1 us (level)
    dynamic_slice x1, local copies, waits for them, and re-layouts: 1.17 us -> 0.02 us  [per_device(): a = b = lax.dynamic_slice_in_dim(orbitals, half * (1 - m) + o, 1, 0)]
    dynamic_slice x0 -> x1, local copies, waits for them, and re-layouts: none -> 1.03 us  [per_device(): c = lax.dynamic_slice_in_dim(orbitals, half * m + o, 1, 0)]
    ppermute x7, starting transfers between devices: 6.44 us -> 7.47 us  [peer(): lax.ppermute(x, ('mem', 'orb'), [(t, t ^ k) for t in range(group)])]
  transfers between devices with their start and end apart: 19 -> 19, of which waited for: 13 -> 12; matrix products, arithmetic and copies ran while one was open for 1% -> 1% of each run, Pallas kernels for 5% -> 5%
where the time goes in v10:
time: 69.1 us; the launch traced here: 68.9 us
  starting transfers between devices  33 us (48%)
  waiting for transfers between devices  25.8 us (37%)
  Pallas kernels  7.35 us (11%)
  local copies, waits for them, and re-layouts  1.06 us (2%)
  other arithmetic  0.9 us (1%)
  between operations  0.74 us (1%)
    ppermute x7, starting transfers between devices, peer(): lax.ppermute(x, ('mem', 'orb'), [(t, t ^ k) for t in range(group)])  7.47 us
    pallas_call x7, Pallas kernels, call(): pl.pallas_call(body, out_shape=[s if isinstance(s, jax.ShapeDtypeStruct)...  7.35 us
    ppermute x2, starting transfers between devices, per_device(): rhi = lax.ppermute(lo, grid_axes, down)  6.89 us
    ppermute x7, waiting for transfers between devices, peer(): lax.ppermute(x, ('mem', 'orb'), [(t, t ^ k) for t in range(group)])  6.79 us
    ppermute x2, starting transfers between devices, per_device(): rb = lax.ppermute(b, grid_axes, cross)  5.98 us
    ppermute x2, waiting for transfers between devices, per_device(): rlo = lax.ppermute(hi, grid_axes, up)  5.08 us
    all_to_all x1, starting transfers between devices, per_device(): sums = lax.all_to_all(sums, ('pair', 'mem', 'orb'), 0, 0, tiled=True)  4.46 us
    ppermute x2, starting transfers between devices, per_device(): ra = lax.ppermute(a, grid_axes, swap)  3.77 us
  transfers between devices with their start and end apart: 19, of which 12 were waited for; matrix products, arithmetic and copies ran while one was open for 1% of the time, Pallas kernels for 5%

profile of v10, /device:TPU:0, one launch (start us, length us, event | category | flops | bytes accessed | tf_op | source)
XLA Modules:
  0.0 68.9 jit_solution(2559434118336689380)
XLA Ops:
  0.6 1.0 %constant_dynamic-slice_fusion = (f32[1,8,32,128]{3,2,1,0:T(8,128)S(1)}, f32[1,8,32,128]{3,2,1,0:T(8,128)S(1)}) fusion(f32[4,8,32,128]{3,2,1,0:T(8,128)} %param.2, s32[]{:T(128)S(6)} %select_n.31, s32[]{:T(128)S(6)} %select_n.28), kind=kLoop, calls=%fused_computation.5 | loop fusion | bytes 524296 | tf_op jit(solution)/shard_map/dynamic_slice | solution.py:279
  1.7 3.0 %collective-permute-start.3 = (f32[1,16,32,128]{3,2,1,0:T(8,128)S(1)}, f32[1,16,32,128]{3,2,1,0:T(8,128)S(1)}, u32[]{:S(2)}, u32[]{:S(2)}) collective-permute-start(f32[1,16,32,128]{3,2,1,0:T(8,128)S(1)} %pad_maximum_fusion), channel_id=1, source_target_pairs={{0,4},{4,0},{8,12},{12,8},{16,20},{20,16},{24,28},{28,24},{1,5},{5... | collective-permute-start | bytes 786440 | tf_op jit(solution)/shard_map/ppermute | solution.py:282
  4.8 3.6 %collective-permute-start.4 = (f32[1,12,32,128]{3,2,1,0:T(8,128)S(1)}, f32[1,12,32,128]{3,2,1,0:T(8,128)S(1)}, u32[]{:S(2)}, u32[]{:S(2)}) collective-permute-start(f32[1,12,32,128]{3,2,1,0:T(8,128)S(1)} %get-tuple-element.63), channel_id=1, source_target_pairs={{0,28},{4,8},{8,4},{12,16},{16,12},{20,24},{24,20},{28,0},{1,29},{... | collective-permute-start | bytes 589832 | tf_op jit(solution)/shard_map/ppermute | solution.py:283
  8.9 2.4 %collective-permute-start.1 = (f32[1,8,32,128]{3,2,1,0:T(8,128)S(1)}, f32[1,8,32,128]{3,2,1,0:T(8,128)S(1)}, u32[]{:S(2)}, u32[]{:S(2)}) collective-permute-start(f32[1,8,32,128]{3,2,1,0:T(8,128)S(1)} %get-tuple-element.61), channel_id=1, source_target_pairs={{0,28},{4,8},{8,4},{12,16},{16,12},{20,24},{24,20},{28,0},{1,29},{... | collective-permute-start | bytes 393224 | tf_op jit(solution)/shard_map/ppermute | solution.py:283
  12.0 3.4 %collective-permute-done.4.rb = f32[1,12,32,128]{3,2,1,0:T(8,128)S(1)} collective-permute-done((f32[1,12,32,128]{3,2,1,0:T(8,128)S(1)}, f32[1,12,32,128]{3,2,1,0:T(8,128)S(1)}, u32[]{:S(2)}, u32[]{:S(2)}) %collective-permute-start.4) | collective-permute-done | bytes 196640 | tf_op jit(solution)/shard_map/ppermute | solution.py:283
  15.4 1.8 %collective-permute-start.2 = (f32[1,8,32,128]{3,2,1,0:T(8,128)S(1)}, f32[1,8,32,128]{3,2,1,0:T(8,128)S(1)}, u32[]{:S(2)}, u32[]{:S(2)}) collective-permute-start(f32[1,8,32,128]{3,2,1,0:T(8,128)S(1)} %get-tuple-element.62.mine), channel_id=1, source_target_pairs={{0,24},{4,12},{8,0},{12,20},{16,8},{20,28},{24,16},{28,4},{1,25},{... | collective-permute-start | bytes 393224 | tf_op jit(solution)/shard_map/ppermute | solution.py:284
  18.4 1.0 %filter_1_2.2 = (f32[1,16,32,128]{3,2,1,0:T(8,128)S(1)}, f32[1,8,32,128]{3,2,1,0:T(8,128)S(1)}, f32[1,20,32,128]{3,2,1,0:T(8,128)S(1)}, f32[24,32,128]{2,1,0:T(8,128)S(1)}) custom-call(bf16[128,384]{1,0:T(8,128)(2,1)S(1)} %get-tuple-element.31.ymat, bf16[384,128]{1,0:T(8,128)(2,1)S(1)} %get-tuple-element.32.zmat, ...), custom_call_target="tpu_custom_call" | custom-call | flops 1000000000 | bytes 3500000 | tf_op jit(solution)/shard_map/filter_1_2/pallas_call | solution.py:238
  19.3 1.6 %collective-permute-start.9 = (f32[1,8,32,128]{3,2,1,0:T(8,128)S(1)}, f32[1,8,32,128]{3,2,1,0:T(8,128)S(1)}, u32[]{:S(2)}, u32[]{:S(2)}) collective-permute-start(f32[1,8,32,128]{3,2,1,0:T(8,128)S(1)} %get-tuple-element.39.hi), channel_id=1, source_target_pairs={{0,8},{4,12},{8,16},{12,20},{16,24},{20,28},{24,0},{28,4},{1,9},{5... | collective-permute-start | bytes 393224 | tf_op jit(solution)/shard_map/ppermute | solution.py:303
  20.9 2.5 %collective-permute-start.8 = (f32[1,16,32,128]{3,2,1,0:T(8,128)S(1)}, f32[1,16,32,128]{3,2,1,0:T(8,128)S(1)}, u32[]{:S(2)}, u32[]{:S(2)}) collective-permute-start(f32[1,16,32,128]{3,2,1,0:T(8,128)S(1)} %get-tuple-element.38.lo), channel_id=1, source_target_pairs={{0,24},{4,28},{8,0},{12,4},{16,8},{20,12},{24,16},{28,20},{1,25},{... | collective-permute-start | bytes 786440 | tf_op jit(solution)/shard_map/ppermute | solution.py:304
  24.6 4.3 %collective-permute-start.7 = (f32[1,12,32,128]{3,2,1,0:T(8,128)S(1)}, f32[1,12,32,128]{3,2,1,0:T(8,128)S(1)}, u32[]{:S(2)}, u32[]{:S(2)}) collective-permute-start(f32[1,12,32,128]{3,2,1,0:T(8,128)S(1)} %get-tuple-element.36.lo), channel_id=1, source_target_pairs={{0,24},{4,28},{8,0},{12,4},{16,8},{20,12},{24,16},{28,20},{1,25},{... | collective-permute-start | bytes 589832 | tf_op jit(solution)/shard_map/ppermute | solution.py:304
  29.0 3.1 %collective-permute-done.8.rhi.v_above = f32[1,16,32,128]{3,2,1,0:T(8,128)S(1)} collective-permute-done((f32[1,16,32,128]{3,2,1,0:T(8,128)S(1)}, f32[1,16,32,128]{3,2,1,0:T(8,128)S(1)}, u32[]{:S(2)}, u32[]{:S(2)}) %collective-permute-start.8) | collective-permute-done | bytes 262176 | tf_op jit(solution)/shard_map/ppermute | solution.py:304
  32.1 1.4 %filter_3_4_hamiltonian.2 = (f32[2,8,32,128]{3,2,1,0:T(8,128)S(1)}, f32[8,2,2,32,128]{4,3,2,1,0:T(8,128)S(1)}) custom-call(bf16[128,384]{1,0:T(8,128)(2,1)S(1)} %get-tuple-element.31.ymat, bf16[384,128]{1,0:T(8,128)(2,1)S(1)} %get-tuple-element.32.zmat, f32[1,8,32,128]{3,2,1,0:T(8,128)S(1)} %collective-permute-done.9.rlo, ...), custom_call_target="tpu_custom_call" | custom-call | flops 1500000000 | bytes 5250000 | tf_op jit(solution)/shard_map/filter_3_4_hamiltonian/pallas_call | solution.py:238
  33.4 5.1 %collective-permute-done.6.rlo = f32[1,8,32,128]{3,2,1,0:T(8,128)S(1)} collective-permute-done((f32[1,8,32,128]{3,2,1,0:T(8,128)S(1)}, f32[1,8,32,128]{3,2,1,0:T(8,128)S(1)}, u32[]{:S(2)}, u32[]{:S(2)}) %collective-permute-start.6) | collective-permute-done | bytes 131104 | tf_op jit(solution)/shard_map/ppermute | solution.py:303
  38.5 1.4 %filter_3_4_hamiltonian.3 = (f32[2,8,32,128]{3,2,1,0:T(8,128)S(1)}, f32[2,8,32,128]{3,2,1,0:T(8,128)S(1)}, f32[2,2,2,32,128]{4,3,2,1,0:T(8,128)S(1)}, f32[2,2,2,...) custom-call(bf16[128,384]{1,0:T(8,128)(2,1)S(1)} %get-tuple-element., ...), custom_call_target="tpu_custom_call" | custom-call | flops 1500000000 | bytes 5250000 | tf_op jit(solution)/shard_map/filter_3_4_hamiltonian/pallas_call | solution.py:238
  39.9 1.4 %collective-permute-start.10 = (f32[2,2,2,32,128]{4,3,2,1,0:T(8,128)S(1)}, f32[2,2,2,32,128]{4,3,2,1,0:T(8,128)S(1)}, u32[]{:S(2)}, u32[]{:S(2)}) collective-permute-start(f32[2,2,2,32,128]{4,3,2,1,0:T(8,128)S(1)} %get-tuple-element.44), channel_id=1, source_target_pairs={{0,4},{1,5},{2,6},{3,7},{4,0},{5,1},{6,2},{7,3},{8,12},{9,13},{10,... | collective-permute-start | bytes 393224 | tf_op jit(solution)/shard_map/ppermute | solution.py:313
  41.3 1.5 %collective-permute-start.11 = (f32[2,2,2,32,128]{4,3,2,1,0:T(8,128)S(1)}, f32[2,2,2,32,128]{4,3,2,1,0:T(8,128)S(1)}, u32[]{:S(2)}, u32[]{:S(2)}) collective-permute-start(f32[2,2,2,32,128]{4,3,2,1,0:T(8,128)S(1)} %get-tuple-element.45), channel_id=1, source_target_pairs={{0,2},{1,3},{2,0},{3,1},{4,6},{5,7},{6,4},{7,5},{8,10},{9,11},{10,... | collective-permute-start | bytes 393224 | tf_op jit(solution)/shard_map/ppermute | solution.py:313
  43.5 2.7 %collective-permute-start.14 = (f32[2,2,2,32,128]{4,3,2,1,0:T(8,128)S(1)}, f32[2,2,2,32,128]{4,3,2,1,0:T(8,128)S(1)}, u32[]{:S(2)}, u32[]{:S(2)}) collective-permute-start(f32[2,2,2,32,128]{4,3,2,1,0:T(8,128)S(1)} %get-tuple-element.48), channel_id=1, source_target_pairs={{0,5},{1,4},{2,7},{3,6},{4,1},{5,0},{6,3},{7,2},{8,13},{9,12},{10,... | collective-permute-start | bytes 393224 | tf_op jit(solution)/shard_map/ppermute | solution.py:313
  46.3 1.2 %collective-permute-start.16 = (f32[2,2,2,32,128]{4,3,2,1,0:T(8,128)S(1)}, f32[2,2,2,32,128]{4,3,2,1,0:T(8,128)S(1)}, u32[]{:S(2)}, u32[]{:S(2)}) collective-permute-start(f32[2,2,2,32,128]{4,3,2,1,0:T(8,128)S(1)} %get-tuple-element.50), channel_id=1, source_target_pairs={{0,1},{1,0},{2,3},{3,2},{4,5},{5,4},{6,7},{7,6},{8,9},{9,8},{10,11... | collective-permute-start | bytes 393224 | tf_op jit(solution)/shard_map/ppermute | solution.py:313
  47.5 2.5 %collective-permute-done.12.refs_2_ = f32[2,2,2,32,128]{4,3,2,1,0:T(8,128)S(1)} collective-permute-done((f32[2,2,2,32,128]{4,3,2,1,0:T(8,128)S(1)}, f32[2,2,2,32,128]{4,3,2,1,0:T(8,128)S(1)}, u32[]{:S(2)}, u32[]{:S(2)}) %collective-permute-start.12) | collective-permute-done | bytes 131104 | tf_op jit(solution)/shard_map/ppermute | solution.py:313
  50.3 3.9 %collective-permute-done.14.refs_4_ = f32[2,2,2,32,128]{4,3,2,1,0:T(8,128)S(1)} collective-permute-done((f32[2,2,2,32,128]{4,3,2,1,0:T(8,128)S(1)}, f32[2,2,2,32,128]{4,3,2,1,0:T(8,128)S(1)}, u32[]{:S(2)}, u32[]{:S(2)}) %collective-permute-start.14) | collective-permute-done | bytes 131104 | tf_op jit(solution)/shard_map/ppermute | solution.py:313
  54.2 1.7 %gram.1 = f32[32,1,128]{2,1,0:T(1,128)} custom-call(f32[2,2,2,32,128]{4,3,2,1,0:T(8,128)S(1)} %collective-permute-done.10.refs_0_, f32[2,2,2,32,128]{4,3,2,1,0:T(8,128)S(1)} %collective-permute-done.11.refs_1_, f32[2,2,2,32,128]{4,3,2,1,0:T(8,128)S(1)} %collective-permute-done.12.refs_2_, f32[2,2,2,32,128]{4,3,2,1,0:T(8,128)S(1)} %collective-permute-done.13.refs_3_, ...), custom_call_target="tpu_custom_call" | custom-call | flops 1300000000 | bytes 4550000 | tf_op jit(solution)/shard_map/gram/pallas_call | solution.py:238
  56.6 4.5 %all-to-all-start = ((f32[32,1,128]{2,1,0:T(1,128)}), f32[32,1,128]{2,1,0:T(1,128)S(1)}, u32[]{:S(2)}, u32[]{:S(2)}) async-start(f32[32,1,128]{2,1,0:T(1,128)} %gram.1), calls=%async_computation | async-start | bytes 32768 | tf_op jit(solution)/shard_map/all_to_all | solution.py:330
  61.1 3.2 %collective-permute-done.17 = f32[2,8,32,128]{3,2,1,0:T(8,128)S(1)} collective-permute-done((f32[2,8,32,128]{3,2,1,0:T(8,128)S(1)}, f32[2,8,32,128]{3,2,1,0:T(8,128)S(1)}, u32[]{:S(2)}, u32[]{:S(2)}) %collective-permute-start.17) | collective-permute-done | bytes 262176 | tf_op jit(solution)/shard_map/ppermute | solution.py:329
  65.1 3.1 %all-to-all-done.x_ref = f32[32,1,128]{2,1,0:T(1,128)S(1)} async-done(((f32[32,1,128]{2,1,0:T(1,128)}), f32[32,1,128]{2,1,0:T(1,128)S(1)}, u32[]{:S(2)}, u32[]{:S(2)}) %all-to-all-start) | async-done | bytes 16416 | tf_op jit(solution)/shard_map/all_to_all | solution.py:330
  (31 shorter events, 6.8 us)
Async XLA Ops:
  0.6 1.0 %copy-start = (f32[8,32,128]{2,1,0:T(8,128)S(1)}, f32[8,32,128]{2,1,0:T(8,128)}, u32[]{:S(2)}) copy-start(f32[8,32,128]{2,1,0:T(8,128)} %refs_0_.1) | copy-start | bytes 393220
  1.7 7.2 %copy-start.1 = (f32[4,8,32,128]{3,2,1,0:T(8,128)S(1)}, f32[4,8,32,128]{3,2,1,0:T(8,128)}, u32[]{:S(2)}) copy-start(f32[4,8,32,128]{3,2,1,0:T(8,128)} %param.2) | copy-start | bytes 1572868
  1.7 16.6 %collective-permute-start.3 = (f32[1,16,32,128]{3,2,1,0:T(8,128)S(1)}, f32[1,16,32,128]{3,2,1,0:T(8,128)S(1)}, u32[]{:S(2)}, u32[]{:S(2)}) collective-permute-start(f32[1,16,32,128]{3,2,1,0:T(8,128)S(1)} %pad_maximum_fusion), channel_id=1, source_target_pairs={{0,4},{4,0},{8,12},{12,8},{16,20},{20,16},{24,28},{28,24},{1,5},{5... | collective-permute-start | bytes 786440 | tf_op jit(solution)/shard_map/ppermute | solution.py:282
  4.8 10.6 %collective-permute-start.4 = (f32[1,12,32,128]{3,2,1,0:T(8,128)S(1)}, f32[1,12,32,128]{3,2,1,0:T(8,128)S(1)}, u32[]{:S(2)}, u32[]{:S(2)}) collective-permute-start(f32[1,12,32,128]{3,2,1,0:T(8,128)S(1)} %get-tuple-element.63), channel_id=1, source_target_pairs={{0,28},{4,8},{8,4},{12,16},{16,12},{20,24},{24,20},{28,0},{1,29},{... | collective-permute-start | bytes 589832 | tf_op jit(solution)/shard_map/ppermute | solution.py:283
  8.4 9.6 %collective-permute-start.5 = (f32[1,12,32,128]{3,2,1,0:T(8,128)S(1)}, f32[1,12,32,128]{3,2,1,0:T(8,128)S(1)}, u32[]{:S(2)}, u32[]{:S(2)}) collective-permute-start(f32[1,12,32,128]{3,2,1,0:T(8,128)S(1)} %get-tuple-element.64.mine), channel_id=1, source_target_pairs={{0,24},{4,12},{8,0},{12,20},{16,8},{20,28},{24,16},{28,4},{1,25},{... | collective-permute-start | bytes 589832 | tf_op jit(solution)/shard_map/ppermute | solution.py:284
  8.9 14.5 %collective-permute-start.1 = (f32[1,8,32,128]{3,2,1,0:T(8,128)S(1)}, f32[1,8,32,128]{3,2,1,0:T(8,128)S(1)}, u32[]{:S(2)}, u32[]{:S(2)}) collective-permute-start(f32[1,8,32,128]{3,2,1,0:T(8,128)S(1)} %get-tuple-element.61), channel_id=1, source_target_pairs={{0,28},{4,8},{8,4},{12,16},{16,12},{20,24},{24,20},{28,0},{1,29},{... | collective-permute-start | bytes 393224 | tf_op jit(solution)/shard_map/ppermute | solution.py:283
  11.3 12.2 %collective-permute-start = (f32[1,8,32,128]{3,2,1,0:T(8,128)S(1)}, f32[1,8,32,128]{3,2,1,0:T(8,128)S(1)}, u32[]{:S(2)}, u32[]{:S(2)}) collective-permute-start(f32[1,8,32,128]{3,2,1,0:T(8,128)S(1)} %get-tuple-element.61), channel_id=1, source_target_pairs={{0,4},{4,0},{8,12},{12,8},{16,20},{20,16},{24,28},{28,24},{1,5},{5... | collective-permute-start | bytes 393224 | tf_op jit(solution)/shard_map/ppermute | solution.py:282
  15.4 8.2 %collective-permute-start.2 = (f32[1,8,32,128]{3,2,1,0:T(8,128)S(1)}, f32[1,8,32,128]{3,2,1,0:T(8,128)S(1)}, u32[]{:S(2)}, u32[]{:S(2)}) collective-permute-start(f32[1,8,32,128]{3,2,1,0:T(8,128)S(1)} %get-tuple-element.62.mine), channel_id=1, source_target_pairs={{0,24},{4,12},{8,0},{12,20},{16,8},{20,28},{24,16},{28,4},{1,25},{... | collective-permute-start | bytes 393224 | tf_op jit(solution)/shard_map/ppermute | solution.py:284
  19.3 9.6 %collective-permute-start.9 = (f32[1,8,32,128]{3,2,1,0:T(8,128)S(1)}, f32[1,8,32,128]{3,2,1,0:T(8,128)S(1)}, u32[]{:S(2)}, u32[]{:S(2)}) collective-permute-start(f32[1,8,32,128]{3,2,1,0:T(8,128)S(1)} %get-tuple-element.39.hi), channel_id=1, source_target_pairs={{0,8},{4,12},{8,16},{12,20},{16,24},{20,28},{24,0},{28,4},{1,9},{5... | collective-permute-start | bytes 393224 | tf_op jit(solution)/shard_map/ppermute | solution.py:303
  20.9 11.2 %collective-permute-start.8 = (f32[1,16,32,128]{3,2,1,0:T(8,128)S(1)}, f32[1,16,32,128]{3,2,1,0:T(8,128)S(1)}, u32[]{:S(2)}, u32[]{:S(2)}) collective-permute-start(f32[1,16,32,128]{3,2,1,0:T(8,128)S(1)} %get-tuple-element.38.lo), channel_id=1, source_target_pairs={{0,24},{4,28},{8,0},{12,4},{16,8},{20,12},{24,16},{28,20},{1,25},{... | collective-permute-start | bytes 786440 | tf_op jit(solution)/shard_map/ppermute | solution.py:304
  24.6 13.9 %collective-permute-start.7 = (f32[1,12,32,128]{3,2,1,0:T(8,128)S(1)}, f32[1,12,32,128]{3,2,1,0:T(8,128)S(1)}, u32[]{:S(2)}, u32[]{:S(2)}) collective-permute-start(f32[1,12,32,128]{3,2,1,0:T(8,128)S(1)} %get-tuple-element.36.lo), channel_id=1, source_target_pairs={{0,24},{4,28},{8,0},{12,4},{16,8},{20,12},{24,16},{28,20},{1,25},{... | collective-permute-start | bytes 589832 | tf_op jit(solution)/shard_map/ppermute | solution.py:304
  28.9 9.6 %collective-permute-start.6 = (f32[1,8,32,128]{3,2,1,0:T(8,128)S(1)}, f32[1,8,32,128]{3,2,1,0:T(8,128)S(1)}, u32[]{:S(2)}, u32[]{:S(2)}) collective-permute-start(f32[1,8,32,128]{3,2,1,0:T(8,128)S(1)} %get-tuple-element.35.hi), channel_id=1, source_target_pairs={{0,8},{4,12},{8,16},{12,20},{16,24},{20,28},{24,0},{28,4},{1,9},{5... | collective-permute-start | bytes 393224 | tf_op jit(solution)/shard_map/ppermute | solution.py:303
  39.9 6.2 %collective-permute-start.10 = (f32[2,2,2,32,128]{4,3,2,1,0:T(8,128)S(1)}, f32[2,2,2,32,128]{4,3,2,1,0:T(8,128)S(1)}, u32[]{:S(2)}, u32[]{:S(2)}) collective-permute-start(f32[2,2,2,32,128]{4,3,2,1,0:T(8,128)S(1)} %get-tuple-element.44), channel_id=1, source_target_pairs={{0,4},{1,5},{2,6},{3,7},{4,0},{5,1},{6,2},{7,3},{8,12},{9,13},{10,... | collective-permute-start | bytes 393224 | tf_op jit(solution)/shard_map/ppermute | solution.py:313
  41.3 5.0 %collective-permute-start.11 = (f32[2,2,2,32,128]{4,3,2,1,0:T(8,128)S(1)}, f32[2,2,2,32,128]{4,3,2,1,0:T(8,128)S(1)}, u32[]{:S(2)}, u32[]{:S(2)}) collective-permute-start(f32[2,2,2,32,128]{4,3,2,1,0:T(8,128)S(1)} %get-tuple-element.45), channel_id=1, source_target_pairs={{0,2},{1,3},{2,0},{3,1},{4,6},{5,7},{6,4},{7,5},{8,10},{9,11},{10,... | collective-permute-start | bytes 393224 | tf_op jit(solution)/shard_map/ppermute | solution.py:313
  42.8 7.3 %collective-permute-start.12 = (f32[2,2,2,32,128]{4,3,2,1,0:T(8,128)S(1)}, f32[2,2,2,32,128]{4,3,2,1,0:T(8,128)S(1)}, u32[]{:S(2)}, u32[]{:S(2)}) collective-permute-start(f32[2,2,2,32,128]{4,3,2,1,0:T(8,128)S(1)} %get-tuple-element.46), channel_id=1, source_target_pairs={{0,6},{1,7},{2,4},{3,5},{4,2},{5,3},{6,0},{7,1},{8,14},{9,15},{10,... | collective-permute-start | bytes 393224 | tf_op jit(solution)/shard_map/ppermute | solution.py:313
  43.5 6.8 %collective-permute-start.13 = (f32[2,2,2,32,128]{4,3,2,1,0:T(8,128)S(1)}, f32[2,2,2,32,128]{4,3,2,1,0:T(8,128)S(1)}, u32[]{:S(2)}, u32[]{:S(2)}) collective-permute-start(f32[2,2,2,32,128]{4,3,2,1,0:T(8,128)S(1)} %get-tuple-element.47), channel_id=1, source_target_pairs={{0,7},{1,6},{2,5},{3,4},{4,3},{5,2},{6,1},{7,0},{8,15},{9,14},{10,... | collective-permute-start | bytes 393224 | tf_op jit(solution)/shard_map/ppermute | solution.py:313
  43.5 10.7 %collective-permute-start.14 = (f32[2,2,2,32,128]{4,3,2,1,0:T(8,128)S(1)}, f32[2,2,2,32,128]{4,3,2,1,0:T(8,128)S(1)}, u32[]{:S(2)}, u32[]{:S(2)}) collective-permute-start(f32[2,2,2,32,128]{4,3,2,1,0:T(8,128)S(1)} %get-tuple-element.48), channel_id=1, source_target_pairs={{0,5},{1,4},{2,7},{3,6},{4,1},{5,0},{6,3},{7,2},{8,13},{9,12},{10,... | collective-permute-start | bytes 393224 | tf_op jit(solution)/shard_map/ppermute | solution.py:313
  46.2 8.0 %collective-permute-start.15 = (f32[2,2,2,32,128]{4,3,2,1,0:T(8,128)S(1)}, f32[2,2,2,32,128]{4,3,2,1,0:T(8,128)S(1)}, u32[]{:S(2)}, u32[]{:S(2)}) collective-permute-start(f32[2,2,2,32,128]{4,3,2,1,0:T(8,128)S(1)} %get-tuple-element.49), channel_id=1, source_target_pairs={{0,3},{1,2},{2,1},{3,0},{4,7},{5,6},{6,5},{7,4},{8,11},{9,10},{10,... | collective-permute-start | bytes 393224 | tf_op jit(solution)/shard_map/ppermute | solution.py:313
  46.3 7.9 %collective-permute-start.16 = (f32[2,2,2,32,128]{4,3,2,1,0:T(8,128)S(1)}, f32[2,2,2,32,128]{4,3,2,1,0:T(8,128)S(1)}, u32[]{:S(2)}, u32[]{:S(2)}) collective-permute-start(f32[2,2,2,32,128]{4,3,2,1,0:T(8,128)S(1)} %get-tuple-element.50), channel_id=1, source_target_pairs={{0,1},{1,0},{2,3},{3,2},{4,5},{5,4},{6,7},{7,6},{8,9},{9,8},{10,11... | collective-permute-start | bytes 393224 | tf_op jit(solution)/shard_map/ppermute | solution.py:313
  55.9 8.3 %collective-permute-start.17 = (f32[2,8,32,128]{3,2,1,0:T(8,128)S(1)}, f32[2,8,32,128]{3,2,1,0:T(8,128)S(1)}, u32[]{:S(2)}, u32[]{:S(2)}) collective-permute-start(f32[2,8,32,128]{3,2,1,0:T(8,128)S(1)} %get-tuple-element.54), channel_id=1, source_target_pairs={{0,4},{4,0},{8,12},{12,8},{16,20},{20,16},{24,28},{28,24},{1,5},{5... | collective-permute-start | bytes 786440 | tf_op jit(solution)/shard_map/ppermute | solution.py:329
  56.6 11.6 %all-to-all-start = ((f32[32,1,128]{2,1,0:T(1,128)}), f32[32,1,128]{2,1,0:T(1,128)S(1)}, u32[]{:S(2)}, u32[]{:S(2)}) async-start(f32[32,1,128]{2,1,0:T(1,128)} %gram.1), calls=%async_computation | async-start | bytes 32768 | tf_op jit(solution)/shard_map/all_to_all | solution.py:330

commit v11 on v6

--- a/solution.py
+++ b/solution.py
@@ -175,21 +175,21 @@
 def gram(*refs):
     *xs, out_ref, part, blocks = refs
     orbs = part.shape[1]
-    half, peers, _, per, ny, nz = blocks.shape
+    half, peers, reach, nz = blocks.shape
+    rows = xs[0].shape[1] * xs[0].shape[2]
     me = places()[2]
     early = len(EARLY)
     for o in range(half):
         for k, x in zip(EARLY, xs[early * o :]):
-            blocks[o, jnp.bitwise_xor(me, k)] = x[...]
+            blocks[o, jnp.bitwise_xor(me, k), : 2 * rows] = x[...].reshape(2 * rows, nz)
         for k, x in zip(LATE, xs[early * half :]):
-            blocks[o, jnp.bitwise_xor(me, k)] = x[o]
-    rows = per * ny
-    flat = blocks.reshape(half * peers * 2 * rows, nz)
+            blocks[o, jnp.bitwise_xor(me, k), : 2 * rows] = x[o].reshape(2 * rows, nz)
+    flat = blocks.reshape(half * peers * reach, nz)
     fields = jnp.concatenate(
         [
             jnp.concatenate(
                 [
-                    flat[pl.ds((o * peers * 2 + which) * rows + r, peers, stride=2 * rows), :]
+                    flat[pl.ds(o * peers * reach + which * rows + r, peers, stride=reach), :]
                     for which in range(2)
                     for o in range(half)
                 ],
@@ -329,14 +329,15 @@
         last_three, (*second[1], home, late), outs, scratch, 1.5, "filter_3_4_hamiltonian"
     )
     tied = lax.optimization_barrier((*blocks[early:-1], *early_a))
-    late = [peer(x, k) for k, x in zip(LATE[:-1], tied)] + blocks[-1:]
     early_b = [peer(x, k) for k, x in zip(EARLY, blocks)]
+    to_sibling, early_b[-1] = lax.optimization_barrier((tied[LATE.index(1)], early_b[-1]))
+    late = [peer(to_sibling if k == 1 else x, k) for k, x in zip(LATE[:-1], tied)] + blocks[-1:]
     xs = [*tied[-early:], *early_b, *late]
     (sums,) = call(
         gram,
         xs,
         [(size * orbs, 1, 2 * own_orbs * count)],
-        [pltpu.VMEM((2, count, nz), f32), pltpu.VMEM((half, group, *block), f32)],
+        [pltpu.VMEM((2, count, nz), f32), pltpu.VMEM((half, group, 2 * per * ny + 8, nz), f32)],
         1.3,
         "gram",
     )

time: 71.7 us -> 73.7 us (1.028)
  starting transfers between devices: 38 us -> 40.2 us
    ppermute x10, starting transfers between devices: 10.2 us -> 11.3 us  [peer(): lax.ppermute(x, ('mem', 'orb'), [(t, t ^ k) for t in range(group)])]
where the time goes in v11:
time: 73.7 us; the launch traced here: 73.5 us
  starting transfers between devices  40.2 us (55%)
  waiting for transfers between devices  23.1 us (31%)
  Pallas kernels  7.35 us (10%)
  local copies, waits for them, and re-layouts  1.18 us (2%)
  other arithmetic  0.9 us (1%)
  between operations  0.76 us (1%)
    ppermute x10, starting transfers between devices, peer(): lax.ppermute(x, ('mem', 'orb'), [(t, t ^ k) for t in range(group)])  11.3 us
    ppermute x10, waiting for transfers between devices, peer(): lax.ppermute(x, ('mem', 'orb'), [(t, t ^ k) for t in range(group)])  7.77 us
    pallas_call x7, Pallas kernels, call(): pl.pallas_call(body, out_shape=[s if isinstance(s, jax.ShapeDtypeStruct)...  7.35 us
    all_to_all x1, starting transfers between devices, per_device(): sums = lax.all_to_all(sums, ('pair', 'mem', 'orb'), 0, 0, tiled=True)  7.31 us
    ppermute x2, starting transfers between devices, per_device(): rhi = lax.ppermute(lo, grid_axes, down)  6.88 us
    all_to_all x1, waiting for transfers between devices, per_device(): sums = lax.all_to_all(sums, ('pair', 'mem', 'orb'), 0, 0, tiled=True)  6.29 us
    ppermute x2, starting transfers between devices, per_device(): rb = lax.ppermute(b, grid_axes, cross)  5.91 us
    ppermute x2, starting transfers between devices, per_device(): ra = lax.ppermute(a, grid_axes, swap)  3.77 us
  transfers between devices with their start and end apart: 22, of which 9 were waited for; matrix products, arithmetic and copies ran while one was open for 1% of the time, Pallas kernels for 7%

profile of v11, /device:TPU:0, one launch (start us, length us, event | category | flops | bytes accessed | tf_op | source)
XLA Modules:
  0.0 73.5 jit_solution(9187933588843544504)
XLA Ops:
  0.6 1.2 %constant_dynamic-slice_fusion = (f32[1,8,32,128]{3,2,1,0:T(8,128)S(1)}, f32[1,8,32,128]{3,2,1,0:T(8,128)S(1)}, f32[1,8,32,128]{3,2,1,0:T(8,128)S(1)}, f32[1,8,32,128]{3,2,1,0:T(8,128)S(1)}) fusion(f32[4,8,32,128]{3,2,1,0:T(8,128)} %param.2, s32[]{:T(128)S(6)} %select_n.33, s32[]{:T(128)S(6)} %select_n.29, s32[]{:T(128)S(6)} %select_n.28, s32[]{:T(128)S(6)} %select_n.30), kind=kLoop, calls=%fused_computation.5 | loop fusion | bytes 1048592 | tf_op jit(solution)/shard_map/dynamic_slice | solution.py:286
  1.9 3.0 %collective-permute-start.3 = (f32[1,16,32,128]{3,2,1,0:T(8,128)S(1)}, f32[1,16,32,128]{3,2,1,0:T(8,128)S(1)}, u32[]{:S(2)}, u32[]{:S(2)}) collective-permute-start(f32[1,16,32,128]{3,2,1,0:T(8,128)S(1)} %pad_maximum_fusion), channel_id=1, source_target_pairs={{0,4},{4,0},{8,12},{12,8},{16,20},{20,16},{24,28},{28,24},{1,5},{5... | collective-permute-start | bytes 786440 | tf_op jit(solution)/shard_map/ppermute | solution.py:290
  4.9 3.6 %collective-permute-start.4 = (f32[1,12,32,128]{3,2,1,0:T(8,128)S(1)}, f32[1,12,32,128]{3,2,1,0:T(8,128)S(1)}, u32[]{:S(2)}, u32[]{:S(2)}) collective-permute-start(f32[1,12,32,128]{3,2,1,0:T(8,128)S(1)} %get-tuple-element.85), channel_id=1, source_target_pairs={{0,28},{4,8},{8,4},{12,16},{16,12},{20,24},{24,20},{28,0},{1,29},{... | collective-permute-start | bytes 589832 | tf_op jit(solution)/shard_map/ppermute | solution.py:291
  9.0 2.3 %collective-permute-start.1 = (f32[1,8,32,128]{3,2,1,0:T(8,128)S(1)}, f32[1,8,32,128]{3,2,1,0:T(8,128)S(1)}, u32[]{:S(2)}, u32[]{:S(2)}) collective-permute-start(f32[1,8,32,128]{3,2,1,0:T(8,128)S(1)} %get-tuple-element.82), channel_id=1, source_target_pairs={{0,28},{4,8},{8,4},{12,16},{16,12},{20,24},{24,20},{28,0},{1,29},{... | collective-permute-start | bytes 393224 | tf_op jit(solution)/shard_map/ppermute | solution.py:291
  12.0 3.5 %collective-permute-done.4.rb = f32[1,12,32,128]{3,2,1,0:T(8,128)S(1)} collective-permute-done((f32[1,12,32,128]{3,2,1,0:T(8,128)S(1)}, f32[1,12,32,128]{3,2,1,0:T(8,128)S(1)}, u32[]{:S(2)}, u32[]{:S(2)}) %collective-permute-start.4) | collective-permute-done | bytes 196640 | tf_op jit(solution)/shard_map/ppermute | solution.py:291
  15.6 1.8 %collective-permute-start.2 = (f32[1,8,32,128]{3,2,1,0:T(8,128)S(1)}, f32[1,8,32,128]{3,2,1,0:T(8,128)S(1)}, u32[]{:S(2)}, u32[]{:S(2)}) collective-permute-start(f32[1,8,32,128]{3,2,1,0:T(8,128)S(1)} %get-tuple-element.83.mine), channel_id=1, source_target_pairs={{0,24},{4,12},{8,0},{12,20},{16,8},{20,28},{24,16},{28,4},{1,25},{... | collective-permute-start | bytes 393224 | tf_op jit(solution)/shard_map/ppermute | solution.py:292
  19.5 1.6 %collective-permute-start.9 = (f32[1,8,32,128]{3,2,1,0:T(8,128)S(1)}, f32[1,8,32,128]{3,2,1,0:T(8,128)S(1)}, u32[]{:S(2)}, u32[]{:S(2)}) collective-permute-start(f32[1,8,32,128]{3,2,1,0:T(8,128)S(1)} %get-tuple-element.49.hi), channel_id=1, source_target_pairs={{0,8},{4,12},{8,16},{12,20},{16,24},{20,28},{24,0},{28,4},{1,9},{5... | collective-permute-start | bytes 393224 | tf_op jit(solution)/shard_map/ppermute | solution.py:310
  21.0 2.5 %collective-permute-start.8 = (f32[1,16,32,128]{3,2,1,0:T(8,128)S(1)}, f32[1,16,32,128]{3,2,1,0:T(8,128)S(1)}, u32[]{:S(2)}, u32[]{:S(2)}) collective-permute-start(f32[1,16,32,128]{3,2,1,0:T(8,128)S(1)} %get-tuple-element.48.lo), channel_id=1, source_target_pairs={{0,24},{4,28},{8,0},{12,4},{16,8},{20,12},{24,16},{28,20},{1,25},{... | collective-permute-start | bytes 786440 | tf_op jit(solution)/shard_map/ppermute | solution.py:311
  24.7 4.3 %collective-permute-start.7 = (f32[1,12,32,128]{3,2,1,0:T(8,128)S(1)}, f32[1,12,32,128]{3,2,1,0:T(8,128)S(1)}, u32[]{:S(2)}, u32[]{:S(2)}) collective-permute-start(f32[1,12,32,128]{3,2,1,0:T(8,128)S(1)} %get-tuple-element.46.lo), channel_id=1, source_target_pairs={{0,24},{4,28},{8,0},{12,4},{16,8},{20,12},{24,16},{28,20},{1,25},{... | collective-permute-start | bytes 589832 | tf_op jit(solution)/shard_map/ppermute | solution.py:311
  29.1 3.1 %collective-permute-done.8.rhi.v_above = f32[1,16,32,128]{3,2,1,0:T(8,128)S(1)} collective-permute-done((f32[1,16,32,128]{3,2,1,0:T(8,128)S(1)}, f32[1,16,32,128]{3,2,1,0:T(8,128)S(1)}, u32[]{:S(2)}, u32[]{:S(2)}) %collective-permute-start.8) | collective-permute-done | bytes 262176 | tf_op jit(solution)/shard_map/ppermute | solution.py:311
  32.2 1.4 %filter_3_4_hamiltonian.2 = (f32[2,8,32,128]{3,2,1,0:T(8,128)S(1)}, f32[5,2,2,32,128]{4,3,2,1,0:T(8,128)S(1)}, f32[2,2,32,128]{3,2,1,0:T(8,128)S(1)}, f32[2,2,32,128]{3,2,1,0:T(8,128)S(1)}, f32[2,2,32,128]{3,2,1,0:T(8,128)S(1)}) custom-call(bf16[128,384]{1,0:T(8,128)(2,1)S(1)} %get-tuple-element.42.ymat, bf16[384,128]{1,0:T(8,128)(2,1)S(1)} %get-tuple-element.43.zmat, ...), custom_call_target="tpu_custom_call" | custom-call | flops 1500000000 | bytes 5250000 | tf_op jit(solution)/shard_map/filter_3_4_hamiltonian/pallas_call | solution.py:246
  33.6 3.2 %collective-permute-start.10 = (f32[2,2,32,128]{3,2,1,0:T(8,128)S(1)}, f32[2,2,32,128]{3,2,1,0:T(8,128)S(1)}, u32[]{:S(2)}, u32[]{:S(2)}) collective-permute-start(f32[2,2,32,128]{3,2,1,0:T(8,128)S(1)} %get-tuple-element.58), channel_id=1, source_target_pairs={{0,6},{1,7},{2,4},{3,5},{4,2},{5,3},{6,0},{7,1},{8,14},{9,15},{10,... | collective-permute-start | bytes 196616 | tf_op jit(solution)/shard_map/ppermute | solution.py:320
  37.4 1.3 %collective-permute-done.6.rlo = f32[1,8,32,128]{3,2,1,0:T(8,128)S(1)} collective-permute-done((f32[1,8,32,128]{3,2,1,0:T(8,128)S(1)}, f32[1,8,32,128]{3,2,1,0:T(8,128)S(1)}, u32[]{:S(2)}, u32[]{:S(2)}) %collective-permute-start.6) | collective-permute-done | bytes 131104 | tf_op jit(solution)/shard_map/ppermute | solution.py:310
  38.7 1.4 %filter_3_4_hamiltonian.3 = (f32[2,8,32,128]{3,2,1,0:T(8,128)S(1)}, f32[2,8,32,128]{3,2,1,0:T(8,128)S(1)}, f32[2,2,32,128]{3,2,1,0:T(8,128)S(1)}, f32[2,2,32,128...) custom-call(bf16[128,384]{1,0:T(8,128)(2,1)S(1)} %get-tuple-element., ...), custom_call_target="tpu_custom_call" | custom-call | flops 1500000000 | bytes 5250000 | tf_op jit(solution)/shard_map/filter_3_4_hamiltonian/pallas_call | solution.py:246
  40.0 1.6 %collective-permute-start.15 = (f32[2,2,32,128]{3,2,1,0:T(8,128)S(1)}, f32[2,2,32,128]{3,2,1,0:T(8,128)S(1)}, u32[]{:S(2)}, u32[]{:S(2)}) collective-permute-start(f32[2,2,32,128]{3,2,1,0:T(8,128)S(1)} %get-tuple-element.67), channel_id=1, source_target_pairs={{0,2},{1,3},{2,0},{3,1},{4,6},{5,7},{6,4},{7,5},{8,10},{9,11},{10,... | collective-permute-start | bytes 196616 | tf_op jit(solution)/shard_map/ppermute | solution.py:320
  41.6 1.3 %collective-permute-start.13 = (f32[2,2,32,128]{3,2,1,0:T(8,128)S(1)}, f32[2,2,32,128]{3,2,1,0:T(8,128)S(1)}, u32[]{:S(2)}, u32[]{:S(2)}) collective-permute-start(f32[2,2,32,128]{3,2,1,0:T(8,128)S(1)} %get-tuple-element.64), channel_id=1, source_target_pairs={{0,6},{1,7},{2,4},{3,5},{4,2},{5,3},{6,0},{7,1},{8,14},{9,15},{10,... | collective-permute-start | bytes 196616 | tf_op jit(solution)/shard_map/ppermute | solution.py:320
  42.9 1.5 %collective-permute-done.15.refs_5_ = f32[2,2,32,128]{3,2,1,0:T(8,128)S(1)} collective-permute-done((f32[2,2,32,128]{3,2,1,0:T(8,128)S(1)}, f32[2,2,32,128]{3,2,1,0:T(8,128)S(1)}, u32[]{:S(2)}, u32[]{:S(2)}) %collective-permute-start.15) | collective-permute-done | bytes 65568 | tf_op jit(solution)/shard_map/ppermute | solution.py:320
  44.4 2.3 %collective-permute-start.16 = (f32[2,2,2,32,128]{4,3,2,1,0:T(8,128)S(1)}, f32[2,2,2,32,128]{4,3,2,1,0:T(8,128)S(1)}, u32[]{:S(2)}, u32[]{:S(2)}) collective-permute-start(f32[2,2,2,32,128]{4,3,2,1,0:T(8,128)S(1)} %get-tuple-element.69), channel_id=1, source_target_pairs={{0,7},{1,6},{2,5},{3,4},{4,3},{5,2},{6,1},{7,0},{8,15},{9,14},{10,... | collective-permute-start | bytes 393224 | tf_op jit(solution)/shard_map/ppermute | solution.py:320
  47.7 1.3 %collective-permute-start.14 = (f32[2,2,32,128]{3,2,1,0:T(8,128)S(1)}, f32[2,2,32,128]{3,2,1,0:T(8,128)S(1)}, u32[]{:S(2)}, u32[]{:S(2)}) collective-permute-start(f32[2,2,32,128]{3,2,1,0:T(8,128)S(1)} %get-tuple-element.65), channel_id=1, source_target_pairs={{0,4},{1,5},{2,6},{3,7},{4,0},{5,1},{6,2},{7,3},{8,12},{9,13},{10,... | collective-permute-start | bytes 196616 | tf_op jit(solution)/shard_map/ppermute | solution.py:320
  49.0 6.3 %collective-permute-done.14.refs_4_ = f32[2,2,32,128]{3,2,1,0:T(8,128)S(1)} collective-permute-done((f32[2,2,32,128]{3,2,1,0:T(8,128)S(1)}, f32[2,2,32,128]{3,2,1,0:T(8,128)S(1)}, u32[]{:S(2)}, u32[]{:S(2)}) %collective-permute-start.14) | collective-permute-done | bytes 65568 | tf_op jit(solution)/shard_map/ppermute | solution.py:320
  55.3 1.7 %gram.1 = f32[32,1,128]{2,1,0:T(1,128)} custom-call(f32[2,2,32,128]{3,2,1,0:T(8,128)S(1)} %collective-permute-done.10.refs_0_, f32[2,2,32,128]{3,2,1,0:T(8,128)S(1)} %collective-permute-done.11.refs_1_, f32[2,2,32,128]{3,2,1,0:T(8,128)S(1)} %collective-permute-done.12.refs_2_, f32[2,2,32,128]{3,2,1,0:T(8,128)S(1)} %collective-permute-done.13.refs_3_, ...), custom_call_target="tpu_custom_call" | custom-call | flops 1300000000 | bytes 4550000 | tf_op jit(solution)/shard_map/gram/pallas_call | solution.py:246
  57.0 1.3 %collective-permute-start.20 = (f32[2,8,32,128]{3,2,1,0:T(8,128)S(1)}, f32[2,8,32,128]{3,2,1,0:T(8,128)S(1)}, u32[]{:S(2)}, u32[]{:S(2)}) collective-permute-start(f32[2,8,32,128]{3,2,1,0:T(8,128)S(1)} %get-tuple-element.76), channel_id=1, source_target_pairs={{0,4},{4,0},{8,12},{12,8},{16,20},{20,16},{24,28},{28,24},{1,5},{5... | collective-permute-start | bytes 786440 | tf_op jit(solution)/shard_map/ppermute | solution.py:345
  58.3 7.3 %all-to-all-start = ((f32[32,1,128]{2,1,0:T(1,128)}), f32[32,1,128]{2,1,0:T(1,128)S(1)}, u32[]{:S(2)}, u32[]{:S(2)}) async-start(f32[32,1,128]{2,1,0:T(1,128)} %gram.1), calls=%async_computation | async-start | bytes 32768 | tf_op jit(solution)/shard_map/all_to_all | solution.py:346
  66.5 6.3 %all-to-all-done.x_ref = f32[32,1,128]{2,1,0:T(1,128)S(1)} async-done(((f32[32,1,128]{2,1,0:T(1,128)}), f32[32,1,128]{2,1,0:T(1,128)S(1)}, u32[]{:S(2)}, u32[]{:S(2)}) %all-to-all-start) | async-done | bytes 16416 | tf_op jit(solution)/shard_map/all_to_all | solution.py:346
  (34 shorter events, 7.7 us)
Async XLA Ops:
  0.6 1.2 %copy-start = (f32[8,32,128]{2,1,0:T(8,128)S(1)}, f32[8,32,128]{2,1,0:T(8,128)}, u32[]{:S(2)}) copy-start(f32[8,32,128]{2,1,0:T(8,128)} %refs_0_.1) | copy-start | bytes 393220
  1.9 16.6 %collective-permute-start.3 = (f32[1,16,32,128]{3,2,1,0:T(8,128)S(1)}, f32[1,16,32,128]{3,2,1,0:T(8,128)S(1)}, u32[]{:S(2)}, u32[]{:S(2)}) collective-permute-start(f32[1,16,32,128]{3,2,1,0:T(8,128)S(1)} %pad_maximum_fusion), channel_id=1, source_target_pairs={{0,4},{4,0},{8,12},{12,8},{16,20},{20,16},{24,28},{28,24},{1,5},{5... | collective-permute-start | bytes 786440 | tf_op jit(solution)/shard_map/ppermute | solution.py:290
  4.9 10.6 %collective-permute-start.4 = (f32[1,12,32,128]{3,2,1,0:T(8,128)S(1)}, f32[1,12,32,128]{3,2,1,0:T(8,128)S(1)}, u32[]{:S(2)}, u32[]{:S(2)}) collective-permute-start(f32[1,12,32,128]{3,2,1,0:T(8,128)S(1)} %get-tuple-element.85), channel_id=1, source_target_pairs={{0,28},{4,8},{8,4},{12,16},{16,12},{20,24},{24,20},{28,0},{1,29},{... | collective-permute-start | bytes 589832 | tf_op jit(solution)/shard_map/ppermute | solution.py:291
  8.6 9.6 %collective-permute-start.5 = (f32[1,12,32,128]{3,2,1,0:T(8,128)S(1)}, f32[1,12,32,128]{3,2,1,0:T(8,128)S(1)}, u32[]{:S(2)}, u32[]{:S(2)}) collective-permute-start(f32[1,12,32,128]{3,2,1,0:T(8,128)S(1)} %get-tuple-element.86.mine), channel_id=1, source_target_pairs={{0,24},{4,12},{8,0},{12,20},{16,8},{20,28},{24,16},{28,4},{1,25},{... | collective-permute-start | bytes 589832 | tf_op jit(solution)/shard_map/ppermute | solution.py:292
  9.0 14.6 %collective-permute-start.1 = (f32[1,8,32,128]{3,2,1,0:T(8,128)S(1)}, f32[1,8,32,128]{3,2,1,0:T(8,128)S(1)}, u32[]{:S(2)}, u32[]{:S(2)}) collective-permute-start(f32[1,8,32,128]{3,2,1,0:T(8,128)S(1)} %get-tuple-element.82), channel_id=1, source_target_pairs={{0,28},{4,8},{8,4},{12,16},{16,12},{20,24},{24,20},{28,0},{1,29},{... | collective-permute-start | bytes 393224 | tf_op jit(solution)/shard_map/ppermute | solution.py:291
  11.3 12.3 %collective-permute-start = (f32[1,8,32,128]{3,2,1,0:T(8,128)S(1)}, f32[1,8,32,128]{3,2,1,0:T(8,128)S(1)}, u32[]{:S(2)}, u32[]{:S(2)}) collective-permute-start(f32[1,8,32,128]{3,2,1,0:T(8,128)S(1)} %get-tuple-element.82), channel_id=1, source_target_pairs={{0,4},{4,0},{8,12},{12,8},{16,20},{20,16},{24,28},{28,24},{1,5},{5... | collective-permute-start | bytes 393224 | tf_op jit(solution)/shard_map/ppermute | solution.py:290
  15.6 8.2 %collective-permute-start.2 = (f32[1,8,32,128]{3,2,1,0:T(8,128)S(1)}, f32[1,8,32,128]{3,2,1,0:T(8,128)S(1)}, u32[]{:S(2)}, u32[]{:S(2)}) collective-permute-start(f32[1,8,32,128]{3,2,1,0:T(8,128)S(1)} %get-tuple-element.83.mine), channel_id=1, source_target_pairs={{0,24},{4,12},{8,0},{12,20},{16,8},{20,28},{24,16},{28,4},{1,25},{... | collective-permute-start | bytes 393224 | tf_op jit(solution)/shard_map/ppermute | solution.py:292
  19.5 9.6 %collective-permute-start.9 = (f32[1,8,32,128]{3,2,1,0:T(8,128)S(1)}, f32[1,8,32,128]{3,2,1,0:T(8,128)S(1)}, u32[]{:S(2)}, u32[]{:S(2)}) collective-permute-start(f32[1,8,32,128]{3,2,1,0:T(8,128)S(1)} %get-tuple-element.49.hi), channel_id=1, source_target_pairs={{0,8},{4,12},{8,16},{12,20},{16,24},{20,28},{24,0},{28,4},{1,9},{5... | collective-permute-start | bytes 393224 | tf_op jit(solution)/shard_map/ppermute | solution.py:310
  21.0 11.2 %collective-permute-start.8 = (f32[1,16,32,128]{3,2,1,0:T(8,128)S(1)}, f32[1,16,32,128]{3,2,1,0:T(8,128)S(1)}, u32[]{:S(2)}, u32[]{:S(2)}) collective-permute-start(f32[1,16,32,128]{3,2,1,0:T(8,128)S(1)} %get-tuple-element.48.lo), channel_id=1, source_target_pairs={{0,24},{4,28},{8,0},{12,4},{16,8},{20,12},{24,16},{28,20},{1,25},{... | collective-permute-start | bytes 786440 | tf_op jit(solution)/shard_map/ppermute | solution.py:311
  24.7 13.9 %collective-permute-start.7 = (f32[1,12,32,128]{3,2,1,0:T(8,128)S(1)}, f32[1,12,32,128]{3,2,1,0:T(8,128)S(1)}, u32[]{:S(2)}, u32[]{:S(2)}) collective-permute-start(f32[1,12,32,128]{3,2,1,0:T(8,128)S(1)} %get-tuple-element.46.lo), channel_id=1, source_target_pairs={{0,24},{4,28},{8,0},{12,4},{16,8},{20,12},{24,16},{28,20},{1,25},{... | collective-permute-start | bytes 589832 | tf_op jit(solution)/shard_map/ppermute | solution.py:311
  29.1 9.6 %collective-permute-start.6 = (f32[1,8,32,128]{3,2,1,0:T(8,128)S(1)}, f32[1,8,32,128]{3,2,1,0:T(8,128)S(1)}, u32[]{:S(2)}, u32[]{:S(2)}) collective-permute-start(f32[1,8,32,128]{3,2,1,0:T(8,128)S(1)} %get-tuple-element.45.hi), channel_id=1, source_target_pairs={{0,8},{4,12},{8,16},{12,20},{16,24},{20,28},{24,0},{28,4},{1,9},{5... | collective-permute-start | bytes 393224 | tf_op jit(solution)/shard_map/ppermute | solution.py:310
  33.6 9.3 %collective-permute-start.10 = (f32[2,2,32,128]{3,2,1,0:T(8,128)S(1)}, f32[2,2,32,128]{3,2,1,0:T(8,128)S(1)}, u32[]{:S(2)}, u32[]{:S(2)}) collective-permute-start(f32[2,2,32,128]{3,2,1,0:T(8,128)S(1)} %get-tuple-element.58), channel_id=1, source_target_pairs={{0,6},{1,7},{2,4},{3,5},{4,2},{5,3},{6,0},{7,1},{8,14},{9,15},{10,... | collective-permute-start | bytes 196616 | tf_op jit(solution)/shard_map/ppermute | solution.py:320
  36.7 6.2 %collective-permute-start.11 = (f32[2,2,32,128]{3,2,1,0:T(8,128)S(1)}, f32[2,2,32,128]{3,2,1,0:T(8,128)S(1)}, u32[]{:S(2)}, u32[]{:S(2)}) collective-permute-start(f32[2,2,32,128]{3,2,1,0:T(8,128)S(1)} %get-tuple-element.59), channel_id=1, source_target_pairs={{0,4},{1,5},{2,6},{3,7},{4,0},{5,1},{6,2},{7,3},{8,12},{9,13},{10,... | collective-permute-start | bytes 196616 | tf_op jit(solution)/shard_map/ppermute | solution.py:320
  36.7 6.2 %collective-permute-start.12 = (f32[2,2,32,128]{3,2,1,0:T(8,128)S(1)}, f32[2,2,32,128]{3,2,1,0:T(8,128)S(1)}, u32[]{:S(2)}, u32[]{:S(2)}) collective-permute-start(f32[2,2,32,128]{3,2,1,0:T(8,128)S(1)} %get-tuple-element.60), channel_id=1, source_target_pairs={{0,2},{1,3},{2,0},{3,1},{4,6},{5,7},{6,4},{7,5},{8,10},{9,11},{10,... | collective-permute-start | bytes 196616 | tf_op jit(solution)/shard_map/ppermute | solution.py:320
  40.0 4.3 %collective-permute-start.15 = (f32[2,2,32,128]{3,2,1,0:T(8,128)S(1)}, f32[2,2,32,128]{3,2,1,0:T(8,128)S(1)}, u32[]{:S(2)}, u32[]{:S(2)}) collective-permute-start(f32[2,2,32,128]{3,2,1,0:T(8,128)S(1)} %get-tuple-element.67), channel_id=1, source_target_pairs={{0,2},{1,3},{2,0},{3,1},{4,6},{5,7},{6,4},{7,5},{8,10},{9,11},{10,... | collective-permute-start | bytes 196616 | tf_op jit(solution)/shard_map/ppermute | solution.py:320
  41.6 6.1 %collective-permute-start.13 = (f32[2,2,32,128]{3,2,1,0:T(8,128)S(1)}, f32[2,2,32,128]{3,2,1,0:T(8,128)S(1)}, u32[]{:S(2)}, u32[]{:S(2)}) collective-permute-start(f32[2,2,32,128]{3,2,1,0:T(8,128)S(1)} %get-tuple-element.64), channel_id=1, source_target_pairs={{0,6},{1,7},{2,4},{3,5},{4,2},{5,3},{6,0},{7,1},{8,14},{9,15},{10,... | collective-permute-start | bytes 196616 | tf_op jit(solution)/shard_map/ppermute | solution.py:320
  44.4 10.9 %collective-permute-start.19 = (f32[2,2,2,32,128]{4,3,2,1,0:T(8,128)S(1)}, f32[2,2,2,32,128]{4,3,2,1,0:T(8,128)S(1)}, u32[]{:S(2)}, u32[]{:S(2)}) collective-permute-start(f32[2,2,2,32,128]{4,3,2,1,0:T(8,128)S(1)} %get-tuple-element.72), channel_id=1, source_target_pairs={{0,1},{1,0},{2,3},{3,2},{4,5},{5,4},{6,7},{7,6},{8,9},{9,8},{10,11... | collective-permute-start | bytes 393224 | tf_op jit(solution)/shard_map/ppermute | solution.py:320
  44.4 10.9 %collective-permute-start.16 = (f32[2,2,2,32,128]{4,3,2,1,0:T(8,128)S(1)}, f32[2,2,2,32,128]{4,3,2,1,0:T(8,128)S(1)}, u32[]{:S(2)}, u32[]{:S(2)}) collective-permute-start(f32[2,2,2,32,128]{4,3,2,1,0:T(8,128)S(1)} %get-tuple-element.69), channel_id=1, source_target_pairs={{0,7},{1,6},{2,5},{3,4},{4,3},{5,2},{6,1},{7,0},{8,15},{9,14},{10,... | collective-permute-start | bytes 393224 | tf_op jit(solution)/shard_map/ppermute | solution.py:320
  46.7 8.6 %collective-permute-start.17 = (f32[2,2,2,32,128]{4,3,2,1,0:T(8,128)S(1)}, f32[2,2,2,32,128]{4,3,2,1,0:T(8,128)S(1)}, u32[]{:S(2)}, u32[]{:S(2)}) collective-permute-start(f32[2,2,2,32,128]{4,3,2,1,0:T(8,128)S(1)} %get-tuple-element.70), channel_id=1, source_target_pairs={{0,5},{1,4},{2,7},{3,6},{4,1},{5,0},{6,3},{7,2},{8,13},{9,12},{10,... | collective-permute-start | bytes 393224 | tf_op jit(solution)/shard_map/ppermute | solution.py:320
  47.1 8.3 %collective-permute-start.18 = (f32[2,2,2,32,128]{4,3,2,1,0:T(8,128)S(1)}, f32[2,2,2,32,128]{4,3,2,1,0:T(8,128)S(1)}, u32[]{:S(2)}, u32[]{:S(2)}) collective-permute-start(f32[2,2,2,32,128]{4,3,2,1,0:T(8,128)S(1)} %get-tuple-element.71), channel_id=1, source_target_pairs={{0,3},{1,2},{2,1},{3,0},{4,7},{5,6},{6,5},{7,4},{8,11},{9,10},{10,... | collective-permute-start | bytes 393224 | tf_op jit(solution)/shard_map/ppermute | solution.py:320
  47.7 7.6 %collective-permute-start.14 = (f32[2,2,32,128]{3,2,1,0:T(8,128)S(1)}, f32[2,2,32,128]{3,2,1,0:T(8,128)S(1)}, u32[]{:S(2)}, u32[]{:S(2)}) collective-permute-start(f32[2,2,32,128]{3,2,1,0:T(8,128)S(1)} %get-tuple-element.65), channel_id=1, source_target_pairs={{0,4},{1,5},{2,6},{3,7},{4,0},{5,1},{6,2},{7,3},{8,12},{9,13},{10,... | collective-permute-start | bytes 196616 | tf_op jit(solution)/shard_map/ppermute | solution.py:320
  57.0 8.6 %collective-permute-start.20 = (f32[2,8,32,128]{3,2,1,0:T(8,128)S(1)}, f32[2,8,32,128]{3,2,1,0:T(8,128)S(1)}, u32[]{:S(2)}, u32[]{:S(2)}) collective-permute-start(f32[2,8,32,128]{3,2,1,0:T(8,128)S(1)} %get-tuple-element.76), channel_id=1, source_target_pairs={{0,4},{4,0},{8,12},{12,8},{16,20},{20,16},{24,28},{28,24},{1,5},{5... | collective-permute-start | bytes 786440 | tf_op jit(solution)/shard_map/ppermute | solution.py:345
  58.3 14.5 %all-to-all-start = ((f32[32,1,128]{2,1,0:T(1,128)}), f32[32,1,128]{2,1,0:T(1,128)S(1)}, u32[]{:S(2)}, u32[]{:S(2)}) async-start(f32[32,1,128]{2,1,0:T(1,128)} %gram.1), calls=%async_computation | async-start | bytes 32768 | tf_op jit(solution)/shard_map/all_to_all | solution.py:346

commit v12 on v9

--- a/solution.py
+++ b/solution.py
@@ -328,7 +328,6 @@
     back = lax.ppermute(send, grid_axes, swap)
     sums = lax.all_to_all(sums, ("pair", "mem", "orb"), 0, 0, tiled=True)
     filtered = jnp.where(m == 0, jnp.concatenate([keep, back]), jnp.concatenate([back, keep]))
-    sums, filtered = lax.optimization_barrier((sums, filtered))
     corr, ham = call(
         functools.partial(finish, float(cells_x * ny * nz)), (sums,), [(own_orbs, count)] * 2, [], 0.3, "finish"
     )

time: 68.6 us -> 68.7 us (level)
  blocking collectives: 0 us -> 11.9 us
  waiting for transfers between devices: 25.5 us -> 19.2 us
  starting transfers between devices: 32.7 us -> 27.9 us
    all_to_all x0 -> x1, blocking collectives: none -> 11.9 us  [per_device(): sums = lax.all_to_all(sums, ('pair', 'mem', 'orb'), 0, 0, tiled=True)]
    all_to_all x1 -> x0, starting transfers between devices: 4.95 us -> none  [per_device(): sums = lax.all_to_all(sums, ('pair', 'mem', 'orb'), 0, 0, tiled=True)]
    all_to_all x1 -> x0, waiting for transfers between devices: 3.51 us -> none  [per_device(): sums = lax.all_to_all(sums, ('pair', 'mem', 'orb'), 0, 0, tiled=True)]
    ppermute x1, waiting for transfers between devices: 2.79 us -> 0.01 us  [per_device(): back = lax.ppermute(send, grid_axes, swap)]
  transfers between devices with their start and end apart: 19 -> 18, of which waited for: 13 -> 11; matrix products, arithmetic and copies ran while one was open for 1% -> 0% of each run, Pallas kernels for 5% -> 6%
where the time goes in v12:
time: 68.7 us; the launch traced here: 68.6 us
  starting transfers between devices  27.9 us (41%)
  waiting for transfers between devices  19.2 us (28%)
  blocking collectives  11.9 us (17%)
  Pallas kernels  6.75 us (10%)
  local copies, waits for them, and re-layouts  1.18 us (2%)
  other arithmetic  0.9 us (1%)
  between operations  0.73 us (1%)
    all_to_all x1, blocking collectives, per_device(): sums = lax.all_to_all(sums, ('pair', 'mem', 'orb'), 0, 0, tiled=True)  11.9 us
    ppermute x2, starting transfers between devices, per_device(): rhi = lax.ppermute(lo, grid_axes, down)  6.88 us
    pallas_call x7, Pallas kernels, call(): pl.pallas_call(body, out_shape=[s if isinstance(s, jax.ShapeDtypeStruct)...  6.75 us
    ppermute x7, starting transfers between devices, peer(): lax.ppermute(x, ('mem', 'orb'), [(t, t ^ k) for t in range(group)])  6.44 us
    ppermute x7, waiting for transfers between devices, peer(): lax.ppermute(x, ('mem', 'orb'), [(t, t ^ k) for t in range(group)])  6.42 us
    ppermute x2, starting transfers between devices, per_device(): rb = lax.ppermute(b, grid_axes, cross)  5.91 us
    ppermute x2, waiting for transfers between devices, per_device(): rlo = lax.ppermute(hi, grid_axes, up)  5.08 us
    ppermute x2, starting transfers between devices, per_device(): ra = lax.ppermute(a, grid_axes, swap)  3.77 us
  transfers between devices with their start and end apart: 18, of which 11 were waited for; matrix products, arithmetic and copies ran while one was open for 0% of the time, Pallas kernels for 6%

profile of v12, /device:TPU:0, one launch (start us, length us, event | category | flops | bytes accessed | tf_op | source)
XLA Modules:
  0.0 68.6 jit_solution(14350304027790809617)
XLA Ops:
  0.6 1.2 %constant_dynamic-slice_fusion = (f32[1,8,32,128]{3,2,1,0:T(8,128)S(1)}, f32[1,8,32,128]{3,2,1,0:T(8,128)S(1)}, f32[1,8,32,128]{3,2,1,0:T(8,128)S(1)}, f32[1,8,32,128]{3,2,1,0:T(8,128)S(1)}) fusion(f32[4,8,32,128]{3,2,1,0:T(8,128)} %param.2, s32[]{:T(128)S(6)} %select_n.34, s32[]{:T(128)S(6)} %select_n.30, s32[]{:T(128)S(6)} %select_n.29, s32[]{:T(128)S(6)} %select_n.31), kind=kLoop, calls=%fused_computation.5 | loop fusion | bytes 1048592 | tf_op jit(solution)/shard_map/dynamic_slice | solution.py:278
  1.9 3.0 %collective-permute-start.3 = (f32[1,16,32,128]{3,2,1,0:T(8,128)S(1)}, f32[1,16,32,128]{3,2,1,0:T(8,128)S(1)}, u32[]{:S(2)}, u32[]{:S(2)}) collective-permute-start(f32[1,16,32,128]{3,2,1,0:T(8,128)S(1)} %pad_maximum_fusion), channel_id=1, source_target_pairs={{0,4},{4,0},{8,12},{12,8},{16,20},{20,16},{24,28},{28,24},{1,5},{5... | collective-permute-start | bytes 786440 | tf_op jit(solution)/shard_map/ppermute | solution.py:282
  4.9 3.6 %collective-permute-start.4 = (f32[1,12,32,128]{3,2,1,0:T(8,128)S(1)}, f32[1,12,32,128]{3,2,1,0:T(8,128)S(1)}, u32[]{:S(2)}, u32[]{:S(2)}) collective-permute-start(f32[1,12,32,128]{3,2,1,0:T(8,128)S(1)} %get-tuple-element.57), channel_id=1, source_target_pairs={{0,28},{4,8},{8,4},{12,16},{16,12},{20,24},{24,20},{28,0},{1,29},{... | collective-permute-start | bytes 589832 | tf_op jit(solution)/shard_map/ppermute | solution.py:283
  9.0 2.3 %collective-permute-start.1 = (f32[1,8,32,128]{3,2,1,0:T(8,128)S(1)}, f32[1,8,32,128]{3,2,1,0:T(8,128)S(1)}, u32[]{:S(2)}, u32[]{:S(2)}) collective-permute-start(f32[1,8,32,128]{3,2,1,0:T(8,128)S(1)} %get-tuple-element.54), channel_id=1, source_target_pairs={{0,28},{4,8},{8,4},{12,16},{16,12},{20,24},{24,20},{28,0},{1,29},{... | collective-permute-start | bytes 393224 | tf_op jit(solution)/shard_map/ppermute | solution.py:283
  12.0 3.5 %collective-permute-done.4.rb = f32[1,12,32,128]{3,2,1,0:T(8,128)S(1)} collective-permute-done((f32[1,12,32,128]{3,2,1,0:T(8,128)S(1)}, f32[1,12,32,128]{3,2,1,0:T(8,128)S(1)}, u32[]{:S(2)}, u32[]{:S(2)}) %collective-permute-start.4) | collective-permute-done | bytes 196640 | tf_op jit(solution)/shard_map/ppermute | solution.py:283
  15.6 1.8 %collective-permute-start.2 = (f32[1,8,32,128]{3,2,1,0:T(8,128)S(1)}, f32[1,8,32,128]{3,2,1,0:T(8,128)S(1)}, u32[]{:S(2)}, u32[]{:S(2)}) collective-permute-start(f32[1,8,32,128]{3,2,1,0:T(8,128)S(1)} %get-tuple-element.55.mine), channel_id=1, source_target_pairs={{0,24},{4,12},{8,0},{12,20},{16,8},{20,28},{24,16},{28,4},{1,25},{... | collective-permute-start | bytes 393224 | tf_op jit(solution)/shard_map/ppermute | solution.py:284
  18.5 1.0 %filter_1_2.2 = (f32[1,16,32,128]{3,2,1,0:T(8,128)S(1)}, f32[1,8,32,128]{3,2,1,0:T(8,128)S(1)}, f32[1,20,32,128]{3,2,1,0:T(8,128)S(1)}, f32[24,32,128]{2,1,0:T(8,128)S(1)}) custom-call(bf16[128,384]{1,0:T(8,128)(2,1)S(1)} %get-tuple-element.28.ymat, bf16[384,128]{1,0:T(8,128)(2,1)S(1)} %get-tuple-element.29.zmat, ...), custom_call_target="tpu_custom_call" | custom-call | flops 1000000000 | bytes 3500000 | tf_op jit(solution)/shard_map/filter_1_2/pallas_call | solution.py:238
  19.5 1.6 %collective-permute-start.9 = (f32[1,8,32,128]{3,2,1,0:T(8,128)S(1)}, f32[1,8,32,128]{3,2,1,0:T(8,128)S(1)}, u32[]{:S(2)}, u32[]{:S(2)}) collective-permute-start(f32[1,8,32,128]{3,2,1,0:T(8,128)S(1)} %get-tuple-element.35.hi), channel_id=1, source_target_pairs={{0,8},{4,12},{8,16},{12,20},{16,24},{20,28},{24,0},{28,4},{1,9},{5... | collective-permute-start | bytes 393224 | tf_op jit(solution)/shard_map/ppermute | solution.py:302
  21.0 2.5 %collective-permute-start.8 = (f32[1,16,32,128]{3,2,1,0:T(8,128)S(1)}, f32[1,16,32,128]{3,2,1,0:T(8,128)S(1)}, u32[]{:S(2)}, u32[]{:S(2)}) collective-permute-start(f32[1,16,32,128]{3,2,1,0:T(8,128)S(1)} %get-tuple-element.34.lo), channel_id=1, source_target_pairs={{0,24},{4,28},{8,0},{12,4},{16,8},{20,12},{24,16},{28,20},{1,25},{... | collective-permute-start | bytes 786440 | tf_op jit(solution)/shard_map/ppermute | solution.py:303
  24.7 4.3 %collective-permute-start.7 = (f32[1,12,32,128]{3,2,1,0:T(8,128)S(1)}, f32[1,12,32,128]{3,2,1,0:T(8,128)S(1)}, u32[]{:S(2)}, u32[]{:S(2)}) collective-permute-start(f32[1,12,32,128]{3,2,1,0:T(8,128)S(1)} %get-tuple-element.32.lo), channel_id=1, source_target_pairs={{0,24},{4,28},{8,0},{12,4},{16,8},{20,12},{24,16},{28,20},{1,25},{... | collective-permute-start | bytes 589832 | tf_op jit(solution)/shard_map/ppermute | solution.py:303
  29.1 3.1 %collective-permute-done.8.rhi.v_above = f32[1,16,32,128]{3,2,1,0:T(8,128)S(1)} collective-permute-done((f32[1,16,32,128]{3,2,1,0:T(8,128)S(1)}, f32[1,16,32,128]{3,2,1,0:T(8,128)S(1)}, u32[]{:S(2)}, u32[]{:S(2)}) %collective-permute-start.8) | collective-permute-done | bytes 262176 | tf_op jit(solution)/shard_map/ppermute | solution.py:303
  32.2 1.4 %filter_3_4_hamiltonian.2 = (f32[2,8,32,128]{3,2,1,0:T(8,128)S(1)}, f32[8,2,2,32,128]{4,3,2,1,0:T(8,128)S(1)}) custom-call(bf16[128,384]{1,0:T(8,128)(2,1)S(1)} %get-tuple-element.28.ymat, bf16[384,128]{1,0:T(8,128)(2,1)S(1)} %get-tuple-element.29.zmat, f32[1,8,32,128]{3,2,1,0:T(8,128)S(1)} %collective-permute-done.9.rlo, ...), custom_call_target="tpu_custom_call" | custom-call | flops 1500000000 | bytes 5250000 | tf_op jit(solution)/shard_map/filter_3_4_hamiltonian/pallas_call | solution.py:238
  33.6 5.1 %collective-permute-done.6.rlo = f32[1,8,32,128]{3,2,1,0:T(8,128)S(1)} collective-permute-done((f32[1,8,32,128]{3,2,1,0:T(8,128)S(1)}, f32[1,8,32,128]{3,2,1,0:T(8,128)S(1)}, u32[]{:S(2)}, u32[]{:S(2)}) %collective-permute-start.6) | collective-permute-done | bytes 131104 | tf_op jit(solution)/shard_map/ppermute | solution.py:302
  38.7 1.4 %filter_3_4_hamiltonian.3 = (f32[2,8,32,128]{3,2,1,0:T(8,128)S(1)}, f32[2,8,32,128]{3,2,1,0:T(8,128)S(1)}, f32[2,2,2,32,128]{4,3,2,1,0:T(8,128)S(1)}, f32[2,2,2,...) custom-call(bf16[128,384]{1,0:T(8,128)(2,1)S(1)} %get-tuple-element., ...), custom_call_target="tpu_custom_call" | custom-call | flops 1500000000 | bytes 5250000 | tf_op jit(solution)/shard_map/filter_3_4_hamiltonian/pallas_call | solution.py:238
  40.1 2.3 %collective-permute-start.10 = (f32[2,2,2,32,128]{4,3,2,1,0:T(8,128)S(1)}, f32[2,2,2,32,128]{4,3,2,1,0:T(8,128)S(1)}, u32[]{:S(2)}, u32[]{:S(2)}) collective-permute-start(f32[2,2,2,32,128]{4,3,2,1,0:T(8,128)S(1)} %get-tuple-element.41), channel_id=1, source_target_pairs={{0,6},{1,7},{2,4},{3,5},{4,2},{5,3},{6,0},{7,1},{8,14},{9,15},{10,... | collective-permute-start | bytes 393224 | tf_op jit(solution)/shard_map/ppermute | solution.py:312
  43.6 2.7 %collective-permute-start.14 = (f32[2,2,2,32,128]{4,3,2,1,0:T(8,128)S(1)}, f32[2,2,2,32,128]{4,3,2,1,0:T(8,128)S(1)}, u32[]{:S(2)}, u32[]{:S(2)}) collective-permute-start(f32[2,2,2,32,128]{4,3,2,1,0:T(8,128)S(1)} %get-tuple-element.45), channel_id=1, source_target_pairs={{0,5},{1,4},{2,7},{3,6},{4,1},{5,0},{6,3},{7,2},{8,13},{9,12},{10,... | collective-permute-start | bytes 393224 | tf_op jit(solution)/shard_map/ppermute | solution.py:312
  46.3 1.2 %collective-permute-done.11.refs_1_ = f32[2,2,2,32,128]{4,3,2,1,0:T(8,128)S(1)} collective-permute-done((f32[2,2,2,32,128]{4,3,2,1,0:T(8,128)S(1)}, f32[2,2,2,32,128]{4,3,2,1,0:T(8,128)S(1)}, u32[]{:S(2)}, u32[]{:S(2)}) %collective-permute-start.11) | collective-permute-done | bytes 131104 | tf_op jit(solution)/shard_map/ppermute | solution.py:312
  47.7 1.1 %collective-permute-done.12.refs_2_ = f32[2,2,2,32,128]{4,3,2,1,0:T(8,128)S(1)} collective-permute-done((f32[2,2,2,32,128]{4,3,2,1,0:T(8,128)S(1)}, f32[2,2,2,32,128]{4,3,2,1,0:T(8,128)S(1)}, u32[]{:S(2)}, u32[]{:S(2)}) %collective-permute-start.12) | collective-permute-done | bytes 131104 | tf_op jit(solution)/shard_map/ppermute | solution.py:312
  48.8 1.6 %collective-permute-done.13.refs_3_ = f32[2,2,2,32,128]{4,3,2,1,0:T(8,128)S(1)} collective-permute-done((f32[2,2,2,32,128]{4,3,2,1,0:T(8,128)S(1)}, f32[2,2,2,32,128]{4,3,2,1,0:T(8,128)S(1)}, u32[]{:S(2)}, u32[]{:S(2)}) %collective-permute-start.13) | collective-permute-done | bytes 131104 | tf_op jit(solution)/shard_map/ppermute | solution.py:312
  50.4 1.5 %collective-permute-done.14.refs_4_ = f32[2,2,2,32,128]{4,3,2,1,0:T(8,128)S(1)} collective-permute-done((f32[2,2,2,32,128]{4,3,2,1,0:T(8,128)S(1)}, f32[2,2,2,32,128]{4,3,2,1,0:T(8,128)S(1)}, u32[]{:S(2)}, u32[]{:S(2)}) %collective-permute-start.14) | collective-permute-done | bytes 131104 | tf_op jit(solution)/shard_map/ppermute | solution.py:312
  51.9 1.0 %collective-permute-done.15.refs_5_ = f32[2,2,2,32,128]{4,3,2,1,0:T(8,128)S(1)} collective-permute-done((f32[2,2,2,32,128]{4,3,2,1,0:T(8,128)S(1)}, f32[2,2,2,32,128]{4,3,2,1,0:T(8,128)S(1)}, u32[]{:S(2)}, u32[]{:S(2)}) %collective-permute-start.15) | collective-permute-done | bytes 131104 | tf_op jit(solution)/shard_map/ppermute | solution.py:312
  52.9 1.1 %gram.1 = f32[32,1,128]{2,1,0:T(1,128)S(1)} custom-call(f32[2,2,2,32,128]{4,3,2,1,0:T(8,128)S(1)} %collective-permute-done.10.refs_0_, f32[2,2,2,32,128]{4,3,2,1,0:T(8,128)S(1)} %collective-permute-done.11.refs_1_, f32[2,2,2,32,128]{4,3,2,1,0:T(8,128)S(1)} %collective-permute-done.12.refs_2_, f32[2,2,2,32,128]{4,3,2,1,0:T(8,128)S(1)} %collective-permute-done.13.refs_3_, ...), custom_call_target="tpu_custom_call" | custom-call | flops 1300000000 | bytes 4550000 | tf_op jit(solution)/shard_map/gram/pallas_call | solution.py:238
  54.0 1.1 %collective-permute-start.17 = (f32[2,8,32,128]{3,2,1,0:T(8,128)S(1)}, f32[2,8,32,128]{3,2,1,0:T(8,128)S(1)}, u32[]{:S(2)}, u32[]{:S(2)}) collective-permute-start(f32[2,8,32,128]{3,2,1,0:T(8,128)S(1)} %get-tuple-element.49), channel_id=1, source_target_pairs={{0,4},{4,0},{8,12},{12,8},{16,20},{20,16},{24,28},{28,24},{1,5},{5... | collective-permute-start | bytes 786440 | tf_op jit(solution)/shard_map/ppermute | solution.py:328
  55.1 11.9 %all_to_all.5.x_ref = f32[32,1,128]{2,1,0:T(1,128)S(1)} all-to-all(f32[32,1,128]{2,1,0:T(1,128)S(1)} %gram.1), channel_id=1, replica_groups=mesh['pair'=4,'mem'=2,'orb'=4] {'pair','mem','orb'}, dimensions={0} | all-to-all | bytes 32768 | tf_op jit(solution)/shard_map/all_to_all | solution.py:329
  (27 shorter events, 6.6 us)
Async XLA Ops:
  0.6 1.2 %copy-start = (f32[8,32,128]{2,1,0:T(8,128)S(1)}, f32[8,32,128]{2,1,0:T(8,128)}, u32[]{:S(2)}) copy-start(f32[8,32,128]{2,1,0:T(8,128)} %refs_0_.1) | copy-start | bytes 393220
  1.9 16.6 %collective-permute-start.3 = (f32[1,16,32,128]{3,2,1,0:T(8,128)S(1)}, f32[1,16,32,128]{3,2,1,0:T(8,128)S(1)}, u32[]{:S(2)}, u32[]{:S(2)}) collective-permute-start(f32[1,16,32,128]{3,2,1,0:T(8,128)S(1)} %pad_maximum_fusion), channel_id=1, source_target_pairs={{0,4},{4,0},{8,12},{12,8},{16,20},{20,16},{24,28},{28,24},{1,5},{5... | collective-permute-start | bytes 786440 | tf_op jit(solution)/shard_map/ppermute | solution.py:282
  4.9 10.6 %collective-permute-start.4 = (f32[1,12,32,128]{3,2,1,0:T(8,128)S(1)}, f32[1,12,32,128]{3,2,1,0:T(8,128)S(1)}, u32[]{:S(2)}, u32[]{:S(2)}) collective-permute-start(f32[1,12,32,128]{3,2,1,0:T(8,128)S(1)} %get-tuple-element.57), channel_id=1, source_target_pairs={{0,28},{4,8},{8,4},{12,16},{16,12},{20,24},{24,20},{28,0},{1,29},{... | collective-permute-start | bytes 589832 | tf_op jit(solution)/shard_map/ppermute | solution.py:283
  8.6 9.6 %collective-permute-start.5 = (f32[1,12,32,128]{3,2,1,0:T(8,128)S(1)}, f32[1,12,32,128]{3,2,1,0:T(8,128)S(1)}, u32[]{:S(2)}, u32[]{:S(2)}) collective-permute-start(f32[1,12,32,128]{3,2,1,0:T(8,128)S(1)} %get-tuple-element.58.mine), channel_id=1, source_target_pairs={{0,24},{4,12},{8,0},{12,20},{16,8},{20,28},{24,16},{28,4},{1,25},{... | collective-permute-start | bytes 589832 | tf_op jit(solution)/shard_map/ppermute | solution.py:284
  9.0 14.6 %collective-permute-start.1 = (f32[1,8,32,128]{3,2,1,0:T(8,128)S(1)}, f32[1,8,32,128]{3,2,1,0:T(8,128)S(1)}, u32[]{:S(2)}, u32[]{:S(2)}) collective-permute-start(f32[1,8,32,128]{3,2,1,0:T(8,128)S(1)} %get-tuple-element.54), channel_id=1, source_target_pairs={{0,28},{4,8},{8,4},{12,16},{16,12},{20,24},{24,20},{28,0},{1,29},{... | collective-permute-start | bytes 393224 | tf_op jit(solution)/shard_map/ppermute | solution.py:283
  11.3 12.3 %collective-permute-start = (f32[1,8,32,128]{3,2,1,0:T(8,128)S(1)}, f32[1,8,32,128]{3,2,1,0:T(8,128)S(1)}, u32[]{:S(2)}, u32[]{:S(2)}) collective-permute-start(f32[1,8,32,128]{3,2,1,0:T(8,128)S(1)} %get-tuple-element.54), channel_id=1, source_target_pairs={{0,4},{4,0},{8,12},{12,8},{16,20},{20,16},{24,28},{28,24},{1,5},{5... | collective-permute-start | bytes 393224 | tf_op jit(solution)/shard_map/ppermute | solution.py:282
  15.6 8.2 %collective-permute-start.2 = (f32[1,8,32,128]{3,2,1,0:T(8,128)S(1)}, f32[1,8,32,128]{3,2,1,0:T(8,128)S(1)}, u32[]{:S(2)}, u32[]{:S(2)}) collective-permute-start(f32[1,8,32,128]{3,2,1,0:T(8,128)S(1)} %get-tuple-element.55.mine), channel_id=1, source_target_pairs={{0,24},{4,12},{8,0},{12,20},{16,8},{20,28},{24,16},{28,4},{1,25},{... | collective-permute-start | bytes 393224 | tf_op jit(solution)/shard_map/ppermute | solution.py:284
  19.5 9.6 %collective-permute-start.9 = (f32[1,8,32,128]{3,2,1,0:T(8,128)S(1)}, f32[1,8,32,128]{3,2,1,0:T(8,128)S(1)}, u32[]{:S(2)}, u32[]{:S(2)}) collective-permute-start(f32[1,8,32,128]{3,2,1,0:T(8,128)S(1)} %get-tuple-element.35.hi), channel_id=1, source_target_pairs={{0,8},{4,12},{8,16},{12,20},{16,24},{20,28},{24,0},{28,4},{1,9},{5... | collective-permute-start | bytes 393224 | tf_op jit(solution)/shard_map/ppermute | solution.py:302
  21.0 11.2 %collective-permute-start.8 = (f32[1,16,32,128]{3,2,1,0:T(8,128)S(1)}, f32[1,16,32,128]{3,2,1,0:T(8,128)S(1)}, u32[]{:S(2)}, u32[]{:S(2)}) collective-permute-start(f32[1,16,32,128]{3,2,1,0:T(8,128)S(1)} %get-tuple-element.34.lo), channel_id=1, source_target_pairs={{0,24},{4,28},{8,0},{12,4},{16,8},{20,12},{24,16},{28,20},{1,25},{... | collective-permute-start | bytes 786440 | tf_op jit(solution)/shard_map/ppermute | solution.py:303
  24.7 13.9 %collective-permute-start.7 = (f32[1,12,32,128]{3,2,1,0:T(8,128)S(1)}, f32[1,12,32,128]{3,2,1,0:T(8,128)S(1)}, u32[]{:S(2)}, u32[]{:S(2)}) collective-permute-start(f32[1,12,32,128]{3,2,1,0:T(8,128)S(1)} %get-tuple-element.32.lo), channel_id=1, source_target_pairs={{0,24},{4,28},{8,0},{12,4},{16,8},{20,12},{24,16},{28,20},{1,25},{... | collective-permute-start | bytes 589832 | tf_op jit(solution)/shard_map/ppermute | solution.py:303
  29.1 9.6 %collective-permute-start.6 = (f32[1,8,32,128]{3,2,1,0:T(8,128)S(1)}, f32[1,8,32,128]{3,2,1,0:T(8,128)S(1)}, u32[]{:S(2)}, u32[]{:S(2)}) collective-permute-start(f32[1,8,32,128]{3,2,1,0:T(8,128)S(1)} %get-tuple-element.31.hi), channel_id=1, source_target_pairs={{0,8},{4,12},{8,16},{12,20},{16,24},{20,28},{24,0},{28,4},{1,9},{5... | collective-permute-start | bytes 393224 | tf_op jit(solution)/shard_map/ppermute | solution.py:302
  40.1 6.2 %collective-permute-start.10 = (f32[2,2,2,32,128]{4,3,2,1,0:T(8,128)S(1)}, f32[2,2,2,32,128]{4,3,2,1,0:T(8,128)S(1)}, u32[]{:S(2)}, u32[]{:S(2)}) collective-permute-start(f32[2,2,2,32,128]{4,3,2,1,0:T(8,128)S(1)} %get-tuple-element.41), channel_id=1, source_target_pairs={{0,6},{1,7},{2,4},{3,5},{4,2},{5,3},{6,0},{7,1},{8,14},{9,15},{10,... | collective-permute-start | bytes 393224 | tf_op jit(solution)/shard_map/ppermute | solution.py:312
  42.4 5.1 %collective-permute-start.11 = (f32[2,2,2,32,128]{4,3,2,1,0:T(8,128)S(1)}, f32[2,2,2,32,128]{4,3,2,1,0:T(8,128)S(1)}, u32[]{:S(2)}, u32[]{:S(2)}) collective-permute-start(f32[2,2,2,32,128]{4,3,2,1,0:T(8,128)S(1)} %get-tuple-element.42), channel_id=1, source_target_pairs={{0,4},{1,5},{2,6},{3,7},{4,0},{5,1},{6,2},{7,3},{8,12},{9,13},{10,... | collective-permute-start | bytes 393224 | tf_op jit(solution)/shard_map/ppermute | solution.py:312
  43.1 5.7 %collective-permute-start.12 = (f32[2,2,2,32,128]{4,3,2,1,0:T(8,128)S(1)}, f32[2,2,2,32,128]{4,3,2,1,0:T(8,128)S(1)}, u32[]{:S(2)}, u32[]{:S(2)}) collective-permute-start(f32[2,2,2,32,128]{4,3,2,1,0:T(8,128)S(1)} %get-tuple-element.43), channel_id=1, source_target_pairs={{0,2},{1,3},{2,0},{3,1},{4,6},{5,7},{6,4},{7,5},{8,10},{9,11},{10,... | collective-permute-start | bytes 393224 | tf_op jit(solution)/shard_map/ppermute | solution.py:312
  43.6 6.8 %collective-permute-start.13 = (f32[2,2,2,32,128]{4,3,2,1,0:T(8,128)S(1)}, f32[2,2,2,32,128]{4,3,2,1,0:T(8,128)S(1)}, u32[]{:S(2)}, u32[]{:S(2)}) collective-permute-start(f32[2,2,2,32,128]{4,3,2,1,0:T(8,128)S(1)} %get-tuple-element.44), channel_id=1, source_target_pairs={{0,7},{1,6},{2,5},{3,4},{4,3},{5,2},{6,1},{7,0},{8,15},{9,14},{10,... | collective-permute-start | bytes 393224 | tf_op jit(solution)/shard_map/ppermute | solution.py:312
  43.6 8.3 %collective-permute-start.14 = (f32[2,2,2,32,128]{4,3,2,1,0:T(8,128)S(1)}, f32[2,2,2,32,128]{4,3,2,1,0:T(8,128)S(1)}, u32[]{:S(2)}, u32[]{:S(2)}) collective-permute-start(f32[2,2,2,32,128]{4,3,2,1,0:T(8,128)S(1)} %get-tuple-element.45), channel_id=1, source_target_pairs={{0,5},{1,4},{2,7},{3,6},{4,1},{5,0},{6,3},{7,2},{8,13},{9,12},{10,... | collective-permute-start | bytes 393224 | tf_op jit(solution)/shard_map/ppermute | solution.py:312
  46.3 6.6 %collective-permute-start.15 = (f32[2,2,2,32,128]{4,3,2,1,0:T(8,128)S(1)}, f32[2,2,2,32,128]{4,3,2,1,0:T(8,128)S(1)}, u32[]{:S(2)}, u32[]{:S(2)}) collective-permute-start(f32[2,2,2,32,128]{4,3,2,1,0:T(8,128)S(1)} %get-tuple-element.46), channel_id=1, source_target_pairs={{0,3},{1,2},{2,1},{3,0},{4,7},{5,6},{6,5},{7,4},{8,11},{9,10},{10,... | collective-permute-start | bytes 393224 | tf_op jit(solution)/shard_map/ppermute | solution.py:312
  47.5 5.4 %collective-permute-start.16 = (f32[2,2,2,32,128]{4,3,2,1,0:T(8,128)S(1)}, f32[2,2,2,32,128]{4,3,2,1,0:T(8,128)S(1)}, u32[]{:S(2)}, u32[]{:S(2)}) collective-permute-start(f32[2,2,2,32,128]{4,3,2,1,0:T(8,128)S(1)} %get-tuple-element.47), channel_id=1, source_target_pairs={{0,1},{1,0},{2,3},{3,2},{4,5},{5,4},{6,7},{7,6},{8,9},{9,8},{10,11... | collective-permute-start | bytes 393224 | tf_op jit(solution)/shard_map/ppermute | solution.py:312
  54.0 13.7 %collective-permute-start.17 = (f32[2,8,32,128]{3,2,1,0:T(8,128)S(1)}, f32[2,8,32,128]{3,2,1,0:T(8,128)S(1)}, u32[]{:S(2)}, u32[]{:S(2)}) collective-permute-start(f32[2,8,32,128]{3,2,1,0:T(8,128)S(1)} %get-tuple-element.49), channel_id=1, source_target_pairs={{0,4},{4,0},{8,12},{12,8},{16,20},{20,16},{24,28},{28,24},{1,5},{5... | collective-permute-start | bytes 786440 | tf_op jit(solution)/shard_map/ppermute | solution.py:328
